TPU v7x, 32 devices: a whole 2x2x4 slice. The times are simulated.
32 devices in a mesh: layer: 4 (over y, x), row: 2 (over core), col: 4 (over z).
Axes of the slice: x: 2, y: 2, z: 4, core: 2. Of those that a mesh axis runs over, the one named last changes fastest.
Arguments:
- left_values: bfloat16 [4096, 4, 1024], P('row', 'layer', 'col'), may hold values from -22 to 22
- left_pattern: int32 [16, 4, 4], P('row', 'layer', 'col'), may hold values from 0 to 1, as said below
- right_values: bfloat16 [4096, 4, 1024], P(('layer', 'row'), None, 'col'), may hold values from -6 to 6
- right_pattern: int32 [16, 4, 4], P(('layer', 'row'), None, 'col'), may hold values from 0 to 1, as said below
Outputs:
- expanded: bfloat16 [4096, 4, 1024], P('row', 'layer', 'col')
Inputs may be any that keep to these rules, and one draw needn't show every extreme that they name: `left_pattern`: 1 marks a stored tile, 0 an absent one. `right_pattern`: 1 marks a stored tile, 0 an absent one.
All inputs are finite; a program needn't handle non-finite values.
Results may differ from a plain program's by a relative error of at most 0.001.
Values may be sent and summed in bfloat16 or wider, within the bound.
No kernel may reach another device: no remote copies, remote signals or barrier semaphores. Data moves between devices by JAX's collectives and lax.ppermute only.
A program may use at most 64 MiB of HBM per device.

v0:
```python
import jax
import jax.numpy as jnp
from jax import lax
from jax.sharding import PartitionSpec as P


def expand_tiles(values, pattern):
    tile_rows, layers, tile_cols = pattern.shape
    tile_size = values.shape[0] // tile_rows
    blocks = values.reshape(tile_rows, tile_size, layers, tile_cols, tile_size)
    blocks = blocks * pattern[:, None, :, :, None].astype(values.dtype)
    return blocks.reshape(values.shape)


def per_device(left_values, left_pattern, right_values, right_pattern):
    left_block = expand_tiles(left_values, left_pattern)
    right_block = expand_tiles(right_values, right_pattern)
    rows_local = left_block.shape[0]
    columns_local = left_block.shape[2]
    left_flat = left_block.reshape(rows_local, columns_local)
    right_rows = lax.all_gather(right_block, "row", axis=0, tiled=True)
    right_mine = lax.all_to_all(right_rows, "layer", split_axis=1, concat_axis=0, tiled=True)
    right_mine = right_mine.reshape(right_mine.shape[0], columns_local)
    product = jnp.dot(
        lax.all_gather(left_flat, ("layer", "col"), axis=1, tiled=True),
        right_mine,
        preferred_element_type=jnp.float32,
    )
    product = product.reshape(rows_local, 1, columns_local)
    squared = product * product
    column = lax.psum(jnp.sum(squared, axis=0, keepdims=True), "row")
    rows_total = rows_local * lax.axis_size("row")
    colmean = column / rows_total
    return (squared / (colmean + 1e-06)).astype(jnp.bfloat16)


def solution(mesh):
    return jax.shard_map(
        per_device,
        mesh=mesh,
        in_specs=(
            P("row", "layer", "col"),
            P("row", "layer", "col"),
            P(("layer", "row"), None, "col"),
            P(("layer", "row"), None, "col"),
        ),
        out_specs=P("row", "layer", "col"),
        check_vma=False,
    )
```

profile of v0, /device:TPU:0, one launch (start us, length us, event | category | flops | bytes accessed | tf_op | source)
XLA Modules:
  0.0 296.3 jit_solution(11809781176042015441)
XLA Ops:
  6.5 0.0 copy-start.1
  6.5 0.0 copy-start
  6.5 0.0 all-gather.5.cloned.1.call-start
  6.5 0.8 convert_element_type.30
  7.3 0.1 copy.7
  7.4 0.1 broadcast_bitcast_fusion
  7.5 2.6 copy_multiply_fusion
  10.1 0.0 all-gather.5.cloned.1.call-update
  10.1 0.0 all-gather.3.cloned.1.call-start
  10.1 0.0 copy-done.1
  10.2 0.1 broadcast_bitcast_fusion.1
  10.2 0.0 copy-done
  10.3 1.3 bitcast_multiply_fusion
  11.6 0.0 all-gather.3.cloned.1.call-update
  11.6 11.9 %all-gather.5.cloned.1.call-done = bf16[1024,4,256]{2,0,1:T(8,128)(2,1)} async-done(((bf16[512,4,256]{2,0,1:T(8,128)(2,1)}), bf16[1024,4,256]{2,0,1:T(8,128)(2,1)}) %all-gather.5.cloned.1.call-update) | async-done | bytes 2097168 | tf_op jit(solution)/shard_map/all_gather | solution.py:21
  23.5 41.0 %all_to_all.15 = bf16[1024,4,256]{2,0,1:T(8,128)(2,1)S(1)} all-to-all(bf16[1024,4,256]{2,0,1:T(8,128)(2,1)} %all-gather.5.cloned.1.call-done), channel_id=1, replica_groups=mesh['layer'=4,'row'=2,'col'=4] {'layer'}, dimensions={1} | all-to-all | bytes 4194304 | tf_op jit(solution)/shard_map/all_to_all | solution.py:22
  64.5 210.0 %all-gather.3.cloned.1.call-done = bf16[2048,4096]{1,0:T(8,128)(2,1)} async-done(((bf16[2048,256]{1,0:T(8,128)(2,1)}), bf16[2048,4096]{1,0:T(8,128)(2,1)}) %all-gather.3.cloned.1.call-update) | async-done | bytes 16777232 | tf_op jit(solution)/shard_map/all_gather | solution.py:25
  274.5 9.8 %fusion.1 = (f32[256]{0:T(256)S(1)}, f32[2048,256]{1,0:T(8,128)}) fusion(bf16[2048,4096]{1,0:T(8,128)(2,1)} %all-gather.3.cloned.1.call-done, bf16[4096,256]{1,0:T(8,128)(2,1)S(1)} %bitcast.24), kind=kOutput, calls=%fused_computation.9 | convolution fusion | flops 4296015872 | bytes 20972544 | tf_op jit(solution)/shard_map/dot_general | solution.py:24
  284.3 2.4 psum.7
  286.7 2.7 fusion
  (4 shorter events, 0.0 us)
Async XLA Ops:
  6.5 3.6 %copy-start.1 = (s32[8,1,1]{0,2,1:T(1,128)S(1)}, s32[8,1,1]{0,2,1:T(1,128)}, u32[]{:S(2)}) copy-start(s32[8,1,1]{0,2,1:T(1,128)} %param.5) | copy-start | bytes 100
  6.5 3.7 %copy-start = (bf16[2048,1,256]{2,0,1:T(8,128)(2,1)S(1)}, bf16[2048,1,256]{2,0,1:T(8,128)(2,1)}, u32[]{:S(2)}) copy-start(bf16[2048,1,256]{2,0,1:T(8,128)(2,1)} %param.4) | copy-start | bytes 3145732
  6.5 17.0 %all-gather.5.cloned.1.call-start = ((), (), s32[]{:S(2)}) async-start(), calls=%async_computation.2 | async-start | bytes 3145728 | tf_op jit(solution)/shard_map/all_gather | solution.py:21
  10.1 264.4 %all-gather.3.cloned.1.call-start = ((), (), s32[]{:S(2)}) async-start(), calls=%async_computation.1 | async-start | bytes 17825792 | tf_op jit(solution)/shard_map/all_gather | solution.py:25
Sparse Core Ops, SparseCore 0:
  10.2 13.2 all-gather.4
  26.3 248.2 all-gather.2
where the time goes:
time: 297 us; the launch traced here: 296 us
  waiting for transfers between devices  222 us (75%)
  blocking collectives  43.4 us (15%)
  between operations  13.4 us (5%)
  matrix products  9.77 us (3%)
  other arithmetic  7.38 us (2%)
    all_gather x1, waiting for transfers between devices, per_device(): lax.all_gather(left_flat, ('layer', 'col'), axis=1, tiled=True)  210 us
    all_to_all x1, blocking collectives, per_device(): lax.all_to_all(right_rows, 'layer', split_axis=1, concat_axis=0, tiled=True)  41 us
    all_gather x1, waiting for transfers between devices, per_device(): right_rows = lax.all_gather(right_block, 'row', axis=0, tiled=True)  11.9 us
    dot_general x1, matrix products, per_device(): jnp.dot(lax.all_gather(left_flat, ('layer', 'col'), axis=1, tiled=True),...  9.77 us
  transfers between devices with their start and end apart: 2, of which 2 were waited for; matrix products, arithmetic and copies ran while one was open for 0% of the time, Pallas kernels for 0%

commit v1 on v0

v1 whole, which is shorter than its diff:
```python
import functools

import jax
import jax.numpy as jnp
from jax import lax
from jax.experimental import pallas as pl
from jax.experimental.pallas import tpu as pltpu
from jax.sharding import PartitionSpec as P

TILE = 256
CHUNKS = 4
SCALE_ROWS = 16
CODE = 64.0
TOP = 32767.0
LEAST = 2.0**-100
VMEM = pl.BlockSpec(memory_space=pltpu.VMEM)
PARAMS = pltpu.CompilerParams(vmem_limit_bytes=40 * 1024 * 1024)


def partial_kernel(n_sources, n_layers, where, *refs):
    lefts = refs[:n_sources]
    right_ref, mine_ref, sent_ref = refs[n_sources:]
    rows = lefts[0].shape[0]
    for step in range(n_layers):
        layer = where[0] ^ step
        total = jnp.zeros((rows, right_ref.shape[3]), jnp.float32)
        for source in range(n_sources):
            start = pl.multiple_of(where[2 + 2 * source], TILE)
            total += jnp.dot(
                lefts[source][...],
                right_ref[where[1 + 2 * source], layer, pl.ds(start, TILE), :],
                preferred_element_type=jnp.float32,
            )
        if step == 0:
            mine_ref[...] = total
            continue
        top = jnp.maximum(jnp.max(jnp.abs(total), axis=0, keepdims=True), LEAST)
        code = jnp.ceil(jnp.log2(top) * CODE + 0.01)
        unit = jnp.exp2(code / -CODE) * TOP
        fixed = jnp.round(total * unit).astype(jnp.int32)
        sent_ref[step - 1, :rows, :] = fixed.astype(jnp.int16)
        codes = jnp.broadcast_to(code.astype(jnp.int32), (SCALE_ROWS, code.shape[1]))
        sent_ref[step - 1, rows:, :] = codes.astype(jnp.int16)


def partial_products(where, lefts, right, n_layers):
    rows, columns = lefts[0].shape[0], right.shape[3]
    return pl.pallas_call(
        functools.partial(partial_kernel, len(lefts), n_layers),
        out_shape=(
            jax.ShapeDtypeStruct((rows, columns), jnp.float32),
            jax.ShapeDtypeStruct((n_layers - 1, rows + SCALE_ROWS, columns), jnp.int16),
        ),
        in_specs=[pl.BlockSpec(memory_space=pltpu.SMEM)] + [VMEM] * (len(lefts) + 1),
        out_specs=(VMEM, VMEM),
        compiler_params=PARAMS,
        cost_estimate=pl.CostEstimate(
            flops=2 * rows * len(lefts) * TILE * columns * n_layers,
            bytes_accessed=right.size * 2 + rows * columns * 14,
            transcendentals=0,
        ),
    )(where, *lefts, right)


def combine_kernel(n_received, mine_ref, *refs):
    received, (squared_ref, sum_ref) = refs[:n_received], refs[n_received:]
    total = mine_ref[...]
    rows = total.shape[0]
    for block in received:
        code = block[rows:, :].astype(jnp.int32)[:1].astype(jnp.float32)
        unit = jnp.exp2(code / CODE) * (1.0 / TOP)
        total += block[:rows, :].astype(jnp.int32).astype(jnp.float32) * unit
    squared = total * total
    squared_ref[...] = squared
    sum_ref[...] = jnp.sum(squared, axis=0, keepdims=True)


def combine(mine, received):
    return pl.pallas_call(
        functools.partial(combine_kernel, len(received)),
        out_shape=(
            jax.ShapeDtypeStruct(mine.shape, jnp.float32),
            jax.ShapeDtypeStruct((1, mine.shape[1]), jnp.float32),
        ),
        in_specs=[VMEM] * (1 + len(received)),
        out_specs=(VMEM, VMEM),
        compiler_params=PARAMS,
        cost_estimate=pl.CostEstimate(
            flops=8 * mine.size, bytes_accessed=mine.size * 14, transcendentals=0
        ),
    )(mine, *received)


def normalise_kernel(n_chunks, rows_total, column_ref, *refs):
    chunks, out_ref = refs[:n_chunks], refs[n_chunks]
    rows = chunks[0].shape[0]
    colmean = column_ref[...] / rows_total
    for i, chunk in enumerate(chunks):
        out_ref[i * rows : (i + 1) * rows, :] = (
            chunk[...] / (colmean + 1e-06)
        ).astype(jnp.bfloat16)


def normalise(column, chunks, rows_total):
    rows, columns = chunks[0].shape
    return pl.pallas_call(
        functools.partial(normalise_kernel, len(chunks), rows_total),
        out_shape=jax.ShapeDtypeStruct((rows * len(chunks), columns), jnp.bfloat16),
        in_specs=[VMEM] * (1 + len(chunks)),
        out_specs=VMEM,
        compiler_params=PARAMS,
        cost_estimate=pl.CostEstimate(
            flops=4 * rows * columns * len(chunks),
            bytes_accessed=6 * rows * columns * len(chunks),
            transcendentals=0,
        ),
    )(column, *chunks)


def expand_tiles(values, pattern):
    tile_rows, layers, tile_cols = pattern.shape
    tile_size = values.shape[0] // tile_rows
    blocks = values.reshape(tile_rows, tile_size, layers, tile_cols, tile_size)
    blocks = blocks * pattern[:, None, :, :, None].astype(values.dtype)
    return blocks.reshape(values.shape)


def shift(x, axis, by):
    n = lax.axis_size(axis)
    return lax.ppermute(x, axis, [(i, (i + by) % n) for i in range(n)])


def per_device(left_values, left_pattern, right_values, right_pattern):
    n_layers, n_rows, n_cols = (lax.axis_size(a) for a in ("layer", "row", "col"))
    layer, row, col = (lax.axis_index(a) for a in ("layer", "row", "col"))
    rows_local, _, columns_local = left_values.shape
    inner_piece = right_values.shape[0]
    rows = rows_local // CHUNKS

    left_block = expand_tiles(left_values, left_pattern).reshape(rows_local, columns_local)
    lefts = []
    for i in range(CHUNKS):
        ring = [left_block[i * rows : (i + 1) * rows]]
        for _ in range(n_cols - 1):
            ring.append(shift(ring[-1], "col", 1))
        lefts.append(ring)

    right_block = expand_tiles(right_values, right_pattern).transpose(1, 0, 2)
    pieces = [right_block]
    for i in range(1, n_rows):
        pieces.append(shift(right_block, "row", i))
    right = jnp.stack(pieces)

    where = [layer]
    for source in range(n_cols):
        inner = (col - source + n_cols) % n_cols * columns_local
        where += [(row - inner // inner_piece + n_rows) % n_rows, inner % inner_piece]
    where = jnp.stack(where).astype(jnp.int32)

    squares, sums = [], []
    for ring in lefts:
        mine, sent = partial_products(where, ring, right, n_layers)
        received = [
            lax.ppermute(sent[j - 1], "layer", [(i, i ^ j) for i in range(n_layers)])
            for j in range(1, n_layers)
        ]
        squared, column = combine(mine, received)
        squares.append(squared)
        sums.append(column)
    column = lax.psum(functools.reduce(jnp.add, sums), "row")
    out = normalise(column, squares, rows_local * n_rows)
    return out.reshape(rows_local, 1, columns_local)


def solution(mesh):
    return jax.shard_map(
        per_device,
        mesh=mesh,
        in_specs=(
            P("row", "layer", "col"),
            P("row", "layer", "col"),
            P(("layer", "row"), None, "col"),
            P(("layer", "row"), None, "col"),
        ),
        out_specs=P("row", "layer", "col"),
        check_vma=False,
    )
```

time: 297 us -> 119 us (0.40)
  waiting for transfers between devices: 222 us -> 74.5 us
  blocking collectives: 43.4 us -> 2.47 us
  starting transfers between devices: 0.04 us -> 25.9 us
  between operations: 13.4 us -> 0.13 us
  Pallas kernels: 0 us -> 10.1 us
  matrix products: 9.77 us -> 0 us
    all_gather x2 -> x0, waiting for transfers between devices: 222 us -> none  [the longest x1 210 us: per_device(): lax.all_gather(left_flat, ('layer', 'col'), axis=1, tiled=True)]
    ppermute x0 -> x25, waiting for transfers between devices: none -> 74.5 us  [the longest x13 52.2 us: shift(): return lax.ppermute(x, axis, [(i, (i + by) % n) for i in range(n)])]
    all_to_all x1 -> x0, blocking collectives: 41 us -> none  [per_device(): lax.all_to_all(right_rows, 'layer', split_axis=1, concat_axis=0, tiled=True)]
    ppermute x0 -> x25, starting transfers between devices: none -> 25.9 us  [the longest x12 19.5 us: per_device(): lax.ppermute(sent[j - 1], 'layer', [(i, i ^ j) for i in range(n_layers)])]
    pallas_call x0 -> x9, Pallas kernels: none -> 10.1 us  [the longest x4 7.91 us: partial_products(): pl.pallas_call(functools.partial(partial_kernel, len(lefts), n_layers), o...]
    dot_general x1 -> x0, matrix products: 9.77 us -> none  [per_device(): jnp.dot(lax.all_gather(left_flat, ('layer', 'col'), axis=1, tiled=True),...]
    another operation x0 -> x2, other arithmetic: none -> 4.61 us  [per_device(): right = jnp.stack(pieces)]
    mul x2 -> x1, other arithmetic: 3.87 us -> 0.14 us  [expand_tiles(): blocks = blocks * pattern[:, None, :, :, None].astype(values.dtype)]
  transfers between devices with their start and end apart: 2 -> 25, of which waited for: 2 -> 16; matrix products, arithmetic and copies ran while one was open for 0% -> 2% of each run, Pallas kernels for 0% -> 7%
where the time goes in v1:
time: 119 us
  waiting for transfers between devices  74.5 us (63%)
  starting transfers between devices  25.9 us (22%)
  Pallas kernels  10.1 us (8%)
  other arithmetic  5.53 us (5%)
  blocking collectives  2.47 us (2%)
    ppermute x13, waiting for transfers between devices, shift(): return lax.ppermute(x, axis, [(i, (i + by) % n) for i in range(n)])  52.2 us
    ppermute x12, waiting for transfers between devices, per_device(): lax.ppermute(sent[j - 1], 'layer', [(i, i ^ j) for i in range(n_layers)])  22.3 us
    ppermute x12, starting transfers between devices, per_device(): lax.ppermute(sent[j - 1], 'layer', [(i, i ^ j) for i in range(n_layers)])  19.5 us
    pallas_call x4, Pallas kernels, partial_products(): pl.pallas_call(functools.partial(partial_kernel, len(lefts), n_layers), o...  7.91 us
    ppermute x13, starting transfers between devices, shift(): return lax.ppermute(x, axis, [(i, (i + by) % n) for i in range(n)])  6.33 us
    another operation x2, other arithmetic, per_device(): right = jnp.stack(pieces)  4.61 us
    psum x1, blocking collectives, per_device(): column = lax.psum(functools.reduce(jnp.add, sums), 'row')  2.47 us
  transfers between devices with their start and end apart: 25, of which 16 were waited for; matrix products, arithmetic and copies ran while one was open for 2% of the time, Pallas kernels for 7%

profile of v1, /device:TPU:0, one launch (start us, length us, event | category | flops | bytes accessed | tf_op | source)
XLA Modules:
  0.0 119.1 jit_solution(12224620504298495067)
XLA Ops:
  1.0 2.9 %fusion = (bf16[1,4,512,256]{3,2,1,0:T(8,128)(2,1)}, bf16[4,512,256]{2,1,0:T(8,128)(2,1)}) fusion(bf16[512,4,256]{2,1,0:T(4,128)(2,1)} %param.6, bf16[512,4]{0,1:T(4,128)(2,1)S(1)} %bitcast.62), kind=kLoop, calls=%fused_computation.2 | loop fusion | flops 524288 | bytes 3149824 | tf_op jit(solution)/shard_map/stack | solution.py:152
  4.5 2.6 %collective-permute-start.7 = (bf16[512,256]{1,0:T(8,128)(2,1)S(1)}, bf16[512,256]{1,0:T(8,128)(2,1)S(1)}, u32[]{:S(2)}, u32[]{:S(2)}) collective-permute-start(bf16[512,256]{1,0:T(8,128)(2,1)S(1)} %bitcast.59), channel_id=1, source_target_pairs={{0,1},{1,2},{2,3},{3,0},{4,5},{5,6},{6,7},{7,4},{8,9},{9,10},{10,1... | collective-permute-start | bytes 786440 | tf_op jit(solution)/shard_map/ppermute | solution.py:130
  10.4 6.0 %collective-permute-done.7.refs_1_ = bf16[512,256]{1,0:T(8,128)(2,1)S(1)} collective-permute-done((bf16[512,256]{1,0:T(8,128)(2,1)S(1)}, bf16[512,256]{1,0:T(8,128)(2,1)S(1)}, u32[]{:S(2)}, u32[]{:S(2)}) %collective-permute-start.7) | collective-permute-done | bytes 262176 | tf_op jit(solution)/shard_map/ppermute | solution.py:130
  16.4 5.6 %collective-permute-done.refs_1_ = bf16[512,256]{1,0:T(8,128)(2,1)S(1)} collective-permute-done((bf16[512,256]{1,0:T(8,128)(2,1)S(1)}, bf16[512,256]{1,0:T(8,128)(2,1)S(1)}, u32[]{:S(2)}, u32[]{:S(2)}) %collective-permute-start) | collective-permute-done | bytes 262176 | tf_op jit(solution)/shard_map/ppermute | solution.py:130
  22.0 5.6 %collective-permute-done.13.refs_1_ = bf16[512,256]{1,0:T(8,128)(2,1)S(1)} collective-permute-done((bf16[512,256]{1,0:T(8,128)(2,1)S(1)}, bf16[512,256]{1,0:T(8,128)(2,1)S(1)}, u32[]{:S(2)}, u32[]{:S(2)}) %collective-permute-start.13) | collective-permute-done | bytes 262176 | tf_op jit(solution)/shard_map/ppermute | solution.py:130
  27.6 5.6 %collective-permute-done.19.refs_1_ = bf16[512,256]{1,0:T(8,128)(2,1)S(1)} collective-permute-done((bf16[512,256]{1,0:T(8,128)(2,1)S(1)}, bf16[512,256]{1,0:T(8,128)(2,1)S(1)}, u32[]{:S(2)}, u32[]{:S(2)}) %collective-permute-start.19) | collective-permute-done | bytes 262176 | tf_op jit(solution)/shard_map/ppermute | solution.py:130
  33.2 5.6 %collective-permute-done.8.refs_2_ = bf16[512,256]{1,0:T(8,128)(2,1)S(1)} collective-permute-done((bf16[512,256]{1,0:T(8,128)(2,1)S(1)}, bf16[512,256]{1,0:T(8,128)(2,1)S(1)}, u32[]{:S(2)}, u32[]{:S(2)}) %collective-permute-start.8) | collective-permute-done | bytes 262176 | tf_op jit(solution)/shard_map/ppermute | solution.py:130
  38.9 5.5 %collective-permute-done.1.refs_2_ = bf16[512,256]{1,0:T(8,128)(2,1)S(1)} collective-permute-done((bf16[512,256]{1,0:T(8,128)(2,1)S(1)}, bf16[512,256]{1,0:T(8,128)(2,1)S(1)}, u32[]{:S(2)}, u32[]{:S(2)}) %collective-permute-start.1) | collective-permute-done | bytes 262176 | tf_op jit(solution)/shard_map/ppermute | solution.py:130
  44.4 5.6 %collective-permute-done.14.refs_2_ = bf16[512,256]{1,0:T(8,128)(2,1)S(1)} collective-permute-done((bf16[512,256]{1,0:T(8,128)(2,1)S(1)}, bf16[512,256]{1,0:T(8,128)(2,1)S(1)}, u32[]{:S(2)}, u32[]{:S(2)}) %collective-permute-start.14) | collective-permute-done | bytes 262176 | tf_op jit(solution)/shard_map/ppermute | solution.py:130
  50.1 5.6 %collective-permute-done.20.refs_2_ = bf16[512,256]{1,0:T(8,128)(2,1)S(1)} collective-permute-done((bf16[512,256]{1,0:T(8,128)(2,1)S(1)}, bf16[512,256]{1,0:T(8,128)(2,1)S(1)}, u32[]{:S(2)}, u32[]{:S(2)}) %collective-permute-start.20) | collective-permute-done | bytes 262176 | tf_op jit(solution)/shard_map/ppermute | solution.py:130
  55.7 1.7 %pad_maximum_fusion.refs_4_ = bf16[2,4,512,256]{3,2,1,0:T(8,128)(2,1)S(1)} fusion(bf16[1,4,512,256]{3,2,1,0:T(8,128)(2,1)} %bitcast.15, bf16[1,4,512,256]{3,2,1,0:T(8,128)(2,1)} %get-tuple-element.37), kind=kLoop, calls=%fused_computation | loop fusion | flops 1048576 | bytes 4194304 | tf_op jit(solution)/shard_map/stack | solution.py:152
  57.4 3.9 %collective-permute-done.9.refs_3_ = bf16[512,256]{1,0:T(8,128)(2,1)S(1)} collective-permute-done((bf16[512,256]{1,0:T(8,128)(2,1)S(1)}, bf16[512,256]{1,0:T(8,128)(2,1)S(1)}, u32[]{:S(2)}, u32[]{:S(2)}) %collective-permute-start.9) | collective-permute-done | bytes 262176 | tf_op jit(solution)/shard_map/ppermute | solution.py:130
  61.3 2.0 %shard_map.48 = (f32[512,256]{1,0:T(8,128)S(1)}, s16[3,528,256]{2,1,0:T(8,128)(2,1)S(1)}) custom-call(s32[9]{0:T(128)S(1)} %stack.48.where, bf16[512,256]{1,0:T(8,128)(2,1)S(1)} %bitcast.60, bf16[512,256]{1,0:T(8,128)(2,1)S(1)} %collective-permute-done.7.refs_1_, bf16[512,256]{1,0:T(8,128)(2,1)S(1)} %collective-permute-done.8.refs_2_, ...), custom_call_target="tpu_custom_call" | custom-call | flops 1073741824 | bytes 3932160 | tf_op jit(solution)/shard_map/pallas_call | solution.py:48
  66.9 2.6 %collective-permute-start.12 = (s16[528,256]{1,0:T(8,128)(2,1)S(1)}, s16[528,256]{1,0:T(8,128)(2,1)S(1)}, u32[]{:S(2)}, u32[]{:S(2)}) collective-permute-start(s16[528,256]{1,0:T(8,128)(2,1)S(1)} %get-tuple-element.43), channel_id=1, source_target_pairs={{0,24},{8,16},{16,8},{24,0},{1,25},{9,17},{17,9},{25,1},{2,26},{10... | collective-permute-start | bytes 811016 | tf_op jit(solution)/shard_map/ppermute | solution.py:164
  69.5 2.0 %shard_map.46 = (f32[512,256]{1,0:T(8,128)S(1)}, s16[3,528,256]{2,1,0:T(8,128)(2,1)S(1)}) custom-call(s32[9]{0:T(128)S(1)} %stack.48.where, bf16[512,256]{1,0:T(8,128)(2,1)S(1)} %bitcast.58, bf16[512,256]{1,0:T(8,128)(2,1)S(1)} %collective-permute-done.refs_1_, bf16[512,256]{1,0:T(8,128)(2,1)S(1)} %collective-permute-done.1.refs_2_, ...), custom_call_target="tpu_custom_call" | custom-call | flops 1073741824 | bytes 3932160 | tf_op jit(solution)/shard_map/pallas_call | solution.py:48
  74.2 2.0 %shard_map.50 = (f32[512,256]{1,0:T(8,128)S(1)}, s16[3,528,256]{2,1,0:T(8,128)(2,1)S(1)}) custom-call(s32[9]{0:T(128)S(1)} %stack.48.where, bf16[512,256]{1,0:T(8,128)(2,1)S(1)} %bitcast.56, bf16[512,256]{1,0:T(8,128)(2,1)S(1)} %collective-permute-done.13.refs_1_, bf16[512,256]{1,0:T(8,128)(2,1)S(1)} %collective-permute-done.14.refs_2_, ...), custom_call_target="tpu_custom_call" | custom-call | flops 1073741824 | bytes 3932160 | tf_op jit(solution)/shard_map/pallas_call | solution.py:48
  76.2 1.8 %collective-permute-done.21.refs_3_ = bf16[512,256]{1,0:T(8,128)(2,1)S(1)} collective-permute-done((bf16[512,256]{1,0:T(8,128)(2,1)S(1)}, bf16[512,256]{1,0:T(8,128)(2,1)S(1)}, u32[]{:S(2)}, u32[]{:S(2)}) %collective-permute-start.21) | collective-permute-done | bytes 262176 | tf_op jit(solution)/shard_map/ppermute | solution.py:130
  81.5 2.0 %shard_map.52 = (f32[512,256]{1,0:T(8,128)S(1)}, s16[3,528,256]{2,1,0:T(8,128)(2,1)S(1)}) custom-call(s32[9]{0:T(128)S(1)} %stack.48.where, bf16[512,256]{1,0:T(8,128)(2,1)S(1)} %bitcast.54, bf16[512,256]{1,0:T(8,128)(2,1)S(1)} %collective-permute-done.19.refs_1_, bf16[512,256]{1,0:T(8,128)(2,1)S(1)} %collective-permute-done.20.refs_2_, ...), custom_call_target="tpu_custom_call" | custom-call | flops 1073741824 | bytes 3932160 | tf_op jit(solution)/shard_map/pallas_call | solution.py:48
  86.8 6.3 %collective-permute-done.5.refs_1_ = s16[528,256]{1,0:T(8,128)(2,1)S(1)} collective-permute-done((s16[528,256]{1,0:T(8,128)(2,1)S(1)}, s16[528,256]{1,0:T(8,128)(2,1)S(1)}, u32[]{:S(2)}, u32[]{:S(2)}) %collective-permute-start.5) | collective-permute-done | bytes 270368 | tf_op jit(solution)/shard_map/ppermute | solution.py:164
  96.1 2.3 %collective-permute-start.24 = (s16[528,256]{1,0:T(8,128)(2,1)S(1)}, s16[528,256]{1,0:T(8,128)(2,1)S(1)}, u32[]{:S(2)}, u32[]{:S(2)}) collective-permute-start(s16[528,256]{1,0:T(8,128)(2,1)S(1)} %get-tuple-element.52), channel_id=1, source_target_pairs={{0,24},{8,16},{16,8},{24,0},{1,25},{9,17},{17,9},{25,1},{2,26},{10... | collective-permute-start | bytes 811016 | tf_op jit(solution)/shard_map/ppermute | solution.py:164
  99.0 5.7 %collective-permute-done.17.refs_1_ = s16[528,256]{1,0:T(8,128)(2,1)S(1)} collective-permute-done((s16[528,256]{1,0:T(8,128)(2,1)S(1)}, s16[528,256]{1,0:T(8,128)(2,1)S(1)}, u32[]{:S(2)}, u32[]{:S(2)}) %collective-permute-start.17) | collective-permute-done | bytes 270368 | tf_op jit(solution)/shard_map/ppermute | solution.py:164
  105.0 2.7 %collective-permute-done.22.refs_0_ = s16[528,256]{1,0:T(8,128)(2,1)S(1)} collective-permute-done((s16[528,256]{1,0:T(8,128)(2,1)S(1)}, s16[528,256]{1,0:T(8,128)(2,1)S(1)}, u32[]{:S(2)}, u32[]{:S(2)}) %collective-permute-start.22) | collective-permute-done | bytes 270368 | tf_op jit(solution)/shard_map/ppermute | solution.py:164
  107.7 7.5 %collective-permute-done.23.refs_1_ = s16[528,256]{1,0:T(8,128)(2,1)S(1)} collective-permute-done((s16[528,256]{1,0:T(8,128)(2,1)S(1)}, s16[528,256]{1,0:T(8,128)(2,1)S(1)}, u32[]{:S(2)}, u32[]{:S(2)}) %collective-permute-start.23) | collective-permute-done | bytes 270368 | tf_op jit(solution)/shard_map/ppermute | solution.py:164
  115.5 2.5 %psum.7.column_ref = f32[1,256]{1,0:T(1,128)S(1)} all-reduce(f32[1,256]{1,0:T(1,128)S(1)} %add_add_fusion), channel_id=1, replica_groups=mesh['layer'=4,'row'=2,'col'=4] {'row'}, use_global_device_ids=true, to_apply=%region_0.1 | all-reduce | flops 256 | bytes 2048 | tf_op jit(solution)/shard_map/psum | solution.py:170
  (55 shorter events, 23.4 us)
Async XLA Ops:
  3.8 51.8 %collective-permute-start.3 = (bf16[4,512,256]{2,1,0:T(8,128)(2,1)}, bf16[4,512,256]{2,1,0:T(8,128)(2,1)}, u32[]{:S(2)}, u32[]{:S(2)}) collective-permute-start(bf16[4,512,256]{2,1,0:T(8,128)(2,1)} %get-tuple-element.38), channel_id=1, source_target_pairs={{0,4},{4,0},{1,5},{5,1},{2,6},{6,2},{3,7},{7,3},{8,12},{12,8},{9,1... | collective-permute-start | bytes 3145736 | tf_op jit(solution)/shard_map/ppermute | solution.py:130
  7.2 14.8 %collective-permute-start = (bf16[512,256]{1,0:T(8,128)(2,1)S(1)}, bf16[512,256]{1,0:T(8,128)(2,1)S(1)}, u32[]{:S(2)}, u32[]{:S(2)}) collective-permute-start(bf16[512,256]{1,0:T(8,128)(2,1)S(1)} %bitcast.57), channel_id=1, source_target_pairs={{0,1},{1,2},{2,3},{3,0},{4,5},{5,6},{6,7},{7,4},{8,9},{9,10},{10,1... | collective-permute-start | bytes 786440 | tf_op jit(solution)/shard_map/ppermute | solution.py:130
  8.7 18.8 %collective-permute-start.13 = (bf16[512,256]{1,0:T(8,128)(2,1)S(1)}, bf16[512,256]{1,0:T(8,128)(2,1)S(1)}, u32[]{:S(2)}, u32[]{:S(2)}) collective-permute-start(bf16[512,256]{1,0:T(8,128)(2,1)S(1)} %bitcast.55), channel_id=1, source_target_pairs={{0,1},{1,2},{2,3},{3,0},{4,5},{5,6},{6,7},{7,4},{8,9},{9,10},{10,1... | collective-permute-start | bytes 786440 | tf_op jit(solution)/shard_map/ppermute | solution.py:130
  10.3 22.9 %collective-permute-start.19 = (bf16[512,256]{1,0:T(8,128)(2,1)S(1)}, bf16[512,256]{1,0:T(8,128)(2,1)S(1)}, u32[]{:S(2)}, u32[]{:S(2)}) collective-permute-start(bf16[512,256]{1,0:T(8,128)(2,1)S(1)} %bitcast.53), channel_id=1, source_target_pairs={{0,1},{1,2},{2,3},{3,0},{4,5},{5,6},{6,7},{7,4},{8,9},{9,10},{10,1... | collective-permute-start | bytes 786440 | tf_op jit(solution)/shard_map/ppermute | solution.py:130
  16.4 22.5 %collective-permute-start.8 = (bf16[512,256]{1,0:T(8,128)(2,1)S(1)}, bf16[512,256]{1,0:T(8,128)(2,1)S(1)}, u32[]{:S(2)}, u32[]{:S(2)}) collective-permute-start(bf16[512,256]{1,0:T(8,128)(2,1)S(1)} %collective-permute-done.7.refs_1_), channel_id=1, source_target_pairs={{0,1},{1,2},{2,3},{3,0},{4,5},{5,6},{6,7},{7,4},{8,9},{9,10},{10,1... | collective-permute-start | bytes 786440 | tf_op jit(solution)/shard_map/ppermute | solution.py:130
  22.0 22.5 %collective-permute-start.1 = (bf16[512,256]{1,0:T(8,128)(2,1)S(1)}, bf16[512,256]{1,0:T(8,128)(2,1)S(1)}, u32[]{:S(2)}, u32[]{:S(2)}) collective-permute-start(bf16[512,256]{1,0:T(8,128)(2,1)S(1)} %collective-permute-done.refs_1_), channel_id=1, source_target_pairs={{0,1},{1,2},{2,3},{3,0},{4,5},{5,6},{6,7},{7,4},{8,9},{9,10},{10,1... | collective-permute-start | bytes 786440 | tf_op jit(solution)/shard_map/ppermute | solution.py:130
  27.6 22.5 %collective-permute-start.14 = (bf16[512,256]{1,0:T(8,128)(2,1)S(1)}, bf16[512,256]{1,0:T(8,128)(2,1)S(1)}, u32[]{:S(2)}, u32[]{:S(2)}) collective-permute-start(bf16[512,256]{1,0:T(8,128)(2,1)S(1)} %collective-permute-done.13.refs_1_), channel_id=1, source_target_pairs={{0,1},{1,2},{2,3},{3,0},{4,5},{5,6},{6,7},{7,4},{8,9},{9,10},{10,1... | collective-permute-start | bytes 786440 | tf_op jit(solution)/shard_map/ppermute | solution.py:130
  33.2 22.5 %collective-permute-start.20 = (bf16[512,256]{1,0:T(8,128)(2,1)S(1)}, bf16[512,256]{1,0:T(8,128)(2,1)S(1)}, u32[]{:S(2)}, u32[]{:S(2)}) collective-permute-start(bf16[512,256]{1,0:T(8,128)(2,1)S(1)} %collective-permute-done.19.refs_1_), channel_id=1, source_target_pairs={{0,1},{1,2},{2,3},{3,0},{4,5},{5,6},{6,7},{7,4},{8,9},{9,10},{10,1... | collective-permute-start | bytes 786440 | tf_op jit(solution)/shard_map/ppermute | solution.py:130
  38.8 22.5 %collective-permute-start.9 = (bf16[512,256]{1,0:T(8,128)(2,1)S(1)}, bf16[512,256]{1,0:T(8,128)(2,1)S(1)}, u32[]{:S(2)}, u32[]{:S(2)}) collective-permute-start(bf16[512,256]{1,0:T(8,128)(2,1)S(1)} %collective-permute-done.8.refs_2_), channel_id=1, source_target_pairs={{0,1},{1,2},{2,3},{3,0},{4,5},{5,6},{6,7},{7,4},{8,9},{9,10},{10,1... | collective-permute-start | bytes 786440 | tf_op jit(solution)/shard_map/ppermute | solution.py:130
  44.4 22.5 %collective-permute-start.2 = (bf16[512,256]{1,0:T(8,128)(2,1)S(1)}, bf16[512,256]{1,0:T(8,128)(2,1)S(1)}, u32[]{:S(2)}, u32[]{:S(2)}) collective-permute-start(bf16[512,256]{1,0:T(8,128)(2,1)S(1)} %collective-permute-done.1.refs_2_), channel_id=1, source_target_pairs={{0,1},{1,2},{2,3},{3,0},{4,5},{5,6},{6,7},{7,4},{8,9},{9,10},{10,1... | collective-permute-start | bytes 786440 | tf_op jit(solution)/shard_map/ppermute | solution.py:130
  50.1 22.5 %collective-permute-start.15 = (bf16[512,256]{1,0:T(8,128)(2,1)S(1)}, bf16[512,256]{1,0:T(8,128)(2,1)S(1)}, u32[]{:S(2)}, u32[]{:S(2)}) collective-permute-start(bf16[512,256]{1,0:T(8,128)(2,1)S(1)} %collective-permute-done.14.refs_2_), channel_id=1, source_target_pairs={{0,1},{1,2},{2,3},{3,0},{4,5},{5,6},{6,7},{7,4},{8,9},{9,10},{10,1... | collective-permute-start | bytes 786440 | tf_op jit(solution)/shard_map/ppermute | solution.py:130
  55.7 22.3 %collective-permute-start.21 = (bf16[512,256]{1,0:T(8,128)(2,1)S(1)}, bf16[512,256]{1,0:T(8,128)(2,1)S(1)}, u32[]{:S(2)}, u32[]{:S(2)}) collective-permute-start(bf16[512,256]{1,0:T(8,128)(2,1)S(1)} %collective-permute-done.20.refs_2_), channel_id=1, source_target_pairs={{0,1},{1,2},{2,3},{3,0},{4,5},{5,6},{6,7},{7,4},{8,9},{9,10},{10,1... | collective-permute-start | bytes 786440 | tf_op jit(solution)/shard_map/ppermute | solution.py:130
  63.3 16.1 %collective-permute-start.10 = (s16[528,256]{1,0:T(8,128)(2,1)S(1)}, s16[528,256]{1,0:T(8,128)(2,1)S(1)}, u32[]{:S(2)}, u32[]{:S(2)}) collective-permute-start(s16[528,256]{1,0:T(8,128)(2,1)S(1)} %get-tuple-element.45), channel_id=1, source_target_pairs={{0,8},{8,0},{16,24},{24,16},{1,9},{9,1},{17,25},{25,17},{2,10},{10... | collective-permute-start | bytes 811016 | tf_op jit(solution)/shard_map/ppermute | solution.py:164
  65.0 15.9 %collective-permute-start.11 = (s16[528,256]{1,0:T(8,128)(2,1)S(1)}, s16[528,256]{1,0:T(8,128)(2,1)S(1)}, u32[]{:S(2)}, u32[]{:S(2)}) collective-permute-start(s16[528,256]{1,0:T(8,128)(2,1)S(1)} %get-tuple-element.44), channel_id=1, source_target_pairs={{0,16},{8,24},{16,0},{24,8},{1,17},{9,25},{17,1},{25,9},{2,18},{10... | collective-permute-start | bytes 811016 | tf_op jit(solution)/shard_map/ppermute | solution.py:164
  66.9 16.6 %collective-permute-start.12 = (s16[528,256]{1,0:T(8,128)(2,1)S(1)}, s16[528,256]{1,0:T(8,128)(2,1)S(1)}, u32[]{:S(2)}, u32[]{:S(2)}) collective-permute-start(s16[528,256]{1,0:T(8,128)(2,1)S(1)} %get-tuple-element.43), channel_id=1, source_target_pairs={{0,24},{8,16},{16,8},{24,0},{1,25},{9,17},{17,9},{25,1},{2,26},{10... | collective-permute-start | bytes 811016 | tf_op jit(solution)/shard_map/ppermute | solution.py:164
  72.5 12.6 %collective-permute-start.4 = (s16[528,256]{1,0:T(8,128)(2,1)S(1)}, s16[528,256]{1,0:T(8,128)(2,1)S(1)}, u32[]{:S(2)}, u32[]{:S(2)}) collective-permute-start(s16[528,256]{1,0:T(8,128)(2,1)S(1)} %get-tuple-element.48), channel_id=1, source_target_pairs={{0,8},{8,0},{16,24},{24,16},{1,9},{9,1},{17,25},{25,17},{2,10},{10... | collective-permute-start | bytes 811016 | tf_op jit(solution)/shard_map/ppermute | solution.py:164
  78.0 15.2 %collective-permute-start.5 = (s16[528,256]{1,0:T(8,128)(2,1)S(1)}, s16[528,256]{1,0:T(8,128)(2,1)S(1)}, u32[]{:S(2)}, u32[]{:S(2)}) collective-permute-start(s16[528,256]{1,0:T(8,128)(2,1)S(1)} %get-tuple-element.47), channel_id=1, source_target_pairs={{0,16},{8,24},{16,0},{24,8},{1,17},{9,25},{17,1},{25,9},{2,18},{10... | collective-permute-start | bytes 811016 | tf_op jit(solution)/shard_map/ppermute | solution.py:164
  79.5 15.1 %collective-permute-start.6 = (s16[528,256]{1,0:T(8,128)(2,1)S(1)}, s16[528,256]{1,0:T(8,128)(2,1)S(1)}, u32[]{:S(2)}, u32[]{:S(2)}) collective-permute-start(s16[528,256]{1,0:T(8,128)(2,1)S(1)} %get-tuple-element.46), channel_id=1, source_target_pairs={{0,24},{8,16},{16,8},{24,0},{1,25},{9,17},{17,9},{25,1},{2,26},{10... | collective-permute-start | bytes 811016 | tf_op jit(solution)/shard_map/ppermute | solution.py:164
  80.9 15.2 %collective-permute-start.16 = (s16[528,256]{1,0:T(8,128)(2,1)S(1)}, s16[528,256]{1,0:T(8,128)(2,1)S(1)}, u32[]{:S(2)}, u32[]{:S(2)}) collective-permute-start(s16[528,256]{1,0:T(8,128)(2,1)S(1)} %get-tuple-element.51), channel_id=1, source_target_pairs={{0,8},{8,0},{16,24},{24,16},{1,9},{9,1},{17,25},{25,17},{2,10},{10... | collective-permute-start | bytes 811016 | tf_op jit(solution)/shard_map/ppermute | solution.py:164
  83.5 21.2 %collective-permute-start.17 = (s16[528,256]{1,0:T(8,128)(2,1)S(1)}, s16[528,256]{1,0:T(8,128)(2,1)S(1)}, u32[]{:S(2)}, u32[]{:S(2)}) collective-permute-start(s16[528,256]{1,0:T(8,128)(2,1)S(1)} %get-tuple-element.50), channel_id=1, source_target_pairs={{0,16},{8,24},{16,0},{24,8},{1,17},{9,25},{17,1},{25,9},{2,18},{10... | collective-permute-start | bytes 811016 | tf_op jit(solution)/shard_map/ppermute | solution.py:164
  85.1 19.6 %collective-permute-start.18 = (s16[528,256]{1,0:T(8,128)(2,1)S(1)}, s16[528,256]{1,0:T(8,128)(2,1)S(1)}, u32[]{:S(2)}, u32[]{:S(2)}) collective-permute-start(s16[528,256]{1,0:T(8,128)(2,1)S(1)} %get-tuple-element.49), channel_id=1, source_target_pairs={{0,24},{8,16},{16,8},{24,0},{1,25},{9,17},{17,9},{25,1},{2,26},{10... | collective-permute-start | bytes 811016 | tf_op jit(solution)/shard_map/ppermute | solution.py:164
  93.1 14.6 %collective-permute-start.22 = (s16[528,256]{1,0:T(8,128)(2,1)S(1)}, s16[528,256]{1,0:T(8,128)(2,1)S(1)}, u32[]{:S(2)}, u32[]{:S(2)}) collective-permute-start(s16[528,256]{1,0:T(8,128)(2,1)S(1)} %get-tuple-element.54), channel_id=1, source_target_pairs={{0,8},{8,0},{16,24},{24,16},{1,9},{9,1},{17,25},{25,17},{2,10},{10... | collective-permute-start | bytes 811016 | tf_op jit(solution)/shard_map/ppermute | solution.py:164
  94.6 20.6 %collective-permute-start.23 = (s16[528,256]{1,0:T(8,128)(2,1)S(1)}, s16[528,256]{1,0:T(8,128)(2,1)S(1)}, u32[]{:S(2)}, u32[]{:S(2)}) collective-permute-start(s16[528,256]{1,0:T(8,128)(2,1)S(1)} %get-tuple-element.53), channel_id=1, source_target_pairs={{0,16},{8,24},{16,0},{24,8},{1,17},{9,25},{17,1},{25,9},{2,18},{10... | collective-permute-start | bytes 811016 | tf_op jit(solution)/shard_map/ppermute | solution.py:164
  96.1 19.1 %collective-permute-start.24 = (s16[528,256]{1,0:T(8,128)(2,1)S(1)}, s16[528,256]{1,0:T(8,128)(2,1)S(1)}, u32[]{:S(2)}, u32[]{:S(2)}) collective-permute-start(s16[528,256]{1,0:T(8,128)(2,1)S(1)} %get-tuple-element.52), channel_id=1, source_target_pairs={{0,24},{8,16},{16,8},{24,0},{1,25},{9,17},{17,9},{25,1},{2,26},{10... | collective-permute-start | bytes 811016 | tf_op jit(solution)/shard_map/ppermute | solution.py:164
  (3 other events, 20.4 us)

commit v2 on v1

--- a/solution.py
+++ b/solution.py
@@ -8,7 +8,7 @@
 from jax.sharding import PartitionSpec as P
 
 TILE = 256
-CHUNKS = 4
+SIXTEENTHS = (4, 5, 4, 3)
 SCALE_ROWS = 16
 CODE = 64.0
 TOP = 32767.0
@@ -17,9 +17,48 @@
 PARAMS = pltpu.CompilerParams(vmem_limit_bytes=40 * 1024 * 1024)
 
 
+def gated_mask_kernel(first, pattern_ref, left_ref, *refs):
+    tile = (first + pl.program_id(0)) * left_ref.shape[0] // TILE
+    refs[-1][...] = left_ref[...] * pattern_ref[tile].astype(jnp.float32).astype(left_ref.dtype)
+
+
+def gated_mask(left, pattern, at, size, after):
+    columns = left.shape[1]
+    block = left.shape[0] // sum(SIXTEENTHS)
+    first = at // block
+    return pl.pallas_call(
+        functools.partial(gated_mask_kernel, first),
+        grid=(size // block,),
+        out_shape=jax.ShapeDtypeStruct((size, columns), left.dtype),
+        in_specs=[
+            pl.BlockSpec(memory_space=pltpu.SMEM),
+            pl.BlockSpec((block, columns), lambda i: (first + i, 0)),
+        ]
+        + [pl.BlockSpec(memory_space=pl.ANY)] * len(after),
+        out_specs=pl.BlockSpec((block, columns), lambda i: (i, 0)),
+        compiler_params=PARAMS,
+        cost_estimate=pl.CostEstimate(
+            flops=size * columns, bytes_accessed=4 * size * columns, transcendentals=0
+        ),
+    )(pattern, left, *after)
+
+
+def gate_kernel(x_ref, after_ref, out_ref):
+    out_ref[...] = x_ref[...]
+
+
+def gate(x, after):
+    return pl.pallas_call(
+        gate_kernel,
+        out_shape=jax.ShapeDtypeStruct(x.shape, x.dtype),
+        in_specs=[VMEM, pl.BlockSpec(memory_space=pl.ANY)],
+        out_specs=VMEM,
+    )(x, after)
+
+
 def partial_kernel(n_sources, n_layers, where, *refs):
     lefts = refs[:n_sources]
-    right_ref, mine_ref, sent_ref = refs[n_sources:]
+    right_ref, mine_ref, *sent_refs = refs[n_sources:]
     rows = lefts[0].shape[0]
     for step in range(n_layers):
         layer = where[0] ^ step
@@ -38,21 +77,19 @@
         code = jnp.ceil(jnp.log2(top) * CODE + 0.01)
         unit = jnp.exp2(code / -CODE) * TOP
         fixed = jnp.round(total * unit).astype(jnp.int32)
-        sent_ref[step - 1, :rows, :] = fixed.astype(jnp.int16)
+        sent_refs[step - 1][:rows, :] = fixed.astype(jnp.int16)
         codes = jnp.broadcast_to(code.astype(jnp.int32), (SCALE_ROWS, code.shape[1]))
-        sent_ref[step - 1, rows:, :] = codes.astype(jnp.int16)
+        sent_refs[step - 1][rows:, :] = codes.astype(jnp.int16)
 
 
 def partial_products(where, lefts, right, n_layers):
     rows, columns = lefts[0].shape[0], right.shape[3]
     return pl.pallas_call(
         functools.partial(partial_kernel, len(lefts), n_layers),
-        out_shape=(
-            jax.ShapeDtypeStruct((rows, columns), jnp.float32),
-            jax.ShapeDtypeStruct((n_layers - 1, rows + SCALE_ROWS, columns), jnp.int16),
-        ),
+        out_shape=[jax.ShapeDtypeStruct((rows, columns), jnp.float32)]
+        + [jax.ShapeDtypeStruct((rows + SCALE_ROWS, columns), jnp.int16)] * (n_layers - 1),
         in_specs=[pl.BlockSpec(memory_space=pltpu.SMEM)] + [VMEM] * (len(lefts) + 1),
-        out_specs=(VMEM, VMEM),
+        out_specs=[VMEM] * n_layers,
         compiler_params=PARAMS,
         cost_estimate=pl.CostEstimate(
             flops=2 * rows * len(lefts) * TILE * columns * n_layers,
@@ -63,7 +100,7 @@
 
 
 def combine_kernel(n_received, mine_ref, *refs):
-    received, (squared_ref, sum_ref) = refs[:n_received], refs[n_received:]
+    received, (before_ref, squared_ref, sum_ref) = refs[:n_received], refs[n_received:]
     total = mine_ref[...]
     rows = total.shape[0]
     for block in received:
@@ -72,46 +109,46 @@
         total += block[:rows, :].astype(jnp.int32).astype(jnp.float32) * unit
     squared = total * total
     squared_ref[...] = squared
-    sum_ref[...] = jnp.sum(squared, axis=0, keepdims=True)
-
-
-def combine(mine, received):
+    sum_ref[...] = before_ref[...] + jnp.sum(squared, axis=0, keepdims=True)
+
+
+def combine(mine, received, before):
     return pl.pallas_call(
         functools.partial(combine_kernel, len(received)),
         out_shape=(
             jax.ShapeDtypeStruct(mine.shape, jnp.float32),
             jax.ShapeDtypeStruct((1, mine.shape[1]), jnp.float32),
         ),
-        in_specs=[VMEM] * (1 + len(received)),
+        in_specs=[VMEM] * (2 + len(received)),
         out_specs=(VMEM, VMEM),
         compiler_params=PARAMS,
         cost_estimate=pl.CostEstimate(
             flops=8 * mine.size, bytes_accessed=mine.size * 14, transcendentals=0
         ),
-    )(mine, *received)
+    )(mine, *received, before)
 
 
 def normalise_kernel(n_chunks, rows_total, column_ref, *refs):
     chunks, out_ref = refs[:n_chunks], refs[n_chunks]
-    rows = chunks[0].shape[0]
     colmean = column_ref[...] / rows_total
-    for i, chunk in enumerate(chunks):
-        out_ref[i * rows : (i + 1) * rows, :] = (
-            chunk[...] / (colmean + 1e-06)
-        ).astype(jnp.bfloat16)
+    at = 0
+    for chunk in chunks:
+        rows = chunk.shape[0]
+        out_ref[at : at + rows, :] = (chunk[...] / (colmean + 1e-06)).astype(jnp.bfloat16)
+        at += rows
 
 
 def normalise(column, chunks, rows_total):
-    rows, columns = chunks[0].shape
+    rows, columns = sum(chunk.shape[0] for chunk in chunks), chunks[0].shape[1]
     return pl.pallas_call(
         functools.partial(normalise_kernel, len(chunks), rows_total),
-        out_shape=jax.ShapeDtypeStruct((rows * len(chunks), columns), jnp.bfloat16),
+        out_shape=jax.ShapeDtypeStruct((rows, columns), jnp.bfloat16),
         in_specs=[VMEM] * (1 + len(chunks)),
         out_specs=VMEM,
         compiler_params=PARAMS,
         cost_estimate=pl.CostEstimate(
-            flops=4 * rows * columns * len(chunks),
-            bytes_accessed=6 * rows * columns * len(chunks),
+            flops=4 * rows * columns,
+            bytes_accessed=6 * rows * columns,
             transcendentals=0,
         ),
     )(column, *chunks)
@@ -135,16 +172,19 @@
     layer, row, col = (lax.axis_index(a) for a in ("layer", "row", "col"))
     rows_local, _, columns_local = left_values.shape
     inner_piece = right_values.shape[0]
-    rows = rows_local // CHUNKS
-
-    left_block = expand_tiles(left_values, left_pattern).reshape(rows_local, columns_local)
-    lefts = []
-    for i in range(CHUNKS):
-        ring = [left_block[i * rows : (i + 1) * rows]]
+    sizes = [rows_local * part // 16 for part in SIXTEENTHS]
+    starts = [sum(sizes[:i]) for i in range(len(sizes))]
+
+    left = left_values.reshape(rows_local, columns_local)
+    pattern = left_pattern.reshape(-1)
+    rings = []
+    for i, (at, size) in enumerate(zip(starts, sizes)):
+        ring = [gated_mask(left, pattern, at, size, [rings[i - 2][-1]] if i > 1 else [])]
         for _ in range(n_cols - 1):
             ring.append(shift(ring[-1], "col", 1))
-        lefts.append(ring)
-
+        rings.append(ring)
+
+    right_pattern = gate(right_pattern, rings[1][0])
     right_block = expand_tiles(right_values, right_pattern).transpose(1, 0, 2)
     pieces = [right_block]
     for i in range(1, n_rows):
@@ -157,17 +197,17 @@
         where += [(row - inner // inner_piece + n_rows) % n_rows, inner % inner_piece]
     where = jnp.stack(where).astype(jnp.int32)
 
-    squares, sums = [], []
-    for ring in lefts:
-        mine, sent = partial_products(where, ring, right, n_layers)
+    squares = []
+    column = jnp.zeros((1, columns_local), jnp.float32)
+    for ring in rings:
+        mine, *sent = partial_products(where, ring, right, n_layers)
         received = [
             lax.ppermute(sent[j - 1], "layer", [(i, i ^ j) for i in range(n_layers)])
             for j in range(1, n_layers)
         ]
-        squared, column = combine(mine, received)
+        squared, column = combine(mine, received, column)
         squares.append(squared)
-        sums.append(column)
-    column = lax.psum(functools.reduce(jnp.add, sums), "row")
+    column = lax.psum(column, "row")
     out = normalise(column, squares, rows_local * n_rows)
     return out.reshape(rows_local, 1, columns_local)
 

time: 119 us -> 113 us (0.950)
  waiting for transfers between devices: 74.5 us -> 64.5 us
  local copies, waits for them, and re-layouts: 0.57 us -> 5.09 us
  Pallas kernels: 10.1 us -> 14.3 us
  starting transfers between devices: 25.9 us -> 22.2 us
  other arithmetic: 5.53 us -> 3.83 us
    ppermute x12, waiting for transfers between devices: 22.3 us -> 15.6 us  [per_device(): lax.ppermute(sent[j - 1], 'layer', [(i, i ^ j) for i in range(n_layers)])]
    unnamed x6 -> x29, local copies, waits for them, and re-layouts: 0.09 us -> 4.88 us
    ppermute x12, starting transfers between devices: 19.5 us -> 15.2 us  [per_device(): lax.ppermute(sent[j - 1], 'layer', [(i, i ^ j) for i in range(n_layers)])]
    pallas_call x0 -> x5, Pallas kernels: none -> 4.13 us  [the longest x4 2.8 us: gated_mask(): pl.pallas_call(functools.partial(gated_mask_kernel, first), grid=(size //...]
    ppermute x13, waiting for transfers between devices: 52.2 us -> 48.9 us  [shift(): return lax.ppermute(x, axis, [(i, (i + by) % n) for i in range(n)])]
    another operation x2, other arithmetic: 4.61 us -> 3.15 us  [per_device(): right = jnp.stack(pieces)]
  transfers between devices with their start and end apart: 25 -> 25, of which waited for: 16 -> 16; matrix products, arithmetic and copies ran while one was open for 2% -> 4% of each run, Pallas kernels for 7% -> 11%
where the time goes in v2:
time: 113 us
  waiting for transfers between devices  64.5 us (57%)
  starting transfers between devices  22.2 us (20%)
  Pallas kernels  14.3 us (13%)
  local copies, waits for them, and re-layouts  5.09 us (5%)
  other arithmetic  3.83 us (3%)
  blocking collectives  2.47 us (2%)
    ppermute x13, waiting for transfers between devices, shift(): return lax.ppermute(x, axis, [(i, (i + by) % n) for i in range(n)])  48.9 us
    ppermute x12, waiting for transfers between devices, per_device(): lax.ppermute(sent[j - 1], 'layer', [(i, i ^ j) for i in range(n_layers)])  15.6 us
    ppermute x12, starting transfers between devices, per_device(): lax.ppermute(sent[j - 1], 'layer', [(i, i ^ j) for i in range(n_layers)])  15.2 us
    pallas_call x4, Pallas kernels, partial_products(): pl.pallas_call(functools.partial(partial_kernel, len(lefts), n_layers), o...  8.01 us
    ppermute x13, starting transfers between devices, shift(): return lax.ppermute(x, axis, [(i, (i + by) % n) for i in range(n)])  7.07 us
    unnamed x29, local copies, waits for them, and re-layouts  4.88 us
    another operation x2, other arithmetic, per_device(): right = jnp.stack(pieces)  3.15 us
    pallas_call x4, Pallas kernels, gated_mask(): pl.pallas_call(functools.partial(gated_mask_kernel, first), grid=(size //...  2.8 us
  transfers between devices with their start and end apart: 25, of which 16 were waited for; matrix products, arithmetic and copies ran while one was open for 4% of the time, Pallas kernels for 11%

profile of v2, /device:TPU:0, one launch (start us, length us, event | category | flops | bytes accessed | tf_op | source)
XLA Modules:
  0.0 112.9 jit_solution(12937993749207352079)
XLA Ops:
  2.6 3.1 %collective-permute-start.10 = (bf16[512,256]{1,0:T(8,128)(2,1)S(1)}, bf16[512,256]{1,0:T(8,128)(2,1)S(1)}, u32[]{:S(2)}, u32[]{:S(2)}) collective-permute-start(bf16[512,256]{1,0:T(8,128)(2,1)S(1)} %shard_map.50.refs_0_), channel_id=1, source_target_pairs={{0,1},{1,2},{2,3},{3,0},{4,5},{5,6},{6,7},{7,4},{8,9},{9,10},{10,1... | collective-permute-start | bytes 786440 | tf_op jit(solution)/shard_map/ppermute | solution.py:167
  10.1 1.7 %fusion = (bf16[1,4,512,256]{3,2,1,0:T(8,128)(2,1)}, bf16[4,512,256]{2,1,0:T(8,128)(2,1)}) fusion(bf16[512,4,256]{2,1,0:T(4,128)(2,1)S(1)} %copy-done.11, bf16[512,4]{0,1:T(4,128)(2,1)S(1)} %bitcast.32), kind=kLoop, calls=%fused_computation.2 | loop fusion | flops 524288 | bytes 3149824 | tf_op jit(solution)/shard_map/stack | solution.py:192
  11.8 1.6 %collective-permute-start = (bf16[640,256]{1,0:T(8,128)(2,1)S(1)}, bf16[640,256]{1,0:T(8,128)(2,1)S(1)}, u32[]{:S(2)}, u32[]{:S(2)}) collective-permute-start(bf16[640,256]{1,0:T(8,128)(2,1)S(1)} %copy-done.3), channel_id=1, source_target_pairs={{0,1},{1,2},{2,3},{3,0},{4,5},{5,6},{6,7},{7,4},{8,9},{9,10},{10,1... | collective-permute-start | bytes 983048 | tf_op jit(solution)/shard_map/ppermute | solution.py:167
  15.7 8.4 %collective-permute-done.refs_1_ = bf16[640,256]{1,0:T(8,128)(2,1)S(1)} collective-permute-done((bf16[640,256]{1,0:T(8,128)(2,1)S(1)}, bf16[640,256]{1,0:T(8,128)(2,1)S(1)}, u32[]{:S(2)}, u32[]{:S(2)}) %collective-permute-start) | collective-permute-done | bytes 327712 | tf_op jit(solution)/shard_map/ppermute | solution.py:167
  24.1 5.6 %collective-permute-done.11.refs_2_ = bf16[512,256]{1,0:T(8,128)(2,1)S(1)} collective-permute-done((bf16[512,256]{1,0:T(8,128)(2,1)S(1)}, bf16[512,256]{1,0:T(8,128)(2,1)S(1)}, u32[]{:S(2)}, u32[]{:S(2)}) %collective-permute-start.11) | collective-permute-done | bytes 262176 | tf_op jit(solution)/shard_map/ppermute | solution.py:167
  30.4 6.3 %collective-permute-done.1.refs_2_ = bf16[640,256]{1,0:T(8,128)(2,1)S(1)} collective-permute-done((bf16[640,256]{1,0:T(8,128)(2,1)S(1)}, bf16[640,256]{1,0:T(8,128)(2,1)S(1)}, u32[]{:S(2)}, u32[]{:S(2)}) %collective-permute-start.1) | collective-permute-done | bytes 327712 | tf_op jit(solution)/shard_map/ppermute | solution.py:167
  36.7 5.6 %collective-permute-done.12.refs_0_.refs_3_ = bf16[512,256]{1,0:T(8,128)(2,1)S(1)} collective-permute-done((bf16[512,256]{1,0:T(8,128)(2,1)S(1)}, bf16[512,256]{1,0:T(8,128)(2,1)S(1)}, u32[]{:S(2)}, u32[]{:S(2)}) %collective-permute-start.12) | collective-permute-done | bytes 262176 | tf_op jit(solution)/shard_map/ppermute | solution.py:167
  43.4 5.9 %collective-permute-done.2.refs_0_.refs_3_ = bf16[640,256]{1,0:T(8,128)(2,1)S(1)} collective-permute-done((bf16[640,256]{1,0:T(8,128)(2,1)S(1)}, bf16[640,256]{1,0:T(8,128)(2,1)S(1)}, u32[]{:S(2)}, u32[]{:S(2)}) %collective-permute-start.2) | collective-permute-done | bytes 327712 | tf_op jit(solution)/shard_map/ppermute | solution.py:167
  50.1 4.9 %collective-permute-done.13.refs_1_ = bf16[512,256]{1,0:T(8,128)(2,1)S(1)} collective-permute-done((bf16[512,256]{1,0:T(8,128)(2,1)S(1)}, bf16[512,256]{1,0:T(8,128)(2,1)S(1)}, u32[]{:S(2)}, u32[]{:S(2)}) %collective-permute-start.13) | collective-permute-done | bytes 262176 | tf_op jit(solution)/shard_map/ppermute | solution.py:167
  56.5 2.0 %shard_map.54 = (f32[512,256]{1,0:T(8,128)S(1)}, s16[528,256]{1,0:T(8,128)(2,1)S(1)}, s16[528,256]{1,0:T(8,128)(2,1)S(1)}, s16[528,256]{1,0:T(8,128)(2,1)S(1)}) custom-call(s32[9]{0:T(128)S(1)} %stack.48.where, bf16[512,256]{1,0:T(8,128)(2,1)S(1)} %shard_map.50.refs_0_, bf16[512,256]{1,0:T(8,128)(2,1)S(1)} %copy-done.7, bf16[512,256]{1,0:T(8,128)(2,1)S(1)} %copy-done.9, ...), custom_call_target="tpu_custom_call" | custom-call | flops 1073741824 | bytes 3932160 | tf_op jit(solution)/shard_map/pallas_call | solution.py:87
  61.6 2.8 %collective-permute-done.14.refs_2_ = bf16[512,256]{1,0:T(8,128)(2,1)S(1)} collective-permute-done((bf16[512,256]{1,0:T(8,128)(2,1)S(1)}, bf16[512,256]{1,0:T(8,128)(2,1)S(1)}, u32[]{:S(2)}, u32[]{:S(2)}) %collective-permute-start.14) | collective-permute-done | bytes 262176 | tf_op jit(solution)/shard_map/ppermute | solution.py:167
  65.8 2.4 %collective-permute-start.24 = (s16[528,256]{1,0:T(8,128)(2,1)S(1)}, s16[528,256]{1,0:T(8,128)(2,1)S(1)}, u32[]{:S(2)}, u32[]{:S(2)}) collective-permute-start(s16[528,256]{1,0:T(8,128)(2,1)S(1)} %get-tuple-element.44), channel_id=1, source_target_pairs={{0,24},{8,16},{16,8},{24,0},{1,25},{9,17},{17,9},{25,1},{2,26},{10... | collective-permute-start | bytes 811016 | tf_op jit(solution)/shard_map/ppermute | solution.py:205
  68.2 2.4 %shard_map.53 = (f32[640,256]{1,0:T(8,128)S(1)}, s16[656,256]{1,0:T(8,128)(2,1)S(1)}, s16[656,256]{1,0:T(8,128)(2,1)S(1)}, s16[656,256]{1,0:T(8,128)(2,1)S(1)}) custom-call(s32[9]{0:T(128)S(1)} %stack.48.where, bf16[640,256]{1,0:T(8,128)(2,1)S(1)} %copy-done.3, bf16[640,256]{1,0:T(8,128)(2,1)S(1)} %collective-permute-done.refs_1_, ...), custom_call_target="tpu_custom_call" | custom-call | flops 1342177280 | bytes 4390912 | tf_op jit(solution)/shard_map/pallas_call | solution.py:87
  71.7 5.4 %collective-permute-done.4.refs_2_ = bf16[384,256]{1,0:T(8,128)(2,1)S(1)} collective-permute-done((bf16[384,256]{1,0:T(8,128)(2,1)S(1)}, bf16[384,256]{1,0:T(8,128)(2,1)S(1)}, u32[]{:S(2)}, u32[]{:S(2)}) %collective-permute-start.4) | collective-permute-done | bytes 196640 | tf_op jit(solution)/shard_map/ppermute | solution.py:167
  77.2 2.4 %collective-permute-start.21 = (s16[656,256]{1,0:T(8,128)(2,1)S(1)}, s16[656,256]{1,0:T(8,128)(2,1)S(1)}, u32[]{:S(2)}, u32[]{:S(2)}) collective-permute-start(s16[656,256]{1,0:T(8,128)(2,1)S(1)} %get-tuple-element.40), channel_id=1, source_target_pairs={{0,24},{8,16},{16,8},{24,0},{1,25},{9,17},{17,9},{25,1},{2,26},{10... | collective-permute-start | bytes 1007624 | tf_op jit(solution)/shard_map/ppermute | solution.py:205
  79.6 2.0 %shard_map.52 = (f32[512,256]{1,0:T(8,128)S(1)}, s16[528,256]{1,0:T(8,128)(2,1)S(1)}, s16[528,256]{1,0:T(8,128)(2,1)S(1)}, s16[528,256]{1,0:T(8,128)(2,1)S(1)}) custom-call(s32[9]{0:T(128)S(1)} %stack.48.where, bf16[512,256]{1,0:T(8,128)(2,1)S(1)} %shard_map.51.refs_0_, bf16[512,256]{1,0:T(8,128)(2,1)S(1)} %collective-permute-done.13.refs_1_, ...), custom_call_target="tpu_custom_call" | custom-call | flops 1073741824 | bytes 3932160 | tf_op jit(solution)/shard_map/pallas_call | solution.py:87
  83.9 3.2 %collective-permute-done.5.refs_3_ = bf16[384,256]{1,0:T(8,128)(2,1)S(1)} collective-permute-done((bf16[384,256]{1,0:T(8,128)(2,1)S(1)}, bf16[384,256]{1,0:T(8,128)(2,1)S(1)}, u32[]{:S(2)}, u32[]{:S(2)}) %collective-permute-start.5) | collective-permute-done | bytes 196640 | tf_op jit(solution)/shard_map/ppermute | solution.py:167
  87.6 1.7 %shard_map.49 = (f32[384,256]{1,0:T(8,128)S(1)}, s16[400,256]{1,0:T(8,128)(2,1)S(1)}, s16[400,256]{1,0:T(8,128)(2,1)S(1)}, s16[400,256]{1,0:T(8,128)(2,1)S(1)}) custom-call(s32[9]{0:T(128)S(1)} %stack.48.where, bf16[384,256]{1,0:T(8,128)(2,1)S(1)} %shard_map.47.refs_0_, bf16[384,256]{1,0:T(8,128)(2,1)S(1)} %collective-permute-done.3.refs_1_, ...), custom_call_target="tpu_custom_call" | custom-call | flops 805306368 | bytes 3473408 | tf_op jit(solution)/shard_map/pallas_call | solution.py:87
  89.2 1.6 %collective-permute-start.7 = (s16[400,256]{1,0:T(8,128)(2,1)S(1)}, s16[400,256]{1,0:T(8,128)(2,1)S(1)}, u32[]{:S(2)}, u32[]{:S(2)}) collective-permute-start(s16[400,256]{1,0:T(8,128)(2,1)S(1)} %get-tuple-element.30), channel_id=1, source_target_pairs={{0,8},{8,0},{16,24},{24,16},{1,9},{9,1},{17,25},{25,17},{2,10},{10... | collective-permute-start | bytes 614408 | tf_op jit(solution)/shard_map/ppermute | solution.py:205
  92.3 4.1 %collective-permute-done.16.refs_0_ = s16[528,256]{1,0:T(8,128)(2,1)S(1)} collective-permute-done((s16[528,256]{1,0:T(8,128)(2,1)S(1)}, s16[528,256]{1,0:T(8,128)(2,1)S(1)}, u32[]{:S(2)}, u32[]{:S(2)}) %collective-permute-start.16) | collective-permute-done | bytes 270368 | tf_op jit(solution)/shard_map/ppermute | solution.py:205
  99.2 3.0 %collective-permute-done.18.refs_2_ = s16[528,256]{1,0:T(8,128)(2,1)S(1)} collective-permute-done((s16[528,256]{1,0:T(8,128)(2,1)S(1)}, s16[528,256]{1,0:T(8,128)(2,1)S(1)}, u32[]{:S(2)}, u32[]{:S(2)}) %collective-permute-start.18) | collective-permute-done | bytes 270368 | tf_op jit(solution)/shard_map/ppermute | solution.py:205
  102.4 4.2 %collective-permute-done.7.refs_0_ = s16[400,256]{1,0:T(8,128)(2,1)S(1)} collective-permute-done((s16[400,256]{1,0:T(8,128)(2,1)S(1)}, s16[400,256]{1,0:T(8,128)(2,1)S(1)}, u32[]{:S(2)}, u32[]{:S(2)}) %collective-permute-start.7) | collective-permute-done | bytes 204832 | tf_op jit(solution)/shard_map/ppermute | solution.py:205
  106.6 2.5 %collective-permute-done.9.refs_2_ = s16[400,256]{1,0:T(8,128)(2,1)S(1)} collective-permute-done((s16[400,256]{1,0:T(8,128)(2,1)S(1)}, s16[400,256]{1,0:T(8,128)(2,1)S(1)}, u32[]{:S(2)}, u32[]{:S(2)}) %collective-permute-start.9) | collective-permute-done | bytes 204832 | tf_op jit(solution)/shard_map/ppermute | solution.py:205
  109.3 2.5 %psum.7.column_ref = f32[1,256]{1,0:T(1,128)S(1)} all-reduce(f32[1,256]{1,0:T(1,128)S(1)} %get-tuple-element.48), channel_id=1, replica_groups=mesh['layer'=4,'row'=2,'col'=4] {'row'}, use_global_device_ids=true, to_apply=%region_0.1 | all-reduce | flops 256 | bytes 2048 | tf_op jit(solution)/shard_map/psum | solution.py:210
  (76 shorter events, 27.2 us)
Async XLA Ops:
  2.6 11.4 %collective-permute-start.10 = (bf16[512,256]{1,0:T(8,128)(2,1)S(1)}, bf16[512,256]{1,0:T(8,128)(2,1)S(1)}, u32[]{:S(2)}, u32[]{:S(2)}) collective-permute-start(bf16[512,256]{1,0:T(8,128)(2,1)S(1)} %shard_map.50.refs_0_), channel_id=1, source_target_pairs={{0,1},{1,2},{2,3},{3,0},{4,5},{5,6},{6,7},{7,4},{8,9},{9,10},{10,1... | collective-permute-start | bytes 786440 | tf_op jit(solution)/shard_map/ppermute | solution.py:167
  11.8 43.2 %collective-permute-start.6 = (bf16[4,512,256]{2,1,0:T(8,128)(2,1)}, bf16[4,512,256]{2,1,0:T(8,128)(2,1)}, u32[]{:S(2)}, u32[]{:S(2)}) collective-permute-start(bf16[4,512,256]{2,1,0:T(8,128)(2,1)} %get-tuple-element.54), channel_id=1, source_target_pairs={{0,4},{4,0},{1,5},{5,1},{2,6},{6,2},{3,7},{7,3},{8,12},{12,8},{9,1... | collective-permute-start | bytes 3145736 | tf_op jit(solution)/shard_map/ppermute | solution.py:167
  11.8 12.3 %collective-permute-start = (bf16[640,256]{1,0:T(8,128)(2,1)S(1)}, bf16[640,256]{1,0:T(8,128)(2,1)S(1)}, u32[]{:S(2)}, u32[]{:S(2)}) collective-permute-start(bf16[640,256]{1,0:T(8,128)(2,1)S(1)} %copy-done.3), channel_id=1, source_target_pairs={{0,1},{1,2},{2,3},{3,0},{4,5},{5,6},{6,7},{7,4},{8,9},{9,10},{10,1... | collective-permute-start | bytes 983048 | tf_op jit(solution)/shard_map/ppermute | solution.py:167
  14.0 15.7 %collective-permute-start.11 = (bf16[512,256]{1,0:T(8,128)(2,1)S(1)}, bf16[512,256]{1,0:T(8,128)(2,1)S(1)}, u32[]{:S(2)}, u32[]{:S(2)}) collective-permute-start(bf16[512,256]{1,0:T(8,128)(2,1)S(1)} %collective-permute-done.10.refs_1_), channel_id=1, source_target_pairs={{0,1},{1,2},{2,3},{3,0},{4,5},{5,6},{6,7},{7,4},{8,9},{9,10},{10,1... | collective-permute-start | bytes 786440 | tf_op jit(solution)/shard_map/ppermute | solution.py:167
  24.1 12.6 %collective-permute-start.1 = (bf16[640,256]{1,0:T(8,128)(2,1)S(1)}, bf16[640,256]{1,0:T(8,128)(2,1)S(1)}, u32[]{:S(2)}, u32[]{:S(2)}) collective-permute-start(bf16[640,256]{1,0:T(8,128)(2,1)S(1)} %collective-permute-done.refs_1_), channel_id=1, source_target_pairs={{0,1},{1,2},{2,3},{3,0},{4,5},{5,6},{6,7},{7,4},{8,9},{9,10},{10,1... | collective-permute-start | bytes 983048 | tf_op jit(solution)/shard_map/ppermute | solution.py:167
  29.7 12.6 %collective-permute-start.12 = (bf16[512,256]{1,0:T(8,128)(2,1)S(1)}, bf16[512,256]{1,0:T(8,128)(2,1)S(1)}, u32[]{:S(2)}, u32[]{:S(2)}) collective-permute-start(bf16[512,256]{1,0:T(8,128)(2,1)S(1)} %collective-permute-done.11.refs_2_), channel_id=1, source_target_pairs={{0,1},{1,2},{2,3},{3,0},{4,5},{5,6},{6,7},{7,4},{8,9},{9,10},{10,1... | collective-permute-start | bytes 786440 | tf_op jit(solution)/shard_map/ppermute | solution.py:167
  36.7 12.6 %collective-permute-start.2 = (bf16[640,256]{1,0:T(8,128)(2,1)S(1)}, bf16[640,256]{1,0:T(8,128)(2,1)S(1)}, u32[]{:S(2)}, u32[]{:S(2)}) collective-permute-start(bf16[640,256]{1,0:T(8,128)(2,1)S(1)} %collective-permute-done.1.refs_2_), channel_id=1, source_target_pairs={{0,1},{1,2},{2,3},{3,0},{4,5},{5,6},{6,7},{7,4},{8,9},{9,10},{10,1... | collective-permute-start | bytes 983048 | tf_op jit(solution)/shard_map/ppermute | solution.py:167
  43.1 11.9 %collective-permute-start.13 = (bf16[512,256]{1,0:T(8,128)(2,1)S(1)}, bf16[512,256]{1,0:T(8,128)(2,1)S(1)}, u32[]{:S(2)}, u32[]{:S(2)}) collective-permute-start(bf16[512,256]{1,0:T(8,128)(2,1)S(1)} %shard_map.51.refs_0_), channel_id=1, source_target_pairs={{0,1},{1,2},{2,3},{3,0},{4,5},{5,6},{6,7},{7,4},{8,9},{9,10},{10,1... | collective-permute-start | bytes 786440 | tf_op jit(solution)/shard_map/ppermute | solution.py:167
  50.0 14.4 %collective-permute-start.3 = (bf16[384,256]{1,0:T(8,128)(2,1)S(1)}, bf16[384,256]{1,0:T(8,128)(2,1)S(1)}, u32[]{:S(2)}, u32[]{:S(2)}) collective-permute-start(bf16[384,256]{1,0:T(8,128)(2,1)S(1)} %shard_map.47.refs_0_), channel_id=1, source_target_pairs={{0,1},{1,2},{2,3},{3,0},{4,5},{5,6},{6,7},{7,4},{8,9},{9,10},{10,1... | collective-permute-start | bytes 589832 | tf_op jit(solution)/shard_map/ppermute | solution.py:167
  55.0 9.4 %collective-permute-start.14 = (bf16[512,256]{1,0:T(8,128)(2,1)S(1)}, bf16[512,256]{1,0:T(8,128)(2,1)S(1)}, u32[]{:S(2)}, u32[]{:S(2)}) collective-permute-start(bf16[512,256]{1,0:T(8,128)(2,1)S(1)} %collective-permute-done.13.refs_1_), channel_id=1, source_target_pairs={{0,1},{1,2},{2,3},{3,0},{4,5},{5,6},{6,7},{7,4},{8,9},{9,10},{10,1... | collective-permute-start | bytes 786440 | tf_op jit(solution)/shard_map/ppermute | solution.py:167
  58.5 12.1 %collective-permute-start.22 = (s16[528,256]{1,0:T(8,128)(2,1)S(1)}, s16[528,256]{1,0:T(8,128)(2,1)S(1)}, u32[]{:S(2)}, u32[]{:S(2)}) collective-permute-start(s16[528,256]{1,0:T(8,128)(2,1)S(1)} %get-tuple-element.42), channel_id=1, source_target_pairs={{0,8},{8,0},{16,24},{24,16},{1,9},{9,1},{17,25},{25,17},{2,10},{10... | collective-permute-start | bytes 811016 | tf_op jit(solution)/shard_map/ppermute | solution.py:205
  60.1 11.1 %collective-permute-start.23 = (s16[528,256]{1,0:T(8,128)(2,1)S(1)}, s16[528,256]{1,0:T(8,128)(2,1)S(1)}, u32[]{:S(2)}, u32[]{:S(2)}) collective-permute-start(s16[528,256]{1,0:T(8,128)(2,1)S(1)} %get-tuple-element.43), channel_id=1, source_target_pairs={{0,16},{8,24},{16,0},{24,8},{1,17},{9,25},{17,1},{25,9},{2,18},{10... | collective-permute-start | bytes 811016 | tf_op jit(solution)/shard_map/ppermute | solution.py:205
  64.4 15.2 %collective-permute-start.15 = (bf16[512,256]{1,0:T(8,128)(2,1)S(1)}, bf16[512,256]{1,0:T(8,128)(2,1)S(1)}, u32[]{:S(2)}, u32[]{:S(2)}) collective-permute-start(bf16[512,256]{1,0:T(8,128)(2,1)S(1)} %collective-permute-done.14.refs_2_), channel_id=1, source_target_pairs={{0,1},{1,2},{2,3},{3,0},{4,5},{5,6},{6,7},{7,4},{8,9},{9,10},{10,1... | collective-permute-start | bytes 786440 | tf_op jit(solution)/shard_map/ppermute | solution.py:167
  64.4 12.7 %collective-permute-start.4 = (bf16[384,256]{1,0:T(8,128)(2,1)S(1)}, bf16[384,256]{1,0:T(8,128)(2,1)S(1)}, u32[]{:S(2)}, u32[]{:S(2)}) collective-permute-start(bf16[384,256]{1,0:T(8,128)(2,1)S(1)} %collective-permute-done.3.refs_1_), channel_id=1, source_target_pairs={{0,1},{1,2},{2,3},{3,0},{4,5},{5,6},{6,7},{7,4},{8,9},{9,10},{10,1... | collective-permute-start | bytes 589832 | tf_op jit(solution)/shard_map/ppermute | solution.py:167
  65.8 15.8 %collective-permute-start.24 = (s16[528,256]{1,0:T(8,128)(2,1)S(1)}, s16[528,256]{1,0:T(8,128)(2,1)S(1)}, u32[]{:S(2)}, u32[]{:S(2)}) collective-permute-start(s16[528,256]{1,0:T(8,128)(2,1)S(1)} %get-tuple-element.44), channel_id=1, source_target_pairs={{0,24},{8,16},{16,8},{24,0},{1,25},{9,17},{17,9},{25,1},{2,26},{10... | collective-permute-start | bytes 811016 | tf_op jit(solution)/shard_map/ppermute | solution.py:205
  70.6 12.7 %collective-permute-start.19 = (s16[656,256]{1,0:T(8,128)(2,1)S(1)}, s16[656,256]{1,0:T(8,128)(2,1)S(1)}, u32[]{:S(2)}, u32[]{:S(2)}) collective-permute-start(s16[656,256]{1,0:T(8,128)(2,1)S(1)} %get-tuple-element.38), channel_id=1, source_target_pairs={{0,8},{8,0},{16,24},{24,16},{1,9},{9,1},{17,25},{25,17},{2,10},{10... | collective-permute-start | bytes 1007624 | tf_op jit(solution)/shard_map/ppermute | solution.py:205
  71.2 18.0 %collective-permute-start.20 = (s16[656,256]{1,0:T(8,128)(2,1)S(1)}, s16[656,256]{1,0:T(8,128)(2,1)S(1)}, u32[]{:S(2)}, u32[]{:S(2)}) collective-permute-start(s16[656,256]{1,0:T(8,128)(2,1)S(1)} %get-tuple-element.39), channel_id=1, source_target_pairs={{0,16},{8,24},{16,0},{24,8},{1,17},{9,25},{17,1},{25,9},{2,18},{10... | collective-permute-start | bytes 1007624 | tf_op jit(solution)/shard_map/ppermute | solution.py:205
  77.2 13.6 %collective-permute-start.21 = (s16[656,256]{1,0:T(8,128)(2,1)S(1)}, s16[656,256]{1,0:T(8,128)(2,1)S(1)}, u32[]{:S(2)}, u32[]{:S(2)}) collective-permute-start(s16[656,256]{1,0:T(8,128)(2,1)S(1)} %get-tuple-element.40), channel_id=1, source_target_pairs={{0,24},{8,16},{16,8},{24,0},{1,25},{9,17},{17,9},{25,1},{2,26},{10... | collective-permute-start | bytes 1007624 | tf_op jit(solution)/shard_map/ppermute | solution.py:205
  81.6 14.8 %collective-permute-start.16 = (s16[528,256]{1,0:T(8,128)(2,1)S(1)}, s16[528,256]{1,0:T(8,128)(2,1)S(1)}, u32[]{:S(2)}, u32[]{:S(2)}) collective-permute-start(s16[528,256]{1,0:T(8,128)(2,1)S(1)} %get-tuple-element.34), channel_id=1, source_target_pairs={{0,8},{8,0},{16,24},{24,16},{1,9},{9,1},{17,25},{25,17},{2,10},{10... | collective-permute-start | bytes 811016 | tf_op jit(solution)/shard_map/ppermute | solution.py:205
  83.4 15.8 %collective-permute-start.17 = (s16[528,256]{1,0:T(8,128)(2,1)S(1)}, s16[528,256]{1,0:T(8,128)(2,1)S(1)}, u32[]{:S(2)}, u32[]{:S(2)}) collective-permute-start(s16[528,256]{1,0:T(8,128)(2,1)S(1)} %get-tuple-element.35), channel_id=1, source_target_pairs={{0,16},{8,24},{16,0},{24,8},{1,17},{9,25},{17,1},{25,9},{2,18},{10... | collective-permute-start | bytes 811016 | tf_op jit(solution)/shard_map/ppermute | solution.py:205
  87.1 15.1 %collective-permute-start.18 = (s16[528,256]{1,0:T(8,128)(2,1)S(1)}, s16[528,256]{1,0:T(8,128)(2,1)S(1)}, u32[]{:S(2)}, u32[]{:S(2)}) collective-permute-start(s16[528,256]{1,0:T(8,128)(2,1)S(1)} %get-tuple-element.36), channel_id=1, source_target_pairs={{0,24},{8,16},{16,8},{24,0},{1,25},{9,17},{17,9},{25,1},{2,26},{10... | collective-permute-start | bytes 811016 | tf_op jit(solution)/shard_map/ppermute | solution.py:205
  89.2 17.4 %collective-permute-start.7 = (s16[400,256]{1,0:T(8,128)(2,1)S(1)}, s16[400,256]{1,0:T(8,128)(2,1)S(1)}, u32[]{:S(2)}, u32[]{:S(2)}) collective-permute-start(s16[400,256]{1,0:T(8,128)(2,1)S(1)} %get-tuple-element.30), channel_id=1, source_target_pairs={{0,8},{8,0},{16,24},{24,16},{1,9},{9,1},{17,25},{25,17},{2,10},{10... | collective-permute-start | bytes 614408 | tf_op jit(solution)/shard_map/ppermute | solution.py:205
  90.8 15.8 %collective-permute-start.8 = (s16[400,256]{1,0:T(8,128)(2,1)S(1)}, s16[400,256]{1,0:T(8,128)(2,1)S(1)}, u32[]{:S(2)}, u32[]{:S(2)}) collective-permute-start(s16[400,256]{1,0:T(8,128)(2,1)S(1)} %get-tuple-element.31), channel_id=1, source_target_pairs={{0,16},{8,24},{16,0},{24,8},{1,17},{9,25},{17,1},{25,9},{2,18},{10... | collective-permute-start | bytes 614408 | tf_op jit(solution)/shard_map/ppermute | solution.py:205
  96.4 12.7 %collective-permute-start.9 = (s16[400,256]{1,0:T(8,128)(2,1)S(1)}, s16[400,256]{1,0:T(8,128)(2,1)S(1)}, u32[]{:S(2)}, u32[]{:S(2)}) collective-permute-start(s16[400,256]{1,0:T(8,128)(2,1)S(1)} %get-tuple-element.32), channel_id=1, source_target_pairs={{0,24},{8,16},{16,8},{24,0},{1,25},{9,17},{17,9},{25,1},{2,26},{10... | collective-permute-start | bytes 614408 | tf_op jit(solution)/shard_map/ppermute | solution.py:205
  (14 other events, 115.7 us)

commit v3 on v2

--- a/solution.py
+++ b/solution.py
@@ -57,16 +57,15 @@
 
 
 def partial_kernel(n_sources, n_layers, where, *refs):
-    lefts = refs[:n_sources]
-    right_ref, mine_ref, *sent_refs = refs[n_sources:]
-    rows = lefts[0].shape[0]
+    left_ref, right_ref, mine_ref, *sent_refs = refs
+    rows = left_ref.shape[1]
     for step in range(n_layers):
         layer = where[0] ^ step
         total = jnp.zeros((rows, right_ref.shape[3]), jnp.float32)
         for source in range(n_sources):
             start = pl.multiple_of(where[2 + 2 * source], TILE)
             total += jnp.dot(
-                lefts[source][...],
+                left_ref[source],
                 right_ref[where[1 + 2 * source], layer, pl.ds(start, TILE), :],
                 preferred_element_type=jnp.float32,
             )
@@ -82,21 +81,21 @@
         sent_refs[step - 1][rows:, :] = codes.astype(jnp.int16)
 
 
-def partial_products(where, lefts, right, n_layers):
-    rows, columns = lefts[0].shape[0], right.shape[3]
-    return pl.pallas_call(
-        functools.partial(partial_kernel, len(lefts), n_layers),
+def partial_products(where, left, right, n_layers):
+    n_sources, rows, columns = left.shape[0], left.shape[1], right.shape[3]
+    return pl.pallas_call(
+        functools.partial(partial_kernel, n_sources, n_layers),
         out_shape=[jax.ShapeDtypeStruct((rows, columns), jnp.float32)]
         + [jax.ShapeDtypeStruct((rows + SCALE_ROWS, columns), jnp.int16)] * (n_layers - 1),
-        in_specs=[pl.BlockSpec(memory_space=pltpu.SMEM)] + [VMEM] * (len(lefts) + 1),
+        in_specs=[pl.BlockSpec(memory_space=pltpu.SMEM)] + [VMEM] * 2,
         out_specs=[VMEM] * n_layers,
         compiler_params=PARAMS,
         cost_estimate=pl.CostEstimate(
-            flops=2 * rows * len(lefts) * TILE * columns * n_layers,
+            flops=2 * rows * n_sources * TILE * columns * n_layers,
             bytes_accessed=right.size * 2 + rows * columns * 14,
             transcendentals=0,
         ),
-    )(where, *lefts, right)
+    )(where, left, right)
 
 
 def combine_kernel(n_received, mine_ref, *refs):
@@ -169,7 +168,7 @@
 
 def per_device(left_values, left_pattern, right_values, right_pattern):
     n_layers, n_rows, n_cols = (lax.axis_size(a) for a in ("layer", "row", "col"))
-    layer, row, col = (lax.axis_index(a) for a in ("layer", "row", "col"))
+    layer, row = lax.axis_index("layer"), lax.axis_index("row")
     rows_local, _, columns_local = left_values.shape
     inner_piece = right_values.shape[0]
     sizes = [rows_local * part // 16 for part in SIXTEENTHS]
@@ -177,14 +176,10 @@
 
     left = left_values.reshape(rows_local, columns_local)
     pattern = left_pattern.reshape(-1)
-    rings = []
-    for i, (at, size) in enumerate(zip(starts, sizes)):
-        ring = [gated_mask(left, pattern, at, size, [rings[i - 2][-1]] if i > 1 else [])]
-        for _ in range(n_cols - 1):
-            ring.append(shift(ring[-1], "col", 1))
-        rings.append(ring)
-
-    right_pattern = gate(right_pattern, rings[1][0])
+    masked = [gated_mask(left, pattern, at, size, []) for at, size in zip(starts, sizes)]
+    rings = [lax.all_gather(block, "col") for block in masked]
+
+    right_pattern = gate(right_pattern, masked[0])
     right_block = expand_tiles(right_values, right_pattern).transpose(1, 0, 2)
     pieces = [right_block]
     for i in range(1, n_rows):
@@ -193,7 +188,7 @@
 
     where = [layer]
     for source in range(n_cols):
-        inner = (col - source + n_cols) % n_cols * columns_local
+        inner = source * columns_local
         where += [(row - inner // inner_piece + n_rows) % n_rows, inner % inner_piece]
     where = jnp.stack(where).astype(jnp.int32)
 

time: 113 us -> 159 us (1.41)
  blocking collectives: 2.47 us -> 20.2 us
  between operations: 0.42 us -> 13.3 us
  waiting for transfers between devices: 64.5 us -> 74.7 us
  starting transfers between devices: 22.2 us -> 15.8 us
  Pallas kernels: 14.3 us -> 20.4 us
  local copies, waits for them, and re-layouts: 5.09 us -> 10.5 us
    all_gather x0 -> x3, waiting for transfers between devices: none -> 64.3 us  [per_device(): rings = [lax.all_gather(block, 'col') for block in masked]]
    ppermute x13 -> x1, waiting for transfers between devices: 48.9 us -> 2.33 us  [shift(): return lax.ppermute(x, axis, [(i, (i + by) % n) for i in range(n)])]
    all_gather x0 -> x1, blocking collectives: none -> 17.7 us  [per_device(): rings = [lax.all_gather(block, 'col') for block in masked]]
    ppermute x12, waiting for transfers between devices: 15.6 us -> 8.1 us  [per_device(): lax.ppermute(sent[j - 1], 'layer', [(i, i ^ j) for i in range(n_layers)])]
    ppermute x13 -> x1, starting transfers between devices: 7.07 us -> 0.45 us  [shift(): return lax.ppermute(x, axis, [(i, (i + by) % n) for i in range(n)])]
    unnamed x29 -> x43, local copies, waits for them, and re-layouts: 4.88 us -> 10.3 us
    pallas_call x4, Pallas kernels: 2.8 us -> 6.99 us  [gated_mask(): pl.pallas_call(functools.partial(gated_mask_kernel, first), grid=(size //...]
  transfers between devices with their start and end apart: 25 -> 16, of which waited for: 16 -> 6; matrix products, arithmetic and copies ran while one was open for 4% -> 3% of each run, Pallas kernels for 11% -> 11%
where the time goes in v3:
time: 159 us
  waiting for transfers between devices  74.7 us (47%)
  Pallas kernels  20.4 us (13%)
  blocking collectives  20.2 us (13%)
  starting transfers between devices  15.8 us (10%)
  between operations  13.3 us (8%)
  local copies, waits for them, and re-layouts  10.5 us (7%)
  other arithmetic  3.72 us (2%)
    all_gather x3, waiting for transfers between devices, per_device(): rings = [lax.all_gather(block, 'col') for block in masked]  64.3 us
    all_gather x1, blocking collectives, per_device(): rings = [lax.all_gather(block, 'col') for block in masked]  17.7 us
    ppermute x12, starting transfers between devices, per_device(): lax.ppermute(sent[j - 1], 'layer', [(i, i ^ j) for i in range(n_layers)])  15.3 us
    unnamed x43, local copies, waits for them, and re-layouts  10.3 us
    pallas_call x4, Pallas kernels, partial_products(): pl.pallas_call(functools.partial(partial_kernel, n_sources, n_layers), ou...  8.91 us
    ppermute x12, waiting for transfers between devices, per_device(): lax.ppermute(sent[j - 1], 'layer', [(i, i ^ j) for i in range(n_layers)])  8.1 us
    pallas_call x4, Pallas kernels, gated_mask(): pl.pallas_call(functools.partial(gated_mask_kernel, first), grid=(size //...  6.99 us
  transfers between devices with their start and end apart: 16, of which 6 were waited for; matrix products, arithmetic and copies ran while one was open for 3% of the time, Pallas kernels for 11%

profile of v3, /device:TPU:0, one launch (start us, length us, event | category | flops | bytes accessed | tf_op | source)
XLA Modules:
  0.0 158.6 jit_solution(8248969274409053173)
XLA Ops:
  8.4 1.9 %shard_map.47.after_ref = bf16[512,256]{1,0:T(8,128)(2,1)} custom-call(s32[8]{0:T(128)S(1)} %bitcast.27, bf16[2048,256]{1,0:T(8,128)(2,1)S(1)} %bitcast.22), custom_call_target="tpu_custom_call" | custom-call | flops 131072 | bytes 524288 | tf_op jit(solution)/shard_map/pallas_call | solution.py:29
  11.1 1.9 %shard_map.50 = bf16[512,256]{1,0:T(8,128)(2,1)} custom-call(s32[8]{0:T(128)S(1)} %bitcast.28, bf16[2048,256]{1,0:T(8,128)(2,1)S(1)} %bitcast.23), custom_call_target="tpu_custom_call" | custom-call | flops 131072 | bytes 524288 | tf_op jit(solution)/shard_map/pallas_call | solution.py:29
  13.1 2.5 %shard_map.52 = bf16[640,256]{1,0:T(8,128)(2,1)} custom-call(s32[8]{0:T(128)S(1)} %bitcast.29, bf16[2048,256]{1,0:T(8,128)(2,1)S(1)} %bitcast.24), custom_call_target="tpu_custom_call" | custom-call | flops 163840 | bytes 655360 | tf_op jit(solution)/shard_map/pallas_call | solution.py:29
  20.3 2.3 %collective-permute-done = bf16[4,512,256]{2,1,0:T(8,128)(2,1)} collective-permute-done((bf16[4,512,256]{2,1,0:T(8,128)(2,1)S(1)}, bf16[4,512,256]{2,1,0:T(8,128)(2,1)}, u32[]{:S(2)}, u32[]{:S(2)}) %collective-permute-start) | collective-permute-done | bytes 1048608 | tf_op jit(solution)/shard_map/ppermute | solution.py:166
  22.7 1.7 %pad_maximum_fusion.refs_1_ = bf16[2,4,512,256]{3,2,1,0:T(8,128)(2,1)S(1)} fusion(bf16[1,4,512,256]{3,2,1,0:T(8,128)(2,1)} %bitcast.9, bf16[1,4,512,256]{3,2,1,0:T(8,128)(2,1)} %get-tuple-element.53), kind=kLoop, calls=%fused_computation | loop fusion | flops 1048576 | bytes 4194304 | tf_op jit(solution)/shard_map/stack | solution.py:187
  24.4 16.7 %all-gather.12.cloned.1.call-done = bf16[2048,256]{1,0:T(8,128)(2,1)} async-done(((bf16[512,256]{1,0:T(8,128)(2,1)}), bf16[2048,256]{1,0:T(8,128)(2,1)}) %all-gather.12.cloned.1.call-update) | async-done | bytes 1048592 | tf_op jit(solution)/shard_map/all_gather | solution.py:180
  42.4 2.8 %shard_map.54 = (f32[512,256]{1,0:T(8,128)S(1)}, s16[528,256]{1,0:T(8,128)(2,1)}, s16[528,256]{1,0:T(8,128)(2,1)}, s16[528,256]{1,0:T(8,128)(2,1)}) custom-call(s32[9]{0:T(128)S(1)} %stack.26.where, bf16[4,512,256]{2,1,0:T(8,128)(2,1)S(1)} %bitcast.33, bf16[2,4,512,256]{3,2,1,0:T(8,128)(2,1)S(1)} %pad_maximum_fusion.refs_1_), custom_call_target="tpu_custom_call" | custom-call | flops 1073741824 | bytes 3932160 | tf_op jit(solution)/shard_map/pallas_call | solution.py:86
  45.2 1.5 collective-permute-start.10
  46.6 1.5 collective-permute-start.11
  49.4 20.8 %all-gather.8.cloned.1.call-done = bf16[2048,256]{1,0:T(8,128)(2,1)} async-done(((bf16[512,256]{1,0:T(8,128)(2,1)}), bf16[2048,256]{1,0:T(8,128)(2,1)}) %all-gather.8.cloned.1.call-update) | async-done | bytes 1048592 | tf_op jit(solution)/shard_map/all_gather | solution.py:180
  71.4 2.1 %shard_map.51 = (f32[512,256]{1,0:T(8,128)S(1)}, s16[528,256]{1,0:T(8,128)(2,1)}, s16[528,256]{1,0:T(8,128)(2,1)S(1)}, s16[528,256]{1,0:T(8,128)(2,1)S(1)}) custom-call(s32[9]{0:T(128)S(1)} %stack.26.where, bf16[4,512,256]{2,1,0:T(8,128)(2,1)S(1)} %bitcast.32, bf16[2,4,512,256]{3,2,1,0:T(8,128)(2,1)S(1)} %pad_maximum_fusion.refs_1_), custom_call_target="tpu_custom_call" | custom-call | flops 1073741824 | bytes 3932160 | tf_op jit(solution)/shard_map/pallas_call | solution.py:86
  75.8 1.5 collective-permute-start.4
  77.2 26.8 %all-gather.10.cloned.1.call-done = bf16[2560,256]{1,0:T(8,128)(2,1)} async-done(((bf16[640,256]{1,0:T(8,128)(2,1)}), bf16[2560,256]{1,0:T(8,128)(2,1)}) %all-gather.10.cloned.1.call-update) | async-done | bytes 1310736 | tf_op jit(solution)/shard_map/all_gather | solution.py:180
  105.3 2.4 %shard_map.53 = (f32[640,256]{1,0:T(8,128)S(1)}, s16[656,256]{1,0:T(8,128)(2,1)S(1)}, s16[656,256]{1,0:T(8,128)(2,1)S(1)}, s16[656,256]{1,0:T(8,128)(2,1)S(1)}) custom-call(s32[9]{0:T(128)S(1)} %stack.26.where, bf16[4,640,256]{2,1,0:T(8,128)(2,1)S(1)} %bitcast.31, bf16[2,4,512,256]{3,2,1,0:T(8,128)(2,1)S(1)} %pad_maximum_fusion.refs_1_), custom_call_target="tpu_custom_call" | custom-call | flops 1342177280 | bytes 4390912 | tf_op jit(solution)/shard_map/pallas_call | solution.py:86
  107.7 1.5 collective-permute-start.7
  109.2 1.5 collective-permute-start.8
  111.2 17.7 %all-gather = bf16[1536,256]{1,0:T(8,128)(2,1)S(1)} all-gather(bf16[384,256]{1,0:T(8,128)(2,1)S(1)} %shard_map.46), channel_id=2, replica_groups=mesh['layer'=4,'row'=2,'col'=4] {'col'}, dimensions={0}, use_global_device_ids=true | all-gather | bytes 983040 | tf_op jit(solution)/shard_map/all_gather | solution.py:180
  128.9 1.6 %collective-permute-start.5 = (s16[528,256]{1,0:T(8,128)(2,1)S(1)}, s16[528,256]{1,0:T(8,128)(2,1)S(1)}, u32[]{:S(2)}, u32[]{:S(2)}) collective-permute-start(s16[528,256]{1,0:T(8,128)(2,1)S(1)} %copy-done.17), channel_id=1, source_target_pairs={{0,16},{8,24},{16,0},{24,8},{1,17},{9,25},{17,1},{25,9},{2,18},{10... | collective-permute-start | bytes 811016 | tf_op jit(solution)/shard_map/ppermute | solution.py:200
  130.6 1.5 collective-permute-start.6
  132.1 1.7 %shard_map.49 = (f32[384,256]{1,0:T(8,128)S(1)}, s16[400,256]{1,0:T(8,128)(2,1)S(1)}, s16[400,256]{1,0:T(8,128)(2,1)S(1)}, s16[400,256]{1,0:T(8,128)(2,1)S(1)}) custom-call(s32[9]{0:T(128)S(1)} %stack.26.where, bf16[4,384,256]{2,1,0:T(8,128)(2,1)S(1)} %bitcast.26, bf16[2,4,512,256]{3,2,1,0:T(8,128)(2,1)S(1)} %pad_maximum_fusion.refs_1_), custom_call_target="tpu_custom_call" | custom-call | flops 805306368 | bytes 3473408 | tf_op jit(solution)/shard_map/pallas_call | solution.py:86
  134.3 1.6 %collective-permute-start.2 = (s16[400,256]{1,0:T(8,128)(2,1)S(1)}, s16[400,256]{1,0:T(8,128)(2,1)S(1)}, u32[]{:S(2)}, u32[]{:S(2)}) collective-permute-start(s16[400,256]{1,0:T(8,128)(2,1)S(1)} %get-tuple-element.31), channel_id=1, source_target_pairs={{0,16},{8,24},{16,0},{24,8},{1,17},{9,25},{17,1},{25,9},{2,18},{10... | collective-permute-start | bytes 614408 | tf_op jit(solution)/shard_map/ppermute | solution.py:200
  135.9 1.5 collective-permute-start.3
  139.0 7.1 %collective-permute-done.5.refs_1_ = s16[528,256]{1,0:T(8,128)(2,1)S(1)} collective-permute-done((s16[528,256]{1,0:T(8,128)(2,1)S(1)}, s16[528,256]{1,0:T(8,128)(2,1)S(1)}, u32[]{:S(2)}, u32[]{:S(2)}) %collective-permute-start.5) | collective-permute-done | bytes 270368 | tf_op jit(solution)/shard_map/ppermute | solution.py:200
  148.5 2.5 %psum.7.column_ref = f32[1,256]{1,0:T(1,128)S(1)} all-reduce(f32[1,256]{1,0:T(1,128)S(1)} %get-tuple-element.48), channel_id=1, replica_groups=mesh['layer'=4,'row'=2,'col'=4] {'row'}, use_global_device_ids=true, to_apply=%region_0.1 | all-reduce | flops 256 | bytes 2048 | tf_op jit(solution)/shard_map/psum | solution.py:205
  (76 shorter events, 20.8 us)
Async XLA Ops:
  6.5 6.5 %copy-start.10 = (s32[8,1,1]{0,2,1:T(1,128)S(1)}, s32[8,1,1]{0,2,1:T(1,128)}, u32[]{:S(2)}) copy-start(s32[8,1,1]{0,2,1:T(1,128)} %param.5) | copy-start | bytes 100
  6.5 34.6 %all-gather.12.cloned.1.call-start = ((), (), s32[]{:S(2)}) async-start(), calls=%async_computation.2 | async-start | bytes 1310720 | tf_op jit(solution)/shard_map/all_gather | solution.py:180
  10.3 5.3 %copy-start.19 = (s32[2,4,1]{1,2,0:T(1,128)S(1)}, s32[2,4,1]{1,2,0:T(1,128)}, u32[]{:S(2)}) copy-start(s32[2,4,1]{1,2,0:T(1,128)} %param.7) | copy-start | bytes 100
  10.4 59.8 %all-gather.8.cloned.1.call-start = ((), (), s32[]{:S(2)}) async-start(), calls=%async_computation | async-start | bytes 1310720 | tf_op jit(solution)/shard_map/all_gather | solution.py:180
  11.1 7.4 %copy-start.18 = (bf16[512,4,256]{2,1,0:T(4,128)(2,1)S(1)}, bf16[512,4,256]{2,1,0:T(4,128)(2,1)}, u32[]{:S(2)}) copy-start(bf16[512,4,256]{2,1,0:T(4,128)(2,1)} %param.6) | copy-start | bytes 3145732
  13.0 91.0 %all-gather.10.cloned.1.call-start = ((), (), s32[]{:S(2)}) async-start(), calls=%async_computation.1 | async-start | bytes 1638400 | tf_op jit(solution)/shard_map/all_gather | solution.py:180
  19.8 2.9 %collective-permute-start = (bf16[4,512,256]{2,1,0:T(8,128)(2,1)S(1)}, bf16[4,512,256]{2,1,0:T(8,128)(2,1)}, u32[]{:S(2)}, u32[]{:S(2)}) collective-permute-start(bf16[4,512,256]{2,1,0:T(8,128)(2,1)S(1)} %get-tuple-element.54), channel_id=1, source_target_pairs={{0,4},{4,0},{1,5},{5,1},{2,6},{6,2},{3,7},{7,3},{8,12},{12,8},{9,1... | collective-permute-start | bytes 3145736 | tf_op jit(solution)/shard_map/ppermute | solution.py:166
  45.2 64.0 %collective-permute-start.10 = (s16[528,256]{1,0:T(8,128)(2,1)}, s16[528,256]{1,0:T(8,128)(2,1)}, u32[]{:S(2)}, u32[]{:S(2)}) collective-permute-start(s16[528,256]{1,0:T(8,128)(2,1)} %get-tuple-element.42), channel_id=1, source_target_pairs={{0,8},{8,0},{16,24},{24,16},{1,9},{9,1},{17,25},{25,17},{2,10},{10... | collective-permute-start | bytes 811016 | tf_op jit(solution)/shard_map/ppermute | solution.py:200
  46.6 64.0 %collective-permute-start.11 = (s16[528,256]{1,0:T(8,128)(2,1)}, s16[528,256]{1,0:T(8,128)(2,1)}, u32[]{:S(2)}, u32[]{:S(2)}) collective-permute-start(s16[528,256]{1,0:T(8,128)(2,1)} %get-tuple-element.43), channel_id=1, source_target_pairs={{0,16},{8,24},{16,0},{24,8},{1,17},{9,25},{17,1},{25,9},{2,18},{10... | collective-permute-start | bytes 811016 | tf_op jit(solution)/shard_map/ppermute | solution.py:200
  48.8 80.1 %collective-permute-start.12 = (s16[528,256]{1,0:T(8,128)(2,1)}, s16[528,256]{1,0:T(8,128)(2,1)S(1)}, u32[]{:S(2)}, u32[]{:S(2)}) collective-permute-start(s16[528,256]{1,0:T(8,128)(2,1)} %get-tuple-element.44), channel_id=1, source_target_pairs={{0,24},{8,16},{16,8},{24,0},{1,25},{9,17},{17,9},{25,1},{2,26},{10... | collective-permute-start | bytes 811016 | tf_op jit(solution)/shard_map/ppermute | solution.py:200
  75.8 54.8 %collective-permute-start.4 = (s16[528,256]{1,0:T(8,128)(2,1)}, s16[528,256]{1,0:T(8,128)(2,1)S(1)}, u32[]{:S(2)}, u32[]{:S(2)}) collective-permute-start(s16[528,256]{1,0:T(8,128)(2,1)} %get-tuple-element.34), channel_id=1, source_target_pairs={{0,8},{8,0},{16,24},{24,16},{1,9},{9,1},{17,25},{25,17},{2,10},{10... | collective-permute-start | bytes 811016 | tf_op jit(solution)/shard_map/ppermute | solution.py:200
  105.3 23.6 %copy-start.17 = (s16[528,256]{1,0:T(8,128)(2,1)S(1)}, s16[528,256]{1,0:T(8,128)(2,1)}, u32[]{:S(2)}) copy-start(s16[528,256]{1,0:T(8,128)(2,1)} %copy-done.16) | copy-start | bytes 811012
  105.3 25.3 %copy-start.15 = (s16[528,256]{1,0:T(8,128)(2,1)S(1)}, s16[528,256]{1,0:T(8,128)(2,1)}, u32[]{:S(2)}) copy-start(s16[528,256]{1,0:T(8,128)(2,1)} %copy-done.14) | copy-start | bytes 811012
  107.7 29.7 %copy-start.5 = (f32[512,256]{1,0:T(8,128)S(1)}, f32[512,256]{1,0:T(8,128)}, u32[]{:S(2)}) copy-start(f32[512,256]{1,0:T(8,128)} %copy-done.4) | copy-start | bytes 1572868
  107.7 26.1 %collective-permute-start.7 = (s16[656,256]{1,0:T(8,128)(2,1)S(1)}, s16[656,256]{1,0:T(8,128)(2,1)S(1)}, u32[]{:S(2)}, u32[]{:S(2)}) collective-permute-start(s16[656,256]{1,0:T(8,128)(2,1)S(1)} %get-tuple-element.38), channel_id=1, source_target_pairs={{0,8},{8,0},{16,24},{24,16},{1,9},{9,1},{17,25},{25,17},{2,10},{10... | collective-permute-start | bytes 1007624 | tf_op jit(solution)/shard_map/ppermute | solution.py:200
  109.2 25.1 %collective-permute-start.8 = (s16[656,256]{1,0:T(8,128)(2,1)S(1)}, s16[656,256]{1,0:T(8,128)(2,1)S(1)}, u32[]{:S(2)}, u32[]{:S(2)}) collective-permute-start(s16[656,256]{1,0:T(8,128)(2,1)S(1)} %get-tuple-element.39), channel_id=1, source_target_pairs={{0,16},{8,24},{16,0},{24,8},{1,17},{9,25},{17,1},{25,9},{2,18},{10... | collective-permute-start | bytes 1007624 | tf_op jit(solution)/shard_map/ppermute | solution.py:200
  110.7 25.2 %collective-permute-start.9 = (s16[656,256]{1,0:T(8,128)(2,1)S(1)}, s16[656,256]{1,0:T(8,128)(2,1)S(1)}, u32[]{:S(2)}, u32[]{:S(2)}) collective-permute-start(s16[656,256]{1,0:T(8,128)(2,1)S(1)} %get-tuple-element.40), channel_id=1, source_target_pairs={{0,24},{8,16},{16,8},{24,0},{1,25},{9,17},{17,9},{25,1},{2,26},{10... | collective-permute-start | bytes 1007624 | tf_op jit(solution)/shard_map/ppermute | solution.py:200
  128.9 17.2 %collective-permute-start.5 = (s16[528,256]{1,0:T(8,128)(2,1)S(1)}, s16[528,256]{1,0:T(8,128)(2,1)S(1)}, u32[]{:S(2)}, u32[]{:S(2)}) collective-permute-start(s16[528,256]{1,0:T(8,128)(2,1)S(1)} %copy-done.17), channel_id=1, source_target_pairs={{0,16},{8,24},{16,0},{24,8},{1,17},{9,25},{17,1},{25,9},{2,18},{10... | collective-permute-start | bytes 811016 | tf_op jit(solution)/shard_map/ppermute | solution.py:200
  130.6 8.1 %copy-start.6 = (s16[528,256]{1,0:T(8,128)(2,1)}, s16[528,256]{1,0:T(8,128)(2,1)S(1)}, u32[]{:S(2)}) copy-start(s16[528,256]{1,0:T(8,128)(2,1)S(1)} %collective-permute-done.4.refs_0_) | copy-start | bytes 811012
  130.6 15.5 %collective-permute-start.6 = (s16[528,256]{1,0:T(8,128)(2,1)S(1)}, s16[528,256]{1,0:T(8,128)(2,1)S(1)}, u32[]{:S(2)}, u32[]{:S(2)}) collective-permute-start(s16[528,256]{1,0:T(8,128)(2,1)S(1)} %copy-done.15), channel_id=1, source_target_pairs={{0,24},{8,16},{16,8},{24,0},{1,25},{9,17},{17,9},{25,1},{2,26},{10... | collective-permute-start | bytes 811016 | tf_op jit(solution)/shard_map/ppermute | solution.py:200
  133.8 12.3 %copy-start.3 = (f32[512,256]{1,0:T(8,128)S(1)}, f32[512,256]{1,0:T(8,128)}, u32[]{:S(2)}) copy-start(f32[512,256]{1,0:T(8,128)} %copy-done.2) | copy-start | bytes 1572868
  133.8 13.5 %collective-permute-start.1 = (s16[400,256]{1,0:T(8,128)(2,1)S(1)}, s16[400,256]{1,0:T(8,128)(2,1)S(1)}, u32[]{:S(2)}, u32[]{:S(2)}) collective-permute-start(s16[400,256]{1,0:T(8,128)(2,1)S(1)} %get-tuple-element.30), channel_id=1, source_target_pairs={{0,8},{8,0},{16,24},{24,16},{1,9},{9,1},{17,25},{25,17},{2,10},{10... | collective-permute-start | bytes 614408 | tf_op jit(solution)/shard_map/ppermute | solution.py:200
  134.3 14.0 %collective-permute-start.2 = (s16[400,256]{1,0:T(8,128)(2,1)S(1)}, s16[400,256]{1,0:T(8,128)(2,1)S(1)}, u32[]{:S(2)}, u32[]{:S(2)}) collective-permute-start(s16[400,256]{1,0:T(8,128)(2,1)S(1)} %get-tuple-element.31), channel_id=1, source_target_pairs={{0,16},{8,24},{16,0},{24,8},{1,17},{9,25},{17,1},{25,9},{2,18},{10... | collective-permute-start | bytes 614408 | tf_op jit(solution)/shard_map/ppermute | solution.py:200
  135.9 12.4 %collective-permute-start.3 = (s16[400,256]{1,0:T(8,128)(2,1)S(1)}, s16[400,256]{1,0:T(8,128)(2,1)S(1)}, u32[]{:S(2)}, u32[]{:S(2)}) collective-permute-start(s16[400,256]{1,0:T(8,128)(2,1)S(1)} %get-tuple-element.32), channel_id=1, source_target_pairs={{0,24},{8,16},{16,8},{24,0},{1,25},{9,17},{17,9},{25,1},{2,26},{10... | collective-permute-start | bytes 614408 | tf_op jit(solution)/shard_map/ppermute | solution.py:200
  (12 other events, 15.1 us)
Sparse Core Ops, SparseCore 0:
  10.5 30.6 all-gather.11
  42.7 27.4 all-gather.7
  71.7 32.1 all-gather.9

commit v4 on v2

v4 whole, which is shorter than its diff:
```python
import functools
import math

import jax
import jax.numpy as jnp
from jax import lax
from jax.experimental import pallas as pl
from jax.experimental.pallas import tpu as pltpu
from jax.sharding import PartitionSpec as P

TILE = 256
SIXTEENTHS = (5, 5, 3, 3)
SCALE_ROWS = 16
CODE = 64.0
TOP = 32767.0
LEAST = 2.0**-100
VMEM = pl.BlockSpec(memory_space=pltpu.VMEM)
PARAMS = pltpu.CompilerParams(vmem_limit_bytes=40 * 1024 * 1024)


def load_kernel(at, pattern_ref, left_ref, *refs):
    out_ref = refs[-1]
    size = out_ref.shape[0]
    step = math.gcd(TILE, math.gcd(at, size))
    for i in range(0, size, step):
        entry = pattern_ref[(at + i) // TILE].astype(jnp.float32).astype(out_ref.dtype)
        out_ref[i : i + step, :] = left_ref[at + i : at + i + step, :] * entry


def load(left, pattern, at, size, after):
    columns = left.shape[1]
    return pl.pallas_call(
        functools.partial(load_kernel, at),
        out_shape=jax.ShapeDtypeStruct((size, columns), left.dtype),
        in_specs=[pl.BlockSpec(memory_space=pltpu.SMEM), VMEM]
        + [pl.BlockSpec(memory_space=pl.ANY)] * len(after),
        out_specs=VMEM,
        compiler_params=PARAMS,
        cost_estimate=pl.CostEstimate(
            flops=size * columns, bytes_accessed=4 * size * columns, transcendentals=0
        ),
    )(pattern, left, *after)


def gate_kernel(x_ref, after_ref, out_ref):
    out_ref[...] = x_ref[...]


def gate(x, after):
    return pl.pallas_call(
        gate_kernel,
        out_shape=jax.ShapeDtypeStruct(x.shape, x.dtype),
        in_specs=[VMEM, pl.BlockSpec(memory_space=pl.ANY)],
        out_specs=VMEM,
    )(x, after)


def put_fixed(ref, at, total):
    rows, columns = total.shape
    top = jnp.maximum(jnp.max(jnp.abs(total), axis=0, keepdims=True), LEAST)
    code = jnp.ceil(jnp.log2(top) * CODE + 0.01)
    fixed = jnp.round(total * (jnp.exp2(code / -CODE) * TOP)).astype(jnp.int32)
    ref[at : at + rows, :] = fixed.astype(jnp.int16)
    codes = jnp.broadcast_to(code.astype(jnp.int32), (SCALE_ROWS, columns))
    ref[at + rows : at + rows + SCALE_ROWS, :] = codes.astype(jnp.int16)


def get_fixed(ref, at, rows):
    code = ref[at + rows : at + rows + SCALE_ROWS, :].astype(jnp.int32)[:1].astype(jnp.float32)
    unit = jnp.exp2(code / CODE) * (1.0 / TOP)
    return ref[at : at + rows, :].astype(jnp.int32).astype(jnp.float32) * unit


def partial_kernel(n_sources, kept, sent, where, *refs):
    lefts, right_ref, outs = refs[:n_sources], refs[n_sources], refs[n_sources + 1 :]
    rows, columns = lefts[0].shape[0], right_ref.shape[3]

    def product(k):
        total = jnp.zeros((rows, columns), jnp.float32)
        for source in range(n_sources):
            start = pl.multiple_of(where[2 + 2 * source], TILE)
            total += jnp.dot(
                lefts[source][...],
                right_ref[where[1 + 2 * source], where[0] ^ k, pl.ds(start, TILE), :],
                preferred_element_type=jnp.float32,
            )
        return total

    for out, ks in zip(outs[len(kept) :], sent):
        for i, k in enumerate(ks):
            put_fixed(out, i * (rows + SCALE_ROWS), product(k))
    for out, k in zip(outs, kept):
        out[...] = product(k)


def partial_products(where, lefts, right, kept, sent):
    rows, columns = lefts[0].shape[0], right.shape[3]
    n_products = len(kept) + sum(len(ks) for ks in sent)
    outs = [jax.ShapeDtypeStruct((rows, columns), jnp.float32)] * len(kept)
    outs += [
        jax.ShapeDtypeStruct((len(ks) * (rows + SCALE_ROWS), columns), jnp.int16) for ks in sent
    ]
    out = pl.pallas_call(
        functools.partial(partial_kernel, len(lefts), kept, sent),
        out_shape=outs,
        in_specs=[pl.BlockSpec(memory_space=pltpu.SMEM)] + [VMEM] * (len(lefts) + 1),
        out_specs=[VMEM] * len(outs),
        compiler_params=PARAMS,
        cost_estimate=pl.CostEstimate(
            flops=2 * rows * len(lefts) * TILE * columns * n_products,
            bytes_accessed=right.size * 2 + rows * columns * 14,
            transcendentals=0,
        ),
    )(where, *lefts, right)
    return out[: len(kept)], out[len(kept) :]


def pass_on_kernel(kept_ref, received_ref, after_ref, out_ref):
    rows = kept_ref.shape[0]
    total = kept_ref[...] + get_fixed(received_ref, rows + SCALE_ROWS, rows)
    put_fixed(out_ref, 0, total)


def pass_on(kept, received, after):
    rows, columns = kept.shape
    return pl.pallas_call(
        pass_on_kernel,
        out_shape=jax.ShapeDtypeStruct((rows + SCALE_ROWS, columns), jnp.int16),
        in_specs=[VMEM, VMEM, pl.BlockSpec(memory_space=pl.ANY)],
        out_specs=VMEM,
        compiler_params=PARAMS,
        cost_estimate=pl.CostEstimate(
            flops=10 * kept.size, bytes_accessed=8 * kept.size, transcendentals=0
        ),
    )(kept, received, after)


def combine_kernel(n_received, kept_ref, *refs):
    received, (before_ref, squared_ref, sum_ref) = refs[:n_received], refs[n_received:]
    total = kept_ref[...]
    for block in received:
        total += get_fixed(block, 0, total.shape[0])
    squared = total * total
    squared_ref[...] = squared
    sum_ref[...] = before_ref[...] + jnp.sum(squared, axis=0, keepdims=True)


def combine(kept, received, before):
    return pl.pallas_call(
        functools.partial(combine_kernel, len(received)),
        out_shape=(
            jax.ShapeDtypeStruct(kept.shape, jnp.float32),
            jax.ShapeDtypeStruct((1, kept.shape[1]), jnp.float32),
        ),
        in_specs=[VMEM] * (2 + len(received)),
        out_specs=(VMEM, VMEM),
        compiler_params=PARAMS,
        cost_estimate=pl.CostEstimate(
            flops=8 * kept.size, bytes_accessed=kept.size * 14, transcendentals=0
        ),
    )(kept, *received, before)


def normalise_kernel(n_chunks, rows_total, column_ref, *refs):
    chunks, out_ref = refs[:n_chunks], refs[n_chunks]
    colmean = column_ref[...] / rows_total
    at = 0
    for chunk in chunks:
        rows = chunk.shape[0]
        out_ref[at : at + rows, :] = (chunk[...] / (colmean + 1e-06)).astype(jnp.bfloat16)
        at += rows


def normalise(column, chunks, rows_total):
    rows, columns = sum(chunk.shape[0] for chunk in chunks), chunks[0].shape[1]
    return pl.pallas_call(
        functools.partial(normalise_kernel, len(chunks), rows_total),
        out_shape=jax.ShapeDtypeStruct((rows, columns), jnp.bfloat16),
        in_specs=[VMEM] * (1 + len(chunks)),
        out_specs=VMEM,
        compiler_params=PARAMS,
        cost_estimate=pl.CostEstimate(
            flops=4 * rows * columns,
            bytes_accessed=6 * rows * columns,
            transcendentals=0,
        ),
    )(column, *chunks)


def expand_tiles(values, pattern):
    tile_rows, layers, tile_cols = pattern.shape
    tile_size = values.shape[0] // tile_rows
    blocks = values.reshape(tile_rows, tile_size, layers, tile_cols, tile_size)
    blocks = blocks * pattern[:, None, :, :, None].astype(values.dtype)
    return blocks.reshape(values.shape)


def shift(x, axis, by):
    n = lax.axis_size(axis)
    return lax.ppermute(x, axis, [(i, (i + by) % n) for i in range(n)])


def swap(x, bits):
    return lax.ppermute(x, "layer", [(i, i ^ bits) for i in range(4)])


def per_device(left_values, left_pattern, right_values, right_pattern):
    n_rows, n_cols = lax.axis_size("row"), lax.axis_size("col")
    layer, row, col = (lax.axis_index(a) for a in ("layer", "row", "col"))
    rows_local, _, columns_local = left_values.shape
    inner_piece = right_values.shape[0]
    sizes = [rows_local * part // sum(SIXTEENTHS) for part in SIXTEENTHS]

    left = left_values.reshape(rows_local, columns_local)
    pattern = left_pattern.reshape(-1)
    starts = [sum(sizes[:i]) for i in range(len(sizes))]
    chunks = []
    for i, (at, size) in enumerate(zip(starts, sizes)):
        ring = [load(left, pattern, at, size, [chunks[i - 2][-1]] if i > 1 else [chunk[0] for chunk in chunks])]
        for _ in range(n_cols - 1):
            ring.append(shift(ring[-1], "col", 1))
        chunks.append(ring)

    right_pattern = gate(right_pattern, chunks[1][0])
    right_block = expand_tiles(right_values, right_pattern).transpose(1, 0, 2)
    pieces = [right_block]
    for i in range(1, n_rows):
        pieces.append(shift(right_block, "row", i))
    right = jnp.stack(pieces)

    where = [layer]
    for source in range(n_cols):
        inner = (col - source + n_cols) % n_cols * columns_local
        where += [(row - inner // inner_piece + n_rows) % n_rows, inner % inner_piece]
    where = jnp.stack(where).astype(jnp.int32)

    sums = []
    for i, chunk in enumerate(chunks):
        if i + 1 < len(chunks):
            first, second = (1, 2) if i % 2 == 0 else (2, 1)
            kept, sent = partial_products(where, chunk, right, (0, second), ((first, 3),))
            sums.append((kept, swap(sent[0], first), second))
        else:
            kept, sent = partial_products(where, chunk, right, (0,), ((1,), (2,), (3,)))
            sums.append((kept, [swap(x, k + 1) for k, x in enumerate(sent)], 0))

    squares = []
    column = jnp.zeros((1, columns_local), jnp.float32)
    for i, (kept, received, second) in enumerate(sums):
        if second:
            after = chunks[i + 2][0] if i + 2 < len(chunks) else sums[-1][0][0]
            received = [received, swap(pass_on(kept[1], received, after), second)]
        squared, column = combine(kept[0], received, column)
        squares.append(squared)
    column = lax.psum(column, "row")
    out = normalise(column, squares, rows_local * n_rows)
    return out.reshape(rows_local, 1, columns_local)


def solution(mesh):
    return jax.shard_map(
        per_device,
        mesh=mesh,
        in_specs=(
            P("row", "layer", "col"),
            P("row", "layer", "col"),
            P(("layer", "row"), None, "col"),
            P(("layer", "row"), None, "col"),
        ),
        out_specs=P("row", "layer", "col"),
        check_vma=False,
    )
```

time: 113 us -> 110 us (0.973)
  starting transfers between devices: 22.2 us -> 16.8 us
  waiting for transfers between devices: 64.5 us -> 69.2 us
  local copies, waits for them, and re-layouts: 5.09 us -> 3.62 us
    ppermute x13, waiting for transfers between devices: 48.9 us -> 61 us  [shift(): return lax.ppermute(x, axis, [(i, (i + by) % n) for i in range(n)])]
    ppermute x12 -> x9, waiting for transfers between devices: 15.6 us -> 8.2 us  [swap(): return lax.ppermute(x, 'layer', [(i, i ^ bits) for i in range(4)])]
    ppermute x12 -> x9, starting transfers between devices: 15.2 us -> 10.7 us  [swap(): return lax.ppermute(x, 'layer', [(i, i ^ bits) for i in range(4)])]
    unnamed x29 -> x21, local copies, waits for them, and re-layouts: 4.88 us -> 3.41 us
    pallas_call x8 -> x11, Pallas kernels: 10.8 us -> 10.5 us  [the longest x4 7.72 us: partial_products(): pl.pallas_call(functools.partial(partial_kernel, len(lefts), kept, sent),...]
  transfers between devices with their start and end apart: 25 -> 22, of which waited for: 16 -> 14; matrix products, arithmetic and copies ran while one was open for 4% -> 1% of each run, Pallas kernels for 11% -> 9%
where the time goes in v4:
time: 110 us
  waiting for transfers between devices  69.2 us (63%)
  starting transfers between devices  16.8 us (15%)
  Pallas kernels  13.7 us (12%)
  other arithmetic  3.75 us (3%)
  local copies, waits for them, and re-layouts  3.62 us (3%)
  blocking collectives  2.47 us (2%)
    ppermute x13, waiting for transfers between devices, shift(): return lax.ppermute(x, axis, [(i, (i + by) % n) for i in range(n)])  61 us
    ppermute x9, starting transfers between devices, swap(): return lax.ppermute(x, 'layer', [(i, i ^ bits) for i in range(4)])  10.7 us
    ppermute x9, waiting for transfers between devices, swap(): return lax.ppermute(x, 'layer', [(i, i ^ bits) for i in range(4)])  8.2 us
    pallas_call x4, Pallas kernels, partial_products(): pl.pallas_call(functools.partial(partial_kernel, len(lefts), kept, sent),...  7.72 us
    ppermute x13, starting transfers between devices, shift(): return lax.ppermute(x, axis, [(i, (i + by) % n) for i in range(n)])  6.03 us
    unnamed x21, local copies, waits for them, and re-layouts  3.41 us
    another operation x2, other arithmetic, per_device(): right = jnp.stack(pieces)  3.08 us
    psum x1, blocking collectives, per_device(): column = lax.psum(column, 'row')  2.47 us
  transfers between devices with their start and end apart: 22, of which 14 were waited for; matrix products, arithmetic and copies ran while one was open for 1% of the time, Pallas kernels for 9%

profile of v4, /device:TPU:0, one launch (start us, length us, event | category | flops | bytes accessed | tf_op | source)
XLA Modules:
  0.0 109.7 jit_solution(8547399764454032146)
XLA Ops:
  6.7 1.7 %fusion = (bf16[1,4,512,256]{3,2,1,0:T(8,128)(2,1)}, bf16[4,512,256]{2,1,0:T(8,128)(2,1)}) fusion(bf16[512,4,256]{2,1,0:T(4,128)(2,1)S(1)} %copy-done.7, bf16[512,4]{0,1:T(4,128)(2,1)S(1)} %bitcast.32), kind=kLoop, calls=%fused_computation.2 | loop fusion | flops 524288 | bytes 3149824 | tf_op jit(solution)/shard_map/stack | solution.py:229
  8.8 2.6 %collective-permute-start.10 = (bf16[640,256]{1,0:T(8,128)(2,1)S(1)}, bf16[640,256]{1,0:T(8,128)(2,1)S(1)}, u32[]{:S(2)}, u32[]{:S(2)}) collective-permute-start(bf16[640,256]{1,0:T(8,128)(2,1)S(1)} %shard_map.46.refs_0_), channel_id=1, source_target_pairs={{0,1},{1,2},{2,3},{3,0},{4,5},{5,6},{6,7},{7,4},{8,9},{9,10},{10,1... | collective-permute-start | bytes 983048 | tf_op jit(solution)/shard_map/ppermute | solution.py:200
  11.4 1.6 %collective-permute-start = (bf16[640,256]{1,0:T(8,128)(2,1)S(1)}, bf16[640,256]{1,0:T(8,128)(2,1)S(1)}, u32[]{:S(2)}, u32[]{:S(2)}) collective-permute-start(bf16[640,256]{1,0:T(8,128)(2,1)S(1)} %copy-done.3), channel_id=1, source_target_pairs={{0,1},{1,2},{2,3},{3,0},{4,5},{5,6},{6,7},{7,4},{8,9},{9,10},{10,1... | collective-permute-start | bytes 983048 | tf_op jit(solution)/shard_map/ppermute | solution.py:200
  13.0 9.0 %collective-permute-done.10.refs_1_ = bf16[640,256]{1,0:T(8,128)(2,1)S(1)} collective-permute-done((bf16[640,256]{1,0:T(8,128)(2,1)S(1)}, bf16[640,256]{1,0:T(8,128)(2,1)S(1)}, u32[]{:S(2)}, u32[]{:S(2)}) %collective-permute-start.10) | collective-permute-done | bytes 327712 | tf_op jit(solution)/shard_map/ppermute | solution.py:200
  22.0 7.0 %collective-permute-done.refs_1_ = bf16[640,256]{1,0:T(8,128)(2,1)S(1)} collective-permute-done((bf16[640,256]{1,0:T(8,128)(2,1)S(1)}, bf16[640,256]{1,0:T(8,128)(2,1)S(1)}, u32[]{:S(2)}, u32[]{:S(2)}) %collective-permute-start) | collective-permute-done | bytes 327712 | tf_op jit(solution)/shard_map/ppermute | solution.py:200
  29.0 7.0 %collective-permute-done.11.refs_2_ = bf16[640,256]{1,0:T(8,128)(2,1)S(1)} collective-permute-done((bf16[640,256]{1,0:T(8,128)(2,1)S(1)}, bf16[640,256]{1,0:T(8,128)(2,1)S(1)}, u32[]{:S(2)}, u32[]{:S(2)}) %collective-permute-start.11) | collective-permute-done | bytes 327712 | tf_op jit(solution)/shard_map/ppermute | solution.py:200
  36.1 6.9 %collective-permute-done.1.refs_2_ = bf16[640,256]{1,0:T(8,128)(2,1)S(1)} collective-permute-done((bf16[640,256]{1,0:T(8,128)(2,1)S(1)}, bf16[640,256]{1,0:T(8,128)(2,1)S(1)}, u32[]{:S(2)}, u32[]{:S(2)}) %collective-permute-start.1) | collective-permute-done | bytes 327712 | tf_op jit(solution)/shard_map/ppermute | solution.py:200
  43.0 7.0 %collective-permute-done.12.refs_0_.refs_3_ = bf16[640,256]{1,0:T(8,128)(2,1)S(1)} collective-permute-done((bf16[640,256]{1,0:T(8,128)(2,1)S(1)}, bf16[640,256]{1,0:T(8,128)(2,1)S(1)}, u32[]{:S(2)}, u32[]{:S(2)}) %collective-permute-start.12) | collective-permute-done | bytes 327712 | tf_op jit(solution)/shard_map/ppermute | solution.py:200
  52.1 2.3 %shard_map.56 = (f32[640,256]{1,0:T(8,128)S(1)}, f32[640,256]{1,0:T(8,128)S(1)}, s16[1312,256]{1,0:T(8,128)(2,1)S(1)}) custom-call(s32[9]{0:T(128)S(1)} %stack.48.where, bf16[640,256]{1,0:T(8,128)(2,1)S(1)} %shard_map.46.refs_0_, bf16[640,256]{1,0:T(8,128)(2,1)S(1)} %collective-permute-done.10.refs_1_, bf16[640,256]{1,0:T(8,128)(2,1)S(1)} %collective-permute-done.11.refs_2_, ...), custom_call_target="tpu_custom_call" | custom-call | flops 1342177280 | bytes 4390912 | tf_op jit(solution)/shard_map/pallas_call | solution.py:103
  54.4 1.7 %collective-permute-start.20 = (s16[1312,256]{1,0:T(8,128)(2,1)S(1)}, s16[1312,256]{1,0:T(8,128)(2,1)S(1)}, u32[]{:S(2)}, u32[]{:S(2)}) collective-permute-start(s16[1312,256]{1,0:T(8,128)(2,1)S(1)} %get-tuple-element.37), channel_id=1, source_target_pairs={{0,8},{8,0},{16,24},{24,16},{1,9},{9,1},{17,25},{25,17},{2,10},{10... | collective-permute-start | bytes 2015240 | tf_op jit(solution)/shard_map/ppermute | solution.py:204
  56.1 5.0 %collective-permute-done.13.refs_1_ = bf16[384,256]{1,0:T(8,128)(2,1)S(1)} collective-permute-done((bf16[384,256]{1,0:T(8,128)(2,1)S(1)}, bf16[384,256]{1,0:T(8,128)(2,1)S(1)}, u32[]{:S(2)}, u32[]{:S(2)}) %collective-permute-start.13) | collective-permute-done | bytes 196640 | tf_op jit(solution)/shard_map/ppermute | solution.py:200
  61.1 2.3 %shard_map.54 = (f32[640,256]{1,0:T(8,128)S(1)}, f32[640,256]{1,0:T(8,128)S(1)}, s16[1312,256]{1,0:T(8,128)(2,1)S(1)}) custom-call(s32[9]{0:T(128)S(1)} %stack.48.where, bf16[640,256]{1,0:T(8,128)(2,1)S(1)} %copy-done.3, bf16[640,256]{1,0:T(8,128)(2,1)S(1)} %collective-permute-done.refs_1_, bf16[640,256]{1,0:T(8,128)(2,1)S(1)} %collective-permute-done.1.refs_2_, ...), custom_call_target="tpu_custom_call" | custom-call | flops 1342177280 | bytes 4390912 | tf_op jit(solution)/shard_map/pallas_call | solution.py:103
  63.4 1.6 %collective-permute-start.18 = (s16[1312,256]{1,0:T(8,128)(2,1)S(1)}, s16[1312,256]{1,0:T(8,128)(2,1)S(1)}, u32[]{:S(2)}, u32[]{:S(2)}) collective-permute-start(s16[1312,256]{1,0:T(8,128)(2,1)S(1)} %get-tuple-element.34), channel_id=1, source_target_pairs={{0,16},{8,24},{16,0},{24,8},{1,17},{9,25},{17,1},{25,9},{2,18},{10... | collective-permute-start | bytes 2015240 | tf_op jit(solution)/shard_map/ppermute | solution.py:204
  66.9 2.8 %collective-permute-done.14.refs_2_ = bf16[384,256]{1,0:T(8,128)(2,1)S(1)} collective-permute-done((bf16[384,256]{1,0:T(8,128)(2,1)S(1)}, bf16[384,256]{1,0:T(8,128)(2,1)S(1)}, u32[]{:S(2)}, u32[]{:S(2)}) %collective-permute-start.14) | collective-permute-done | bytes 196640 | tf_op jit(solution)/shard_map/ppermute | solution.py:200
  69.7 4.8 %collective-permute-done.3.refs_1_ = bf16[384,256]{1,0:T(8,128)(2,1)S(1)} collective-permute-done((bf16[384,256]{1,0:T(8,128)(2,1)S(1)}, bf16[384,256]{1,0:T(8,128)(2,1)S(1)}, u32[]{:S(2)}, u32[]{:S(2)}) %collective-permute-start.3) | collective-permute-done | bytes 196640 | tf_op jit(solution)/shard_map/ppermute | solution.py:200
  74.5 4.5 %collective-permute-done.15.refs_3_ = bf16[384,256]{1,0:T(8,128)(2,1)S(1)} collective-permute-done((bf16[384,256]{1,0:T(8,128)(2,1)S(1)}, bf16[384,256]{1,0:T(8,128)(2,1)S(1)}, u32[]{:S(2)}, u32[]{:S(2)}) %collective-permute-start.15) | collective-permute-done | bytes 196640 | tf_op jit(solution)/shard_map/ppermute | solution.py:200
  79.1 1.6 %shard_map.52 = (f32[384,256]{1,0:T(8,128)S(1)}, f32[384,256]{1,0:T(8,128)S(1)}, s16[800,256]{1,0:T(8,128)(2,1)S(1)}) custom-call(s32[9]{0:T(128)S(1)} %stack.48.where, bf16[384,256]{1,0:T(8,128)(2,1)S(1)} %shard_map.51.refs_0_.after_ref, bf16[384,256]{1,0:T(8,128)(2,1)S(1)} %collective-permute-done.13.refs_1_, ...), custom_call_target="tpu_custom_call" | custom-call | flops 805306368 | bytes 3473408 | tf_op jit(solution)/shard_map/pallas_call | solution.py:103
  84.1 6.8 %collective-permute-done.5.refs_3_ = bf16[384,256]{1,0:T(8,128)(2,1)S(1)} collective-permute-done((bf16[384,256]{1,0:T(8,128)(2,1)S(1)}, bf16[384,256]{1,0:T(8,128)(2,1)S(1)}, u32[]{:S(2)}, u32[]{:S(2)}) %collective-permute-start.5) | collective-permute-done | bytes 196640 | tf_op jit(solution)/shard_map/ppermute | solution.py:200
  90.9 1.6 %shard_map.50 = (f32[384,256]{1,0:T(8,128)S(1)}, s16[400,256]{1,0:T(8,128)(2,1)S(1)}, s16[400,256]{1,0:T(8,128)(2,1)S(1)}, s16[400,256]{1,0:T(8,128)(2,1)S(1)}) custom-call(s32[9]{0:T(128)S(1)} %stack.48.where, bf16[384,256]{1,0:T(8,128)(2,1)S(1)} %shard_map.48.refs_0_.after_ref, bf16[384,256]{1,0:T(8,128)(2,1)S(1)} %collective-permute-done.3.refs_1_, ...), custom_call_target="tpu_custom_call" | custom-call | flops 805306368 | bytes 3473408 | tf_op jit(solution)/shard_map/pallas_call | solution.py:103
  94.2 1.6 %collective-permute-start.7 = (s16[400,256]{1,0:T(8,128)(2,1)S(1)}, s16[400,256]{1,0:T(8,128)(2,1)S(1)}, u32[]{:S(2)}, u32[]{:S(2)}) collective-permute-start(s16[400,256]{1,0:T(8,128)(2,1)S(1)} %get-tuple-element.27), channel_id=1, source_target_pairs={{0,8},{8,0},{16,24},{24,16},{1,9},{9,1},{17,25},{25,17},{2,10},{10... | collective-permute-start | bytes 614408 | tf_op jit(solution)/shard_map/ppermute | solution.py:204
  97.9 2.4 %collective-permute-done.19.refs_1_ = s16[656,256]{1,0:T(8,128)(2,1)S(1)} collective-permute-done((s16[656,256]{1,0:T(8,128)(2,1)S(1)}, s16[656,256]{1,0:T(8,128)(2,1)S(1)}, u32[]{:S(2)}, u32[]{:S(2)}) %collective-permute-start.19) | collective-permute-done | bytes 335904 | tf_op jit(solution)/shard_map/ppermute | solution.py:204
  100.7 3.0 %collective-permute-done.7.refs_0_ = s16[400,256]{1,0:T(8,128)(2,1)S(1)} collective-permute-done((s16[400,256]{1,0:T(8,128)(2,1)S(1)}, s16[400,256]{1,0:T(8,128)(2,1)S(1)}, u32[]{:S(2)}, u32[]{:S(2)}) %collective-permute-start.7) | collective-permute-done | bytes 204832 | tf_op jit(solution)/shard_map/ppermute | solution.py:204
  103.7 2.3 %collective-permute-done.9.refs_2_ = s16[400,256]{1,0:T(8,128)(2,1)S(1)} collective-permute-done((s16[400,256]{1,0:T(8,128)(2,1)S(1)}, s16[400,256]{1,0:T(8,128)(2,1)S(1)}, u32[]{:S(2)}, u32[]{:S(2)}) %collective-permute-start.9) | collective-permute-done | bytes 204832 | tf_op jit(solution)/shard_map/ppermute | solution.py:204
  106.1 2.5 %psum.7.column_ref = f32[1,256]{1,0:T(1,128)S(1)} all-reduce(f32[1,256]{1,0:T(1,128)S(1)} %get-tuple-element.42), channel_id=1, replica_groups=mesh['layer'=4,'row'=2,'col'=4] {'row'}, use_global_device_ids=true, to_apply=%region_0.1 | all-reduce | flops 256 | bytes 2048 | tf_op jit(solution)/shard_map/psum | solution.py:255
  (65 shorter events, 20.0 us)
Async XLA Ops:
  3.8 46.3 %copy-start.1 = (bf16[2048,1,256]{2,0,1:T(8,128)(2,1)S(1)}, bf16[2048,1,256]{2,0,1:T(8,128)(2,1)}, u32[]{:S(2)}) copy-start(bf16[2048,1,256]{2,0,1:T(8,128)(2,1)} %param.4) | copy-start | bytes 3145732
  3.8 46.3 %copy-start.5 = (s32[8,1,1]{0,2,1:T(1,128)S(1)}, s32[8,1,1]{0,2,1:T(1,128)}, u32[]{:S(2)}) copy-start(s32[8,1,1]{0,2,1:T(1,128)} %param.5) | copy-start | bytes 100
  8.3 42.3 %collective-permute-start.6 = (bf16[4,512,256]{2,1,0:T(8,128)(2,1)}, bf16[4,512,256]{2,1,0:T(8,128)(2,1)}, u32[]{:S(2)}, u32[]{:S(2)}) collective-permute-start(bf16[4,512,256]{2,1,0:T(8,128)(2,1)} %get-tuple-element.48), channel_id=1, source_target_pairs={{0,4},{4,0},{1,5},{5,1},{2,6},{6,2},{3,7},{7,3},{8,12},{12,8},{9,1... | collective-permute-start | bytes 3145736 | tf_op jit(solution)/shard_map/ppermute | solution.py:200
  8.8 13.2 %collective-permute-start.10 = (bf16[640,256]{1,0:T(8,128)(2,1)S(1)}, bf16[640,256]{1,0:T(8,128)(2,1)S(1)}, u32[]{:S(2)}, u32[]{:S(2)}) collective-permute-start(bf16[640,256]{1,0:T(8,128)(2,1)S(1)} %shard_map.46.refs_0_), channel_id=1, source_target_pairs={{0,1},{1,2},{2,3},{3,0},{4,5},{5,6},{6,7},{7,4},{8,9},{9,10},{10,1... | collective-permute-start | bytes 983048 | tf_op jit(solution)/shard_map/ppermute | solution.py:200
  11.4 17.6 %collective-permute-start = (bf16[640,256]{1,0:T(8,128)(2,1)S(1)}, bf16[640,256]{1,0:T(8,128)(2,1)S(1)}, u32[]{:S(2)}, u32[]{:S(2)}) collective-permute-start(bf16[640,256]{1,0:T(8,128)(2,1)S(1)} %copy-done.3), channel_id=1, source_target_pairs={{0,1},{1,2},{2,3},{3,0},{4,5},{5,6},{6,7},{7,4},{8,9},{9,10},{10,1... | collective-permute-start | bytes 983048 | tf_op jit(solution)/shard_map/ppermute | solution.py:200
  22.0 14.0 %collective-permute-start.11 = (bf16[640,256]{1,0:T(8,128)(2,1)S(1)}, bf16[640,256]{1,0:T(8,128)(2,1)S(1)}, u32[]{:S(2)}, u32[]{:S(2)}) collective-permute-start(bf16[640,256]{1,0:T(8,128)(2,1)S(1)} %collective-permute-done.10.refs_1_), channel_id=1, source_target_pairs={{0,1},{1,2},{2,3},{3,0},{4,5},{5,6},{6,7},{7,4},{8,9},{9,10},{10,1... | collective-permute-start | bytes 983048 | tf_op jit(solution)/shard_map/ppermute | solution.py:200
  29.0 14.0 %collective-permute-start.1 = (bf16[640,256]{1,0:T(8,128)(2,1)S(1)}, bf16[640,256]{1,0:T(8,128)(2,1)S(1)}, u32[]{:S(2)}, u32[]{:S(2)}) collective-permute-start(bf16[640,256]{1,0:T(8,128)(2,1)S(1)} %collective-permute-done.refs_1_), channel_id=1, source_target_pairs={{0,1},{1,2},{2,3},{3,0},{4,5},{5,6},{6,7},{7,4},{8,9},{9,10},{10,1... | collective-permute-start | bytes 983048 | tf_op jit(solution)/shard_map/ppermute | solution.py:200
  36.0 14.0 %collective-permute-start.12 = (bf16[640,256]{1,0:T(8,128)(2,1)S(1)}, bf16[640,256]{1,0:T(8,128)(2,1)S(1)}, u32[]{:S(2)}, u32[]{:S(2)}) collective-permute-start(bf16[640,256]{1,0:T(8,128)(2,1)S(1)} %collective-permute-done.11.refs_2_), channel_id=1, source_target_pairs={{0,1},{1,2},{2,3},{3,0},{4,5},{5,6},{6,7},{7,4},{8,9},{9,10},{10,1... | collective-permute-start | bytes 983048 | tf_op jit(solution)/shard_map/ppermute | solution.py:200
  43.0 18.1 %collective-permute-start.2 = (bf16[640,256]{1,0:T(8,128)(2,1)S(1)}, bf16[640,256]{1,0:T(8,128)(2,1)S(1)}, u32[]{:S(2)}, u32[]{:S(2)}) collective-permute-start(bf16[640,256]{1,0:T(8,128)(2,1)S(1)} %collective-permute-done.1.refs_2_), channel_id=1, source_target_pairs={{0,1},{1,2},{2,3},{3,0},{4,5},{5,6},{6,7},{7,4},{8,9},{9,10},{10,1... | collective-permute-start | bytes 983048 | tf_op jit(solution)/shard_map/ppermute | solution.py:200
  50.6 10.5 %collective-permute-start.13 = (bf16[384,256]{1,0:T(8,128)(2,1)S(1)}, bf16[384,256]{1,0:T(8,128)(2,1)S(1)}, u32[]{:S(2)}, u32[]{:S(2)}) collective-permute-start(bf16[384,256]{1,0:T(8,128)(2,1)S(1)} %shard_map.51.refs_0_.after_ref), channel_id=1, source_target_pairs={{0,1},{1,2},{2,3},{3,0},{4,5},{5,6},{6,7},{7,4},{8,9},{9,10},{10,1... | collective-permute-start | bytes 589832 | tf_op jit(solution)/shard_map/ppermute | solution.py:200
  54.4 27.8 %collective-permute-start.20 = (s16[1312,256]{1,0:T(8,128)(2,1)S(1)}, s16[1312,256]{1,0:T(8,128)(2,1)S(1)}, u32[]{:S(2)}, u32[]{:S(2)}) collective-permute-start(s16[1312,256]{1,0:T(8,128)(2,1)S(1)} %get-tuple-element.37), channel_id=1, source_target_pairs={{0,8},{8,0},{16,24},{24,16},{1,9},{9,1},{17,25},{25,17},{2,10},{10... | collective-permute-start | bytes 2015240 | tf_op jit(solution)/shard_map/ppermute | solution.py:204
  61.1 8.6 %collective-permute-start.14 = (bf16[384,256]{1,0:T(8,128)(2,1)S(1)}, bf16[384,256]{1,0:T(8,128)(2,1)S(1)}, u32[]{:S(2)}, u32[]{:S(2)}) collective-permute-start(bf16[384,256]{1,0:T(8,128)(2,1)S(1)} %collective-permute-done.13.refs_1_), channel_id=1, source_target_pairs={{0,1},{1,2},{2,3},{3,0},{4,5},{5,6},{6,7},{7,4},{8,9},{9,10},{10,1... | collective-permute-start | bytes 589832 | tf_op jit(solution)/shard_map/ppermute | solution.py:200
  63.4 20.1 %collective-permute-start.18 = (s16[1312,256]{1,0:T(8,128)(2,1)S(1)}, s16[1312,256]{1,0:T(8,128)(2,1)S(1)}, u32[]{:S(2)}, u32[]{:S(2)}) collective-permute-start(s16[1312,256]{1,0:T(8,128)(2,1)S(1)} %get-tuple-element.34), channel_id=1, source_target_pairs={{0,16},{8,24},{16,0},{24,8},{1,17},{9,25},{17,1},{25,9},{2,18},{10... | collective-permute-start | bytes 2015240 | tf_op jit(solution)/shard_map/ppermute | solution.py:204
  65.5 9.0 %collective-permute-start.3 = (bf16[384,256]{1,0:T(8,128)(2,1)S(1)}, bf16[384,256]{1,0:T(8,128)(2,1)S(1)}, u32[]{:S(2)}, u32[]{:S(2)}) collective-permute-start(bf16[384,256]{1,0:T(8,128)(2,1)S(1)} %shard_map.48.refs_0_.after_ref), channel_id=1, source_target_pairs={{0,1},{1,2},{2,3},{3,0},{4,5},{5,6},{6,7},{7,4},{8,9},{9,10},{10,1... | collective-permute-start | bytes 589832 | tf_op jit(solution)/shard_map/ppermute | solution.py:200
  69.7 9.4 %collective-permute-start.15 = (bf16[384,256]{1,0:T(8,128)(2,1)S(1)}, bf16[384,256]{1,0:T(8,128)(2,1)S(1)}, u32[]{:S(2)}, u32[]{:S(2)}) collective-permute-start(bf16[384,256]{1,0:T(8,128)(2,1)S(1)} %collective-permute-done.14.refs_2_), channel_id=1, source_target_pairs={{0,1},{1,2},{2,3},{3,0},{4,5},{5,6},{6,7},{7,4},{8,9},{9,10},{10,1... | collective-permute-start | bytes 589832 | tf_op jit(solution)/shard_map/ppermute | solution.py:200
  74.5 8.9 %collective-permute-start.4 = (bf16[384,256]{1,0:T(8,128)(2,1)S(1)}, bf16[384,256]{1,0:T(8,128)(2,1)S(1)}, u32[]{:S(2)}, u32[]{:S(2)}) collective-permute-start(bf16[384,256]{1,0:T(8,128)(2,1)S(1)} %collective-permute-done.3.refs_1_), channel_id=1, source_target_pairs={{0,1},{1,2},{2,3},{3,0},{4,5},{5,6},{6,7},{7,4},{8,9},{9,10},{10,1... | collective-permute-start | bytes 589832 | tf_op jit(solution)/shard_map/ppermute | solution.py:200
  80.6 12.5 %collective-permute-start.16 = (s16[800,256]{1,0:T(8,128)(2,1)S(1)}, s16[800,256]{1,0:T(8,128)(2,1)S(1)}, u32[]{:S(2)}, u32[]{:S(2)}) collective-permute-start(s16[800,256]{1,0:T(8,128)(2,1)S(1)} %get-tuple-element.31), channel_id=1, source_target_pairs={{0,8},{8,0},{16,24},{24,16},{1,9},{9,1},{17,25},{25,17},{2,10},{10... | collective-permute-start | bytes 1228808 | tf_op jit(solution)/shard_map/ppermute | solution.py:204
  82.4 14.4 %collective-permute-start.21 = (s16[656,256]{1,0:T(8,128)(2,1)S(1)}, s16[656,256]{1,0:T(8,128)(2,1)S(1)}, u32[]{:S(2)}, u32[]{:S(2)}) collective-permute-start(s16[656,256]{1,0:T(8,128)(2,1)S(1)} %shard_map.57), channel_id=1, source_target_pairs={{0,16},{8,24},{16,0},{24,8},{1,17},{9,25},{17,1},{25,9},{2,18},{10... | collective-permute-start | bytes 1007624 | tf_op jit(solution)/shard_map/ppermute | solution.py:204
  83.5 7.5 %collective-permute-start.5 = (bf16[384,256]{1,0:T(8,128)(2,1)S(1)}, bf16[384,256]{1,0:T(8,128)(2,1)S(1)}, u32[]{:S(2)}, u32[]{:S(2)}) collective-permute-start(bf16[384,256]{1,0:T(8,128)(2,1)S(1)} %collective-permute-done.4.refs_2_), channel_id=1, source_target_pairs={{0,1},{1,2},{2,3},{3,0},{4,5},{5,6},{6,7},{7,4},{8,9},{9,10},{10,1... | collective-permute-start | bytes 589832 | tf_op jit(solution)/shard_map/ppermute | solution.py:200
  83.7 16.6 %collective-permute-start.19 = (s16[656,256]{1,0:T(8,128)(2,1)S(1)}, s16[656,256]{1,0:T(8,128)(2,1)S(1)}, u32[]{:S(2)}, u32[]{:S(2)}) collective-permute-start(s16[656,256]{1,0:T(8,128)(2,1)S(1)} %shard_map.55), channel_id=1, source_target_pairs={{0,8},{8,0},{16,24},{24,16},{1,9},{9,1},{17,25},{25,17},{2,10},{10... | collective-permute-start | bytes 1007624 | tf_op jit(solution)/shard_map/ppermute | solution.py:204
  93.2 7.3 %collective-permute-start.17 = (s16[400,256]{1,0:T(8,128)(2,1)S(1)}, s16[400,256]{1,0:T(8,128)(2,1)S(1)}, u32[]{:S(2)}, u32[]{:S(2)}) collective-permute-start(s16[400,256]{1,0:T(8,128)(2,1)S(1)} %shard_map.53), channel_id=1, source_target_pairs={{0,16},{8,24},{16,0},{24,8},{1,17},{9,25},{17,1},{25,9},{2,18},{10... | collective-permute-start | bytes 614408 | tf_op jit(solution)/shard_map/ppermute | solution.py:204
  94.2 9.5 %collective-permute-start.7 = (s16[400,256]{1,0:T(8,128)(2,1)S(1)}, s16[400,256]{1,0:T(8,128)(2,1)S(1)}, u32[]{:S(2)}, u32[]{:S(2)}) collective-permute-start(s16[400,256]{1,0:T(8,128)(2,1)S(1)} %get-tuple-element.27), channel_id=1, source_target_pairs={{0,8},{8,0},{16,24},{24,16},{1,9},{9,1},{17,25},{25,17},{2,10},{10... | collective-permute-start | bytes 614408 | tf_op jit(solution)/shard_map/ppermute | solution.py:204
  95.8 7.9 %collective-permute-start.8 = (s16[400,256]{1,0:T(8,128)(2,1)S(1)}, s16[400,256]{1,0:T(8,128)(2,1)S(1)}, u32[]{:S(2)}, u32[]{:S(2)}) collective-permute-start(s16[400,256]{1,0:T(8,128)(2,1)S(1)} %get-tuple-element.28), channel_id=1, source_target_pairs={{0,16},{8,24},{16,0},{24,8},{1,17},{9,25},{17,1},{25,9},{2,18},{10... | collective-permute-start | bytes 614408 | tf_op jit(solution)/shard_map/ppermute | solution.py:204
  96.8 9.1 %collective-permute-start.9 = (s16[400,256]{1,0:T(8,128)(2,1)S(1)}, s16[400,256]{1,0:T(8,128)(2,1)S(1)}, u32[]{:S(2)}, u32[]{:S(2)}) collective-permute-start(s16[400,256]{1,0:T(8,128)(2,1)S(1)} %get-tuple-element.29), channel_id=1, source_target_pairs={{0,24},{8,16},{16,8},{24,0},{1,25},{9,17},{17,9},{25,1},{2,26},{10... | collective-permute-start | bytes 614408 | tf_op jit(solution)/shard_map/ppermute | solution.py:204
  (7 other events, 32.7 us)

commit v5 on v4

--- a/solution.py
+++ b/solution.py
@@ -5,11 +5,12 @@
 import jax.numpy as jnp
 from jax import lax
 from jax.experimental import pallas as pl
+from jax.experimental.layout import Layout, with_layout_constraint
 from jax.experimental.pallas import tpu as pltpu
 from jax.sharding import PartitionSpec as P
 
 TILE = 256
-SIXTEENTHS = (5, 5, 3, 3)
+SIXTEENTHS = (4, 5, 4, 3)
 SCALE_ROWS = 16
 CODE = 64.0
 TOP = 32767.0
@@ -40,19 +41,6 @@
             flops=size * columns, bytes_accessed=4 * size * columns, transcendentals=0
         ),
     )(pattern, left, *after)
-
-
-def gate_kernel(x_ref, after_ref, out_ref):
-    out_ref[...] = x_ref[...]
-
-
-def gate(x, after):
-    return pl.pallas_call(
-        gate_kernel,
-        out_shape=jax.ShapeDtypeStruct(x.shape, x.dtype),
-        in_specs=[VMEM, pl.BlockSpec(memory_space=pl.ANY)],
-        out_specs=VMEM,
-    )(x, after)
 
 
 def put_fixed(ref, at, total):
@@ -71,17 +59,25 @@
     return ref[at : at + rows, :].astype(jnp.int32).astype(jnp.float32) * unit
 
 
-def partial_kernel(n_sources, kept, sent, where, *refs):
-    lefts, right_ref, outs = refs[:n_sources], refs[n_sources], refs[n_sources + 1 :]
-    rows, columns = lefts[0].shape[0], right_ref.shape[3]
+def partial_kernel(n_sources, n_pieces, kept, sent, where, *refs):
+    lefts, pieces = refs[:n_sources], refs[n_sources : n_sources + n_pieces]
+    outs = refs[-len(kept) - len(sent) :]
+    rows, columns = lefts[0].shape[0], pieces[0].shape[2]
+
+    def right(source, layer):
+        start = pl.multiple_of(where[2 + 2 * source], TILE)
+        tile = pieces[0][layer, pl.ds(start, TILE), :]
+        for i in range(1, n_pieces):
+            here = where[1 + 2 * source] == i
+            tile = jnp.where(here, pieces[i][layer, pl.ds(start, TILE), :], tile)
+        return tile
 
     def product(k):
         total = jnp.zeros((rows, columns), jnp.float32)
         for source in range(n_sources):
-            start = pl.multiple_of(where[2 + 2 * source], TILE)
             total += jnp.dot(
                 lefts[source][...],
-                right_ref[where[1 + 2 * source], where[0] ^ k, pl.ds(start, TILE), :],
+                right(source, where[0] ^ k),
                 preferred_element_type=jnp.float32,
             )
         return total
@@ -93,25 +89,27 @@
         out[...] = product(k)
 
 
-def partial_products(where, lefts, right, kept, sent):
-    rows, columns = lefts[0].shape[0], right.shape[3]
+def partial_products(where, lefts, pieces, after, kept, sent):
+    rows, columns = lefts[0].shape[0], pieces[0].shape[2]
     n_products = len(kept) + sum(len(ks) for ks in sent)
     outs = [jax.ShapeDtypeStruct((rows, columns), jnp.float32)] * len(kept)
     outs += [
         jax.ShapeDtypeStruct((len(ks) * (rows + SCALE_ROWS), columns), jnp.int16) for ks in sent
     ]
     out = pl.pallas_call(
-        functools.partial(partial_kernel, len(lefts), kept, sent),
+        functools.partial(partial_kernel, len(lefts), len(pieces), kept, sent),
         out_shape=outs,
-        in_specs=[pl.BlockSpec(memory_space=pltpu.SMEM)] + [VMEM] * (len(lefts) + 1),
+        in_specs=[pl.BlockSpec(memory_space=pltpu.SMEM)]
+        + [VMEM] * (len(lefts) + len(pieces))
+        + [pl.BlockSpec(memory_space=pl.ANY)] * len(after),
         out_specs=[VMEM] * len(outs),
         compiler_params=PARAMS,
         cost_estimate=pl.CostEstimate(
             flops=2 * rows * len(lefts) * TILE * columns * n_products,
-            bytes_accessed=right.size * 2 + rows * columns * 14,
+            bytes_accessed=len(pieces) * pieces[0].size * 2 + rows * columns * 14,
             transcendentals=0,
         ),
-    )(where, *lefts, right)
+    )(where, *lefts, *pieces, *after)
     return out[: len(kept)], out[len(kept) :]
 
 
@@ -200,6 +198,10 @@
     return lax.ppermute(x, axis, [(i, (i + by) % n) for i in range(n)])
 
 
+def as_it_lies(x):
+    return with_layout_constraint(x, Layout(tuple(range(x.ndim))))
+
+
 def swap(x, bits):
     return lax.ppermute(x, "layer", [(i, i ^ bits) for i in range(4)])
 
@@ -213,44 +215,62 @@
 
     left = left_values.reshape(rows_local, columns_local)
     pattern = left_pattern.reshape(-1)
-    starts = [sum(sizes[:i]) for i in range(len(sizes))]
-    chunks = []
-    for i, (at, size) in enumerate(zip(starts, sizes)):
-        ring = [load(left, pattern, at, size, [chunks[i - 2][-1]] if i > 1 else [chunk[0] for chunk in chunks])]
-        for _ in range(n_cols - 1):
-            ring.append(shift(ring[-1], "col", 1))
-        chunks.append(ring)
-
-    right_pattern = gate(right_pattern, chunks[1][0])
-    right_block = expand_tiles(right_values, right_pattern).transpose(1, 0, 2)
-    pieces = [right_block]
-    for i in range(1, n_rows):
-        pieces.append(shift(right_block, "row", i))
-    right = jnp.stack(pieces)
-
     where = [layer]
     for source in range(n_cols):
         inner = (col - source + n_cols) % n_cols * columns_local
         where += [(row - inner // inner_piece + n_rows) % n_rows, inner % inner_piece]
     where = jnp.stack(where).astype(jnp.int32)
 
-    sums = []
-    for i, chunk in enumerate(chunks):
-        if i + 1 < len(chunks):
-            first, second = (1, 2) if i % 2 == 0 else (2, 1)
-            kept, sent = partial_products(where, chunk, right, (0, second), ((first, 3),))
-            sums.append((kept, swap(sent[0], first), second))
+    starts = [sum(sizes[:i]) for i in range(len(sizes))]
+    rings, kept, received, last = [], [], [], []
+
+    def open_ring(i):
+        after = [rings[0][-1]] if i == 2 else []
+        ring = [load(left, pattern, starts[i], sizes[i], after + last)]
+        for _ in range(n_cols - 1):
+            ring.append(shift(ring[-1], "col", 1))
+        rings.append(ring)
+        last[:] = [ring[0]]
+
+    def sum_ring(i):
+        if i + 1 < len(sizes):
+            ks, sent_ks = (0, second(i)), ((3 - second(i), 3),)
         else:
-            kept, sent = partial_products(where, chunk, right, (0,), ((1,), (2,), (3,)))
-            sums.append((kept, [swap(x, k + 1) for k, x in enumerate(sent)], 0))
+            ks, sent_ks = (0,), ((1,), (2,), (3,))
+        mine, sent = partial_products(where, rings[i], pieces, last, ks, sent_ks)
+        kept.append(mine)
+        received.append([swap(x, k[0]) for x, k in zip(sent, sent_ks)])
+        last[:] = [mine[0]]
+
+    def second(i):
+        return 2 - i % 2
+
+    def send_on(i):
+        block = pass_on(kept[i][1], received[i][0], last[0])
+        received[i].append(swap(block, second(i)))
+        last[:] = [block]
+
+    pieces = []
+    for i in range(n_rows):
+        values, tiles = right_values, right_pattern
+        if i:
+            values, tiles = as_it_lies(shift(values, "row", i)), shift(tiles, "row", i)
+        pieces.append(expand_tiles(values, tiles).transpose(1, 0, 2))
+
+    open_ring(0)
+    open_ring(1)
+    last += pieces
+    for i in range(len(sizes)):
+        if i + 2 < len(sizes):
+            open_ring(i + 2)
+        sum_ring(i)
+        if i > 0:
+            send_on(i - 1)
 
     squares = []
     column = jnp.zeros((1, columns_local), jnp.float32)
-    for i, (kept, received, second) in enumerate(sums):
-        if second:
-            after = chunks[i + 2][0] if i + 2 < len(chunks) else sums[-1][0][0]
-            received = [received, swap(pass_on(kept[1], received, after), second)]
-        squared, column = combine(kept[0], received, column)
+    for mine, blocks in zip(kept, received):
+        squared, column = combine(mine[0], blocks, column)
         squares.append(squared)
     column = lax.psum(column, "row")
     out = normalise(column, squares, rows_local * n_rows)

time: 110 us -> 112 us (1.018)
  starting transfers between devices: 16.8 us -> 19.3 us
  waiting for transfers between devices: 69.2 us -> 66.9 us
  local copies, waits for them, and re-layouts: 3.62 us -> 5.57 us
  other arithmetic: 3.75 us -> 1.99 us
    another operation x2 -> x0, other arithmetic: 3.08 us -> none  [per_device(): right = jnp.stack(pieces)]
    ppermute x9, starting transfers between devices: 10.7 us -> 13 us  [swap(): return lax.ppermute(x, 'layer', [(i, i ^ bits) for i in range(4)])]
    transpose x0 -> x2, other arithmetic: none -> 1.99 us  [per_device(): pieces.append(expand_tiles(values, tiles).transpose(1, 0, 2))]
    unnamed x21 -> x26, local copies, waits for them, and re-layouts: 3.41 us -> 5.27 us
    ppermute x9, waiting for transfers between devices: 8.2 us -> 6.58 us  [swap(): return lax.ppermute(x, 'layer', [(i, i ^ bits) for i in range(4)])]
    ppermute x13 -> x14, waiting for transfers between devices: 61 us -> 60.4 us  [shift(): return lax.ppermute(x, axis, [(i, (i + by) % n) for i in range(n)])]
    pallas_call x5 -> x4, Pallas kernels: 9.04 us -> 9.37 us  [partial_products(): pl.pallas_call(functools.partial(partial_kernel, len(lefts), len(pieces),...]
    ppermute x13 -> x14, starting transfers between devices: 6.03 us -> 6.3 us  [shift(): return lax.ppermute(x, axis, [(i, (i + by) % n) for i in range(n)])]
  transfers between devices with their start and end apart: 22 -> 23, of which waited for: 14 -> 11; matrix products, arithmetic and copies ran while one was open for 1% -> 2% of each run, Pallas kernels for 9% -> 12%
where the time goes in v5:
time: 112 us; the launch traced here: 111 us
  waiting for transfers between devices  66.9 us (60%)
  starting transfers between devices  19.3 us (17%)
  Pallas kernels  14.8 us (13%)
  local copies, waits for them, and re-layouts  5.57 us (5%)
  blocking collectives  2.47 us (2%)
  other arithmetic  1.99 us (2%)
    ppermute x14, waiting for transfers between devices, shift(): return lax.ppermute(x, axis, [(i, (i + by) % n) for i in range(n)])  60.4 us
    ppermute x9, starting transfers between devices, swap(): return lax.ppermute(x, 'layer', [(i, i ^ bits) for i in range(4)])  13 us
    pallas_call x4, Pallas kernels, partial_products(): pl.pallas_call(functools.partial(partial_kernel, len(lefts), len(pieces),...  9.37 us
    ppermute x9, waiting for transfers between devices, swap(): return lax.ppermute(x, 'layer', [(i, i ^ bits) for i in range(4)])  6.58 us
    ppermute x14, starting transfers between devices, shift(): return lax.ppermute(x, axis, [(i, (i + by) % n) for i in range(n)])  6.3 us
    unnamed x26, local copies, waits for them, and re-layouts  5.27 us
    pallas_call x4, Pallas kernels, load(): pl.pallas_call(functools.partial(load_kernel, at), out_shape=jax.ShapeDty...  2.97 us
    psum x1, blocking collectives, per_device(): column = lax.psum(column, 'row')  2.47 us
  transfers between devices with their start and end apart: 23, of which 11 were waited for; matrix products, arithmetic and copies ran while one was open for 2% of the time, Pallas kernels for 12%

profile of v5, /device:TPU:0, one launch (start us, length us, event | category | flops | bytes accessed | tf_op | source)
XLA Modules:
  0.0 111.2 jit_solution(14430456781738993947)
XLA Ops:
  2.9 2.6 %collective-permute-start = (bf16[512,256]{1,0:T(8,128)(2,1)S(1)}, bf16[512,256]{1,0:T(8,128)(2,1)S(1)}, u32[]{:S(2)}, u32[]{:S(2)}) collective-permute-start(bf16[512,256]{1,0:T(8,128)(2,1)S(1)} %shard_map.46.refs_0_), channel_id=1, source_target_pairs={{0,1},{1,2},{2,3},{3,0},{4,5},{5,6},{6,7},{7,4},{8,9},{9,10},{10,1... | collective-permute-start | bytes 786440 | tf_op jit(solution)/shard_map/ppermute | solution.py:198
  6.4 1.6 %collective-permute-start.8 = (bf16[640,256]{1,0:T(8,128)(2,1)S(1)}, bf16[640,256]{1,0:T(8,128)(2,1)}, u32[]{:S(2)}, u32[]{:S(2)}) collective-permute-start(bf16[640,256]{1,0:T(8,128)(2,1)S(1)} %shard_map.47.refs_1_.refs_0_), channel_id=1, source_target_pairs={{0,1},{1,2},{2,3},{3,0},{4,5},{5,6},{6,7},{7,4},{8,9},{9,10},{10,1... | collective-permute-start | bytes 983048 | tf_op jit(solution)/shard_map/ppermute | solution.py:198
  8.2 6.5 %collective-permute-done.refs_1_ = bf16[512,256]{1,0:T(8,128)(2,1)S(1)} collective-permute-done((bf16[512,256]{1,0:T(8,128)(2,1)S(1)}, bf16[512,256]{1,0:T(8,128)(2,1)S(1)}, u32[]{:S(2)}, u32[]{:S(2)}) %collective-permute-start) | collective-permute-done | bytes 262176 | tf_op jit(solution)/shard_map/ppermute | solution.py:198
  15.7 6.2 %collective-permute-done.8.refs_1_ = bf16[640,256]{1,0:T(8,128)(2,1)} collective-permute-done((bf16[640,256]{1,0:T(8,128)(2,1)S(1)}, bf16[640,256]{1,0:T(8,128)(2,1)}, u32[]{:S(2)}, u32[]{:S(2)}) %collective-permute-start.8) | collective-permute-done | bytes 327712 | tf_op jit(solution)/shard_map/ppermute | solution.py:198
  21.9 5.6 %collective-permute-done.1.refs_2_ = bf16[512,256]{1,0:T(8,128)(2,1)} collective-permute-done((bf16[512,256]{1,0:T(8,128)(2,1)S(1)}, bf16[512,256]{1,0:T(8,128)(2,1)}, u32[]{:S(2)}, u32[]{:S(2)}) %collective-permute-start.1) | collective-permute-done | bytes 262176 | tf_op jit(solution)/shard_map/ppermute | solution.py:198
  27.5 1.6 %fusion.refs_3_.refs_5_ = bf16[4,512,256]{2,1,0:T(8,128)(2,1)S(1)} fusion(bf16[512,4,256]{2,1,0:T(4,128)(2,1)} %collective-permute-done.3, bf16[512,4]{0,1:T(4,128)(2,1)S(1)} %bitcast.36), kind=kLoop, calls=%fused_computation.1 | loop fusion | flops 524288 | bytes 2101248 | tf_op jit(solution)/shard_map/transpose | solution.py:258
  29.2 10.7 %collective-permute-done.2.refs_0_.refs_3_ = bf16[512,256]{1,0:T(8,128)(2,1)S(1)} collective-permute-done((bf16[512,256]{1,0:T(8,128)(2,1)}, bf16[512,256]{1,0:T(8,128)(2,1)S(1)}, u32[]{:S(2)}, u32[]{:S(2)}) %collective-permute-start.2) | collective-permute-done | bytes 262176 | tf_op jit(solution)/shard_map/ppermute | solution.py:198
  45.4 2.4 %shard_map.49 = (f32[512,256]{1,0:T(8,128)S(1)}, f32[512,256]{1,0:T(8,128)S(1)}, s16[1056,256]{1,0:T(8,128)(2,1)S(1)}) custom-call(s32[9]{0:T(128)S(1)} %stack.39.where, bf16[512,256]{1,0:T(8,128)(2,1)S(1)} %copy-done.3, bf16[512,256]{1,0:T(8,128)(2,1)S(1)} %copy-done.8, bf16[512,256]{1,0:T(8,128)(2,1)} %collective-permute-done.1.refs_2_, ...), custom_call_target="tpu_custom_call" | custom-call | flops 1073741824 | bytes 3932160 | tf_op jit(solution)/shard_map/pallas_call | solution.py:99
  47.8 1.6 %collective-permute-start.15 = (s16[1056,256]{1,0:T(8,128)(2,1)S(1)}, s16[1056,256]{1,0:T(8,128)(2,1)S(1)}, u32[]{:S(2)}, u32[]{:S(2)}) collective-permute-start(s16[1056,256]{1,0:T(8,128)(2,1)S(1)} %get-tuple-element.30), channel_id=1, source_target_pairs={{0,8},{8,0},{16,24},{24,16},{1,9},{9,1},{17,25},{25,17},{2,10},{10... | collective-permute-start | bytes 1622024 | tf_op jit(solution)/shard_map/ppermute | solution.py:206
  49.4 3.1 %collective-permute-done.12.refs_1_ = bf16[512,256]{1,0:T(8,128)(2,1)} collective-permute-done((bf16[512,256]{1,0:T(8,128)(2,1)}, bf16[512,256]{1,0:T(8,128)(2,1)}, u32[]{:S(2)}, u32[]{:S(2)}) %collective-permute-start.12) | collective-permute-done | bytes 262176 | tf_op jit(solution)/shard_map/ppermute | solution.py:198
  52.4 11.4 %collective-permute-done.13.refs_2_ = bf16[512,256]{1,0:T(8,128)(2,1)S(1)} collective-permute-done((bf16[512,256]{1,0:T(8,128)(2,1)}, bf16[512,256]{1,0:T(8,128)(2,1)S(1)}, u32[]{:S(2)}, u32[]{:S(2)}) %collective-permute-start.13) | collective-permute-done | bytes 262176 | tf_op jit(solution)/shard_map/ppermute | solution.py:198
  64.4 2.8 %shard_map.51 = (f32[640,256]{1,0:T(8,128)S(1)}, f32[640,256]{1,0:T(8,128)S(1)}, s16[1312,256]{1,0:T(8,128)(2,1)S(1)}) custom-call(s32[9]{0:T(128)S(1)} %stack.39.where, bf16[640,256]{1,0:T(8,128)(2,1)S(1)} %shard_map.47.refs_1_.refs_0_, bf16[640,256]{1,0:T(8,128)(2,1)} %collective-permute-done.8.refs_1_, bf16[640,256]{1,0:T(8,128)(2,1)} %collective-permute-done.9.refs_2_, ...), custom_call_target="tpu_custom_call" | custom-call | flops 1342177280 | bytes 4390912 | tf_op jit(solution)/shard_map/pallas_call | solution.py:99
  67.2 1.5 %collective-permute-start.11 = (s16[1312,256]{1,0:T(8,128)(2,1)S(1)}, s16[1312,256]{1,0:T(8,128)(2,1)S(1)}, u32[]{:S(2)}, u32[]{:S(2)}) collective-permute-start(s16[1312,256]{1,0:T(8,128)(2,1)S(1)} %get-tuple-element.28), channel_id=1, source_target_pairs={{0,16},{8,24},{16,0},{24,8},{1,17},{9,25},{17,1},{25,9},{2,18},{10... | collective-permute-start | bytes 2015240 | tf_op jit(solution)/shard_map/ppermute | solution.py:206
  68.8 5.0 %collective-permute-done.14.refs_3_ = bf16[512,256]{1,0:T(8,128)(2,1)S(1)} collective-permute-done((bf16[512,256]{1,0:T(8,128)(2,1)S(1)}, bf16[512,256]{1,0:T(8,128)(2,1)S(1)}, u32[]{:S(2)}, u32[]{:S(2)}) %collective-permute-start.14) | collective-permute-done | bytes 262176 | tf_op jit(solution)/shard_map/ppermute | solution.py:198
  73.8 2.5 %shard_map.53 = (f32[512,256]{1,0:T(8,128)S(1)}, f32[512,256]{1,0:T(8,128)S(1)}, s16[1056,256]{1,0:T(8,128)(2,1)S(1)}) custom-call(s32[9]{0:T(128)S(1)} %stack.39.where, bf16[512,256]{1,0:T(8,128)(2,1)} %shard_map.48.refs_6_.refs_0_, bf16[512,256]{1,0:T(8,128)(2,1)} %collective-permute-done.12.refs_1_, bf16[512,256]{1,0:T(8,128)(2,1)S(1)} %collective-permute-done.13.refs_2_, ...), custom_call_target="tpu_custom_call" | custom-call | flops 1073741824 | bytes 3932160 | tf_op jit(solution)/shard_map/pallas_call | solution.py:99
  77.3 7.5 %collective-permute-done.6.refs_2_ = bf16[384,256]{1,0:T(8,128)(2,1)S(1)} collective-permute-done((bf16[384,256]{1,0:T(8,128)(2,1)S(1)}, bf16[384,256]{1,0:T(8,128)(2,1)S(1)}, u32[]{:S(2)}, u32[]{:S(2)}) %collective-permute-start.6) | collective-permute-done | bytes 196640 | tf_op jit(solution)/shard_map/ppermute | solution.py:198
  84.8 2.5 %collective-permute-start.22 = (s16[528,256]{1,0:T(8,128)(2,1)S(1)}, s16[528,256]{1,0:T(8,128)(2,1)S(1)}, u32[]{:S(2)}, u32[]{:S(2)}) collective-permute-start(s16[528,256]{1,0:T(8,128)(2,1)S(1)} %shard_map.52.refs_6_), channel_id=1, source_target_pairs={{0,16},{8,24},{16,0},{24,8},{1,17},{9,25},{17,1},{25,9},{2,18},{10... | collective-permute-start | bytes 811016 | tf_op jit(solution)/shard_map/ppermute | solution.py:206
  87.9 4.4 %collective-permute-done.7.refs_3_ = bf16[384,256]{1,0:T(8,128)(2,1)S(1)} collective-permute-done((bf16[384,256]{1,0:T(8,128)(2,1)S(1)}, bf16[384,256]{1,0:T(8,128)(2,1)S(1)}, u32[]{:S(2)}, u32[]{:S(2)}) %collective-permute-start.7) | collective-permute-done | bytes 196640 | tf_op jit(solution)/shard_map/ppermute | solution.py:198
  92.3 1.7 %shard_map.55 = (f32[384,256]{1,0:T(8,128)S(1)}, s16[400,256]{1,0:T(8,128)(2,1)S(1)}, s16[400,256]{1,0:T(8,128)(2,1)S(1)}, s16[400,256]{1,0:T(8,128)(2,1)S(1)}) custom-call(s32[9]{0:T(128)S(1)} %stack.39.where, bf16[384,256]{1,0:T(8,128)(2,1)S(1)} %shard_map.50.refs_6_.refs_0_, bf16[384,256]{1,0:T(8,128)(2,1)S(1)} %collective-permute-done.5.refs_1_, ...), custom_call_target="tpu_custom_call" | custom-call | flops 805306368 | bytes 3473408 | tf_op jit(solution)/shard_map/pallas_call | solution.py:99
  94.2 2.6 %collective-permute-start.20 = (s16[528,256]{1,0:T(8,128)(2,1)S(1)}, s16[528,256]{1,0:T(8,128)(2,1)S(1)}, u32[]{:S(2)}, u32[]{:S(2)}) collective-permute-start(s16[528,256]{1,0:T(8,128)(2,1)S(1)} %shard_map.56), channel_id=1, source_target_pairs={{0,16},{8,24},{16,0},{24,8},{1,17},{9,25},{17,1},{25,9},{2,18},{10... | collective-permute-start | bytes 811016 | tf_op jit(solution)/shard_map/ppermute | solution.py:206
  97.3 2.9 %collective-permute-start.18 = (s16[400,256]{1,0:T(8,128)(2,1)S(1)}, s16[400,256]{1,0:T(8,128)(2,1)S(1)}, u32[]{:S(2)}, u32[]{:S(2)}) collective-permute-start(s16[400,256]{1,0:T(8,128)(2,1)S(1)} %get-tuple-element.36), channel_id=1, source_target_pairs={{0,24},{8,16},{16,8},{24,0},{1,25},{9,17},{17,9},{25,1},{2,26},{10... | collective-permute-start | bytes 614408 | tf_op jit(solution)/shard_map/ppermute | solution.py:206
  100.7 4.6 %collective-permute-done.20.refs_1_ = s16[528,256]{1,0:T(8,128)(2,1)S(1)} collective-permute-done((s16[528,256]{1,0:T(8,128)(2,1)S(1)}, s16[528,256]{1,0:T(8,128)(2,1)S(1)}, u32[]{:S(2)}, u32[]{:S(2)}) %collective-permute-start.20) | collective-permute-done | bytes 270368 | tf_op jit(solution)/shard_map/ppermute | solution.py:206
  105.5 2.0 %collective-permute-done.17.refs_1_ = s16[400,256]{1,0:T(8,128)(2,1)S(1)} collective-permute-done((s16[400,256]{1,0:T(8,128)(2,1)S(1)}, s16[400,256]{1,0:T(8,128)(2,1)S(1)}, u32[]{:S(2)}, u32[]{:S(2)}) %collective-permute-start.17) | collective-permute-done | bytes 204832 | tf_op jit(solution)/shard_map/ppermute | solution.py:206
  107.7 2.5 %psum.7.column_ref = f32[1,256]{1,0:T(1,128)S(1)} all-reduce(f32[1,256]{1,0:T(1,128)S(1)} %get-tuple-element.42), channel_id=1, replica_groups=mesh['layer'=4,'row'=2,'col'=4] {'row'}, use_global_device_ids=true, to_apply=%region_0.1 | all-reduce | flops 256 | bytes 2048 | tf_op jit(solution)/shard_map/psum | solution.py:275
  (73 shorter events, 15.3 us)
Async XLA Ops:
  0.0 27.5 %collective-permute-start.3 = (bf16[512,4,256]{2,1,0:T(4,128)(2,1)}, bf16[512,4,256]{2,1,0:T(4,128)(2,1)}, u32[]{:S(2)}, u32[]{:S(2)}) collective-permute-start(bf16[512,4,256]{2,1,0:T(4,128)(2,1)} %param.6), channel_id=1, source_target_pairs={{0,4},{4,0},{1,5},{5,1},{2,6},{6,2},{3,7},{7,3},{8,12},{12,8},{9,1... | collective-permute-start | bytes 3145736 | tf_op jit(solution)/shard_map/ppermute | solution.py:198
  2.9 11.8 %collective-permute-start = (bf16[512,256]{1,0:T(8,128)(2,1)S(1)}, bf16[512,256]{1,0:T(8,128)(2,1)S(1)}, u32[]{:S(2)}, u32[]{:S(2)}) collective-permute-start(bf16[512,256]{1,0:T(8,128)(2,1)S(1)} %shard_map.46.refs_0_), channel_id=1, source_target_pairs={{0,1},{1,2},{2,3},{3,0},{4,5},{5,6},{6,7},{7,4},{8,9},{9,10},{10,1... | collective-permute-start | bytes 786440 | tf_op jit(solution)/shard_map/ppermute | solution.py:198
  5.6 9.9 %collective-permute-start.4 = (s32[2,4,1]{1,2,0:T(1,128)S(1)}, s32[2,4,1]{1,2,0:T(1,128)S(1)}, u32[]{:S(2)}, u32[]{:S(2)}) collective-permute-start(s32[2,4,1]{1,2,0:T(1,128)S(1)} %copy-done.10), channel_id=1, source_target_pairs={{0,4},{4,0},{1,5},{5,1},{2,6},{6,2},{3,7},{7,3},{8,12},{12,8},{9,1... | collective-permute-start | bytes 104 | tf_op jit(solution)/shard_map/ppermute | solution.py:198
  6.4 15.5 %collective-permute-start.8 = (bf16[640,256]{1,0:T(8,128)(2,1)S(1)}, bf16[640,256]{1,0:T(8,128)(2,1)}, u32[]{:S(2)}, u32[]{:S(2)}) collective-permute-start(bf16[640,256]{1,0:T(8,128)(2,1)S(1)} %shard_map.47.refs_1_.refs_0_), channel_id=1, source_target_pairs={{0,1},{1,2},{2,3},{3,0},{4,5},{5,6},{6,7},{7,4},{8,9},{9,10},{10,1... | collective-permute-start | bytes 983048 | tf_op jit(solution)/shard_map/ppermute | solution.py:198
  14.7 12.7 %collective-permute-start.1 = (bf16[512,256]{1,0:T(8,128)(2,1)S(1)}, bf16[512,256]{1,0:T(8,128)(2,1)}, u32[]{:S(2)}, u32[]{:S(2)}) collective-permute-start(bf16[512,256]{1,0:T(8,128)(2,1)S(1)} %collective-permute-done.refs_1_), channel_id=1, source_target_pairs={{0,1},{1,2},{2,3},{3,0},{4,5},{5,6},{6,7},{7,4},{8,9},{9,10},{10,1... | collective-permute-start | bytes 786440 | tf_op jit(solution)/shard_map/ppermute | solution.py:198
  21.9 19.3 %collective-permute-start.9 = (bf16[640,256]{1,0:T(8,128)(2,1)}, bf16[640,256]{1,0:T(8,128)(2,1)}, u32[]{:S(2)}, u32[]{:S(2)}) collective-permute-start(bf16[640,256]{1,0:T(8,128)(2,1)} %collective-permute-done.8.refs_1_), channel_id=1, source_target_pairs={{0,1},{1,2},{2,3},{3,0},{4,5},{5,6},{6,7},{7,4},{8,9},{9,10},{10,1... | collective-permute-start | bytes 983048 | tf_op jit(solution)/shard_map/ppermute | solution.py:198
  27.5 12.4 %collective-permute-start.2 = (bf16[512,256]{1,0:T(8,128)(2,1)}, bf16[512,256]{1,0:T(8,128)(2,1)S(1)}, u32[]{:S(2)}, u32[]{:S(2)}) collective-permute-start(bf16[512,256]{1,0:T(8,128)(2,1)} %collective-permute-done.1.refs_2_), channel_id=1, source_target_pairs={{0,1},{1,2},{2,3},{3,0},{4,5},{5,6},{6,7},{7,4},{8,9},{9,10},{10,1... | collective-permute-start | bytes 786440 | tf_op jit(solution)/shard_map/ppermute | solution.py:198
  27.5 12.3 %copy-start.1 = (bf16[2048,1,256]{2,0,1:T(8,128)(2,1)S(1)}, bf16[2048,1,256]{2,0,1:T(8,128)(2,1)}, u32[]{:S(2)}) copy-start(bf16[2048,1,256]{2,0,1:T(8,128)(2,1)} %param.4) | copy-start | bytes 3145732
  41.1 11.3 %collective-permute-start.12 = (bf16[512,256]{1,0:T(8,128)(2,1)}, bf16[512,256]{1,0:T(8,128)(2,1)}, u32[]{:S(2)}, u32[]{:S(2)}) collective-permute-start(bf16[512,256]{1,0:T(8,128)(2,1)} %shard_map.48.refs_6_.refs_0_), channel_id=1, source_target_pairs={{0,1},{1,2},{2,3},{3,0},{4,5},{5,6},{6,7},{7,4},{8,9},{9,10},{10,1... | collective-permute-start | bytes 786440 | tf_op jit(solution)/shard_map/ppermute | solution.py:198
  41.2 23.2 %collective-permute-start.10 = (bf16[640,256]{1,0:T(8,128)(2,1)}, bf16[640,256]{1,0:T(8,128)(2,1)S(1)}, u32[]{:S(2)}, u32[]{:S(2)}) collective-permute-start(bf16[640,256]{1,0:T(8,128)(2,1)} %collective-permute-done.9.refs_2_), channel_id=1, source_target_pairs={{0,1},{1,2},{2,3},{3,0},{4,5},{5,6},{6,7},{7,4},{8,9},{9,10},{10,1... | collective-permute-start | bytes 983048 | tf_op jit(solution)/shard_map/ppermute | solution.py:198
  47.8 20.9 %collective-permute-start.15 = (s16[1056,256]{1,0:T(8,128)(2,1)S(1)}, s16[1056,256]{1,0:T(8,128)(2,1)S(1)}, u32[]{:S(2)}, u32[]{:S(2)}) collective-permute-start(s16[1056,256]{1,0:T(8,128)(2,1)S(1)} %get-tuple-element.30), channel_id=1, source_target_pairs={{0,8},{8,0},{16,24},{24,16},{1,9},{9,1},{17,25},{25,17},{2,10},{10... | collective-permute-start | bytes 1622024 | tf_op jit(solution)/shard_map/ppermute | solution.py:206
  52.4 11.4 %collective-permute-start.13 = (bf16[512,256]{1,0:T(8,128)(2,1)}, bf16[512,256]{1,0:T(8,128)(2,1)S(1)}, u32[]{:S(2)}, u32[]{:S(2)}) collective-permute-start(bf16[512,256]{1,0:T(8,128)(2,1)} %collective-permute-done.12.refs_1_), channel_id=1, source_target_pairs={{0,1},{1,2},{2,3},{3,0},{4,5},{5,6},{6,7},{7,4},{8,9},{9,10},{10,1... | collective-permute-start | bytes 786440 | tf_op jit(solution)/shard_map/ppermute | solution.py:198
  63.8 10.0 %collective-permute-start.14 = (bf16[512,256]{1,0:T(8,128)(2,1)S(1)}, bf16[512,256]{1,0:T(8,128)(2,1)S(1)}, u32[]{:S(2)}, u32[]{:S(2)}) collective-permute-start(bf16[512,256]{1,0:T(8,128)(2,1)S(1)} %collective-permute-done.13.refs_2_), channel_id=1, source_target_pairs={{0,1},{1,2},{2,3},{3,0},{4,5},{5,6},{6,7},{7,4},{8,9},{9,10},{10,1... | collective-permute-start | bytes 786440 | tf_op jit(solution)/shard_map/ppermute | solution.py:198
  67.2 20.1 %collective-permute-start.11 = (s16[1312,256]{1,0:T(8,128)(2,1)S(1)}, s16[1312,256]{1,0:T(8,128)(2,1)S(1)}, u32[]{:S(2)}, u32[]{:S(2)}) collective-permute-start(s16[1312,256]{1,0:T(8,128)(2,1)S(1)} %get-tuple-element.28), channel_id=1, source_target_pairs={{0,16},{8,24},{16,0},{24,8},{1,17},{9,25},{17,1},{25,9},{2,18},{10... | collective-permute-start | bytes 2015240 | tf_op jit(solution)/shard_map/ppermute | solution.py:206
  68.7 8.7 %collective-permute-start.5 = (bf16[384,256]{1,0:T(8,128)(2,1)S(1)}, bf16[384,256]{1,0:T(8,128)(2,1)S(1)}, u32[]{:S(2)}, u32[]{:S(2)}) collective-permute-start(bf16[384,256]{1,0:T(8,128)(2,1)S(1)} %shard_map.50.refs_6_.refs_0_), channel_id=1, source_target_pairs={{0,1},{1,2},{2,3},{3,0},{4,5},{5,6},{6,7},{7,4},{8,9},{9,10},{10,1... | collective-permute-start | bytes 589832 | tf_op jit(solution)/shard_map/ppermute | solution.py:198
  76.3 17.7 %collective-permute-start.19 = (s16[1056,256]{1,0:T(8,128)(2,1)S(1)}, s16[1056,256]{1,0:T(8,128)(2,1)S(1)}, u32[]{:S(2)}, u32[]{:S(2)}) collective-permute-start(s16[1056,256]{1,0:T(8,128)(2,1)S(1)} %get-tuple-element.37), channel_id=1, source_target_pairs={{0,8},{8,0},{16,24},{24,16},{1,9},{9,1},{17,25},{25,17},{2,10},{10... | collective-permute-start | bytes 1622024 | tf_op jit(solution)/shard_map/ppermute | solution.py:206
  77.3 7.5 %collective-permute-start.6 = (bf16[384,256]{1,0:T(8,128)(2,1)S(1)}, bf16[384,256]{1,0:T(8,128)(2,1)S(1)}, u32[]{:S(2)}, u32[]{:S(2)}) collective-permute-start(bf16[384,256]{1,0:T(8,128)(2,1)S(1)} %collective-permute-done.5.refs_1_), channel_id=1, source_target_pairs={{0,1},{1,2},{2,3},{3,0},{4,5},{5,6},{6,7},{7,4},{8,9},{9,10},{10,1... | collective-permute-start | bytes 589832 | tf_op jit(solution)/shard_map/ppermute | solution.py:198
  84.8 7.5 %collective-permute-start.7 = (bf16[384,256]{1,0:T(8,128)(2,1)S(1)}, bf16[384,256]{1,0:T(8,128)(2,1)S(1)}, u32[]{:S(2)}, u32[]{:S(2)}) collective-permute-start(bf16[384,256]{1,0:T(8,128)(2,1)S(1)} %collective-permute-done.6.refs_2_), channel_id=1, source_target_pairs={{0,1},{1,2},{2,3},{3,0},{4,5},{5,6},{6,7},{7,4},{8,9},{9,10},{10,1... | collective-permute-start | bytes 589832 | tf_op jit(solution)/shard_map/ppermute | solution.py:198
  84.8 12.5 %collective-permute-start.22 = (s16[528,256]{1,0:T(8,128)(2,1)S(1)}, s16[528,256]{1,0:T(8,128)(2,1)S(1)}, u32[]{:S(2)}, u32[]{:S(2)}) collective-permute-start(s16[528,256]{1,0:T(8,128)(2,1)S(1)} %shard_map.52.refs_6_), channel_id=1, source_target_pairs={{0,16},{8,24},{16,0},{24,8},{1,17},{9,25},{17,1},{25,9},{2,18},{10... | collective-permute-start | bytes 811016 | tf_op jit(solution)/shard_map/ppermute | solution.py:206
  87.5 12.9 %collective-permute-start.21 = (s16[656,256]{1,0:T(8,128)(2,1)S(1)}, s16[656,256]{1,0:T(8,128)(2,1)S(1)}, u32[]{:S(2)}, u32[]{:S(2)}) collective-permute-start(s16[656,256]{1,0:T(8,128)(2,1)S(1)} %shard_map.54.refs_6_), channel_id=1, source_target_pairs={{0,8},{8,0},{16,24},{24,16},{1,9},{9,1},{17,25},{25,17},{2,10},{10... | collective-permute-start | bytes 1007624 | tf_op jit(solution)/shard_map/ppermute | solution.py:206
  94.2 11.1 %collective-permute-start.20 = (s16[528,256]{1,0:T(8,128)(2,1)S(1)}, s16[528,256]{1,0:T(8,128)(2,1)S(1)}, u32[]{:S(2)}, u32[]{:S(2)}) collective-permute-start(s16[528,256]{1,0:T(8,128)(2,1)S(1)} %shard_map.56), channel_id=1, source_target_pairs={{0,16},{8,24},{16,0},{24,8},{1,17},{9,25},{17,1},{25,9},{2,18},{10... | collective-permute-start | bytes 811016 | tf_op jit(solution)/shard_map/ppermute | solution.py:206
  96.8 8.7 %collective-permute-start.16 = (s16[400,256]{1,0:T(8,128)(2,1)S(1)}, s16[400,256]{1,0:T(8,128)(2,1)S(1)}, u32[]{:S(2)}, u32[]{:S(2)}) collective-permute-start(s16[400,256]{1,0:T(8,128)(2,1)S(1)} %get-tuple-element.34), channel_id=1, source_target_pairs={{0,8},{8,0},{16,24},{24,16},{1,9},{9,1},{17,25},{25,17},{2,10},{10... | collective-permute-start | bytes 614408 | tf_op jit(solution)/shard_map/ppermute | solution.py:206
  97.0 10.4 %collective-permute-start.17 = (s16[400,256]{1,0:T(8,128)(2,1)S(1)}, s16[400,256]{1,0:T(8,128)(2,1)S(1)}, u32[]{:S(2)}, u32[]{:S(2)}) collective-permute-start(s16[400,256]{1,0:T(8,128)(2,1)S(1)} %get-tuple-element.35), channel_id=1, source_target_pairs={{0,16},{8,24},{16,0},{24,8},{1,17},{9,25},{17,1},{25,9},{2,18},{10... | collective-permute-start | bytes 614408 | tf_op jit(solution)/shard_map/ppermute | solution.py:206
  97.3 10.1 %collective-permute-start.18 = (s16[400,256]{1,0:T(8,128)(2,1)S(1)}, s16[400,256]{1,0:T(8,128)(2,1)S(1)}, u32[]{:S(2)}, u32[]{:S(2)}) collective-permute-start(s16[400,256]{1,0:T(8,128)(2,1)S(1)} %get-tuple-element.36), channel_id=1, source_target_pairs={{0,24},{8,16},{16,8},{24,0},{1,25},{9,17},{17,9},{25,1},{2,26},{10... | collective-permute-start | bytes 614408 | tf_op jit(solution)/shard_map/ppermute | solution.py:206
  (10 other events, 25.2 us)

commit v6 on v5

--- a/solution.py
+++ b/solution.py
@@ -10,7 +10,7 @@
 from jax.sharding import PartitionSpec as P
 
 TILE = 256
-SIXTEENTHS = (4, 5, 4, 3)
+SIXTEENTHS = (4, 4, 3, 3, 2)
 SCALE_ROWS = 16
 CODE = 64.0
 TOP = 32767.0
@@ -19,28 +19,37 @@
 PARAMS = pltpu.CompilerParams(vmem_limit_bytes=40 * 1024 * 1024)
 
 
-def load_kernel(at, pattern_ref, left_ref, *refs):
-    out_ref = refs[-1]
-    size = out_ref.shape[0]
-    step = math.gcd(TILE, math.gcd(at, size))
-    for i in range(0, size, step):
-        entry = pattern_ref[(at + i) // TILE].astype(jnp.float32).astype(out_ref.dtype)
-        out_ref[i : i + step, :] = left_ref[at + i : at + i + step, :] * entry
-
-
-def load(left, pattern, at, size, after):
+def load_kernel(at, size, moving, pattern_ref, left_ref, *refs):
+    outs = refs[-len(moving) :]
+    for arrived, out, parts in zip(refs, outs, moving):
+        done = 0
+        for first, rows in parts:
+            out[done : done + rows, :] = arrived[first : first + rows, :]
+            done += rows
+        step = math.gcd(TILE, math.gcd(at, size))
+        for i in range(0, size, step):
+            entry = pattern_ref[(at + i) // TILE].astype(jnp.float32).astype(out.dtype)
+            block = left_ref[at + i : at + i + step, :] * entry
+            out[done + i : done + i + step, :] = block
+
+
+def load(left, pattern, at, size, arrived, moving, after):
     columns = left.shape[1]
+    totals = [size + sum(rows for _, rows in parts) for parts in moving]
     return pl.pallas_call(
-        functools.partial(load_kernel, at),
-        out_shape=jax.ShapeDtypeStruct((size, columns), left.dtype),
+        functools.partial(load_kernel, at, size, moving),
+        out_shape=[jax.ShapeDtypeStruct((total, columns), left.dtype) for total in totals],
         in_specs=[pl.BlockSpec(memory_space=pltpu.SMEM), VMEM]
+        + [VMEM if parts else pl.BlockSpec(memory_space=pl.ANY) for parts in moving]
         + [pl.BlockSpec(memory_space=pl.ANY)] * len(after),
-        out_specs=VMEM,
-        compiler_params=PARAMS,
-        cost_estimate=pl.CostEstimate(
-            flops=size * columns, bytes_accessed=4 * size * columns, transcendentals=0
-        ),
-    )(pattern, left, *after)
+        out_specs=[VMEM] * len(moving),
+        compiler_params=PARAMS,
+        cost_estimate=pl.CostEstimate(
+            flops=sum(totals) * columns,
+            bytes_accessed=4 * sum(totals) * columns,
+            transcendentals=0,
+        ),
+    )(pattern, left, *arrived, *after)
 
 
 def put_fixed(ref, at, total):
@@ -59,10 +68,11 @@
     return ref[at : at + rows, :].astype(jnp.int32).astype(jnp.float32) * unit
 
 
-def partial_kernel(n_sources, n_pieces, kept, sent, where, *refs):
+def partial_kernel(rows, firsts, n_pieces, kept, sent, where, *refs):
+    n_sources = len(firsts)
     lefts, pieces = refs[:n_sources], refs[n_sources : n_sources + n_pieces]
     outs = refs[-len(kept) - len(sent) :]
-    rows, columns = lefts[0].shape[0], pieces[0].shape[2]
+    columns = pieces[0].shape[2]
 
     def right(source, layer):
         start = pl.multiple_of(where[2 + 2 * source], TILE)
@@ -76,7 +86,7 @@
         total = jnp.zeros((rows, columns), jnp.float32)
         for source in range(n_sources):
             total += jnp.dot(
-                lefts[source][...],
+                lefts[source][firsts[source] : firsts[source] + rows, :],
                 right(source, where[0] ^ k),
                 preferred_element_type=jnp.float32,
             )
@@ -89,15 +99,16 @@
         out[...] = product(k)
 
 
-def partial_products(where, lefts, pieces, after, kept, sent):
-    rows, columns = lefts[0].shape[0], pieces[0].shape[2]
+def partial_products(where, lefts, rows, pieces, after, kept, sent):
+    columns = pieces[0].shape[2]
+    firsts = tuple(first for _, first in lefts)
     n_products = len(kept) + sum(len(ks) for ks in sent)
     outs = [jax.ShapeDtypeStruct((rows, columns), jnp.float32)] * len(kept)
     outs += [
         jax.ShapeDtypeStruct((len(ks) * (rows + SCALE_ROWS), columns), jnp.int16) for ks in sent
     ]
     out = pl.pallas_call(
-        functools.partial(partial_kernel, len(lefts), len(pieces), kept, sent),
+        functools.partial(partial_kernel, rows, firsts, len(pieces), kept, sent),
         out_shape=outs,
         in_specs=[pl.BlockSpec(memory_space=pltpu.SMEM)]
         + [VMEM] * (len(lefts) + len(pieces))
@@ -109,7 +120,7 @@
             bytes_accessed=len(pieces) * pieces[0].size * 2 + rows * columns * 14,
             transcendentals=0,
         ),
-    )(where, *lefts, *pieces, *after)
+    )(where, *(block for block, _ in lefts), *pieces, *after)
     return out[: len(kept)], out[len(kept) :]
 
 
@@ -134,7 +145,8 @@
 
 
 def combine_kernel(n_received, kept_ref, *refs):
-    received, (before_ref, squared_ref, sum_ref) = refs[:n_received], refs[n_received:]
+    received, before_ref = refs[:n_received], refs[n_received]
+    squared_ref, sum_ref = refs[-2:]
     total = kept_ref[...]
     for block in received:
         total += get_fixed(block, 0, total.shape[0])
@@ -143,20 +155,20 @@
     sum_ref[...] = before_ref[...] + jnp.sum(squared, axis=0, keepdims=True)
 
 
-def combine(kept, received, before):
+def combine(kept, received, before, after):
     return pl.pallas_call(
         functools.partial(combine_kernel, len(received)),
         out_shape=(
             jax.ShapeDtypeStruct(kept.shape, jnp.float32),
             jax.ShapeDtypeStruct((1, kept.shape[1]), jnp.float32),
         ),
-        in_specs=[VMEM] * (2 + len(received)),
+        in_specs=[VMEM] * (2 + len(received)) + [pl.BlockSpec(memory_space=pl.ANY)] * len(after),
         out_specs=(VMEM, VMEM),
         compiler_params=PARAMS,
         cost_estimate=pl.CostEstimate(
             flops=8 * kept.size, bytes_accessed=kept.size * 14, transcendentals=0
         ),
-    )(kept, *received, before)
+    )(kept, *received, before, *after)
 
 
 def normalise_kernel(n_chunks, rows_total, column_ref, *refs):
@@ -215,29 +227,45 @@
 
     left = left_values.reshape(rows_local, columns_local)
     pattern = left_pattern.reshape(-1)
+    reach = (n_cols // 2, n_cols - 1 - n_cols // 2)
     where = [layer]
-    for source in range(n_cols):
-        inner = (col - source + n_cols) % n_cols * columns_local
+    for source in [0] + [-1 - i for i in range(reach[0])] + [1 + i for i in range(reach[1])]:
+        inner = (col + source + n_cols) % n_cols * columns_local
         where += [(row - inner // inner_piece + n_rows) % n_rows, inner % inner_piece]
     where = jnp.stack(where).astype(jnp.int32)
 
     starts = [sum(sizes[:i]) for i in range(len(sizes))]
-    rings, kept, received, last = [], [], [], []
-
-    def open_ring(i):
-        after = [rings[0][-1]] if i == 2 else []
-        ring = [load(left, pattern, starts[i], sizes[i], after + last)]
-        for _ in range(n_cols - 1):
-            ring.append(shift(ring[-1], "col", 1))
-        rings.append(ring)
-        last[:] = [ring[0]]
-
-    def sum_ring(i):
+    own = []
+    found = [([], []) for _ in sizes]
+    kept, received, last = [], [], []
+
+    def open_slot(slot):
+        at, size = (starts[slot], sizes[slot]) if slot < len(sizes) else (0, 0)
+        going = [d for d in (0, 1) if slot < len(sizes) - 1 + reach[d]]
+        arrived, moving, riders = [], [], []
+        for d in going:
+            on = [c for c in range(min(slot, len(sizes))) if len(found[c][d]) < reach[d]]
+            arrived.append(found[on[0]][d][-1][0] if on else left)
+            moving.append(tuple((found[c][d][-1][1], sizes[c]) for c in on))
+            riders.append(on + ([slot] if size else []))
+        blocks = load(left, pattern, at, size, arrived, moving, last)
+        last[:] = [blocks[0]]
+        for d, block, chunks in zip(going, blocks, riders):
+            got, first = shift(block, "col", 1 - 2 * d), 0
+            for c in chunks:
+                found[c][d].append((got, first))
+                if c == slot and d == going[-1]:
+                    own.append((block, first))
+                first += sizes[c]
+
+    def sum_chunk(i):
         if i + 1 < len(sizes):
             ks, sent_ks = (0, second(i)), ((3 - second(i), 3),)
         else:
             ks, sent_ks = (0,), ((1,), (2,), (3,))
-        mine, sent = partial_products(where, rings[i], pieces, last, ks, sent_ks)
+        mine, sent = partial_products(
+            where, [own[i], *found[i][0], *found[i][1]], sizes[i], pieces, last, ks, sent_ks
+        )
         kept.append(mine)
         received.append([swap(x, k[0]) for x, k in zip(sent, sent_ks)])
         last[:] = [mine[0]]
@@ -257,22 +285,31 @@
             values, tiles = as_it_lies(shift(values, "row", i)), shift(tiles, "row", i)
         pieces.append(expand_tiles(values, tiles).transpose(1, 0, 2))
 
-    open_ring(0)
-    open_ring(1)
+    squares, columns = [], [jnp.zeros((1, columns_local), jnp.float32)]
+
+    def square(i):
+        squared, column = combine(kept[i][0], received[i], columns[-1], last)
+        squares.append(squared)
+        columns.append(column)
+        last[:] = [column]
+
+    open_slot(0)
+    open_slot(1)
     last += pieces
     for i in range(len(sizes)):
-        if i + 2 < len(sizes):
-            open_ring(i + 2)
-        sum_ring(i)
+        while len(own) < len(sizes) and len(own) <= i + reach[0]:
+            open_slot(len(own))
+        if i + reach[0] >= len(sizes) and i + reach[0] < len(sizes) - 1 + reach[0]:
+            open_slot(i + reach[0])
+        sum_chunk(i)
         if i > 0:
             send_on(i - 1)
-
-    squares = []
-    column = jnp.zeros((1, columns_local), jnp.float32)
-    for mine, blocks in zip(kept, received):
-        squared, column = combine(mine[0], blocks, column)
-        squares.append(squared)
-    column = lax.psum(column, "row")
+        if i > 1:
+            square(i - 2)
+    square(len(sizes) - 2)
+    square(len(sizes) - 1)
+
+    column = lax.psum(columns[-1], "row")
     out = normalise(column, squares, rows_local * n_rows)
     return out.reshape(rows_local, 1, columns_local)
 

time: 112 us -> 111 us (level)
  the two profiles are of different devices: /device:TPU:0 before, /device:TPU:9 now
where the time goes in v6:
time: 111 us; the launch traced here: 110 us
  waiting for transfers between devices  49.3 us (44%)
  starting transfers between devices  30.3 us (27%)
  Pallas kernels  19.5 us (18%)
  blocking collectives  4.79 us (4%)
  local copies, waits for them, and re-layouts  4.22 us (4%)
  other arithmetic  1.91 us (2%)
    ppermute x13, waiting for transfers between devices, shift(): return lax.ppermute(x, axis, [(i, (i + by) % n) for i in range(n)])  39.4 us
    ppermute x11, starting transfers between devices, swap(): return lax.ppermute(x, 'layer', [(i, i ^ bits) for i in range(4)])  19.3 us
    ppermute x13, starting transfers between devices, shift(): return lax.ppermute(x, axis, [(i, (i + by) % n) for i in range(n)])  10.9 us
    pallas_call x5, Pallas kernels, partial_products(): pl.pallas_call(functools.partial(partial_kernel, rows, firsts, len(pieces...  10.3 us
    ppermute x11, waiting for transfers between devices, swap(): return lax.ppermute(x, 'layer', [(i, i ^ bits) for i in range(4)])  9.84 us
    pallas_call x6, Pallas kernels, load(): pl.pallas_call(functools.partial(load_kernel, at, size, moving), out_shap...  6.74 us
    psum x1, blocking collectives, per_device(): column = lax.psum(columns[-1], 'row')  4.79 us
    unnamed x26, local copies, waits for them, and re-layouts  3.92 us
  transfers between devices with their start and end apart: 24, of which 9 were waited for; matrix products, arithmetic and copies ran while one was open for 2% of the time, Pallas kernels for 17%

profile of v6, /device:TPU:9, one launch (start us, length us, event | category | flops | bytes accessed | tf_op | source)
XLA Modules:
  0.0 110.3 jit_solution(4702203215069785217)
XLA Ops:
  3.8 1.3 %collective-permute-start = (bf16[512,256]{1,0:T(8,128)(2,1)S(1)}, bf16[512,256]{1,0:T(8,128)(2,1)S(1)}, u32[]{:S(2)}, u32[]{:S(2)}) collective-permute-start(bf16[512,256]{1,0:T(8,128)(2,1)S(1)} %get-tuple-element.41.refs_2_), channel_id=1, source_target_pairs={{0,1},{1,2},{2,3},{3,0},{4,5},{5,6},{6,7},{7,4},{8,9},{9,10},{10,1... | collective-permute-start | bytes 786440 | tf_op jit(solution)/shard_map/ppermute | solution.py:210
  5.8 6.0 %collective-permute-done.refs_0_.refs_1_ = bf16[512,256]{1,0:T(8,128)(2,1)S(1)} collective-permute-done((bf16[512,256]{1,0:T(8,128)(2,1)S(1)}, bf16[512,256]{1,0:T(8,128)(2,1)S(1)}, u32[]{:S(2)}, u32[]{:S(2)}) %collective-permute-start) | collective-permute-done | bytes 262176 | tf_op jit(solution)/shard_map/ppermute | solution.py:210
  11.8 1.4 %shard_map.47 = (bf16[1024,256]{1,0:T(8,128)(2,1)}, bf16[512,256]{1,0:T(8,128)(2,1)S(1)}) custom-call(s32[8]{0:T(128)S(1)} %bitcast.41, bf16[2048,256]{1,0:T(8,128)(2,1)S(1)} %bitcast.31, bf16[512,256]{1,0:T(8,128)(2,1)S(1)} %collective-permute-done.refs_0_.refs_1_, bf16[2048,256]{1,0:T(8,128)(2,1)S(1)} %bitcast.32, ...), custom_call_target="tpu_custom_call" | custom-call | flops 393216 | bytes 1572864 | tf_op jit(solution)/shard_map/pallas_call | solution.py:39
  13.2 1.4 %collective-permute-start.1 = (bf16[1024,256]{1,0:T(8,128)(2,1)}, bf16[1024,256]{1,0:T(8,128)(2,1)}, u32[]{:S(2)}, u32[]{:S(2)}) collective-permute-start(bf16[1024,256]{1,0:T(8,128)(2,1)} %get-tuple-element.42.refs_2_), channel_id=1, source_target_pairs={{0,1},{1,2},{2,3},{3,0},{4,5},{5,6},{6,7},{7,4},{8,9},{9,10},{10,1... | collective-permute-start | bytes 1572872 | tf_op jit(solution)/shard_map/ppermute | solution.py:210
  15.1 1.6 %fusion.refs_4_.refs_5_ = bf16[4,512,256]{2,1,0:T(8,128)(2,1)S(1)} fusion(bf16[512,4,256]{2,1,0:T(4,128)(2,1)} %collective-permute-done.2, bf16[512,4]{0,1:T(4,128)(2,1)S(1)} %bitcast.47), kind=kLoop, calls=%fused_computation.1 | loop fusion | flops 524288 | bytes 2101248 | tf_op jit(solution)/shard_map/transpose | solution.py:286
  16.7 12.1 %collective-permute-done.1.refs_0_.refs_2_.refs_1_ = bf16[1024,256]{1,0:T(8,128)(2,1)} collective-permute-done((bf16[1024,256]{1,0:T(8,128)(2,1)}, bf16[1024,256]{1,0:T(8,128)(2,1)}, u32[]{:S(2)}, u32[]{:S(2)}) %collective-permute-start.1) | collective-permute-done | bytes 524320 | tf_op jit(solution)/shard_map/ppermute | solution.py:210
  28.8 1.9 %shard_map.48 = (bf16[896,256]{1,0:T(8,128)(2,1)}, bf16[384,256]{1,0:T(8,128)(2,1)S(1)}) custom-call(s32[8]{0:T(128)S(1)} %bitcast.42, bf16[2048,256]{1,0:T(8,128)(2,1)S(1)} %bitcast.33, bf16[1024,256]{1,0:T(8,128)(2,1)} %collective-permute-done.1.refs_0_.refs_2_.refs_1_, bf16[2048,256]{1,0:T(8,128)(2,1)S(1)} %bitcast.34, ...), custom_call_target="tpu_custom_call" | custom-call | flops 327680 | bytes 1310720 | tf_op jit(solution)/shard_map/pallas_call | solution.py:39
  31.4 1.5 %collective-permute-start.8 = (bf16[512,256]{1,0:T(8,128)(2,1)S(1)}, bf16[512,256]{1,0:T(8,128)(2,1)S(1)}, u32[]{:S(2)}, u32[]{:S(2)}) collective-permute-start(bf16[512,256]{1,0:T(8,128)(2,1)S(1)} %get-tuple-element.49.refs_0_), channel_id=1, source_target_pairs={{0,3},{1,0},{2,1},{3,2},{4,7},{5,4},{6,5},{7,6},{8,11},{9,8},{10,9... | collective-permute-start | bytes 786440 | tf_op jit(solution)/shard_map/ppermute | solution.py:210
  33.9 2.6 %shard_map.49 = (f32[512,256]{1,0:T(8,128)S(1)}, f32[512,256]{1,0:T(8,128)S(1)}, s16[1056,256]{1,0:T(8,128)(2,1)S(1)}) custom-call(s32[9]{0:T(128)S(1)} %stack.39.where, bf16[512,256]{1,0:T(8,128)(2,1)} %get-tuple-element.44.refs_0_, bf16[512,256]{1,0:T(8,128)(2,1)S(1)} %copy-done.5, bf16[1024,256]{1,0:T(8,128)(2,1)} %collective-permute-done.1.refs_0_.refs_2_.refs_1_, ...), custom_call_target="tpu_custom_call" | custom-call | flops 1073741824 | bytes 3932160 | tf_op jit(solution)/shard_map/pallas_call | solution.py:110
  37.8 4.5 %collective-permute-done.4.refs_0_.refs_2_.refs_1_ = bf16[896,256]{1,0:T(8,128)(2,1)} collective-permute-done((bf16[896,256]{1,0:T(8,128)(2,1)}, bf16[896,256]{1,0:T(8,128)(2,1)}, u32[]{:S(2)}, u32[]{:S(2)}) %collective-permute-start.4) | collective-permute-done | bytes 458784 | tf_op jit(solution)/shard_map/ppermute | solution.py:210
  43.4 9.5 %collective-permute-done.8.refs_3_ = bf16[512,256]{1,0:T(8,128)(2,1)S(1)} collective-permute-done((bf16[512,256]{1,0:T(8,128)(2,1)S(1)}, bf16[512,256]{1,0:T(8,128)(2,1)S(1)}, u32[]{:S(2)}, u32[]{:S(2)}) %collective-permute-start.8) | collective-permute-done | bytes 262176 | tf_op jit(solution)/shard_map/ppermute | solution.py:210
  52.9 2.6 %shard_map.51 = (f32[512,256]{1,0:T(8,128)S(1)}, f32[512,256]{1,0:T(8,128)S(1)}, s16[1056,256]{1,0:T(8,128)(2,1)S(1)}) custom-call(s32[9]{0:T(128)S(1)} %stack.39.where, bf16[512,256]{1,0:T(8,128)(2,1)S(1)} %get-tuple-element.49.refs_0_, bf16[1024,256]{1,0:T(8,128)(2,1)} %collective-permute-done.1.refs_0_.refs_2_.refs_1_, ...), custom_call_target="tpu_custom_call" | custom-call | flops 1073741824 | bytes 3932160 | tf_op jit(solution)/shard_map/pallas_call | solution.py:110
  59.7 2.6 %collective-permute-start.17 = (bf16[384,256]{1,0:T(8,128)(2,1)S(1)}, bf16[384,256]{1,0:T(8,128)(2,1)S(1)}, u32[]{:S(2)}, u32[]{:S(2)}) collective-permute-start(bf16[384,256]{1,0:T(8,128)(2,1)S(1)} %get-tuple-element.60.refs_0_), channel_id=1, source_target_pairs={{0,3},{1,0},{2,1},{3,2},{4,7},{5,4},{6,5},{7,6},{8,11},{9,8},{10,9... | collective-permute-start | bytes 589832 | tf_op jit(solution)/shard_map/ppermute | solution.py:210
  62.3 7.3 %collective-permute-done.12.refs_3_ = bf16[384,256]{1,0:T(8,128)(2,1)S(1)} collective-permute-done((bf16[384,256]{1,0:T(8,128)(2,1)S(1)}, bf16[384,256]{1,0:T(8,128)(2,1)S(1)}, u32[]{:S(2)}, u32[]{:S(2)}) %collective-permute-start.12) | collective-permute-done | bytes 196640 | tf_op jit(solution)/shard_map/ppermute | solution.py:210
  69.7 2.1 %shard_map.54 = (f32[384,256]{1,0:T(8,128)S(1)}, f32[384,256]{1,0:T(8,128)S(1)}, s16[800,256]{1,0:T(8,128)(2,1)S(1)}) custom-call(s32[9]{0:T(128)S(1)} %stack.39.where, bf16[384,256]{1,0:T(8,128)(2,1)S(1)} %copy-done.7, bf16[896,256]{1,0:T(8,128)(2,1)} %collective-permute-done.4.refs_0_.refs_2_.refs_1_, ...), custom_call_target="tpu_custom_call" | custom-call | flops 805306368 | bytes 3473408 | tf_op jit(solution)/shard_map/pallas_call | solution.py:110
  71.8 3.0 %collective-permute-start.16 = (s16[800,256]{1,0:T(8,128)(2,1)S(1)}, s16[800,256]{1,0:T(8,128)(2,1)S(1)}, u32[]{:S(2)}, u32[]{:S(2)}) collective-permute-start(s16[800,256]{1,0:T(8,128)(2,1)S(1)} %get-tuple-element.59), channel_id=1, source_target_pairs={{0,8},{8,0},{16,24},{24,16},{1,9},{9,1},{17,25},{25,17},{2,10},{10... | collective-permute-start | bytes 1228808 | tf_op jit(solution)/shard_map/ppermute | solution.py:218
  76.0 1.6 %shard_map.58 = (f32[384,256]{1,0:T(8,128)S(1)}, f32[384,256]{1,0:T(8,128)S(1)}, s16[800,256]{1,0:T(8,128)(2,1)S(1)}) custom-call(s32[9]{0:T(128)S(1)} %stack.39.where, bf16[384,256]{1,0:T(8,128)(2,1)S(1)} %get-tuple-element.60.refs_0_, bf16[768,256]{1,0:T(8,128)(2,1)S(1)} %collective-permute-done.6.refs_0_.refs_2_.refs_1_, ...), custom_call_target="tpu_custom_call" | custom-call | flops 805306368 | bytes 3473408 | tf_op jit(solution)/shard_map/pallas_call | solution.py:110
  77.6 2.1 %collective-permute-start.21 = (s16[800,256]{1,0:T(8,128)(2,1)S(1)}, s16[800,256]{1,0:T(8,128)(2,1)S(1)}, u32[]{:S(2)}, u32[]{:S(2)}) collective-permute-start(s16[800,256]{1,0:T(8,128)(2,1)S(1)} %get-tuple-element.67), channel_id=1, source_target_pairs={{0,16},{8,24},{16,0},{24,8},{1,17},{9,25},{17,1},{25,9},{2,18},{10... | collective-permute-start | bytes 1228808 | tf_op jit(solution)/shard_map/ppermute | solution.py:218
  82.1 4.2 %collective-permute-start.23 = (s16[400,256]{1,0:T(8,128)(2,1)S(1)}, s16[400,256]{1,0:T(8,128)(2,1)S(1)}, u32[]{:S(2)}, u32[]{:S(2)}) collective-permute-start(s16[400,256]{1,0:T(8,128)(2,1)S(1)} %shard_map.59.refs_3_), channel_id=1, source_target_pairs={{0,16},{8,24},{16,0},{24,8},{1,17},{9,25},{17,1},{25,9},{2,18},{10... | collective-permute-start | bytes 614408 | tf_op jit(solution)/shard_map/ppermute | solution.py:218
  86.3 1.9 %collective-permute-done.15.refs_1_ = s16[528,256]{1,0:T(8,128)(2,1)S(1)} collective-permute-done((s16[528,256]{1,0:T(8,128)(2,1)S(1)}, s16[528,256]{1,0:T(8,128)(2,1)S(1)}, u32[]{:S(2)}, u32[]{:S(2)}) %collective-permute-start.15) | collective-permute-done | bytes 270368 | tf_op jit(solution)/shard_map/ppermute | solution.py:218
  88.4 1.4 %shard_map.61 = (f32[256,256]{1,0:T(8,128)S(1)}, s16[272,256]{1,0:T(8,128)(2,1)S(1)}, s16[272,256]{1,0:T(8,128)(2,1)S(1)}, s16[272,256]{1,0:T(8,128)(2,1)S(1)}) custom-call(s32[9]{0:T(128)S(1)} %stack.39.where, bf16[256,256]{1,0:T(8,128)(2,1)S(1)} %get-tuple-element.51.refs_0_, bf16[640,256]{1,0:T(8,128)(2,1)S(1)} %collective-permute-done.9.refs_0_.refs_2_.refs_1_, ...), custom_call_target="tpu_custom_call" | custom-call | flops 536870912 | bytes 3014656 | tf_op jit(solution)/shard_map/pallas_call | solution.py:110
  91.5 3.7 %collective-permute-start.19 = (s16[272,256]{1,0:T(8,128)(2,1)S(1)}, s16[272,256]{1,0:T(8,128)(2,1)S(1)}, u32[]{:S(2)}, u32[]{:S(2)}) collective-permute-start(s16[272,256]{1,0:T(8,128)(2,1)S(1)} %get-tuple-element.65), channel_id=1, source_target_pairs={{0,16},{8,24},{16,0},{24,8},{1,17},{9,25},{17,1},{25,9},{2,18},{10... | collective-permute-start | bytes 417800 | tf_op jit(solution)/shard_map/ppermute | solution.py:218
  97.9 6.3 %collective-permute-done.20.refs_2_ = s16[272,256]{1,0:T(8,128)(2,1)S(1)} collective-permute-done((s16[272,256]{1,0:T(8,128)(2,1)S(1)}, s16[272,256]{1,0:T(8,128)(2,1)S(1)}, u32[]{:S(2)}, u32[]{:S(2)}) %collective-permute-start.20) | collective-permute-done | bytes 139296 | tf_op jit(solution)/shard_map/ppermute | solution.py:218
  104.4 4.8 %psum.7.column_ref = f32[1,256]{1,0:T(1,128)S(1)} all-reduce(f32[1,256]{1,0:T(1,128)S(1)} %get-tuple-element.71), channel_id=1, replica_groups=mesh['layer'=4,'row'=2,'col'=4] {'row'}, use_global_device_ids=true, to_apply=%region_0.1 | all-reduce | flops 256 | bytes 2048 | tf_op jit(solution)/shard_map/psum | solution.py:312
  (80 shorter events, 22.7 us)
Async XLA Ops:
  0.0 15.1 %collective-permute-start.2 = (bf16[512,4,256]{2,1,0:T(4,128)(2,1)}, bf16[512,4,256]{2,1,0:T(4,128)(2,1)}, u32[]{:S(2)}, u32[]{:S(2)}) collective-permute-start(bf16[512,4,256]{2,1,0:T(4,128)(2,1)} %param.6), channel_id=1, source_target_pairs={{0,4},{4,0},{1,5},{5,1},{2,6},{6,2},{3,7},{7,3},{8,12},{12,8},{9,1... | collective-permute-start | bytes 3145736 | tf_op jit(solution)/shard_map/ppermute | solution.py:210
  3.8 7.9 %collective-permute-start = (bf16[512,256]{1,0:T(8,128)(2,1)S(1)}, bf16[512,256]{1,0:T(8,128)(2,1)S(1)}, u32[]{:S(2)}, u32[]{:S(2)}) collective-permute-start(bf16[512,256]{1,0:T(8,128)(2,1)S(1)} %get-tuple-element.41.refs_2_), channel_id=1, source_target_pairs={{0,1},{1,2},{2,3},{3,0},{4,5},{5,6},{6,7},{7,4},{8,9},{9,10},{10,1... | collective-permute-start | bytes 786440 | tf_op jit(solution)/shard_map/ppermute | solution.py:210
  5.1 9.8 %collective-permute-start.3 = (s32[2,4,1]{1,2,0:T(1,128)S(1)}, s32[2,4,1]{1,2,0:T(1,128)S(1)}, u32[]{:S(2)}, u32[]{:S(2)}) collective-permute-start(s32[2,4,1]{1,2,0:T(1,128)S(1)} %copy-done.10), channel_id=1, source_target_pairs={{0,4},{4,0},{1,5},{5,1},{2,6},{6,2},{3,7},{7,3},{8,12},{12,8},{9,1... | collective-permute-start | bytes 104 | tf_op jit(solution)/shard_map/ppermute | solution.py:210
  5.4 27.5 %collective-permute-start.5 = (bf16[512,256]{1,0:T(8,128)(2,1)}, bf16[512,256]{1,0:T(8,128)(2,1)}, u32[]{:S(2)}, u32[]{:S(2)}) collective-permute-start(bf16[512,256]{1,0:T(8,128)(2,1)} %get-tuple-element.44.refs_0_), channel_id=1, source_target_pairs={{0,3},{1,0},{2,1},{3,2},{4,7},{5,4},{6,5},{7,6},{8,11},{9,8},{10,9... | collective-permute-start | bytes 786440 | tf_op jit(solution)/shard_map/ppermute | solution.py:210
  13.2 15.6 %collective-permute-start.1 = (bf16[1024,256]{1,0:T(8,128)(2,1)}, bf16[1024,256]{1,0:T(8,128)(2,1)}, u32[]{:S(2)}, u32[]{:S(2)}) collective-permute-start(bf16[1024,256]{1,0:T(8,128)(2,1)} %get-tuple-element.42.refs_2_), channel_id=1, source_target_pairs={{0,1},{1,2},{2,3},{3,0},{4,5},{5,6},{6,7},{7,4},{8,9},{9,10},{10,1... | collective-permute-start | bytes 1572872 | tf_op jit(solution)/shard_map/ppermute | solution.py:210
  31.3 11.0 %collective-permute-start.4 = (bf16[896,256]{1,0:T(8,128)(2,1)}, bf16[896,256]{1,0:T(8,128)(2,1)}, u32[]{:S(2)}, u32[]{:S(2)}) collective-permute-start(bf16[896,256]{1,0:T(8,128)(2,1)} %get-tuple-element.43.refs_6_), channel_id=1, source_target_pairs={{0,1},{1,2},{2,3},{3,0},{4,5},{5,6},{6,7},{7,4},{8,9},{9,10},{10,1... | collective-permute-start | bytes 1376264 | tf_op jit(solution)/shard_map/ppermute | solution.py:210
  31.4 21.5 %collective-permute-start.8 = (bf16[512,256]{1,0:T(8,128)(2,1)S(1)}, bf16[512,256]{1,0:T(8,128)(2,1)S(1)}, u32[]{:S(2)}, u32[]{:S(2)}) collective-permute-start(bf16[512,256]{1,0:T(8,128)(2,1)S(1)} %get-tuple-element.49.refs_0_), channel_id=1, source_target_pairs={{0,3},{1,0},{2,1},{3,2},{4,7},{5,4},{6,5},{7,6},{8,11},{9,8},{10,9... | collective-permute-start | bytes 786440 | tf_op jit(solution)/shard_map/ppermute | solution.py:210
  36.5 20.2 %collective-permute-start.7 = (s16[1056,256]{1,0:T(8,128)(2,1)S(1)}, s16[1056,256]{1,0:T(8,128)(2,1)S(1)}, u32[]{:S(2)}, u32[]{:S(2)}) collective-permute-start(s16[1056,256]{1,0:T(8,128)(2,1)S(1)} %get-tuple-element.48), channel_id=1, source_target_pairs={{0,8},{8,0},{16,24},{24,16},{1,9},{9,1},{17,25},{25,17},{2,10},{10... | collective-permute-start | bytes 1622024 | tf_op jit(solution)/shard_map/ppermute | solution.py:218
  43.4 13.5 %collective-permute-start.6 = (bf16[768,256]{1,0:T(8,128)(2,1)S(1)}, bf16[768,256]{1,0:T(8,128)(2,1)S(1)}, u32[]{:S(2)}, u32[]{:S(2)}) collective-permute-start(bf16[768,256]{1,0:T(8,128)(2,1)S(1)} %get-tuple-element.46.refs_6_), channel_id=1, source_target_pairs={{0,1},{1,2},{2,3},{3,0},{4,5},{5,6},{6,7},{7,4},{8,9},{9,10},{10,1... | collective-permute-start | bytes 1179656 | tf_op jit(solution)/shard_map/ppermute | solution.py:210
  55.5 19.3 %collective-permute-start.11 = (s16[1056,256]{1,0:T(8,128)(2,1)S(1)}, s16[1056,256]{1,0:T(8,128)(2,1)S(1)}, u32[]{:S(2)}, u32[]{:S(2)}) collective-permute-start(s16[1056,256]{1,0:T(8,128)(2,1)S(1)} %get-tuple-element.54), channel_id=1, source_target_pairs={{0,16},{8,24},{16,0},{24,8},{1,17},{9,25},{17,1},{25,9},{2,18},{10... | collective-permute-start | bytes 1622024 | tf_op jit(solution)/shard_map/ppermute | solution.py:218
  57.5 17.7 %collective-permute-start.9 = (bf16[640,256]{1,0:T(8,128)(2,1)S(1)}, bf16[640,256]{1,0:T(8,128)(2,1)S(1)}, u32[]{:S(2)}, u32[]{:S(2)}) collective-permute-start(bf16[640,256]{1,0:T(8,128)(2,1)S(1)} %get-tuple-element.52.refs_6_), channel_id=1, source_target_pairs={{0,1},{1,2},{2,3},{3,0},{4,5},{5,6},{6,7},{7,4},{8,9},{9,10},{10,1... | collective-permute-start | bytes 983048 | tf_op jit(solution)/shard_map/ppermute | solution.py:210
  58.1 11.6 %collective-permute-start.12 = (bf16[384,256]{1,0:T(8,128)(2,1)S(1)}, bf16[384,256]{1,0:T(8,128)(2,1)S(1)}, u32[]{:S(2)}, u32[]{:S(2)}) collective-permute-start(bf16[384,256]{1,0:T(8,128)(2,1)S(1)} %copy-done.7), channel_id=1, source_target_pairs={{0,3},{1,0},{2,1},{3,2},{4,7},{5,4},{6,5},{7,6},{8,11},{9,8},{10,9... | collective-permute-start | bytes 589832 | tf_op jit(solution)/shard_map/ppermute | solution.py:210
  59.0 16.0 %collective-permute-start.10 = (s16[528,256]{1,0:T(8,128)(2,1)S(1)}, s16[528,256]{1,0:T(8,128)(2,1)S(1)}, u32[]{:S(2)}, u32[]{:S(2)}) collective-permute-start(s16[528,256]{1,0:T(8,128)(2,1)S(1)} %shard_map.52.refs_2_), channel_id=1, source_target_pairs={{0,16},{8,24},{16,0},{24,8},{1,17},{9,25},{17,1},{25,9},{2,18},{10... | collective-permute-start | bytes 811016 | tf_op jit(solution)/shard_map/ppermute | solution.py:218
  59.7 16.2 %collective-permute-start.17 = (bf16[384,256]{1,0:T(8,128)(2,1)S(1)}, bf16[384,256]{1,0:T(8,128)(2,1)S(1)}, u32[]{:S(2)}, u32[]{:S(2)}) collective-permute-start(bf16[384,256]{1,0:T(8,128)(2,1)S(1)} %get-tuple-element.60.refs_0_), channel_id=1, source_target_pairs={{0,3},{1,0},{2,1},{3,2},{4,7},{5,4},{6,5},{7,6},{8,11},{9,8},{10,9... | collective-permute-start | bytes 589832 | tf_op jit(solution)/shard_map/ppermute | solution.py:210
  71.8 10.2 %collective-permute-start.16 = (s16[800,256]{1,0:T(8,128)(2,1)S(1)}, s16[800,256]{1,0:T(8,128)(2,1)S(1)}, u32[]{:S(2)}, u32[]{:S(2)}) collective-permute-start(s16[800,256]{1,0:T(8,128)(2,1)S(1)} %get-tuple-element.59), channel_id=1, source_target_pairs={{0,8},{8,0},{16,24},{24,16},{1,9},{9,1},{17,25},{25,17},{2,10},{10... | collective-permute-start | bytes 1228808 | tf_op jit(solution)/shard_map/ppermute | solution.py:218
  77.6 12.2 %collective-permute-start.21 = (s16[800,256]{1,0:T(8,128)(2,1)S(1)}, s16[800,256]{1,0:T(8,128)(2,1)S(1)}, u32[]{:S(2)}, u32[]{:S(2)}) collective-permute-start(s16[800,256]{1,0:T(8,128)(2,1)S(1)} %get-tuple-element.67), channel_id=1, source_target_pairs={{0,16},{8,24},{16,0},{24,8},{1,17},{9,25},{17,1},{25,9},{2,18},{10... | collective-permute-start | bytes 1228808 | tf_op jit(solution)/shard_map/ppermute | solution.py:218
  79.7 8.6 %collective-permute-start.15 = (s16[528,256]{1,0:T(8,128)(2,1)S(1)}, s16[528,256]{1,0:T(8,128)(2,1)S(1)}, u32[]{:S(2)}, u32[]{:S(2)}) collective-permute-start(s16[528,256]{1,0:T(8,128)(2,1)S(1)} %shard_map.55.refs_3_), channel_id=1, source_target_pairs={{0,8},{8,0},{16,24},{24,16},{1,9},{9,1},{17,25},{25,17},{2,10},{10... | collective-permute-start | bytes 811016 | tf_op jit(solution)/shard_map/ppermute | solution.py:218
  80.5 7.9 %collective-permute-start.14 = (bf16[256,256]{1,0:T(8,128)(2,1)S(1)}, bf16[256,256]{1,0:T(8,128)(2,1)S(1)}, u32[]{:S(2)}, u32[]{:S(2)}) collective-permute-start(bf16[256,256]{1,0:T(8,128)(2,1)S(1)} %get-tuple-element.51.refs_0_), channel_id=1, source_target_pairs={{0,3},{1,0},{2,1},{3,2},{4,7},{5,4},{6,5},{7,6},{8,11},{9,8},{10,9... | collective-permute-start | bytes 393224 | tf_op jit(solution)/shard_map/ppermute | solution.py:210
  80.7 7.7 %collective-permute-start.13 = (bf16[256,256]{1,0:T(8,128)(2,1)S(1)}, bf16[256,256]{1,0:T(8,128)(2,1)S(1)}, u32[]{:S(2)}, u32[]{:S(2)}) collective-permute-start(bf16[256,256]{1,0:T(8,128)(2,1)S(1)} %shard_map.57.refs_6_), channel_id=1, source_target_pairs={{0,1},{1,2},{2,3},{3,0},{4,5},{5,6},{6,7},{7,4},{8,9},{9,10},{10,1... | collective-permute-start | bytes 393224 | tf_op jit(solution)/shard_map/ppermute | solution.py:210
  82.1 13.9 %collective-permute-start.23 = (s16[400,256]{1,0:T(8,128)(2,1)S(1)}, s16[400,256]{1,0:T(8,128)(2,1)S(1)}, u32[]{:S(2)}, u32[]{:S(2)}) collective-permute-start(s16[400,256]{1,0:T(8,128)(2,1)S(1)} %shard_map.59.refs_3_), channel_id=1, source_target_pairs={{0,16},{8,24},{16,0},{24,8},{1,17},{9,25},{17,1},{25,9},{2,18},{10... | collective-permute-start | bytes 614408 | tf_op jit(solution)/shard_map/ppermute | solution.py:218
  90.0 6.2 %collective-permute-start.22 = (s16[400,256]{1,0:T(8,128)(2,1)S(1)}, s16[400,256]{1,0:T(8,128)(2,1)S(1)}, u32[]{:S(2)}, u32[]{:S(2)}) collective-permute-start(s16[400,256]{1,0:T(8,128)(2,1)S(1)} %shard_map.62.refs_3_), channel_id=1, source_target_pairs={{0,8},{8,0},{16,24},{24,16},{1,9},{9,1},{17,25},{25,17},{2,10},{10... | collective-permute-start | bytes 614408 | tf_op jit(solution)/shard_map/ppermute | solution.py:218
  90.9 5.9 %collective-permute-start.18 = (s16[272,256]{1,0:T(8,128)(2,1)S(1)}, s16[272,256]{1,0:T(8,128)(2,1)S(1)}, u32[]{:S(2)}, u32[]{:S(2)}) collective-permute-start(s16[272,256]{1,0:T(8,128)(2,1)S(1)} %get-tuple-element.64), channel_id=1, source_target_pairs={{0,8},{8,0},{16,24},{24,16},{1,9},{9,1},{17,25},{25,17},{2,10},{10... | collective-permute-start | bytes 417800 | tf_op jit(solution)/shard_map/ppermute | solution.py:218
  91.5 6.4 %collective-permute-start.19 = (s16[272,256]{1,0:T(8,128)(2,1)S(1)}, s16[272,256]{1,0:T(8,128)(2,1)S(1)}, u32[]{:S(2)}, u32[]{:S(2)}) collective-permute-start(s16[272,256]{1,0:T(8,128)(2,1)S(1)} %get-tuple-element.65), channel_id=1, source_target_pairs={{0,16},{8,24},{16,0},{24,8},{1,17},{9,25},{17,1},{25,9},{2,18},{10... | collective-permute-start | bytes 417800 | tf_op jit(solution)/shard_map/ppermute | solution.py:218
  95.2 9.0 %collective-permute-start.20 = (s16[272,256]{1,0:T(8,128)(2,1)S(1)}, s16[272,256]{1,0:T(8,128)(2,1)S(1)}, u32[]{:S(2)}, u32[]{:S(2)}) collective-permute-start(s16[272,256]{1,0:T(8,128)(2,1)S(1)} %get-tuple-element.66), channel_id=1, source_target_pairs={{0,24},{8,16},{16,8},{24,0},{1,25},{9,17},{17,9},{25,1},{2,26},{10... | collective-permute-start | bytes 417800 | tf_op jit(solution)/shard_map/ppermute | solution.py:218
  (11 other events, 39.1 us)

commit v7 on v6

--- a/solution.py
+++ b/solution.py
@@ -10,46 +10,42 @@
 from jax.sharding import PartitionSpec as P
 
 TILE = 256
-SIXTEENTHS = (4, 4, 3, 3, 2)
+SIXTEENTHS = (3, 4, 4, 3, 2)
 SCALE_ROWS = 16
 CODE = 64.0
 TOP = 32767.0
 LEAST = 2.0**-100
 VMEM = pl.BlockSpec(memory_space=pltpu.VMEM)
-PARAMS = pltpu.CompilerParams(vmem_limit_bytes=40 * 1024 * 1024)
-
-
-def load_kernel(at, size, moving, pattern_ref, left_ref, *refs):
-    outs = refs[-len(moving) :]
-    for arrived, out, parts in zip(refs, outs, moving):
-        done = 0
-        for first, rows in parts:
-            out[done : done + rows, :] = arrived[first : first + rows, :]
-            done += rows
-        step = math.gcd(TILE, math.gcd(at, size))
-        for i in range(0, size, step):
-            entry = pattern_ref[(at + i) // TILE].astype(jnp.float32).astype(out.dtype)
-            block = left_ref[at + i : at + i + step, :] * entry
-            out[done + i : done + i + step, :] = block
-
-
-def load(left, pattern, at, size, arrived, moving, after):
+PARAMS = pltpu.CompilerParams(vmem_limit_bytes=16 * 1024 * 1024)
+
+
+def load_kernel(at, size, parts, pattern_ref, left_ref, arrived, *refs):
+    out = refs[-1]
+    done = 0
+    for first, rows in parts:
+        out[done : done + rows, :] = arrived[first : first + rows, :]
+        done += rows
+    step = math.gcd(TILE, math.gcd(at, size))
+    for i in range(0, size, step):
+        entry = pattern_ref[(at + i) // TILE].astype(jnp.float32).astype(out.dtype)
+        out[done + i : done + i + step, :] = left_ref[at + i : at + i + step, :] * entry
+
+
+def load(left, pattern, at, size, arrived, parts, after):
     columns = left.shape[1]
-    totals = [size + sum(rows for _, rows in parts) for parts in moving]
+    total = size + sum(rows for _, rows in parts)
     return pl.pallas_call(
-        functools.partial(load_kernel, at, size, moving),
-        out_shape=[jax.ShapeDtypeStruct((total, columns), left.dtype) for total in totals],
+        functools.partial(load_kernel, at, size, parts),
+        out_shape=jax.ShapeDtypeStruct((total, columns), left.dtype),
         in_specs=[pl.BlockSpec(memory_space=pltpu.SMEM), VMEM]
-        + [VMEM if parts else pl.BlockSpec(memory_space=pl.ANY) for parts in moving]
+        + [VMEM if parts else pl.BlockSpec(memory_space=pl.ANY)]
         + [pl.BlockSpec(memory_space=pl.ANY)] * len(after),
-        out_specs=[VMEM] * len(moving),
-        compiler_params=PARAMS,
-        cost_estimate=pl.CostEstimate(
-            flops=sum(totals) * columns,
-            bytes_accessed=4 * sum(totals) * columns,
-            transcendentals=0,
-        ),
-    )(pattern, left, *arrived, *after)
+        out_specs=VMEM,
+        compiler_params=PARAMS,
+        cost_estimate=pl.CostEstimate(
+            flops=total * columns, bytes_accessed=4 * total * columns, transcendentals=0
+        ),
+    )(pattern, left, arrived, *after)
 
 
 def put_fixed(ref, at, total):
@@ -68,9 +64,10 @@
     return ref[at : at + rows, :].astype(jnp.int32).astype(jnp.float32) * unit
 
 
-def partial_kernel(rows, firsts, n_pieces, kept, sent, where, *refs):
-    n_sources = len(firsts)
-    lefts, pieces = refs[:n_sources], refs[n_sources : n_sources + n_pieces]
+def partial_kernel(sources, n_pieces, kept, sent, where, *refs):
+    n_lefts = sum(len(parts) for parts in sources)
+    pieces = refs[n_lefts : n_lefts + n_pieces]
+    rows = sum(part[2] for part in sources[0])
     outs = refs[-len(kept) - len(sent) :]
     columns = pieces[0].shape[2]
 
@@ -84,12 +81,15 @@
 
     def product(k):
         total = jnp.zeros((rows, columns), jnp.float32)
-        for source in range(n_sources):
-            total += jnp.dot(
-                lefts[source][firsts[source] : firsts[source] + rows, :],
-                right(source, where[0] ^ k),
-                preferred_element_type=jnp.float32,
-            )
+        for source, parts in enumerate(sources):
+            tile = right(source, where[0] ^ k)
+            terms = [
+                jnp.dot(
+                    refs[i][first : first + count, :], tile, preferred_element_type=jnp.float32
+                )
+                for i, first, count in parts
+            ]
+            total += terms[0] if len(terms) == 1 else jnp.concatenate(terms, axis=0)
         return total
 
     for out, ks in zip(outs[len(kept) :], sent):
@@ -99,16 +99,19 @@
         out[...] = product(k)
 
 
-def partial_products(where, lefts, rows, pieces, after, kept, sent):
+def partial_products(where, sources, pieces, after, kept, sent):
     columns = pieces[0].shape[2]
-    firsts = tuple(first for _, first in lefts)
+    rows = sum(part[2] for part in sources[0])
+    lefts = [array for parts in sources for array, _, _ in parts]
+    numbers = iter(range(len(lefts)))
+    shapes = tuple(tuple((next(numbers), *part[1:]) for part in parts) for parts in sources)
     n_products = len(kept) + sum(len(ks) for ks in sent)
     outs = [jax.ShapeDtypeStruct((rows, columns), jnp.float32)] * len(kept)
     outs += [
         jax.ShapeDtypeStruct((len(ks) * (rows + SCALE_ROWS), columns), jnp.int16) for ks in sent
     ]
     out = pl.pallas_call(
-        functools.partial(partial_kernel, rows, firsts, len(pieces), kept, sent),
+        functools.partial(partial_kernel, shapes, len(pieces), kept, sent),
         out_shape=outs,
         in_specs=[pl.BlockSpec(memory_space=pltpu.SMEM)]
         + [VMEM] * (len(lefts) + len(pieces))
@@ -116,11 +119,11 @@
         out_specs=[VMEM] * len(outs),
         compiler_params=PARAMS,
         cost_estimate=pl.CostEstimate(
-            flops=2 * rows * len(lefts) * TILE * columns * n_products,
+            flops=2 * rows * len(sources) * TILE * columns * n_products,
             bytes_accessed=len(pieces) * pieces[0].size * 2 + rows * columns * 14,
             transcendentals=0,
         ),
-    )(where, *(block for block, _ in lefts), *pieces, *after)
+    )(where, *lefts, *pieces, *after)
     return out[: len(kept)], out[len(kept) :]
 
 
@@ -227,9 +230,10 @@
 
     left = left_values.reshape(rows_local, columns_local)
     pattern = left_pattern.reshape(-1)
-    reach = (n_cols // 2, n_cols - 1 - n_cols // 2)
+    reach = n_cols // 2
+    away = list(range(1, reach))
     where = [layer]
-    for source in [0] + [-1 - i for i in range(reach[0])] + [1 + i for i in range(reach[1])]:
+    for source in [0] + [-i for i in away] + away + [reach]:
         inner = (col + source + n_cols) % n_cols * columns_local
         where += [(row - inner // inner_piece + n_rows) % n_rows, inner % inner_piece]
     where = jnp.stack(where).astype(jnp.int32)
@@ -241,31 +245,38 @@
 
     def open_slot(slot):
         at, size = (starts[slot], sizes[slot]) if slot < len(sizes) else (0, 0)
-        going = [d for d in (0, 1) if slot < len(sizes) - 1 + reach[d]]
-        arrived, moving, riders = [], [], []
-        for d in going:
-            on = [c for c in range(min(slot, len(sizes))) if len(found[c][d]) < reach[d]]
-            arrived.append(found[on[0]][d][-1][0] if on else left)
-            moving.append(tuple((found[c][d][-1][1], sizes[c]) for c in on))
-            riders.append(on + ([slot] if size else []))
-        blocks = load(left, pattern, at, size, arrived, moving, last)
-        last[:] = [blocks[0]]
-        for d, block, chunks in zip(going, blocks, riders):
-            got, first = shift(block, "col", 1 - 2 * d), 0
-            for c in chunks:
-                found[c][d].append((got, first))
-                if c == slot and d == going[-1]:
-                    own.append((block, first))
-                first += sizes[c]
+        for d in (0, 1):
+            riders = [c for c in range(min(slot, len(sizes))) if len(found[c][d]) < reach]
+            parts = []
+            for c in riders:
+                _, first, rows = found[c][d][-1]
+                if len(found[c][d]) == reach - 1:
+                    first, rows = first + d * (rows // 2), rows // 2
+                parts.append((first, rows))
+            arrived = found[riders[0]][d][-1][0] if riders else left
+            block = load(left, pattern, at, size, arrived, tuple(parts), last)
+            last[:] = [block]
+            got = shift(block, "col", 1 - 2 * d)
+            first = 0
+            for c, (_, rows) in zip(riders, parts):
+                found[c][d].append((got, first, rows))
+                first += rows
+            if size:
+                found[slot][d].append((got, first, size))
+                if d == 0:
+                    own.append((block, first, size))
+
+    def sources(i):
+        (*below, last_below), (*above, last_above) = found[i]
+        near = [own[i]] + below + above
+        return [[part] for part in near] + [[last_below, last_above]]
 
     def sum_chunk(i):
         if i + 1 < len(sizes):
             ks, sent_ks = (0, second(i)), ((3 - second(i), 3),)
         else:
             ks, sent_ks = (0,), ((1,), (2,), (3,))
-        mine, sent = partial_products(
-            where, [own[i], *found[i][0], *found[i][1]], sizes[i], pieces, last, ks, sent_ks
-        )
+        mine, sent = partial_products(where, sources(i), pieces, last, ks, sent_ks)
         kept.append(mine)
         received.append([swap(x, k[0]) for x, k in zip(sent, sent_ks)])
         last[:] = [mine[0]]
@@ -293,14 +304,13 @@
         columns.append(column)
         last[:] = [column]
 
-    open_slot(0)
-    open_slot(1)
-    last += pieces
+    opened = 0
     for i in range(len(sizes)):
-        while len(own) < len(sizes) and len(own) <= i + reach[0]:
-            open_slot(len(own))
-        if i + reach[0] >= len(sizes) and i + reach[0] < len(sizes) - 1 + reach[0]:
-            open_slot(i + reach[0])
+        while opened < min(len(sizes) + reach - 1, i + reach + 1):
+            open_slot(opened)
+            opened += 1
+            if opened == 2:
+                last += pieces
         sum_chunk(i)
         if i > 0:
             send_on(i - 1)

time: 111 us -> 111 us (level)
  the two profiles are of different devices: /device:TPU:9 before, /device:TPU:0 now
where the time goes in v7:
time: 111 us; the launch traced here: 110 us
  starting transfers between devices  38.7 us (35%)
  waiting for transfers between devices  37 us (33%)
  Pallas kernels  20.8 us (19%)
  local copies, waits for them, and re-layouts  7.48 us (7%)
  other arithmetic  3.22 us (3%)
  blocking collectives  2.47 us (2%)
    ppermute x14, waiting for transfers between devices, shift(): return lax.ppermute(x, axis, [(i, (i + by) % n) for i in range(n)])  27.2 us
    ppermute x14, starting transfers between devices, shift(): return lax.ppermute(x, axis, [(i, (i + by) % n) for i in range(n)])  23.5 us
    ppermute x11, starting transfers between devices, swap(): return lax.ppermute(x, 'layer', [(i, i ^ bits) for i in range(4)])  15.2 us
    pallas_call x5, Pallas kernels, partial_products(): pl.pallas_call(functools.partial(partial_kernel, shapes, len(pieces), kep...  9.95 us
    ppermute x11, waiting for transfers between devices, swap(): return lax.ppermute(x, 'layer', [(i, i ^ bits) for i in range(4)])  9.84 us
    pallas_call x12, Pallas kernels, load(): pl.pallas_call(functools.partial(load_kernel, at, size, parts), out_shape...  8.42 us
    unnamed x38, local copies, waits for them, and re-layouts  7.18 us
    transpose x2, other arithmetic, per_device(): pieces.append(expand_tiles(values, tiles).transpose(1, 0, 2))  3.21 us
  transfers between devices with their start and end apart: 25, of which 14 were waited for; matrix products, arithmetic and copies ran while one was open for 3% of the time, Pallas kernels for 18%

profile of v7, /device:TPU:0, one launch (start us, length us, event | category | flops | bytes accessed | tf_op | source)
XLA Modules:
  0.0 110.0 jit_solution(15646638624886785492)
XLA Ops:
  2.9 2.6 %collective-permute-start = (bf16[384,256]{1,0:T(8,128)(2,1)S(1)}, bf16[384,256]{1,0:T(8,128)(2,1)S(1)}, u32[]{:S(2)}, u32[]{:S(2)}) collective-permute-start(bf16[384,256]{1,0:T(8,128)(2,1)S(1)} %shard_map.46.refs_0_), channel_id=1, source_target_pairs={{0,1},{1,2},{2,3},{3,0},{4,5},{5,6},{6,7},{7,4},{8,9},{9,10},{10,1... | collective-permute-start | bytes 589832 | tf_op jit(solution)/shard_map/ppermute | solution.py:213
  6.1 2.1 %collective-permute-start.2 = (bf16[384,256]{1,0:T(8,128)(2,1)S(1)}, bf16[384,256]{1,0:T(8,128)(2,1)S(1)}, u32[]{:S(2)}, u32[]{:S(2)}) collective-permute-start(bf16[384,256]{1,0:T(8,128)(2,1)S(1)} %shard_map.47.refs_0_), channel_id=1, source_target_pairs={{0,3},{1,0},{2,1},{3,2},{4,7},{5,4},{6,5},{7,6},{8,11},{9,8},{10,9... | collective-permute-start | bytes 589832 | tf_op jit(solution)/shard_map/ppermute | solution.py:213
  10.4 2.9 %collective-permute-done.arrived.refs_1_ = bf16[384,256]{1,0:T(8,128)(2,1)S(1)} collective-permute-done((bf16[384,256]{1,0:T(8,128)(2,1)S(1)}, bf16[384,256]{1,0:T(8,128)(2,1)S(1)}, u32[]{:S(2)}, u32[]{:S(2)}) %collective-permute-start) | collective-permute-done | bytes 196640 | tf_op jit(solution)/shard_map/ppermute | solution.py:213
  14.1 3.3 %collective-permute-done.2.arrived.refs_2_ = bf16[384,256]{1,0:T(8,128)(2,1)S(1)} collective-permute-done((bf16[384,256]{1,0:T(8,128)(2,1)S(1)}, bf16[384,256]{1,0:T(8,128)(2,1)S(1)}, u32[]{:S(2)}, u32[]{:S(2)}) %collective-permute-start.2) | collective-permute-done | bytes 196640 | tf_op jit(solution)/shard_map/ppermute | solution.py:213
  18.0 2.4 %collective-permute-start.6 = (bf16[704,256]{1,0:T(8,128)(2,1)S(1)}, bf16[704,256]{1,0:T(8,128)(2,1)S(1)}, u32[]{:S(2)}, u32[]{:S(2)}) collective-permute-start(bf16[704,256]{1,0:T(8,128)(2,1)S(1)} %shard_map.49.refs_0_), channel_id=1, source_target_pairs={{0,3},{1,0},{2,1},{3,2},{4,7},{5,4},{6,5},{7,6},{8,11},{9,8},{10,9... | collective-permute-start | bytes 1081352 | tf_op jit(solution)/shard_map/ppermute | solution.py:213
  22.1 6.9 %collective-permute-done.1.arrived.refs_3_.refs_1_ = bf16[704,256]{1,0:T(8,128)(2,1)S(1)} collective-permute-done((bf16[704,256]{1,0:T(8,128)(2,1)S(1)}, bf16[704,256]{1,0:T(8,128)(2,1)S(1)}, u32[]{:S(2)}, u32[]{:S(2)}) %collective-permute-start.1) | collective-permute-done | bytes 360480 | tf_op jit(solution)/shard_map/ppermute | solution.py:213
  29.7 6.9 %collective-permute-done.6.arrived.refs_4_.refs_2_ = bf16[704,256]{1,0:T(8,128)(2,1)S(1)} collective-permute-done((bf16[704,256]{1,0:T(8,128)(2,1)S(1)}, bf16[704,256]{1,0:T(8,128)(2,1)S(1)}, u32[]{:S(2)}, u32[]{:S(2)}) %collective-permute-start.6) | collective-permute-done | bytes 360480 | tf_op jit(solution)/shard_map/ppermute | solution.py:213
  47.1 2.1 %collective-permute-start.7 = (bf16[640,256]{1,0:T(8,128)(2,1)S(1)}, bf16[640,256]{1,0:T(8,128)(2,1)S(1)}, u32[]{:S(2)}, u32[]{:S(2)}) collective-permute-start(bf16[640,256]{1,0:T(8,128)(2,1)S(1)} %shard_map.53.refs_0_), channel_id=1, source_target_pairs={{0,1},{1,2},{2,3},{3,0},{4,5},{5,6},{6,7},{7,4},{8,9},{9,10},{10,1... | collective-permute-start | bytes 983048 | tf_op jit(solution)/shard_map/ppermute | solution.py:213
  49.1 2.6 %collective-permute-done.9.arrived.refs_4_.refs_2_ = bf16[768,256]{1,0:T(8,128)(2,1)} collective-permute-done((bf16[768,256]{1,0:T(8,128)(2,1)}, bf16[768,256]{1,0:T(8,128)(2,1)}, u32[]{:S(2)}, u32[]{:S(2)}) %collective-permute-start.9) | collective-permute-done | bytes 393248 | tf_op jit(solution)/shard_map/ppermute | solution.py:213
  52.8 3.2 %collective-permute-start.11 = (bf16[640,256]{1,0:T(8,128)(2,1)S(1)}, bf16[640,256]{1,0:T(8,128)(2,1)S(1)}, u32[]{:S(2)}, u32[]{:S(2)}) collective-permute-start(bf16[640,256]{1,0:T(8,128)(2,1)S(1)} %shard_map.54.refs_7_), channel_id=1, source_target_pairs={{0,3},{1,0},{2,1},{3,2},{4,7},{5,4},{6,5},{7,6},{8,11},{9,8},{10,9... | collective-permute-start | bytes 983048 | tf_op jit(solution)/shard_map/ppermute | solution.py:213
  56.0 2.6 %shard_map.55 = (f32[512,256]{1,0:T(8,128)S(1)}, f32[512,256]{1,0:T(8,128)S(1)}, s16[1056,256]{1,0:T(8,128)(2,1)S(1)}) custom-call(s32[9]{0:T(128)S(1)} %stack.39.where, bf16[704,256]{1,0:T(8,128)(2,1)S(1)} %copy-done.6, bf16[704,256]{1,0:T(8,128)(2,1)S(1)} %copy-done.8, bf16[704,256]{1,0:T(8,128)(2,1)S(1)} %copy-done.4, ...), custom_call_target="tpu_custom_call" | custom-call | flops 1073741824 | bytes 3932160 | tf_op jit(solution)/shard_map/pallas_call | solution.py:113
  60.4 1.9 %collective-permute-done.7.arrived.refs_3_.refs_1_ = bf16[640,256]{1,0:T(8,128)(2,1)S(1)} collective-permute-done((bf16[640,256]{1,0:T(8,128)(2,1)S(1)}, bf16[640,256]{1,0:T(8,128)(2,1)S(1)}, u32[]{:S(2)}, u32[]{:S(2)}) %collective-permute-start.7) | collective-permute-done | bytes 327712 | tf_op jit(solution)/shard_map/ppermute | solution.py:213
  62.9 2.6 %collective-permute-start.10 = (bf16[448,256]{1,0:T(8,128)(2,1)S(1)}, bf16[448,256]{1,0:T(8,128)(2,1)S(1)}, u32[]{:S(2)}, u32[]{:S(2)}) collective-permute-start(bf16[448,256]{1,0:T(8,128)(2,1)S(1)} %shard_map.57.refs_0_), channel_id=1, source_target_pairs={{0,1},{1,2},{2,3},{3,0},{4,5},{5,6},{6,7},{7,4},{8,9},{9,10},{10,1... | collective-permute-start | bytes 688136 | tf_op jit(solution)/shard_map/ppermute | solution.py:213
  65.6 2.4 %collective-permute-done.11.arrived.refs_4_.refs_2_ = bf16[640,256]{1,0:T(8,128)(2,1)S(1)} collective-permute-done((bf16[640,256]{1,0:T(8,128)(2,1)S(1)}, bf16[640,256]{1,0:T(8,128)(2,1)S(1)}, u32[]{:S(2)}, u32[]{:S(2)}) %collective-permute-start.11) | collective-permute-done | bytes 327712 | tf_op jit(solution)/shard_map/ppermute | solution.py:213
  68.5 4.7 %collective-permute-start.12 = (bf16[448,256]{1,0:T(8,128)(2,1)S(1)}, bf16[448,256]{1,0:T(8,128)(2,1)S(1)}, u32[]{:S(2)}, u32[]{:S(2)}) collective-permute-start(bf16[448,256]{1,0:T(8,128)(2,1)S(1)} %shard_map.58.refs_7_), channel_id=1, source_target_pairs={{0,3},{1,0},{2,1},{3,2},{4,7},{5,4},{6,5},{7,6},{8,11},{9,8},{10,9... | collective-permute-start | bytes 688136 | tf_op jit(solution)/shard_map/ppermute | solution.py:213
  73.2 3.4 %collective-permute-start.13 = (s16[400,256]{1,0:T(8,128)(2,1)S(1)}, s16[400,256]{1,0:T(8,128)(2,1)S(1)}, u32[]{:S(2)}, u32[]{:S(2)}) collective-permute-start(s16[400,256]{1,0:T(8,128)(2,1)S(1)} %shard_map.56.refs_0_), channel_id=1, source_target_pairs={{0,16},{8,24},{16,0},{24,8},{1,17},{9,25},{17,1},{25,9},{2,18},{10... | collective-permute-start | bytes 614408 | tf_op jit(solution)/shard_map/ppermute | solution.py:221
  76.6 2.6 %shard_map.59 = (f32[512,256]{1,0:T(8,128)S(1)}, f32[512,256]{1,0:T(8,128)S(1)}, s16[1056,256]{1,0:T(8,128)(2,1)S(1)}) custom-call(s32[9]{0:T(128)S(1)} %stack.39.where, bf16[768,256]{1,0:T(8,128)(2,1)S(1)} %shard_map.50.refs_0_, bf16[768,256]{1,0:T(8,128)(2,1)} %collective-permute-done.5.arrived.refs_3_.refs_1_, ...), custom_call_target="tpu_custom_call" | custom-call | flops 1073741824 | bytes 3932160 | tf_op jit(solution)/shard_map/pallas_call | solution.py:113
  83.3 2.2 %collective-permute-start.22 = (s16[800,256]{1,0:T(8,128)(2,1)S(1)}, s16[800,256]{1,0:T(8,128)(2,1)S(1)}, u32[]{:S(2)}, u32[]{:S(2)}) collective-permute-start(s16[800,256]{1,0:T(8,128)(2,1)S(1)} %get-tuple-element.47), channel_id=1, source_target_pairs={{0,16},{8,24},{16,0},{24,8},{1,17},{9,25},{17,1},{25,9},{2,18},{10... | collective-permute-start | bytes 1228808 | tf_op jit(solution)/shard_map/ppermute | solution.py:221
  85.6 3.2 %collective-permute-start.16 = (bf16[128,256]{1,0:T(8,128)(2,1)S(1)}, bf16[128,256]{1,0:T(8,128)(2,1)S(1)}, u32[]{:S(2)}, u32[]{:S(2)}) collective-permute-start(bf16[128,256]{1,0:T(8,128)(2,1)S(1)} %shard_map.63.refs_7_), channel_id=1, source_target_pairs={{0,3},{1,0},{2,1},{3,2},{4,7},{5,4},{6,5},{7,6},{8,11},{9,8},{10,9... | collective-permute-start | bytes 196616 | tf_op jit(solution)/shard_map/ppermute | solution.py:213
  88.8 2.7 %collective-permute-done.18.received_ref.refs_0_ = s16[1056,256]{1,0:T(8,128)(2,1)S(1)} collective-permute-done((s16[1056,256]{1,0:T(8,128)(2,1)S(1)}, s16[1056,256]{1,0:T(8,128)(2,1)S(1)}, u32[]{:S(2)}, u32[]{:S(2)}) %collective-permute-start.18) | collective-permute-done | bytes 540704 | tf_op jit(solution)/shard_map/ppermute | solution.py:221
  92.2 2.2 %collective-permute-done.17.refs_1_ = s16[528,256]{1,0:T(8,128)(2,1)S(1)} collective-permute-done((s16[528,256]{1,0:T(8,128)(2,1)S(1)}, s16[528,256]{1,0:T(8,128)(2,1)S(1)}, u32[]{:S(2)}, u32[]{:S(2)}) %collective-permute-start.17) | collective-permute-done | bytes 270368 | tf_op jit(solution)/shard_map/ppermute | solution.py:221
  96.4 2.1 %collective-permute-start.23 = (s16[400,256]{1,0:T(8,128)(2,1)S(1)}, s16[400,256]{1,0:T(8,128)(2,1)S(1)}, u32[]{:S(2)}, u32[]{:S(2)}) collective-permute-start(s16[400,256]{1,0:T(8,128)(2,1)S(1)} %shard_map.68.refs_3_), channel_id=1, source_target_pairs={{0,8},{8,0},{16,24},{24,16},{1,9},{9,1},{17,25},{25,17},{2,10},{10... | collective-permute-start | bytes 614408 | tf_op jit(solution)/shard_map/ppermute | solution.py:221
  98.8 3.3 %collective-permute-start.21 = (s16[272,256]{1,0:T(8,128)(2,1)S(1)}, s16[272,256]{1,0:T(8,128)(2,1)S(1)}, u32[]{:S(2)}, u32[]{:S(2)}) collective-permute-start(s16[272,256]{1,0:T(8,128)(2,1)S(1)} %get-tuple-element.46), channel_id=1, source_target_pairs={{0,24},{8,16},{16,8},{24,0},{1,25},{9,17},{17,9},{25,1},{2,26},{10... | collective-permute-start | bytes 417800 | tf_op jit(solution)/shard_map/ppermute | solution.py:221
  106.5 2.5 %psum.7.column_ref = f32[1,256]{1,0:T(1,128)S(1)} all-reduce(f32[1,256]{1,0:T(1,128)S(1)} %get-tuple-element.51), channel_id=1, replica_groups=mesh['layer'=4,'row'=2,'col'=4] {'row'}, use_global_device_ids=true, to_apply=%region_0.1 | all-reduce | flops 256 | bytes 2048 | tf_op jit(solution)/shard_map/psum | solution.py:322
  (100 shorter events, 36.3 us)
Async XLA Ops:
  0.0 20.5 %collective-permute-start.3 = (bf16[512,4,256]{2,1,0:T(4,128)(2,1)}, bf16[512,4,256]{2,1,0:T(4,128)(2,1)}, u32[]{:S(2)}, u32[]{:S(2)}) collective-permute-start(bf16[512,4,256]{2,1,0:T(4,128)(2,1)} %param.6), channel_id=1, source_target_pairs={{0,4},{4,0},{1,5},{5,1},{2,6},{6,2},{3,7},{7,3},{8,12},{12,8},{9,1... | collective-permute-start | bytes 3145736 | tf_op jit(solution)/shard_map/ppermute | solution.py:213
  2.9 10.5 %collective-permute-start = (bf16[384,256]{1,0:T(8,128)(2,1)S(1)}, bf16[384,256]{1,0:T(8,128)(2,1)S(1)}, u32[]{:S(2)}, u32[]{:S(2)}) collective-permute-start(bf16[384,256]{1,0:T(8,128)(2,1)S(1)} %shard_map.46.refs_0_), channel_id=1, source_target_pairs={{0,1},{1,2},{2,3},{3,0},{4,5},{5,6},{6,7},{7,4},{8,9},{9,10},{10,1... | collective-permute-start | bytes 589832 | tf_op jit(solution)/shard_map/ppermute | solution.py:213
  6.1 11.2 %collective-permute-start.2 = (bf16[384,256]{1,0:T(8,128)(2,1)S(1)}, bf16[384,256]{1,0:T(8,128)(2,1)S(1)}, u32[]{:S(2)}, u32[]{:S(2)}) collective-permute-start(bf16[384,256]{1,0:T(8,128)(2,1)S(1)} %shard_map.47.refs_0_), channel_id=1, source_target_pairs={{0,3},{1,0},{2,1},{3,2},{4,7},{5,4},{6,5},{7,6},{8,11},{9,8},{10,9... | collective-permute-start | bytes 589832 | tf_op jit(solution)/shard_map/ppermute | solution.py:213
  14.1 14.9 %collective-permute-start.1 = (bf16[704,256]{1,0:T(8,128)(2,1)S(1)}, bf16[704,256]{1,0:T(8,128)(2,1)S(1)}, u32[]{:S(2)}, u32[]{:S(2)}) collective-permute-start(bf16[704,256]{1,0:T(8,128)(2,1)S(1)} %shard_map.48.refs_0_), channel_id=1, source_target_pairs={{0,1},{1,2},{2,3},{3,0},{4,5},{5,6},{6,7},{7,4},{8,9},{9,10},{10,1... | collective-permute-start | bytes 1081352 | tf_op jit(solution)/shard_map/ppermute | solution.py:213
  18.0 18.6 %collective-permute-start.6 = (bf16[704,256]{1,0:T(8,128)(2,1)S(1)}, bf16[704,256]{1,0:T(8,128)(2,1)S(1)}, u32[]{:S(2)}, u32[]{:S(2)}) collective-permute-start(bf16[704,256]{1,0:T(8,128)(2,1)S(1)} %shard_map.49.refs_0_), channel_id=1, source_target_pairs={{0,3},{1,0},{2,1},{3,2},{4,7},{5,4},{6,5},{7,6},{8,11},{9,8},{10,9... | collective-permute-start | bytes 1081352 | tf_op jit(solution)/shard_map/ppermute | solution.py:213
  29.7 16.3 %collective-permute-start.5 = (bf16[768,256]{1,0:T(8,128)(2,1)S(1)}, bf16[768,256]{1,0:T(8,128)(2,1)}, u32[]{:S(2)}, u32[]{:S(2)}) collective-permute-start(bf16[768,256]{1,0:T(8,128)(2,1)S(1)} %shard_map.50.refs_0_), channel_id=1, source_target_pairs={{0,1},{1,2},{2,3},{3,0},{4,5},{5,6},{6,7},{7,4},{8,9},{9,10},{10,1... | collective-permute-start | bytes 1179656 | tf_op jit(solution)/shard_map/ppermute | solution.py:213
  37.9 13.8 %collective-permute-start.9 = (bf16[768,256]{1,0:T(8,128)(2,1)}, bf16[768,256]{1,0:T(8,128)(2,1)}, u32[]{:S(2)}, u32[]{:S(2)}) collective-permute-start(bf16[768,256]{1,0:T(8,128)(2,1)} %shard_map.51.refs_7_), channel_id=1, source_target_pairs={{0,3},{1,0},{2,1},{3,2},{4,7},{5,4},{6,5},{7,6},{8,11},{9,8},{10,9... | collective-permute-start | bytes 1179656 | tf_op jit(solution)/shard_map/ppermute | solution.py:213
  44.4 15.9 %collective-permute-start.8 = (s16[800,256]{1,0:T(8,128)(2,1)S(1)}, s16[800,256]{1,0:T(8,128)(2,1)S(1)}, u32[]{:S(2)}, u32[]{:S(2)}) collective-permute-start(s16[800,256]{1,0:T(8,128)(2,1)S(1)} %get-tuple-element.33), channel_id=1, source_target_pairs={{0,8},{8,0},{16,24},{24,16},{1,9},{9,1},{17,25},{25,17},{2,10},{10... | collective-permute-start | bytes 1228808 | tf_op jit(solution)/shard_map/ppermute | solution.py:221
  47.1 15.3 %collective-permute-start.7 = (bf16[640,256]{1,0:T(8,128)(2,1)S(1)}, bf16[640,256]{1,0:T(8,128)(2,1)S(1)}, u32[]{:S(2)}, u32[]{:S(2)}) collective-permute-start(bf16[640,256]{1,0:T(8,128)(2,1)S(1)} %shard_map.53.refs_0_), channel_id=1, source_target_pairs={{0,1},{1,2},{2,3},{3,0},{4,5},{5,6},{6,7},{7,4},{8,9},{9,10},{10,1... | collective-permute-start | bytes 983048 | tf_op jit(solution)/shard_map/ppermute | solution.py:213
  52.8 15.1 %collective-permute-start.11 = (bf16[640,256]{1,0:T(8,128)(2,1)S(1)}, bf16[640,256]{1,0:T(8,128)(2,1)S(1)}, u32[]{:S(2)}, u32[]{:S(2)}) collective-permute-start(bf16[640,256]{1,0:T(8,128)(2,1)S(1)} %shard_map.54.refs_7_), channel_id=1, source_target_pairs={{0,3},{1,0},{2,1},{3,2},{4,7},{5,4},{6,5},{7,6},{8,11},{9,8},{10,9... | collective-permute-start | bytes 983048 | tf_op jit(solution)/shard_map/ppermute | solution.py:213
  58.6 20.7 %collective-permute-start.14 = (s16[1056,256]{1,0:T(8,128)(2,1)S(1)}, s16[1056,256]{1,0:T(8,128)(2,1)S(1)}, u32[]{:S(2)}, u32[]{:S(2)}) collective-permute-start(s16[1056,256]{1,0:T(8,128)(2,1)S(1)} %get-tuple-element.36), channel_id=1, source_target_pairs={{0,16},{8,24},{16,0},{24,8},{1,17},{9,25},{17,1},{25,9},{2,18},{10... | collective-permute-start | bytes 1622024 | tf_op jit(solution)/shard_map/ppermute | solution.py:221
  62.9 17.6 %collective-permute-start.10 = (bf16[448,256]{1,0:T(8,128)(2,1)S(1)}, bf16[448,256]{1,0:T(8,128)(2,1)S(1)}, u32[]{:S(2)}, u32[]{:S(2)}) collective-permute-start(bf16[448,256]{1,0:T(8,128)(2,1)S(1)} %shard_map.57.refs_0_), channel_id=1, source_target_pairs={{0,1},{1,2},{2,3},{3,0},{4,5},{5,6},{6,7},{7,4},{8,9},{9,10},{10,1... | collective-permute-start | bytes 688136 | tf_op jit(solution)/shard_map/ppermute | solution.py:213
  68.5 12.6 %collective-permute-start.12 = (bf16[448,256]{1,0:T(8,128)(2,1)S(1)}, bf16[448,256]{1,0:T(8,128)(2,1)S(1)}, u32[]{:S(2)}, u32[]{:S(2)}) collective-permute-start(bf16[448,256]{1,0:T(8,128)(2,1)S(1)} %shard_map.58.refs_7_), channel_id=1, source_target_pairs={{0,3},{1,0},{2,1},{3,2},{4,7},{5,4},{6,5},{7,6},{8,11},{9,8},{10,9... | collective-permute-start | bytes 688136 | tf_op jit(solution)/shard_map/ppermute | solution.py:213
  73.2 7.2 %collective-permute-start.13 = (s16[400,256]{1,0:T(8,128)(2,1)S(1)}, s16[400,256]{1,0:T(8,128)(2,1)S(1)}, u32[]{:S(2)}, u32[]{:S(2)}) collective-permute-start(s16[400,256]{1,0:T(8,128)(2,1)S(1)} %shard_map.56.refs_0_), channel_id=1, source_target_pairs={{0,16},{8,24},{16,0},{24,8},{1,17},{9,25},{17,1},{25,9},{2,18},{10... | collective-permute-start | bytes 614408 | tf_op jit(solution)/shard_map/ppermute | solution.py:221
  79.2 12.3 %collective-permute-start.18 = (s16[1056,256]{1,0:T(8,128)(2,1)S(1)}, s16[1056,256]{1,0:T(8,128)(2,1)S(1)}, u32[]{:S(2)}, u32[]{:S(2)}) collective-permute-start(s16[1056,256]{1,0:T(8,128)(2,1)S(1)} %get-tuple-element.40), channel_id=1, source_target_pairs={{0,8},{8,0},{16,24},{24,16},{1,9},{9,1},{17,25},{25,17},{2,10},{10... | collective-permute-start | bytes 1622024 | tf_op jit(solution)/shard_map/ppermute | solution.py:221
  83.3 13.0 %collective-permute-start.22 = (s16[800,256]{1,0:T(8,128)(2,1)S(1)}, s16[800,256]{1,0:T(8,128)(2,1)S(1)}, u32[]{:S(2)}, u32[]{:S(2)}) collective-permute-start(s16[800,256]{1,0:T(8,128)(2,1)S(1)} %get-tuple-element.47), channel_id=1, source_target_pairs={{0,16},{8,24},{16,0},{24,8},{1,17},{9,25},{17,1},{25,9},{2,18},{10... | collective-permute-start | bytes 1228808 | tf_op jit(solution)/shard_map/ppermute | solution.py:221
  85.5 8.9 %collective-permute-start.17 = (s16[528,256]{1,0:T(8,128)(2,1)S(1)}, s16[528,256]{1,0:T(8,128)(2,1)S(1)}, u32[]{:S(2)}, u32[]{:S(2)}) collective-permute-start(s16[528,256]{1,0:T(8,128)(2,1)S(1)} %shard_map.60.refs_3_), channel_id=1, source_target_pairs={{0,8},{8,0},{16,24},{24,16},{1,9},{9,1},{17,25},{25,17},{2,10},{10... | collective-permute-start | bytes 811016 | tf_op jit(solution)/shard_map/ppermute | solution.py:221
  85.6 9.0 %collective-permute-start.16 = (bf16[128,256]{1,0:T(8,128)(2,1)S(1)}, bf16[128,256]{1,0:T(8,128)(2,1)S(1)}, u32[]{:S(2)}, u32[]{:S(2)}) collective-permute-start(bf16[128,256]{1,0:T(8,128)(2,1)S(1)} %shard_map.63.refs_7_), channel_id=1, source_target_pairs={{0,3},{1,0},{2,1},{3,2},{4,7},{5,4},{6,5},{7,6},{8,11},{9,8},{10,9... | collective-permute-start | bytes 196616 | tf_op jit(solution)/shard_map/ppermute | solution.py:213
  88.8 6.1 %collective-permute-start.15 = (bf16[128,256]{1,0:T(8,128)(2,1)S(1)}, bf16[128,256]{1,0:T(8,128)(2,1)S(1)}, u32[]{:S(2)}, u32[]{:S(2)}) collective-permute-start(bf16[128,256]{1,0:T(8,128)(2,1)S(1)} %shard_map.62.refs_0_), channel_id=1, source_target_pairs={{0,1},{1,2},{2,3},{3,0},{4,5},{5,6},{6,7},{7,4},{8,9},{9,10},{10,1... | collective-permute-start | bytes 196616 | tf_op jit(solution)/shard_map/ppermute | solution.py:213
  91.7 10.3 %collective-permute-start.24 = (s16[528,256]{1,0:T(8,128)(2,1)S(1)}, s16[528,256]{1,0:T(8,128)(2,1)S(1)}, u32[]{:S(2)}, u32[]{:S(2)}) collective-permute-start(s16[528,256]{1,0:T(8,128)(2,1)S(1)} %shard_map.65.refs_3_), channel_id=1, source_target_pairs={{0,16},{8,24},{16,0},{24,8},{1,17},{9,25},{17,1},{25,9},{2,18},{10... | collective-permute-start | bytes 811016 | tf_op jit(solution)/shard_map/ppermute | solution.py:221
  96.4 7.0 %collective-permute-start.23 = (s16[400,256]{1,0:T(8,128)(2,1)S(1)}, s16[400,256]{1,0:T(8,128)(2,1)S(1)}, u32[]{:S(2)}, u32[]{:S(2)}) collective-permute-start(s16[400,256]{1,0:T(8,128)(2,1)S(1)} %shard_map.68.refs_3_), channel_id=1, source_target_pairs={{0,8},{8,0},{16,24},{24,16},{1,9},{9,1},{17,25},{25,17},{2,10},{10... | collective-permute-start | bytes 614408 | tf_op jit(solution)/shard_map/ppermute | solution.py:221
  98.5 6.4 %collective-permute-start.19 = (s16[272,256]{1,0:T(8,128)(2,1)S(1)}, s16[272,256]{1,0:T(8,128)(2,1)S(1)}, u32[]{:S(2)}, u32[]{:S(2)}) collective-permute-start(s16[272,256]{1,0:T(8,128)(2,1)S(1)} %get-tuple-element.44), channel_id=1, source_target_pairs={{0,8},{8,0},{16,24},{24,16},{1,9},{9,1},{17,25},{25,17},{2,10},{10... | collective-permute-start | bytes 417800 | tf_op jit(solution)/shard_map/ppermute | solution.py:221
  98.6 6.3 %collective-permute-start.20 = (s16[272,256]{1,0:T(8,128)(2,1)S(1)}, s16[272,256]{1,0:T(8,128)(2,1)S(1)}, u32[]{:S(2)}, u32[]{:S(2)}) collective-permute-start(s16[272,256]{1,0:T(8,128)(2,1)S(1)} %get-tuple-element.45), channel_id=1, source_target_pairs={{0,16},{8,24},{16,0},{24,8},{1,17},{9,25},{17,1},{25,9},{2,18},{10... | collective-permute-start | bytes 417800 | tf_op jit(solution)/shard_map/ppermute | solution.py:221
  98.8 7.6 %collective-permute-start.21 = (s16[272,256]{1,0:T(8,128)(2,1)S(1)}, s16[272,256]{1,0:T(8,128)(2,1)S(1)}, u32[]{:S(2)}, u32[]{:S(2)}) collective-permute-start(s16[272,256]{1,0:T(8,128)(2,1)S(1)} %get-tuple-element.46), channel_id=1, source_target_pairs={{0,24},{8,16},{16,8},{24,0},{1,25},{9,17},{17,9},{25,1},{2,26},{10... | collective-permute-start | bytes 417800 | tf_op jit(solution)/shard_map/ppermute | solution.py:221
  (18 other events, 47.2 us)

commit v8 on v7

--- a/solution.py
+++ b/solution.py
@@ -5,7 +5,6 @@
 import jax.numpy as jnp
 from jax import lax
 from jax.experimental import pallas as pl
-from jax.experimental.layout import Layout, with_layout_constraint
 from jax.experimental.pallas import tpu as pltpu
 from jax.sharding import PartitionSpec as P
 
@@ -17,6 +16,10 @@
 LEAST = 2.0**-100
 VMEM = pl.BlockSpec(memory_space=pltpu.VMEM)
 PARAMS = pltpu.CompilerParams(vmem_limit_bytes=16 * 1024 * 1024)
+
+
+def cost(flops, bytes_accessed):
+    return pl.CostEstimate(flops=flops, bytes_accessed=bytes_accessed, transcendentals=0)
 
 
 def load_kernel(at, size, parts, pattern_ref, left_ref, arrived, *refs):
@@ -42,10 +45,31 @@
         + [pl.BlockSpec(memory_space=pl.ANY)] * len(after),
         out_specs=VMEM,
         compiler_params=PARAMS,
-        cost_estimate=pl.CostEstimate(
-            flops=total * columns, bytes_accessed=4 * total * columns, transcendentals=0
-        ),
+        cost_estimate=cost(total * columns, 4 * total * columns),
     )(pattern, left, arrived, *after)
+
+
+def mask_right_kernel(pattern_ref, values_ref, *refs):
+    out = refs[-1]
+    layers, rows, _ = out.shape
+    for i in range(0, rows, TILE):
+        block = jnp.swapaxes(values_ref[i : i + TILE].astype(jnp.float32), 0, 1)
+        for j in range(layers):
+            entry = pattern_ref[i // TILE, j].astype(jnp.float32)
+            out[j, i : i + TILE, :] = (block[j] * entry).astype(out.dtype)
+
+
+def mask_right(pattern, values, after):
+    rows, layers, columns = values.shape
+    return pl.pallas_call(
+        mask_right_kernel,
+        out_shape=jax.ShapeDtypeStruct((layers, rows, columns), values.dtype),
+        in_specs=[pl.BlockSpec(memory_space=pltpu.SMEM), VMEM]
+        + [pl.BlockSpec(memory_space=pl.ANY)] * len(after),
+        out_specs=VMEM,
+        compiler_params=PARAMS,
+        cost_estimate=cost(values.size, 4 * values.size),
+    )(pattern.reshape(rows // TILE, layers), values, *after)
 
 
 def put_fixed(ref, at, total):
@@ -118,10 +142,9 @@
         + [pl.BlockSpec(memory_space=pl.ANY)] * len(after),
         out_specs=[VMEM] * len(outs),
         compiler_params=PARAMS,
-        cost_estimate=pl.CostEstimate(
-            flops=2 * rows * len(sources) * TILE * columns * n_products,
-            bytes_accessed=len(pieces) * pieces[0].size * 2 + rows * columns * 14,
-            transcendentals=0,
+        cost_estimate=cost(
+            2 * rows * len(sources) * TILE * columns * n_products,
+            2 * len(pieces) * pieces[0].size + 14 * rows * columns,
         ),
     )(where, *lefts, *pieces, *after)
     return out[: len(kept)], out[len(kept) :]
@@ -141,9 +164,7 @@
         in_specs=[VMEM, VMEM, pl.BlockSpec(memory_space=pl.ANY)],
         out_specs=VMEM,
         compiler_params=PARAMS,
-        cost_estimate=pl.CostEstimate(
-            flops=10 * kept.size, bytes_accessed=8 * kept.size, transcendentals=0
-        ),
+        cost_estimate=cost(10 * kept.size, 8 * kept.size),
     )(kept, received, after)
 
 
@@ -168,9 +189,7 @@
         in_specs=[VMEM] * (2 + len(received)) + [pl.BlockSpec(memory_space=pl.ANY)] * len(after),
         out_specs=(VMEM, VMEM),
         compiler_params=PARAMS,
-        cost_estimate=pl.CostEstimate(
-            flops=8 * kept.size, bytes_accessed=kept.size * 14, transcendentals=0
-        ),
+        cost_estimate=cost(8 * kept.size, 14 * kept.size),
     )(kept, *received, before, *after)
 
 
@@ -192,29 +211,13 @@
         in_specs=[VMEM] * (1 + len(chunks)),
         out_specs=VMEM,
         compiler_params=PARAMS,
-        cost_estimate=pl.CostEstimate(
-            flops=4 * rows * columns,
-            bytes_accessed=6 * rows * columns,
-            transcendentals=0,
-        ),
+        cost_estimate=cost(4 * rows * columns, 6 * rows * columns),
     )(column, *chunks)
-
-
-def expand_tiles(values, pattern):
-    tile_rows, layers, tile_cols = pattern.shape
-    tile_size = values.shape[0] // tile_rows
-    blocks = values.reshape(tile_rows, tile_size, layers, tile_cols, tile_size)
-    blocks = blocks * pattern[:, None, :, :, None].astype(values.dtype)
-    return blocks.reshape(values.shape)
 
 
 def shift(x, axis, by):
     n = lax.axis_size(axis)
     return lax.ppermute(x, axis, [(i, (i + by) % n) for i in range(n)])
-
-
-def as_it_lies(x):
-    return with_layout_constraint(x, Layout(tuple(range(x.ndim))))
 
 
 def swap(x, bits):
@@ -268,8 +271,7 @@
 
     def sources(i):
         (*below, last_below), (*above, last_above) = found[i]
-        near = [own[i]] + below + above
-        return [[part] for part in near] + [[last_below, last_above]]
+        return [[part] for part in [own[i]] + below + above] + [[last_below, last_above]]
 
     def sum_chunk(i):
         if i + 1 < len(sizes):
@@ -289,12 +291,10 @@
         received[i].append(swap(block, second(i)))
         last[:] = [block]
 
+    raw = [(right_pattern, right_values)]
+    for i in range(1, n_rows):
+        raw.append((shift(right_pattern, "row", i), shift(right_values, "row", i)))
     pieces = []
-    for i in range(n_rows):
-        values, tiles = right_values, right_pattern
-        if i:
-            values, tiles = as_it_lies(shift(values, "row", i)), shift(tiles, "row", i)
-        pieces.append(expand_tiles(values, tiles).transpose(1, 0, 2))
 
     squares, columns = [], [jnp.zeros((1, columns_local), jnp.float32)]
 
@@ -310,14 +310,16 @@
             open_slot(opened)
             opened += 1
             if opened == 2:
-                last += pieces
+                for tiles, values in raw:
+                    pieces.append(mask_right(tiles, values, last))
+                    last[:] = pieces[-1:]
         sum_chunk(i)
         if i > 0:
             send_on(i - 1)
-        if i > 1:
+        if 1 < i < len(sizes) - 2:
             square(i - 2)
-    square(len(sizes) - 2)
-    square(len(sizes) - 1)
+    for i in range(len(squares), len(sizes)):
+        square(i)
 
     column = lax.psum(columns[-1], "row")
     out = normalise(column, squares, rows_local * n_rows)

time: 111 us -> 111 us (level)
  other arithmetic: 3.22 us -> 0 us
  Pallas kernels: 20.8 us -> 22.9 us
  waiting for transfers between devices: 37 us -> 38.4 us
    ppermute x14, starting transfers between devices: 23.5 us -> 27.4 us  [shift(): return lax.ppermute(x, axis, [(i, (i + by) % n) for i in range(n)])]
    ppermute x11, starting transfers between devices: 15.2 us -> 11.3 us  [swap(): return lax.ppermute(x, 'layer', [(i, i ^ bits) for i in range(4)])]
    ppermute x11, waiting for transfers between devices: 9.84 us -> 13.3 us  [swap(): return lax.ppermute(x, 'layer', [(i, i ^ bits) for i in range(4)])]
    transpose x2 -> x0, other arithmetic: 3.21 us -> none  [per_device(): pieces.append(expand_tiles(values, tiles).transpose(1, 0, 2))]
    pallas_call x0 -> x2, Pallas kernels: none -> 2.27 us  [mask_right(): pl.pallas_call(mask_right_kernel, out_shape=jax.ShapeDtypeStruct((layers,...]
    ppermute x14, waiting for transfers between devices: 27.2 us -> 25.1 us  [shift(): return lax.ppermute(x, axis, [(i, (i + by) % n) for i in range(n)])]
    unnamed x38 -> x36, local copies, waits for them, and re-layouts: 7.18 us -> 8.17 us
  transfers between devices with their start and end apart: 25 -> 25, of which waited for: 14 -> 15; matrix products, arithmetic and copies ran while one was open for 3% -> 0% of each run, Pallas kernels for 18% -> 19%
where the time goes in v8:
time: 111 us
  starting transfers between devices  38.7 us (35%)
  waiting for transfers between devices  38.4 us (35%)
  Pallas kernels  22.9 us (21%)
  local copies, waits for them, and re-layouts  8.26 us (7%)
  blocking collectives  2.47 us (2%)
    ppermute x14, starting transfers between devices, shift(): return lax.ppermute(x, axis, [(i, (i + by) % n) for i in range(n)])  27.4 us
    ppermute x14, waiting for transfers between devices, shift(): return lax.ppermute(x, axis, [(i, (i + by) % n) for i in range(n)])  25.1 us
    ppermute x11, waiting for transfers between devices, swap(): return lax.ppermute(x, 'layer', [(i, i ^ bits) for i in range(4)])  13.3 us
    ppermute x11, starting transfers between devices, swap(): return lax.ppermute(x, 'layer', [(i, i ^ bits) for i in range(4)])  11.3 us
    pallas_call x5, Pallas kernels, partial_products(): pl.pallas_call(functools.partial(partial_kernel, shapes, len(pieces), kep...  9.69 us
    pallas_call x12, Pallas kernels, load(): pl.pallas_call(functools.partial(load_kernel, at, size, parts), out_shape...  8.42 us
    unnamed x36, local copies, waits for them, and re-layouts  8.17 us
    psum x1, blocking collectives, per_device(): column = lax.psum(columns[-1], 'row')  2.47 us
  transfers between devices with their start and end apart: 25, of which 15 were waited for; matrix products, arithmetic and copies ran while one was open for 0% of the time, Pallas kernels for 19%

profile of v8, /device:TPU:0, one launch (start us, length us, event | category | flops | bytes accessed | tf_op | source)
XLA Modules:
  0.0 111.0 jit_solution(16148865480163890980)
XLA Ops:
  2.9 2.6 %collective-permute-start = (bf16[384,256]{1,0:T(8,128)(2,1)S(1)}, bf16[384,256]{1,0:T(8,128)(2,1)S(1)}, u32[]{:S(2)}, u32[]{:S(2)}) collective-permute-start(bf16[384,256]{1,0:T(8,128)(2,1)S(1)} %shard_map.46.refs_0_), channel_id=1, source_target_pairs={{0,1},{1,2},{2,3},{3,0},{4,5},{5,6},{6,7},{7,4},{8,9},{9,10},{10,1... | collective-permute-start | bytes 589832 | tf_op jit(solution)/shard_map/ppermute | solution.py:220
  6.1 2.1 %collective-permute-start.4 = (bf16[384,256]{1,0:T(8,128)(2,1)S(1)}, bf16[384,256]{1,0:T(8,128)(2,1)S(1)}, u32[]{:S(2)}, u32[]{:S(2)}) collective-permute-start(bf16[384,256]{1,0:T(8,128)(2,1)S(1)} %shard_map.47.refs_0_), channel_id=1, source_target_pairs={{0,3},{1,0},{2,1},{3,2},{4,7},{5,4},{6,5},{7,6},{8,11},{9,8},{10,9... | collective-permute-start | bytes 589832 | tf_op jit(solution)/shard_map/ppermute | solution.py:220
  8.2 5.1 %collective-permute-done.arrived.refs_1_ = bf16[384,256]{1,0:T(8,128)(2,1)S(1)} collective-permute-done((bf16[384,256]{1,0:T(8,128)(2,1)S(1)}, bf16[384,256]{1,0:T(8,128)(2,1)S(1)}, u32[]{:S(2)}, u32[]{:S(2)}) %collective-permute-start) | collective-permute-done | bytes 196640 | tf_op jit(solution)/shard_map/ppermute | solution.py:220
  14.6 2.7 %collective-permute-done.4.arrived.refs_2_ = bf16[384,256]{1,0:T(8,128)(2,1)S(1)} collective-permute-done((bf16[384,256]{1,0:T(8,128)(2,1)S(1)}, bf16[384,256]{1,0:T(8,128)(2,1)S(1)}, u32[]{:S(2)}, u32[]{:S(2)}) %collective-permute-start.4) | collective-permute-done | bytes 196640 | tf_op jit(solution)/shard_map/ppermute | solution.py:220
  18.6 3.2 %collective-permute-start.6 = (bf16[704,256]{1,0:T(8,128)(2,1)S(1)}, bf16[704,256]{1,0:T(8,128)(2,1)S(1)}, u32[]{:S(2)}, u32[]{:S(2)}) collective-permute-start(bf16[704,256]{1,0:T(8,128)(2,1)S(1)} %shard_map.49.refs_0_), channel_id=1, source_target_pairs={{0,3},{1,0},{2,1},{3,2},{4,7},{5,4},{6,5},{7,6},{8,11},{9,8},{10,9... | collective-permute-start | bytes 1081352 | tf_op jit(solution)/shard_map/ppermute | solution.py:220
  24.1 5.6 %collective-permute-done.1.arrived.refs_3_.refs_1_ = bf16[704,256]{1,0:T(8,128)(2,1)S(1)} collective-permute-done((bf16[704,256]{1,0:T(8,128)(2,1)S(1)}, bf16[704,256]{1,0:T(8,128)(2,1)S(1)}, u32[]{:S(2)}, u32[]{:S(2)}) %collective-permute-start.1) | collective-permute-done | bytes 360480 | tf_op jit(solution)/shard_map/ppermute | solution.py:220
  30.5 3.4 %collective-permute-start.5 = (bf16[768,256]{1,0:T(8,128)(2,1)S(1)}, bf16[768,256]{1,0:T(8,128)(2,1)}, u32[]{:S(2)}, u32[]{:S(2)}) collective-permute-start(bf16[768,256]{1,0:T(8,128)(2,1)S(1)} %shard_map.52.refs_0_), channel_id=1, source_target_pairs={{0,1},{1,2},{2,3},{3,0},{4,5},{5,6},{6,7},{7,4},{8,9},{9,10},{10,1... | collective-permute-start | bytes 1179656 | tf_op jit(solution)/shard_map/ppermute | solution.py:220
  33.9 3.5 %collective-permute-done.6.arrived.refs_4_.refs_2_ = bf16[704,256]{1,0:T(8,128)(2,1)S(1)} collective-permute-done((bf16[704,256]{1,0:T(8,128)(2,1)S(1)}, bf16[704,256]{1,0:T(8,128)(2,1)S(1)}, u32[]{:S(2)}, u32[]{:S(2)}) %collective-permute-start.6) | collective-permute-done | bytes 360480 | tf_op jit(solution)/shard_map/ppermute | solution.py:220
  43.5 1.6 %shard_map.54 = (f32[384,256]{1,0:T(8,128)S(1)}, f32[384,256]{1,0:T(8,128)S(1)}, s16[800,256]{1,0:T(8,128)(2,1)S(1)}) custom-call(s32[9]{0:T(128)S(1)} %stack.39.where, bf16[384,256]{1,0:T(8,128)(2,1)S(1)} %copy-done.10, bf16[384,256]{1,0:T(8,128)(2,1)S(1)} %copy-done.15, bf16[384,256]{1,0:T(8,128)(2,1)S(1)} %copy-done.13, bf16[704,256]{1,0:T(8,128)(2,1)S(1)} %copy-done.3, ...), custom_call_target="tpu_custom_call" | custom-call | flops 805306368 | bytes 3473408 | tf_op jit(solution)/shard_map/pallas_call | solution.py:137
  47.8 4.2 %collective-permute-start.7 = (bf16[640,256]{1,0:T(8,128)(2,1)S(1)}, bf16[640,256]{1,0:T(8,128)(2,1)S(1)}, u32[]{:S(2)}, u32[]{:S(2)}) collective-permute-start(bf16[640,256]{1,0:T(8,128)(2,1)S(1)} %shard_map.55.refs_0_), channel_id=1, source_target_pairs={{0,1},{1,2},{2,3},{3,0},{4,5},{5,6},{6,7},{7,4},{8,9},{9,10},{10,1... | collective-permute-start | bytes 983048 | tf_op jit(solution)/shard_map/ppermute | solution.py:220
  52.0 4.1 %collective-permute-done.9.arrived.refs_4_.refs_2_ = bf16[768,256]{1,0:T(8,128)(2,1)} collective-permute-done((bf16[768,256]{1,0:T(8,128)(2,1)}, bf16[768,256]{1,0:T(8,128)(2,1)}, u32[]{:S(2)}, u32[]{:S(2)}) %collective-permute-start.9) | collective-permute-done | bytes 393248 | tf_op jit(solution)/shard_map/ppermute | solution.py:220
  57.3 2.6 %shard_map.57 = (f32[512,256]{1,0:T(8,128)S(1)}, f32[512,256]{1,0:T(8,128)S(1)}, s16[1056,256]{1,0:T(8,128)(2,1)S(1)}) custom-call(s32[9]{0:T(128)S(1)} %stack.39.where, bf16[704,256]{1,0:T(8,128)(2,1)S(1)} %copy-done.8, bf16[704,256]{1,0:T(8,128)(2,1)S(1)} %copy-done.3, bf16[704,256]{1,0:T(8,128)(2,1)S(1)} %copy-done.6, ...), custom_call_target="tpu_custom_call" | custom-call | flops 1073741824 | bytes 3932160 | tf_op jit(solution)/shard_map/pallas_call | solution.py:137
  59.8 1.7 %collective-permute-start.14 = (s16[1056,256]{1,0:T(8,128)(2,1)S(1)}, s16[1056,256]{1,0:T(8,128)(2,1)S(1)}, u32[]{:S(2)}, u32[]{:S(2)}) collective-permute-start(s16[1056,256]{1,0:T(8,128)(2,1)S(1)} %get-tuple-element.36), channel_id=1, source_target_pairs={{0,16},{8,24},{16,0},{24,8},{1,17},{9,25},{17,1},{25,9},{2,18},{10... | collective-permute-start | bytes 1622024 | tf_op jit(solution)/shard_map/ppermute | solution.py:224
  63.1 4.0 %collective-permute-start.10 = (bf16[448,256]{1,0:T(8,128)(2,1)S(1)}, bf16[448,256]{1,0:T(8,128)(2,1)S(1)}, u32[]{:S(2)}, u32[]{:S(2)}) collective-permute-start(bf16[448,256]{1,0:T(8,128)(2,1)S(1)} %shard_map.59.refs_0_), channel_id=1, source_target_pairs={{0,1},{1,2},{2,3},{3,0},{4,5},{5,6},{6,7},{7,4},{8,9},{9,10},{10,1... | collective-permute-start | bytes 688136 | tf_op jit(solution)/shard_map/ppermute | solution.py:220
  67.0 2.2 %collective-permute-done.11.arrived.refs_4_.refs_2_ = bf16[640,256]{1,0:T(8,128)(2,1)S(1)} collective-permute-done((bf16[640,256]{1,0:T(8,128)(2,1)S(1)}, bf16[640,256]{1,0:T(8,128)(2,1)S(1)}, u32[]{:S(2)}, u32[]{:S(2)}) %collective-permute-start.11) | collective-permute-done | bytes 327712 | tf_op jit(solution)/shard_map/ppermute | solution.py:220
  69.8 5.4 %collective-permute-start.12 = (bf16[448,256]{1,0:T(8,128)(2,1)S(1)}, bf16[448,256]{1,0:T(8,128)(2,1)S(1)}, u32[]{:S(2)}, u32[]{:S(2)}) collective-permute-start(bf16[448,256]{1,0:T(8,128)(2,1)S(1)} %shard_map.60.refs_7_), channel_id=1, source_target_pairs={{0,3},{1,0},{2,1},{3,2},{4,7},{5,4},{6,5},{7,6},{8,11},{9,8},{10,9... | collective-permute-start | bytes 688136 | tf_op jit(solution)/shard_map/ppermute | solution.py:220
  75.2 2.5 %shard_map.61 = (f32[512,256]{1,0:T(8,128)S(1)}, f32[512,256]{1,0:T(8,128)S(1)}, s16[1056,256]{1,0:T(8,128)(2,1)S(1)}) custom-call(s32[9]{0:T(128)S(1)} %stack.39.where, bf16[768,256]{1,0:T(8,128)(2,1)S(1)} %shard_map.52.refs_0_, bf16[768,256]{1,0:T(8,128)(2,1)} %collective-permute-done.5.arrived.refs_3_.refs_1_, ...), custom_call_target="tpu_custom_call" | custom-call | flops 1073741824 | bytes 3932160 | tf_op jit(solution)/shard_map/pallas_call | solution.py:137
  78.0 2.9 %collective-permute-done.13.refs_1_ = s16[400,256]{1,0:T(8,128)(2,1)S(1)} collective-permute-done((s16[400,256]{1,0:T(8,128)(2,1)S(1)}, s16[400,256]{1,0:T(8,128)(2,1)S(1)}, u32[]{:S(2)}, u32[]{:S(2)}) %collective-permute-start.13) | collective-permute-done | bytes 204832 | tf_op jit(solution)/shard_map/ppermute | solution.py:224
  82.2 1.6 %shard_map.66 = (f32[384,256]{1,0:T(8,128)S(1)}, f32[384,256]{1,0:T(8,128)S(1)}, s16[800,256]{1,0:T(8,128)(2,1)S(1)}) custom-call(s32[9]{0:T(128)S(1)} %stack.39.where, bf16[640,256]{1,0:T(8,128)(2,1)S(1)} %shard_map.55.refs_0_, bf16[640,256]{1,0:T(8,128)(2,1)S(1)} %collective-permute-done.7.arrived.refs_3_.refs_1_, ...), custom_call_target="tpu_custom_call" | custom-call | flops 805306368 | bytes 3473408 | tf_op jit(solution)/shard_map/pallas_call | solution.py:137
  86.4 1.9 %collective-permute-start.16 = (bf16[128,256]{1,0:T(8,128)(2,1)S(1)}, bf16[128,256]{1,0:T(8,128)(2,1)S(1)}, u32[]{:S(2)}, u32[]{:S(2)}) collective-permute-start(bf16[128,256]{1,0:T(8,128)(2,1)S(1)} %shard_map.65.refs_7_), channel_id=1, source_target_pairs={{0,3},{1,0},{2,1},{3,2},{4,7},{5,4},{6,5},{7,6},{8,11},{9,8},{10,9... | collective-permute-start | bytes 196616 | tf_op jit(solution)/shard_map/ppermute | solution.py:220
  88.4 4.1 %collective-permute-done.17.received_ref.refs_0_ = s16[1056,256]{1,0:T(8,128)(2,1)S(1)} collective-permute-done((s16[1056,256]{1,0:T(8,128)(2,1)S(1)}, s16[1056,256]{1,0:T(8,128)(2,1)S(1)}, u32[]{:S(2)}, u32[]{:S(2)}) %collective-permute-start.17) | collective-permute-done | bytes 540704 | tf_op jit(solution)/shard_map/ppermute | solution.py:224
  101.3 1.6 %collective-permute-done.23.refs_1_ = s16[528,256]{1,0:T(8,128)(2,1)S(1)} collective-permute-done((s16[528,256]{1,0:T(8,128)(2,1)S(1)}, s16[528,256]{1,0:T(8,128)(2,1)S(1)}, u32[]{:S(2)}, u32[]{:S(2)}) %collective-permute-start.23) | collective-permute-done | bytes 270368 | tf_op jit(solution)/shard_map/ppermute | solution.py:224
  105.4 1.9 %collective-permute-done.20.refs_2_ = s16[272,256]{1,0:T(8,128)(2,1)S(1)} collective-permute-done((s16[272,256]{1,0:T(8,128)(2,1)S(1)}, s16[272,256]{1,0:T(8,128)(2,1)S(1)}, u32[]{:S(2)}, u32[]{:S(2)}) %collective-permute-start.20) | collective-permute-done | bytes 139296 | tf_op jit(solution)/shard_map/ppermute | solution.py:224
  107.4 2.5 %psum.7.column_ref = f32[1,256]{1,0:T(1,128)S(1)} all-reduce(f32[1,256]{1,0:T(1,128)S(1)} %get-tuple-element.51), channel_id=1, replica_groups=mesh['layer'=4,'row'=2,'col'=4] {'row'}, use_global_device_ids=true, to_apply=%region_0.1 | all-reduce | flops 256 | bytes 2048 | tf_op jit(solution)/shard_map/psum | solution.py:324
  (94 shorter events, 37.7 us)
Async XLA Ops:
  0.0 22.9 %collective-permute-start.3 = (bf16[512,4,256]{2,1,0:T(4,128)(2,1)}, bf16[512,4,256]{2,1,0:T(4,128)(2,1)S(1)}, u32[]{:S(2)}, u32[]{:S(2)}) collective-permute-start(bf16[512,4,256]{2,1,0:T(4,128)(2,1)} %values_ref.1), channel_id=1, source_target_pairs={{0,4},{4,0},{1,5},{5,1},{2,6},{6,2},{3,7},{7,3},{8,12},{12,8},{9,1... | collective-permute-start | bytes 3145736 | tf_op jit(solution)/shard_map/ppermute | solution.py:220
  2.9 10.5 %collective-permute-start = (bf16[384,256]{1,0:T(8,128)(2,1)S(1)}, bf16[384,256]{1,0:T(8,128)(2,1)S(1)}, u32[]{:S(2)}, u32[]{:S(2)}) collective-permute-start(bf16[384,256]{1,0:T(8,128)(2,1)S(1)} %shard_map.46.refs_0_), channel_id=1, source_target_pairs={{0,1},{1,2},{2,3},{3,0},{4,5},{5,6},{6,7},{7,4},{8,9},{9,10},{10,1... | collective-permute-start | bytes 589832 | tf_op jit(solution)/shard_map/ppermute | solution.py:220
  6.1 11.2 %collective-permute-start.4 = (bf16[384,256]{1,0:T(8,128)(2,1)S(1)}, bf16[384,256]{1,0:T(8,128)(2,1)S(1)}, u32[]{:S(2)}, u32[]{:S(2)}) collective-permute-start(bf16[384,256]{1,0:T(8,128)(2,1)S(1)} %shard_map.47.refs_0_), channel_id=1, source_target_pairs={{0,3},{1,0},{2,1},{3,2},{4,7},{5,4},{6,5},{7,6},{8,11},{9,8},{10,9... | collective-permute-start | bytes 589832 | tf_op jit(solution)/shard_map/ppermute | solution.py:220
  14.6 15.1 %collective-permute-start.1 = (bf16[704,256]{1,0:T(8,128)(2,1)S(1)}, bf16[704,256]{1,0:T(8,128)(2,1)S(1)}, u32[]{:S(2)}, u32[]{:S(2)}) collective-permute-start(bf16[704,256]{1,0:T(8,128)(2,1)S(1)} %shard_map.48.refs_0_), channel_id=1, source_target_pairs={{0,1},{1,2},{2,3},{3,0},{4,5},{5,6},{6,7},{7,4},{8,9},{9,10},{10,1... | collective-permute-start | bytes 1081352 | tf_op jit(solution)/shard_map/ppermute | solution.py:220
  18.6 18.8 %collective-permute-start.6 = (bf16[704,256]{1,0:T(8,128)(2,1)S(1)}, bf16[704,256]{1,0:T(8,128)(2,1)S(1)}, u32[]{:S(2)}, u32[]{:S(2)}) collective-permute-start(bf16[704,256]{1,0:T(8,128)(2,1)S(1)} %shard_map.49.refs_0_), channel_id=1, source_target_pairs={{0,3},{1,0},{2,1},{3,2},{4,7},{5,4},{6,5},{7,6},{8,11},{9,8},{10,9... | collective-permute-start | bytes 1081352 | tf_op jit(solution)/shard_map/ppermute | solution.py:220
  30.5 16.3 %collective-permute-start.5 = (bf16[768,256]{1,0:T(8,128)(2,1)S(1)}, bf16[768,256]{1,0:T(8,128)(2,1)}, u32[]{:S(2)}, u32[]{:S(2)}) collective-permute-start(bf16[768,256]{1,0:T(8,128)(2,1)S(1)} %shard_map.52.refs_0_), channel_id=1, source_target_pairs={{0,1},{1,2},{2,3},{3,0},{4,5},{5,6},{6,7},{7,4},{8,9},{9,10},{10,1... | collective-permute-start | bytes 1179656 | tf_op jit(solution)/shard_map/ppermute | solution.py:220
  38.7 17.4 %collective-permute-start.9 = (bf16[768,256]{1,0:T(8,128)(2,1)}, bf16[768,256]{1,0:T(8,128)(2,1)}, u32[]{:S(2)}, u32[]{:S(2)}) collective-permute-start(bf16[768,256]{1,0:T(8,128)(2,1)} %shard_map.53.refs_7_), channel_id=1, source_target_pairs={{0,3},{1,0},{2,1},{3,2},{4,7},{5,4},{6,5},{7,6},{8,11},{9,8},{10,9... | collective-permute-start | bytes 1179656 | tf_op jit(solution)/shard_map/ppermute | solution.py:220
  45.1 16.4 %collective-permute-start.8 = (s16[800,256]{1,0:T(8,128)(2,1)S(1)}, s16[800,256]{1,0:T(8,128)(2,1)S(1)}, u32[]{:S(2)}, u32[]{:S(2)}) collective-permute-start(s16[800,256]{1,0:T(8,128)(2,1)S(1)} %get-tuple-element.33), channel_id=1, source_target_pairs={{0,8},{8,0},{16,24},{24,16},{1,9},{9,1},{17,25},{25,17},{2,10},{10... | collective-permute-start | bytes 1228808 | tf_op jit(solution)/shard_map/ppermute | solution.py:224
  47.8 14.7 %collective-permute-start.7 = (bf16[640,256]{1,0:T(8,128)(2,1)S(1)}, bf16[640,256]{1,0:T(8,128)(2,1)S(1)}, u32[]{:S(2)}, u32[]{:S(2)}) collective-permute-start(bf16[640,256]{1,0:T(8,128)(2,1)S(1)} %shard_map.55.refs_0_), channel_id=1, source_target_pairs={{0,1},{1,2},{2,3},{3,0},{4,5},{5,6},{6,7},{7,4},{8,9},{9,10},{10,1... | collective-permute-start | bytes 983048 | tf_op jit(solution)/shard_map/ppermute | solution.py:220
  57.2 12.0 %collective-permute-start.11 = (bf16[640,256]{1,0:T(8,128)(2,1)S(1)}, bf16[640,256]{1,0:T(8,128)(2,1)S(1)}, u32[]{:S(2)}, u32[]{:S(2)}) collective-permute-start(bf16[640,256]{1,0:T(8,128)(2,1)S(1)} %shard_map.56.refs_7_), channel_id=1, source_target_pairs={{0,3},{1,0},{2,1},{3,2},{4,7},{5,4},{6,5},{7,6},{8,11},{9,8},{10,9... | collective-permute-start | bytes 983048 | tf_op jit(solution)/shard_map/ppermute | solution.py:220
  59.8 18.0 %collective-permute-start.14 = (s16[1056,256]{1,0:T(8,128)(2,1)S(1)}, s16[1056,256]{1,0:T(8,128)(2,1)S(1)}, u32[]{:S(2)}, u32[]{:S(2)}) collective-permute-start(s16[1056,256]{1,0:T(8,128)(2,1)S(1)} %get-tuple-element.36), channel_id=1, source_target_pairs={{0,16},{8,24},{16,0},{24,8},{1,17},{9,25},{17,1},{25,9},{2,18},{10... | collective-permute-start | bytes 1622024 | tf_op jit(solution)/shard_map/ppermute | solution.py:224
  63.1 18.0 %collective-permute-start.10 = (bf16[448,256]{1,0:T(8,128)(2,1)S(1)}, bf16[448,256]{1,0:T(8,128)(2,1)S(1)}, u32[]{:S(2)}, u32[]{:S(2)}) collective-permute-start(bf16[448,256]{1,0:T(8,128)(2,1)S(1)} %shard_map.59.refs_0_), channel_id=1, source_target_pairs={{0,1},{1,2},{2,3},{3,0},{4,5},{5,6},{6,7},{7,4},{8,9},{9,10},{10,1... | collective-permute-start | bytes 688136 | tf_op jit(solution)/shard_map/ppermute | solution.py:220
  69.8 11.9 %collective-permute-start.12 = (bf16[448,256]{1,0:T(8,128)(2,1)S(1)}, bf16[448,256]{1,0:T(8,128)(2,1)S(1)}, u32[]{:S(2)}, u32[]{:S(2)}) collective-permute-start(bf16[448,256]{1,0:T(8,128)(2,1)S(1)} %shard_map.60.refs_7_), channel_id=1, source_target_pairs={{0,3},{1,0},{2,1},{3,2},{4,7},{5,4},{6,5},{7,6},{8,11},{9,8},{10,9... | collective-permute-start | bytes 688136 | tf_op jit(solution)/shard_map/ppermute | solution.py:220
  75.2 5.8 %collective-permute-start.13 = (s16[400,256]{1,0:T(8,128)(2,1)S(1)}, s16[400,256]{1,0:T(8,128)(2,1)S(1)}, u32[]{:S(2)}, u32[]{:S(2)}) collective-permute-start(s16[400,256]{1,0:T(8,128)(2,1)S(1)} %shard_map.58.refs_0_), channel_id=1, source_target_pairs={{0,16},{8,24},{16,0},{24,8},{1,17},{9,25},{17,1},{25,9},{2,18},{10... | collective-permute-start | bytes 614408 | tf_op jit(solution)/shard_map/ppermute | solution.py:224
  77.7 14.8 %collective-permute-start.17 = (s16[1056,256]{1,0:T(8,128)(2,1)S(1)}, s16[1056,256]{1,0:T(8,128)(2,1)S(1)}, u32[]{:S(2)}, u32[]{:S(2)}) collective-permute-start(s16[1056,256]{1,0:T(8,128)(2,1)S(1)} %get-tuple-element.40), channel_id=1, source_target_pairs={{0,8},{8,0},{16,24},{24,16},{1,9},{9,1},{17,25},{25,17},{2,10},{10... | collective-permute-start | bytes 1622024 | tf_op jit(solution)/shard_map/ppermute | solution.py:224
  83.8 12.5 %collective-permute-start.21 = (s16[800,256]{1,0:T(8,128)(2,1)S(1)}, s16[800,256]{1,0:T(8,128)(2,1)S(1)}, u32[]{:S(2)}, u32[]{:S(2)}) collective-permute-start(s16[800,256]{1,0:T(8,128)(2,1)S(1)} %get-tuple-element.46), channel_id=1, source_target_pairs={{0,16},{8,24},{16,0},{24,8},{1,17},{9,25},{17,1},{25,9},{2,18},{10... | collective-permute-start | bytes 1228808 | tf_op jit(solution)/shard_map/ppermute | solution.py:224
  85.2 14.6 %collective-permute-start.24 = (s16[528,256]{1,0:T(8,128)(2,1)S(1)}, s16[528,256]{1,0:T(8,128)(2,1)S(1)}, u32[]{:S(2)}, u32[]{:S(2)}) collective-permute-start(s16[528,256]{1,0:T(8,128)(2,1)S(1)} %shard_map.62.refs_3_), channel_id=1, source_target_pairs={{0,8},{8,0},{16,24},{24,16},{1,9},{9,1},{17,25},{25,17},{2,10},{10... | collective-permute-start | bytes 811016 | tf_op jit(solution)/shard_map/ppermute | solution.py:224
  86.4 7.0 %collective-permute-start.16 = (bf16[128,256]{1,0:T(8,128)(2,1)S(1)}, bf16[128,256]{1,0:T(8,128)(2,1)S(1)}, u32[]{:S(2)}, u32[]{:S(2)}) collective-permute-start(bf16[128,256]{1,0:T(8,128)(2,1)S(1)} %shard_map.65.refs_7_), channel_id=1, source_target_pairs={{0,3},{1,0},{2,1},{3,2},{4,7},{5,4},{6,5},{7,6},{8,11},{9,8},{10,9... | collective-permute-start | bytes 196616 | tf_op jit(solution)/shard_map/ppermute | solution.py:220
  88.2 6.1 %collective-permute-start.15 = (bf16[128,256]{1,0:T(8,128)(2,1)S(1)}, bf16[128,256]{1,0:T(8,128)(2,1)S(1)}, u32[]{:S(2)}, u32[]{:S(2)}) collective-permute-start(bf16[128,256]{1,0:T(8,128)(2,1)S(1)} %shard_map.64.refs_0_), channel_id=1, source_target_pairs={{0,1},{1,2},{2,3},{3,0},{4,5},{5,6},{6,7},{7,4},{8,9},{9,10},{10,1... | collective-permute-start | bytes 196616 | tf_op jit(solution)/shard_map/ppermute | solution.py:220
  92.7 10.3 %collective-permute-start.23 = (s16[528,256]{1,0:T(8,128)(2,1)S(1)}, s16[528,256]{1,0:T(8,128)(2,1)S(1)}, u32[]{:S(2)}, u32[]{:S(2)}) collective-permute-start(s16[528,256]{1,0:T(8,128)(2,1)S(1)} %shard_map.67.refs_7_), channel_id=1, source_target_pairs={{0,16},{8,24},{16,0},{24,8},{1,17},{9,25},{17,1},{25,9},{2,18},{10... | collective-permute-start | bytes 811016 | tf_op jit(solution)/shard_map/ppermute | solution.py:224
  96.4 6.7 %collective-permute-start.22 = (s16[400,256]{1,0:T(8,128)(2,1)S(1)}, s16[400,256]{1,0:T(8,128)(2,1)S(1)}, u32[]{:S(2)}, u32[]{:S(2)}) collective-permute-start(s16[400,256]{1,0:T(8,128)(2,1)S(1)} %shard_map.69.refs_3_), channel_id=1, source_target_pairs={{0,8},{8,0},{16,24},{24,16},{1,9},{9,1},{17,25},{25,17},{2,10},{10... | collective-permute-start | bytes 614408 | tf_op jit(solution)/shard_map/ppermute | solution.py:224
  97.6 6.8 %collective-permute-start.18 = (s16[272,256]{1,0:T(8,128)(2,1)S(1)}, s16[272,256]{1,0:T(8,128)(2,1)S(1)}, u32[]{:S(2)}, u32[]{:S(2)}) collective-permute-start(s16[272,256]{1,0:T(8,128)(2,1)S(1)} %get-tuple-element.43), channel_id=1, source_target_pairs={{0,8},{8,0},{16,24},{24,16},{1,9},{9,1},{17,25},{25,17},{2,10},{10... | collective-permute-start | bytes 417800 | tf_op jit(solution)/shard_map/ppermute | solution.py:224
  98.5 6.9 %collective-permute-start.19 = (s16[272,256]{1,0:T(8,128)(2,1)S(1)}, s16[272,256]{1,0:T(8,128)(2,1)S(1)}, u32[]{:S(2)}, u32[]{:S(2)}) collective-permute-start(s16[272,256]{1,0:T(8,128)(2,1)S(1)} %get-tuple-element.44), channel_id=1, source_target_pairs={{0,16},{8,24},{16,0},{24,8},{1,17},{9,25},{17,1},{25,9},{2,18},{10... | collective-permute-start | bytes 417800 | tf_op jit(solution)/shard_map/ppermute | solution.py:224
  99.8 7.5 %collective-permute-start.20 = (s16[272,256]{1,0:T(8,128)(2,1)S(1)}, s16[272,256]{1,0:T(8,128)(2,1)S(1)}, u32[]{:S(2)}, u32[]{:S(2)}) collective-permute-start(s16[272,256]{1,0:T(8,128)(2,1)S(1)} %get-tuple-element.45), channel_id=1, source_target_pairs={{0,24},{8,16},{16,8},{24,0},{1,25},{9,17},{17,9},{25,1},{2,26},{10... | collective-permute-start | bytes 417800 | tf_op jit(solution)/shard_map/ppermute | solution.py:224
  (19 other events, 57.7 us)

commit v9 on v8

--- a/solution.py
+++ b/solution.py
@@ -88,25 +88,28 @@
     return ref[at : at + rows, :].astype(jnp.int32).astype(jnp.float32) * unit
 
 
-def partial_kernel(sources, n_pieces, kept, sent, where, *refs):
+def partial_kernel(steps, sources, n_pieces, kept, sent, *refs):
+    layer, row, col = (lax.axis_index(a) for a in ("layer", "row", "col"))
+    n_cols = lax.axis_size("col")
     n_lefts = sum(len(parts) for parts in sources)
     pieces = refs[n_lefts : n_lefts + n_pieces]
     rows = sum(part[2] for part in sources[0])
     outs = refs[-len(kept) - len(sent) :]
-    columns = pieces[0].shape[2]
-
-    def right(source, layer):
-        start = pl.multiple_of(where[2 + 2 * source], TILE)
-        tile = pieces[0][layer, pl.ds(start, TILE), :]
+    _, piece_rows, columns = pieces[0].shape
+
+    def right(step, k):
+        inner = lax.rem(col + (step + n_cols), n_cols) * TILE
+        piece = lax.rem(row - lax.div(inner, piece_rows) + n_pieces, n_pieces)
+        start = pl.multiple_of(lax.rem(inner, piece_rows), TILE)
+        tile = pieces[0][layer ^ k, pl.ds(start, TILE), :]
         for i in range(1, n_pieces):
-            here = where[1 + 2 * source] == i
-            tile = jnp.where(here, pieces[i][layer, pl.ds(start, TILE), :], tile)
+            tile = jnp.where(piece == i, pieces[i][layer ^ k, pl.ds(start, TILE), :], tile)
         return tile
 
     def product(k):
         total = jnp.zeros((rows, columns), jnp.float32)
-        for source, parts in enumerate(sources):
-            tile = right(source, where[0] ^ k)
+        for step, parts in zip(steps, sources):
+            tile = right(step, k)
             terms = [
                 jnp.dot(
                     refs[i][first : first + count, :], tile, preferred_element_type=jnp.float32
@@ -123,7 +126,7 @@
         out[...] = product(k)
 
 
-def partial_products(where, sources, pieces, after, kept, sent):
+def partial_products(steps, sources, pieces, after, kept, sent):
     columns = pieces[0].shape[2]
     rows = sum(part[2] for part in sources[0])
     lefts = [array for parts in sources for array, _, _ in parts]
@@ -135,10 +138,11 @@
         jax.ShapeDtypeStruct((len(ks) * (rows + SCALE_ROWS), columns), jnp.int16) for ks in sent
     ]
     out = pl.pallas_call(
-        functools.partial(partial_kernel, shapes, len(pieces), kept, sent),
+        functools.partial(
+            partial_kernel, tuple(steps), shapes, len(pieces), kept, sent
+        ),
         out_shape=outs,
-        in_specs=[pl.BlockSpec(memory_space=pltpu.SMEM)]
-        + [VMEM] * (len(lefts) + len(pieces))
+        in_specs=[VMEM] * (len(lefts) + len(pieces))
         + [pl.BlockSpec(memory_space=pl.ANY)] * len(after),
         out_specs=[VMEM] * len(outs),
         compiler_params=PARAMS,
@@ -146,7 +150,7 @@
             2 * rows * len(sources) * TILE * columns * n_products,
             2 * len(pieces) * pieces[0].size + 14 * rows * columns,
         ),
-    )(where, *lefts, *pieces, *after)
+    )(*lefts, *pieces, *after)
     return out[: len(kept)], out[len(kept) :]
 
 
@@ -168,29 +172,32 @@
     )(kept, received, after)
 
 
-def combine_kernel(n_received, kept_ref, *refs):
-    received, before_ref = refs[:n_received], refs[n_received]
+def combine_kernel(n_received, n_before, kept_ref, *refs):
+    received, before = refs[:n_received], refs[n_received : n_received + n_before]
     squared_ref, sum_ref = refs[-2:]
     total = kept_ref[...]
     for block in received:
         total += get_fixed(block, 0, total.shape[0])
     squared = total * total
     squared_ref[...] = squared
-    sum_ref[...] = before_ref[...] + jnp.sum(squared, axis=0, keepdims=True)
+    column = jnp.sum(squared, axis=0, keepdims=True)
+    for ref in before:
+        column += ref[...]
+    sum_ref[...] = column
 
 
 def combine(kept, received, before, after):
     return pl.pallas_call(
-        functools.partial(combine_kernel, len(received)),
+        functools.partial(combine_kernel, len(received), len(before)),
         out_shape=(
             jax.ShapeDtypeStruct(kept.shape, jnp.float32),
             jax.ShapeDtypeStruct((1, kept.shape[1]), jnp.float32),
         ),
-        in_specs=[VMEM] * (2 + len(received)) + [pl.BlockSpec(memory_space=pl.ANY)] * len(after),
+        in_specs=[VMEM] * (1 + len(received) + len(before)) + [pl.BlockSpec(memory_space=pl.ANY)] * len(after),
         out_specs=(VMEM, VMEM),
         compiler_params=PARAMS,
         cost_estimate=cost(8 * kept.size, 14 * kept.size),
-    )(kept, *received, before, *after)
+    )(kept, *received, *before, *after)
 
 
 def normalise_kernel(n_chunks, rows_total, column_ref, *refs):
@@ -226,20 +233,14 @@
 
 def per_device(left_values, left_pattern, right_values, right_pattern):
     n_rows, n_cols = lax.axis_size("row"), lax.axis_size("col")
-    layer, row, col = (lax.axis_index(a) for a in ("layer", "row", "col"))
     rows_local, _, columns_local = left_values.shape
-    inner_piece = right_values.shape[0]
     sizes = [rows_local * part // sum(SIXTEENTHS) for part in SIXTEENTHS]
 
     left = left_values.reshape(rows_local, columns_local)
     pattern = left_pattern.reshape(-1)
     reach = n_cols // 2
     away = list(range(1, reach))
-    where = [layer]
-    for source in [0] + [-i for i in away] + away + [reach]:
-        inner = (col + source + n_cols) % n_cols * columns_local
-        where += [(row - inner // inner_piece + n_rows) % n_rows, inner % inner_piece]
-    where = jnp.stack(where).astype(jnp.int32)
+    steps = [0] + [-i for i in away] + away + [reach]
 
     starts = [sum(sizes[:i]) for i in range(len(sizes))]
     own = []
@@ -278,7 +279,7 @@
             ks, sent_ks = (0, second(i)), ((3 - second(i), 3),)
         else:
             ks, sent_ks = (0,), ((1,), (2,), (3,))
-        mine, sent = partial_products(where, sources(i), pieces, last, ks, sent_ks)
+        mine, sent = partial_products(steps, sources(i), pieces, last, ks, sent_ks)
         kept.append(mine)
         received.append([swap(x, k[0]) for x, k in zip(sent, sent_ks)])
         last[:] = [mine[0]]
@@ -296,10 +297,10 @@
         raw.append((shift(right_pattern, "row", i), shift(right_values, "row", i)))
     pieces = []
 
-    squares, columns = [], [jnp.zeros((1, columns_local), jnp.float32)]
+    squares, columns = [], []
 
     def square(i):
-        squared, column = combine(kept[i][0], received[i], columns[-1], last)
+        squared, column = combine(kept[i][0], received[i], columns[-1:], last)
         squares.append(squared)
         columns.append(column)
         last[:] = [column]

time: 111 us -> 104 us (0.937)
  waiting for transfers between devices: 38.4 us -> 54 us
  starting transfers between devices: 38.7 us -> 27.4 us
  local copies, waits for them, and re-layouts: 8.26 us -> 1.9 us
  Pallas kernels: 22.9 us -> 17.4 us
    ppermute x14, waiting for transfers between devices: 25.1 us -> 47.2 us  [shift(): return lax.ppermute(x, axis, [(i, (i + by) % n) for i in range(n)])]
    ppermute x14, starting transfers between devices: 27.4 us -> 12.7 us  [shift(): return lax.ppermute(x, axis, [(i, (i + by) % n) for i in range(n)])]
    ppermute x11, waiting for transfers between devices: 13.3 us -> 6.72 us  [swap(): return lax.ppermute(x, 'layer', [(i, i ^ bits) for i in range(4)])]
    unnamed x36 -> x10, local copies, waits for them, and re-layouts: 8.17 us -> 1.9 us
    pallas_call x10, Pallas kernels: 10.5 us -> 6.72 us  [the longest x5 5.9 us: partial_products(): pl.pallas_call(functools.partial(partial_kernel, tuple(steps), shapes, le...]
    ppermute x11, starting transfers between devices: 11.3 us -> 14.7 us  [swap(): return lax.ppermute(x, 'layer', [(i, i ^ bits) for i in range(4)])]
    pallas_call x12, Pallas kernels: 8.42 us -> 6.74 us  [load(): pl.pallas_call(functools.partial(load_kernel, at, size, parts), out_shape...]
  transfers between devices with their start and end apart: 25 -> 25, of which waited for: 15 -> 14; matrix products, arithmetic and copies ran while one was open for 0% -> 0% of each run, Pallas kernels for 19% -> 16%
where the time goes in v9:
time: 104 us
  waiting for transfers between devices  54 us (52%)
  starting transfers between devices  27.4 us (26%)
  Pallas kernels  17.4 us (17%)
  blocking collectives  2.47 us (2%)
  local copies, waits for them, and re-layouts  1.9 us (2%)
    ppermute x14, waiting for transfers between devices, shift(): return lax.ppermute(x, axis, [(i, (i + by) % n) for i in range(n)])  47.2 us
    ppermute x11, starting transfers between devices, swap(): return lax.ppermute(x, 'layer', [(i, i ^ bits) for i in range(4)])  14.7 us
    ppermute x14, starting transfers between devices, shift(): return lax.ppermute(x, axis, [(i, (i + by) % n) for i in range(n)])  12.7 us
    pallas_call x12, Pallas kernels, load(): pl.pallas_call(functools.partial(load_kernel, at, size, parts), out_shape...  6.74 us
    ppermute x11, waiting for transfers between devices, swap(): return lax.ppermute(x, 'layer', [(i, i ^ bits) for i in range(4)])  6.72 us
    pallas_call x5, Pallas kernels, partial_products(): pl.pallas_call(functools.partial(partial_kernel, tuple(steps), shapes, le...  5.9 us
    psum x1, blocking collectives, per_device(): column = lax.psum(columns[-1], 'row')  2.47 us
    pallas_call x2, Pallas kernels, mask_right(): pl.pallas_call(mask_right_kernel, out_shape=jax.ShapeDtypeStruct((layers,...  2.27 us
  transfers between devices with their start and end apart: 25, of which 14 were waited for; matrix products, arithmetic and copies ran while one was open for 0% of the time, Pallas kernels for 16%

profile of v9, /device:TPU:0, one launch (start us, length us, event | category | flops | bytes accessed | tf_op | source)
XLA Modules:
  0.0 103.5 jit_solution(12353627172116915263)
XLA Ops:
  2.9 2.6 %collective-permute-start = (bf16[384,256]{1,0:T(8,128)(2,1)S(1)}, bf16[384,256]{1,0:T(8,128)(2,1)S(1)}, u32[]{:S(2)}, u32[]{:S(2)}) collective-permute-start(bf16[384,256]{1,0:T(8,128)(2,1)S(1)} %shard_map.46.refs_0_), channel_id=1, source_target_pairs={{0,1},{1,2},{2,3},{3,0},{4,5},{5,6},{6,7},{7,4},{8,9},{9,10},{10,1... | collective-permute-start | bytes 589832 | tf_op jit(solution)/shard_map/ppermute | solution.py:227
  6.1 2.1 %collective-permute-start.4 = (bf16[384,256]{1,0:T(8,128)(2,1)S(1)}, bf16[384,256]{1,0:T(8,128)(2,1)S(1)}, u32[]{:S(2)}, u32[]{:S(2)}) collective-permute-start(bf16[384,256]{1,0:T(8,128)(2,1)S(1)} %shard_map.47.refs_0_), channel_id=1, source_target_pairs={{0,3},{1,0},{2,1},{3,2},{4,7},{5,4},{6,5},{7,6},{8,11},{9,8},{10,9... | collective-permute-start | bytes 589832 | tf_op jit(solution)/shard_map/ppermute | solution.py:227
  8.2 5.2 %collective-permute-done.arrived.refs_1_ = bf16[384,256]{1,0:T(8,128)(2,1)S(1)} collective-permute-done((bf16[384,256]{1,0:T(8,128)(2,1)S(1)}, bf16[384,256]{1,0:T(8,128)(2,1)S(1)}, u32[]{:S(2)}, u32[]{:S(2)}) %collective-permute-start) | collective-permute-done | bytes 196640 | tf_op jit(solution)/shard_map/ppermute | solution.py:227
  14.0 3.3 %collective-permute-done.4.arrived.refs_2_ = bf16[384,256]{1,0:T(8,128)(2,1)S(1)} collective-permute-done((bf16[384,256]{1,0:T(8,128)(2,1)S(1)}, bf16[384,256]{1,0:T(8,128)(2,1)S(1)}, u32[]{:S(2)}, u32[]{:S(2)}) %collective-permute-start.4) | collective-permute-done | bytes 196640 | tf_op jit(solution)/shard_map/ppermute | solution.py:227
  17.9 2.3 %collective-permute-start.6 = (bf16[704,256]{1,0:T(8,128)(2,1)S(1)}, bf16[704,256]{1,0:T(8,128)(2,1)S(1)}, u32[]{:S(2)}, u32[]{:S(2)}) collective-permute-start(bf16[704,256]{1,0:T(8,128)(2,1)S(1)} %shard_map.49.refs_0_), channel_id=1, source_target_pairs={{0,3},{1,0},{2,1},{3,2},{4,7},{5,4},{6,5},{7,6},{8,11},{9,8},{10,9... | collective-permute-start | bytes 1081352 | tf_op jit(solution)/shard_map/ppermute | solution.py:227
  22.5 6.4 %collective-permute-done.1.arrived.refs_3_.refs_1_ = bf16[704,256]{1,0:T(8,128)(2,1)S(1)} collective-permute-done((bf16[704,256]{1,0:T(8,128)(2,1)S(1)}, bf16[704,256]{1,0:T(8,128)(2,1)S(1)}, u32[]{:S(2)}, u32[]{:S(2)}) %collective-permute-start.1) | collective-permute-done | bytes 360480 | tf_op jit(solution)/shard_map/ppermute | solution.py:227
  29.6 7.0 %collective-permute-done.6.arrived.refs_4_.refs_2_ = bf16[704,256]{1,0:T(8,128)(2,1)S(1)} collective-permute-done((bf16[704,256]{1,0:T(8,128)(2,1)S(1)}, bf16[704,256]{1,0:T(8,128)(2,1)S(1)}, u32[]{:S(2)}, u32[]{:S(2)}) %collective-permute-start.6) | collective-permute-done | bytes 360480 | tf_op jit(solution)/shard_map/ppermute | solution.py:227
  38.3 1.6 %collective-permute-start.8 = (s16[800,256]{1,0:T(8,128)(2,1)S(1)}, s16[800,256]{1,0:T(8,128)(2,1)S(1)}, u32[]{:S(2)}, u32[]{:S(2)}) collective-permute-start(s16[800,256]{1,0:T(8,128)(2,1)S(1)} %get-tuple-element.33), channel_id=1, source_target_pairs={{0,8},{8,0},{16,24},{24,16},{1,9},{9,1},{17,25},{25,17},{2,10},{10... | collective-permute-start | bytes 1228808 | tf_op jit(solution)/shard_map/ppermute | solution.py:231
  39.9 5.5 %collective-permute-done.5.arrived.refs_3_.refs_1_ = bf16[768,256]{1,0:T(8,128)(2,1)S(1)} collective-permute-done((bf16[768,256]{1,0:T(8,128)(2,1)S(1)}, bf16[768,256]{1,0:T(8,128)(2,1)S(1)}, u32[]{:S(2)}, u32[]{:S(2)}) %collective-permute-start.5) | collective-permute-done | bytes 393248 | tf_op jit(solution)/shard_map/ppermute | solution.py:227
  46.0 10.3 %collective-permute-done.9.arrived.refs_4_.refs_2_ = bf16[768,256]{1,0:T(8,128)(2,1)S(1)} collective-permute-done((bf16[768,256]{1,0:T(8,128)(2,1)S(1)}, bf16[768,256]{1,0:T(8,128)(2,1)S(1)}, u32[]{:S(2)}, u32[]{:S(2)}) %collective-permute-start.9) | collective-permute-done | bytes 393248 | tf_op jit(solution)/shard_map/ppermute | solution.py:227
  57.0 1.5 %shard_map.57 = (f32[512,256]{1,0:T(8,128)S(1)}, f32[512,256]{1,0:T(8,128)S(1)}, s16[1056,256]{1,0:T(8,128)(2,1)S(1)}) custom-call(bf16[704,256]{1,0:T(8,128)(2,1)S(1)} %shard_map.48.refs_0_, bf16[704,256]{1,0:T(8,128)(2,1)S(1)} %collective-permute-done.1.arrived.refs_3_.refs_1_, bf16[704,256]{1,0:T(8,128)(2,1)S(1)} %collective-permute-done.6.arrived.refs_4_.refs_2_, ...), custom_call_target="tpu_custom_call" | custom-call | flops 1073741824 | bytes 3932160 | tf_op jit(solution)/shard_map/pallas_call | solution.py:140
  58.4 1.6 %collective-permute-start.14 = (s16[1056,256]{1,0:T(8,128)(2,1)S(1)}, s16[1056,256]{1,0:T(8,128)(2,1)S(1)}, u32[]{:S(2)}, u32[]{:S(2)}) collective-permute-start(s16[1056,256]{1,0:T(8,128)(2,1)S(1)} %get-tuple-element.36), channel_id=1, source_target_pairs={{0,16},{8,24},{16,0},{24,8},{1,17},{9,25},{17,1},{25,9},{2,18},{10... | collective-permute-start | bytes 1622024 | tf_op jit(solution)/shard_map/ppermute | solution.py:231
  60.8 2.0 %collective-permute-start.10 = (bf16[448,256]{1,0:T(8,128)(2,1)S(1)}, bf16[448,256]{1,0:T(8,128)(2,1)S(1)}, u32[]{:S(2)}, u32[]{:S(2)}) collective-permute-start(bf16[448,256]{1,0:T(8,128)(2,1)S(1)} %shard_map.59.refs_0_), channel_id=1, source_target_pairs={{0,1},{1,2},{2,3},{3,0},{4,5},{5,6},{6,7},{7,4},{8,9},{9,10},{10,1... | collective-permute-start | bytes 688136 | tf_op jit(solution)/shard_map/ppermute | solution.py:227
  62.8 7.2 %collective-permute-done.11.arrived.refs_4_.refs_2_ = bf16[640,256]{1,0:T(8,128)(2,1)S(1)} collective-permute-done((bf16[640,256]{1,0:T(8,128)(2,1)S(1)}, bf16[640,256]{1,0:T(8,128)(2,1)S(1)}, u32[]{:S(2)}, u32[]{:S(2)}) %collective-permute-start.11) | collective-permute-done | bytes 327712 | tf_op jit(solution)/shard_map/ppermute | solution.py:227
  70.7 1.8 %collective-permute-start.13 = (s16[400,256]{1,0:T(8,128)(2,1)S(1)}, s16[400,256]{1,0:T(8,128)(2,1)S(1)}, u32[]{:S(2)}, u32[]{:S(2)}) collective-permute-start(s16[400,256]{1,0:T(8,128)(2,1)S(1)} %shard_map.58.refs_0_), channel_id=1, source_target_pairs={{0,16},{8,24},{16,0},{24,8},{1,17},{9,25},{17,1},{25,9},{2,18},{10... | collective-permute-start | bytes 614408 | tf_op jit(solution)/shard_map/ppermute | solution.py:231
  72.5 1.4 %shard_map.61 = (f32[512,256]{1,0:T(8,128)S(1)}, f32[512,256]{1,0:T(8,128)S(1)}, s16[1056,256]{1,0:T(8,128)(2,1)S(1)}) custom-call(bf16[768,256]{1,0:T(8,128)(2,1)S(1)} %shard_map.52.refs_0_, bf16[768,256]{1,0:T(8,128)(2,1)S(1)} %collective-permute-done.5.arrived.refs_3_.refs_1_, bf16[768,256]{1,0:T(8,128)(2,1)S(1)} %collective-permute-done.9.arrived.refs_4_.refs_2_, ...), custom_call_target="tpu_custom_call" | custom-call | flops 1073741824 | bytes 3932160 | tf_op jit(solution)/shard_map/pallas_call | solution.py:140
  74.0 1.6 %collective-permute-start.17 = (s16[1056,256]{1,0:T(8,128)(2,1)S(1)}, s16[1056,256]{1,0:T(8,128)(2,1)S(1)}, u32[]{:S(2)}, u32[]{:S(2)}) collective-permute-start(s16[1056,256]{1,0:T(8,128)(2,1)S(1)} %get-tuple-element.40), channel_id=1, source_target_pairs={{0,8},{8,0},{16,24},{24,16},{1,9},{9,1},{17,25},{25,17},{2,10},{10... | collective-permute-start | bytes 1622024 | tf_op jit(solution)/shard_map/ppermute | solution.py:231
  78.9 1.8 %collective-permute-start.21 = (s16[800,256]{1,0:T(8,128)(2,1)S(1)}, s16[800,256]{1,0:T(8,128)(2,1)S(1)}, u32[]{:S(2)}, u32[]{:S(2)}) collective-permute-start(s16[800,256]{1,0:T(8,128)(2,1)S(1)} %get-tuple-element.46), channel_id=1, source_target_pairs={{0,16},{8,24},{16,0},{24,8},{1,17},{9,25},{17,1},{25,9},{2,18},{10... | collective-permute-start | bytes 1228808 | tf_op jit(solution)/shard_map/ppermute | solution.py:231
  80.7 1.5 %collective-permute-start.24 = (s16[528,256]{1,0:T(8,128)(2,1)S(1)}, s16[528,256]{1,0:T(8,128)(2,1)S(1)}, u32[]{:S(2)}, u32[]{:S(2)}) collective-permute-start(s16[528,256]{1,0:T(8,128)(2,1)S(1)} %shard_map.62.refs_2_), channel_id=1, source_target_pairs={{0,8},{8,0},{16,24},{24,16},{1,9},{9,1},{17,25},{25,17},{2,10},{10... | collective-permute-start | bytes 811016 | tf_op jit(solution)/shard_map/ppermute | solution.py:231
  83.5 1.7 %collective-permute-start.15 = (bf16[128,256]{1,0:T(8,128)(2,1)S(1)}, bf16[128,256]{1,0:T(8,128)(2,1)S(1)}, u32[]{:S(2)}, u32[]{:S(2)}) collective-permute-start(bf16[128,256]{1,0:T(8,128)(2,1)S(1)} %shard_map.64.refs_0_), channel_id=1, source_target_pairs={{0,1},{1,2},{2,3},{3,0},{4,5},{5,6},{6,7},{7,4},{8,9},{9,10},{10,1... | collective-permute-start | bytes 196616 | tf_op jit(solution)/shard_map/ppermute | solution.py:227
  85.1 1.7 %collective-permute-done.17.received_ref.refs_0_ = s16[1056,256]{1,0:T(8,128)(2,1)S(1)} collective-permute-done((s16[1056,256]{1,0:T(8,128)(2,1)S(1)}, s16[1056,256]{1,0:T(8,128)(2,1)S(1)}, u32[]{:S(2)}, u32[]{:S(2)}) %collective-permute-start.17) | collective-permute-done | bytes 540704 | tf_op jit(solution)/shard_map/ppermute | solution.py:231
  87.4 2.2 %collective-permute-done.15.refs_3_ = bf16[128,256]{1,0:T(8,128)(2,1)S(1)} collective-permute-done((bf16[128,256]{1,0:T(8,128)(2,1)S(1)}, bf16[128,256]{1,0:T(8,128)(2,1)S(1)}, u32[]{:S(2)}, u32[]{:S(2)}) %collective-permute-start.15) | collective-permute-done | bytes 65568 | tf_op jit(solution)/shard_map/ppermute | solution.py:227
  98.1 1.8 %collective-permute-done.20.refs_2_ = s16[272,256]{1,0:T(8,128)(2,1)S(1)} collective-permute-done((s16[272,256]{1,0:T(8,128)(2,1)S(1)}, s16[272,256]{1,0:T(8,128)(2,1)S(1)}, u32[]{:S(2)}, u32[]{:S(2)}) %collective-permute-start.20) | collective-permute-done | bytes 139296 | tf_op jit(solution)/shard_map/ppermute | solution.py:231
  100.0 2.5 %psum.7.column_ref = f32[1,256]{1,0:T(1,128)S(1)} all-reduce(f32[1,256]{1,0:T(1,128)S(1)} %get-tuple-element.51), channel_id=1, replica_groups=mesh['layer'=4,'row'=2,'col'=4] {'row'}, use_global_device_ids=true, to_apply=%region_0.0 | all-reduce | flops 256 | bytes 2048 | tf_op jit(solution)/shard_map/psum | solution.py:325
  (66 shorter events, 26.6 us)
Async XLA Ops:
  0.0 21.4 %collective-permute-start.3 = (bf16[512,4,256]{2,1,0:T(4,128)(2,1)}, bf16[512,4,256]{2,1,0:T(4,128)(2,1)S(1)}, u32[]{:S(2)}, u32[]{:S(2)}) collective-permute-start(bf16[512,4,256]{2,1,0:T(4,128)(2,1)} %values_ref.1), channel_id=1, source_target_pairs={{0,4},{4,0},{1,5},{5,1},{2,6},{6,2},{3,7},{7,3},{8,12},{12,8},{9,1... | collective-permute-start | bytes 3145736 | tf_op jit(solution)/shard_map/ppermute | solution.py:227
  2.9 10.5 %collective-permute-start = (bf16[384,256]{1,0:T(8,128)(2,1)S(1)}, bf16[384,256]{1,0:T(8,128)(2,1)S(1)}, u32[]{:S(2)}, u32[]{:S(2)}) collective-permute-start(bf16[384,256]{1,0:T(8,128)(2,1)S(1)} %shard_map.46.refs_0_), channel_id=1, source_target_pairs={{0,1},{1,2},{2,3},{3,0},{4,5},{5,6},{6,7},{7,4},{8,9},{9,10},{10,1... | collective-permute-start | bytes 589832 | tf_op jit(solution)/shard_map/ppermute | solution.py:227
  6.1 11.2 %collective-permute-start.4 = (bf16[384,256]{1,0:T(8,128)(2,1)S(1)}, bf16[384,256]{1,0:T(8,128)(2,1)S(1)}, u32[]{:S(2)}, u32[]{:S(2)}) collective-permute-start(bf16[384,256]{1,0:T(8,128)(2,1)S(1)} %shard_map.47.refs_0_), channel_id=1, source_target_pairs={{0,3},{1,0},{2,1},{3,2},{4,7},{5,4},{6,5},{7,6},{8,11},{9,8},{10,9... | collective-permute-start | bytes 589832 | tf_op jit(solution)/shard_map/ppermute | solution.py:227
  14.0 15.0 %collective-permute-start.1 = (bf16[704,256]{1,0:T(8,128)(2,1)S(1)}, bf16[704,256]{1,0:T(8,128)(2,1)S(1)}, u32[]{:S(2)}, u32[]{:S(2)}) collective-permute-start(bf16[704,256]{1,0:T(8,128)(2,1)S(1)} %shard_map.48.refs_0_), channel_id=1, source_target_pairs={{0,1},{1,2},{2,3},{3,0},{4,5},{5,6},{6,7},{7,4},{8,9},{9,10},{10,1... | collective-permute-start | bytes 1081352 | tf_op jit(solution)/shard_map/ppermute | solution.py:227
  17.9 18.6 %collective-permute-start.6 = (bf16[704,256]{1,0:T(8,128)(2,1)S(1)}, bf16[704,256]{1,0:T(8,128)(2,1)S(1)}, u32[]{:S(2)}, u32[]{:S(2)}) collective-permute-start(bf16[704,256]{1,0:T(8,128)(2,1)S(1)} %shard_map.49.refs_0_), channel_id=1, source_target_pairs={{0,3},{1,0},{2,1},{3,2},{4,7},{5,4},{6,5},{7,6},{8,11},{9,8},{10,9... | collective-permute-start | bytes 1081352 | tf_op jit(solution)/shard_map/ppermute | solution.py:227
  29.5 15.8 %collective-permute-start.5 = (bf16[768,256]{1,0:T(8,128)(2,1)S(1)}, bf16[768,256]{1,0:T(8,128)(2,1)S(1)}, u32[]{:S(2)}, u32[]{:S(2)}) collective-permute-start(bf16[768,256]{1,0:T(8,128)(2,1)S(1)} %shard_map.52.refs_0_), channel_id=1, source_target_pairs={{0,1},{1,2},{2,3},{3,0},{4,5},{5,6},{6,7},{7,4},{8,9},{9,10},{10,1... | collective-permute-start | bytes 1179656 | tf_op jit(solution)/shard_map/ppermute | solution.py:227
  37.1 19.2 %collective-permute-start.9 = (bf16[768,256]{1,0:T(8,128)(2,1)S(1)}, bf16[768,256]{1,0:T(8,128)(2,1)S(1)}, u32[]{:S(2)}, u32[]{:S(2)}) collective-permute-start(bf16[768,256]{1,0:T(8,128)(2,1)S(1)} %shard_map.53.refs_7_), channel_id=1, source_target_pairs={{0,3},{1,0},{2,1},{3,2},{4,7},{5,4},{6,5},{7,6},{8,11},{9,8},{10,9... | collective-permute-start | bytes 1179656 | tf_op jit(solution)/shard_map/ppermute | solution.py:227
  38.3 21.8 %collective-permute-start.8 = (s16[800,256]{1,0:T(8,128)(2,1)S(1)}, s16[800,256]{1,0:T(8,128)(2,1)S(1)}, u32[]{:S(2)}, u32[]{:S(2)}) collective-permute-start(s16[800,256]{1,0:T(8,128)(2,1)S(1)} %get-tuple-element.33), channel_id=1, source_target_pairs={{0,8},{8,0},{16,24},{24,16},{1,9},{9,1},{17,25},{25,17},{2,10},{10... | collective-permute-start | bytes 1228808 | tf_op jit(solution)/shard_map/ppermute | solution.py:231
  45.9 14.3 %collective-permute-start.7 = (bf16[640,256]{1,0:T(8,128)(2,1)S(1)}, bf16[640,256]{1,0:T(8,128)(2,1)S(1)}, u32[]{:S(2)}, u32[]{:S(2)}) collective-permute-start(bf16[640,256]{1,0:T(8,128)(2,1)S(1)} %shard_map.55.refs_0_), channel_id=1, source_target_pairs={{0,1},{1,2},{2,3},{3,0},{4,5},{5,6},{6,7},{7,4},{8,9},{9,10},{10,1... | collective-permute-start | bytes 983048 | tf_op jit(solution)/shard_map/ppermute | solution.py:227
  56.9 13.2 %collective-permute-start.11 = (bf16[640,256]{1,0:T(8,128)(2,1)S(1)}, bf16[640,256]{1,0:T(8,128)(2,1)S(1)}, u32[]{:S(2)}, u32[]{:S(2)}) collective-permute-start(bf16[640,256]{1,0:T(8,128)(2,1)S(1)} %shard_map.56.refs_7_), channel_id=1, source_target_pairs={{0,3},{1,0},{2,1},{3,2},{4,7},{5,4},{6,5},{7,6},{8,11},{9,8},{10,9... | collective-permute-start | bytes 983048 | tf_op jit(solution)/shard_map/ppermute | solution.py:227
  58.4 17.1 %collective-permute-start.14 = (s16[1056,256]{1,0:T(8,128)(2,1)S(1)}, s16[1056,256]{1,0:T(8,128)(2,1)S(1)}, u32[]{:S(2)}, u32[]{:S(2)}) collective-permute-start(s16[1056,256]{1,0:T(8,128)(2,1)S(1)} %get-tuple-element.36), channel_id=1, source_target_pairs={{0,16},{8,24},{16,0},{24,8},{1,17},{9,25},{17,1},{25,9},{2,18},{10... | collective-permute-start | bytes 1622024 | tf_op jit(solution)/shard_map/ppermute | solution.py:231
  60.8 15.9 %collective-permute-start.10 = (bf16[448,256]{1,0:T(8,128)(2,1)S(1)}, bf16[448,256]{1,0:T(8,128)(2,1)S(1)}, u32[]{:S(2)}, u32[]{:S(2)}) collective-permute-start(bf16[448,256]{1,0:T(8,128)(2,1)S(1)} %shard_map.59.refs_0_), channel_id=1, source_target_pairs={{0,1},{1,2},{2,3},{3,0},{4,5},{5,6},{6,7},{7,4},{8,9},{9,10},{10,1... | collective-permute-start | bytes 688136 | tf_op jit(solution)/shard_map/ppermute | solution.py:227
  70.6 6.6 %collective-permute-start.12 = (bf16[448,256]{1,0:T(8,128)(2,1)S(1)}, bf16[448,256]{1,0:T(8,128)(2,1)S(1)}, u32[]{:S(2)}, u32[]{:S(2)}) collective-permute-start(bf16[448,256]{1,0:T(8,128)(2,1)S(1)} %shard_map.60.refs_7_), channel_id=1, source_target_pairs={{0,3},{1,0},{2,1},{3,2},{4,7},{5,4},{6,5},{7,6},{8,11},{9,8},{10,9... | collective-permute-start | bytes 688136 | tf_op jit(solution)/shard_map/ppermute | solution.py:227
  70.7 5.8 %collective-permute-start.13 = (s16[400,256]{1,0:T(8,128)(2,1)S(1)}, s16[400,256]{1,0:T(8,128)(2,1)S(1)}, u32[]{:S(2)}, u32[]{:S(2)}) collective-permute-start(s16[400,256]{1,0:T(8,128)(2,1)S(1)} %shard_map.58.refs_0_), channel_id=1, source_target_pairs={{0,16},{8,24},{16,0},{24,8},{1,17},{9,25},{17,1},{25,9},{2,18},{10... | collective-permute-start | bytes 614408 | tf_op jit(solution)/shard_map/ppermute | solution.py:231
  74.0 12.9 %collective-permute-start.17 = (s16[1056,256]{1,0:T(8,128)(2,1)S(1)}, s16[1056,256]{1,0:T(8,128)(2,1)S(1)}, u32[]{:S(2)}, u32[]{:S(2)}) collective-permute-start(s16[1056,256]{1,0:T(8,128)(2,1)S(1)} %get-tuple-element.40), channel_id=1, source_target_pairs={{0,8},{8,0},{16,24},{24,16},{1,9},{9,1},{17,25},{25,17},{2,10},{10... | collective-permute-start | bytes 1622024 | tf_op jit(solution)/shard_map/ppermute | solution.py:231
  78.9 11.5 %collective-permute-start.21 = (s16[800,256]{1,0:T(8,128)(2,1)S(1)}, s16[800,256]{1,0:T(8,128)(2,1)S(1)}, u32[]{:S(2)}, u32[]{:S(2)}) collective-permute-start(s16[800,256]{1,0:T(8,128)(2,1)S(1)} %get-tuple-element.46), channel_id=1, source_target_pairs={{0,16},{8,24},{16,0},{24,8},{1,17},{9,25},{17,1},{25,9},{2,18},{10... | collective-permute-start | bytes 1228808 | tf_op jit(solution)/shard_map/ppermute | solution.py:231
  80.7 13.0 %collective-permute-start.24 = (s16[528,256]{1,0:T(8,128)(2,1)S(1)}, s16[528,256]{1,0:T(8,128)(2,1)S(1)}, u32[]{:S(2)}, u32[]{:S(2)}) collective-permute-start(s16[528,256]{1,0:T(8,128)(2,1)S(1)} %shard_map.62.refs_2_), channel_id=1, source_target_pairs={{0,8},{8,0},{16,24},{24,16},{1,9},{9,1},{17,25},{25,17},{2,10},{10... | collective-permute-start | bytes 811016 | tf_op jit(solution)/shard_map/ppermute | solution.py:231
  82.2 5.2 %collective-permute-start.16 = (bf16[128,256]{1,0:T(8,128)(2,1)S(1)}, bf16[128,256]{1,0:T(8,128)(2,1)S(1)}, u32[]{:S(2)}, u32[]{:S(2)}) collective-permute-start(bf16[128,256]{1,0:T(8,128)(2,1)S(1)} %shard_map.65.refs_7_), channel_id=1, source_target_pairs={{0,3},{1,0},{2,1},{3,2},{4,7},{5,4},{6,5},{7,6},{8,11},{9,8},{10,9... | collective-permute-start | bytes 196616 | tf_op jit(solution)/shard_map/ppermute | solution.py:227
  83.5 6.1 %collective-permute-start.15 = (bf16[128,256]{1,0:T(8,128)(2,1)S(1)}, bf16[128,256]{1,0:T(8,128)(2,1)S(1)}, u32[]{:S(2)}, u32[]{:S(2)}) collective-permute-start(bf16[128,256]{1,0:T(8,128)(2,1)S(1)} %shard_map.64.refs_0_), channel_id=1, source_target_pairs={{0,1},{1,2},{2,3},{3,0},{4,5},{5,6},{6,7},{7,4},{8,9},{9,10},{10,1... | collective-permute-start | bytes 196616 | tf_op jit(solution)/shard_map/ppermute | solution.py:227
  87.0 8.3 %collective-permute-start.23 = (s16[528,256]{1,0:T(8,128)(2,1)S(1)}, s16[528,256]{1,0:T(8,128)(2,1)S(1)}, u32[]{:S(2)}, u32[]{:S(2)}) collective-permute-start(s16[528,256]{1,0:T(8,128)(2,1)S(1)} %shard_map.67.refs_7_), channel_id=1, source_target_pairs={{0,16},{8,24},{16,0},{24,8},{1,17},{9,25},{17,1},{25,9},{2,18},{10... | collective-permute-start | bytes 811016 | tf_op jit(solution)/shard_map/ppermute | solution.py:231
  90.5 6.1 %collective-permute-start.22 = (s16[400,256]{1,0:T(8,128)(2,1)S(1)}, s16[400,256]{1,0:T(8,128)(2,1)S(1)}, u32[]{:S(2)}, u32[]{:S(2)}) collective-permute-start(s16[400,256]{1,0:T(8,128)(2,1)S(1)} %shard_map.69.refs_3_), channel_id=1, source_target_pairs={{0,8},{8,0},{16,24},{24,16},{1,9},{9,1},{17,25},{25,17},{2,10},{10... | collective-permute-start | bytes 614408 | tf_op jit(solution)/shard_map/ppermute | solution.py:231
  91.6 6.4 %collective-permute-start.18 = (s16[272,256]{1,0:T(8,128)(2,1)S(1)}, s16[272,256]{1,0:T(8,128)(2,1)S(1)}, u32[]{:S(2)}, u32[]{:S(2)}) collective-permute-start(s16[272,256]{1,0:T(8,128)(2,1)S(1)} %get-tuple-element.43), channel_id=1, source_target_pairs={{0,8},{8,0},{16,24},{24,16},{1,9},{9,1},{17,25},{25,17},{2,10},{10... | collective-permute-start | bytes 417800 | tf_op jit(solution)/shard_map/ppermute | solution.py:231
  92.6 5.5 %collective-permute-start.19 = (s16[272,256]{1,0:T(8,128)(2,1)S(1)}, s16[272,256]{1,0:T(8,128)(2,1)S(1)}, u32[]{:S(2)}, u32[]{:S(2)}) collective-permute-start(s16[272,256]{1,0:T(8,128)(2,1)S(1)} %get-tuple-element.44), channel_id=1, source_target_pairs={{0,16},{8,24},{16,0},{24,8},{1,17},{9,25},{17,1},{25,9},{2,18},{10... | collective-permute-start | bytes 417800 | tf_op jit(solution)/shard_map/ppermute | solution.py:231
  93.7 6.1 %collective-permute-start.20 = (s16[272,256]{1,0:T(8,128)(2,1)S(1)}, s16[272,256]{1,0:T(8,128)(2,1)S(1)}, u32[]{:S(2)}, u32[]{:S(2)}) collective-permute-start(s16[272,256]{1,0:T(8,128)(2,1)S(1)} %get-tuple-element.45), channel_id=1, source_target_pairs={{0,24},{8,16},{16,8},{24,0},{1,25},{9,17},{17,9},{25,1},{2,26},{10... | collective-permute-start | bytes 417800 | tf_op jit(solution)/shard_map/ppermute | solution.py:231
  (6 other events, 23.1 us)

commit v10 on v9

--- a/solution.py
+++ b/solution.py
@@ -9,7 +9,8 @@
 from jax.sharding import PartitionSpec as P
 
 TILE = 256
-SIXTEENTHS = (3, 4, 4, 3, 2)
+SIXTEENTHS = (3, 3, 3, 3, 1, 3)
+MINUS = (3, 3, 3, 3, 1, 3)
 SCALE_ROWS = 16
 CODE = 64.0
 TOP = 32767.0
@@ -200,9 +201,9 @@
     )(kept, *received, *before, *after)
 
 
-def normalise_kernel(n_chunks, rows_total, column_ref, *refs):
-    chunks, out_ref = refs[:n_chunks], refs[n_chunks]
-    colmean = column_ref[...] / rows_total
+def normalise_kernel(n_columns, rows_total, *refs):
+    columns, chunks, out_ref = refs[:n_columns], refs[n_columns:-1], refs[-1]
+    colmean = sum(ref[...] for ref in columns) / rows_total
     at = 0
     for chunk in chunks:
         rows = chunk.shape[0]
@@ -210,16 +211,16 @@
         at += rows
 
 
-def normalise(column, chunks, rows_total):
+def normalise(sums, chunks, rows_total):
     rows, columns = sum(chunk.shape[0] for chunk in chunks), chunks[0].shape[1]
     return pl.pallas_call(
-        functools.partial(normalise_kernel, len(chunks), rows_total),
+        functools.partial(normalise_kernel, len(sums), rows_total),
         out_shape=jax.ShapeDtypeStruct((rows, columns), jnp.bfloat16),
-        in_specs=[VMEM] * (1 + len(chunks)),
+        in_specs=[VMEM] * (len(sums) + len(chunks)),
         out_specs=VMEM,
         compiler_params=PARAMS,
         cost_estimate=cost(4 * rows * columns, 6 * rows * columns),
-    )(column, *chunks)
+    )(*sums, *chunks)
 
 
 def shift(x, axis, by):
@@ -234,48 +235,70 @@
 def per_device(left_values, left_pattern, right_values, right_pattern):
     n_rows, n_cols = lax.axis_size("row"), lax.axis_size("col")
     rows_local, _, columns_local = left_values.shape
-    sizes = [rows_local * part // sum(SIXTEENTHS) for part in SIXTEENTHS]
+    unit = rows_local // sum(SIXTEENTHS)
+    ends = [[unit * sum(cut[: i + 1]) for i in range(len(cut))] for cut in (SIXTEENTHS, MINUS)]
+    spans = [list(zip([0] + end, end)) for end in ends]
+    chunks = spans[0]
 
     left = left_values.reshape(rows_local, columns_local)
     pattern = left_pattern.reshape(-1)
     reach = n_cols // 2
     away = list(range(1, reach))
     steps = [0] + [-i for i in away] + away + [reach]
-
-    starts = [sum(sizes[:i]) for i in range(len(sizes))]
+    halves = [[], []]
+    for start, end in chunks:
+        middle = (start + end) // 2 if end < rows_local else end
+        halves[0].append((start, middle))
+        halves[1].append((middle, end))
+
     own = []
-    found = [([], []) for _ in sizes]
+    found = [[[] for _ in range(reach)] for _ in (0, 1)]
     kept, received, last = [], [], []
+    moving = [[], []]
+    arrived = [left, left]
+
+    def within(spans, start, end):
+        cut = [(max(a, start), min(b, end)) for a, b in spans]
+        return [(a, b) for a, b in cut if a < b]
 
     def open_slot(slot):
-        at, size = (starts[slot], sizes[slot]) if slot < len(sizes) else (0, 0)
         for d in (0, 1):
-            riders = [c for c in range(min(slot, len(sizes))) if len(found[c][d]) < reach]
-            parts = []
-            for c in riders:
-                _, first, rows = found[c][d][-1]
-                if len(found[c][d]) == reach - 1:
-                    first, rows = first + d * (rows // 2), rows // 2
-                parts.append((first, rows))
-            arrived = found[riders[0]][d][-1][0] if riders else left
-            block = load(left, pattern, at, size, arrived, tuple(parts), last)
+            riders = []
+            for step, (start, end), first in moving[d]:
+                if step < reach:
+                    on = [(start, end)] if step < reach - 1 else within(halves[d], start, end)
+                    riders += [(step + 1, span, first + span[0] - start) for span in on]
+            new = spans[d][slot] if slot < len(spans[d]) else (0, 0)
+            if not riders and new == (0, 0):
+                continue
+            parts = tuple((first, span[1] - span[0]) for _, span, first in riders)
+            block = load(left, pattern, new[0], new[1] - new[0], arrived[d], parts, last)
             last[:] = [block]
-            got = shift(block, "col", 1 - 2 * d)
-            first = 0
-            for c, (_, rows) in zip(riders, parts):
-                found[c][d].append((got, first, rows))
-                first += rows
-            if size:
-                found[slot][d].append((got, first, size))
-                if d == 0:
-                    own.append((block, first, size))
+            arrived[d] = shift(block, "col", 1 - 2 * d)
+            moving[d], first = [], 0
+            for step, span, _ in riders + [(1, new, 0)] * (new != (0, 0)):
+                moving[d].append((step, span, first))
+                found[d][step - 1].append((span, arrived[d], first))
+                first += span[1] - span[0]
+            if d == 0 and new != (0, 0):
+                own.append((new, block, first - (new[1] - new[0])))
 
     def sources(i):
-        (*below, last_below), (*above, last_above) = found[i]
-        return [[part] for part in [own[i]] + below + above] + [[last_below, last_above]]
+        held = [own] + [found[d][j - 1] for d in (0, 1) for j in away]
+        held += [found[0][reach - 1] + found[1][reach - 1]]
+        parts = []
+        for entries in held:
+            met = [
+                (rows, array, first + rows[0] - span[0])
+                for span, array, first in entries
+                for rows in within([span], *chunks[i])
+            ]
+            met.sort(key=lambda entry: entry[0])
+            parts.append([(array, first, rows[1] - rows[0]) for rows, array, first in met])
+        return parts
 
     def sum_chunk(i):
-        if i + 1 < len(sizes):
+        if i + 1 < len(chunks):
             ks, sent_ks = (0, second(i)), ((3 - second(i), 3),)
         else:
             ks, sent_ks = (0,), ((1,), (2,), (3,))
@@ -306,8 +329,8 @@
         last[:] = [column]
 
     opened = 0
-    for i in range(len(sizes)):
-        while opened < min(len(sizes) + reach - 1, i + reach + 1):
+    for i in range(len(chunks)):
+        while opened < min(len(chunks) + reach - 1, i + reach + 1):
             open_slot(opened)
             opened += 1
             if opened == 2:
@@ -317,13 +340,13 @@
         sum_chunk(i)
         if i > 0:
             send_on(i - 1)
-        if 1 < i < len(sizes) - 2:
+        if 1 < i < len(chunks) - 2:
             square(i - 2)
-    for i in range(len(squares), len(sizes)):
+    for i in range(len(squares), len(chunks)):
         square(i)
 
-    column = lax.psum(columns[-1], "row")
-    out = normalise(column, squares, rows_local * n_rows)
+    sums = columns[-1:] + [shift(columns[-1], "row", i) for i in range(1, n_rows)]
+    out = normalise(sums, squares, rows_local * n_rows)
     return out.reshape(rows_local, 1, columns_local)
 
 

time: 104 us -> 106 us (1.019)
  starting transfers between devices: 27.4 us -> 47.4 us
  waiting for transfers between devices: 54 us -> 37.8 us
  blocking collectives: 2.47 us -> 0 us
    ppermute x14 -> x16, starting transfers between devices: 12.7 us -> 29.3 us  [shift(): return lax.ppermute(x, axis, [(i, (i + by) % n) for i in range(n)])]
    ppermute x14 -> x16, waiting for transfers between devices: 47.2 us -> 31.2 us  [shift(): return lax.ppermute(x, axis, [(i, (i + by) % n) for i in range(n)])]
    ppermute x11 -> x13, starting transfers between devices: 14.7 us -> 18.1 us  [swap(): return lax.ppermute(x, 'layer', [(i, i ^ bits) for i in range(4)])]
    psum x1 -> x0, blocking collectives: 2.47 us -> none  [per_device(): column = lax.psum(columns[-1], 'row')]
    pallas_call x12 -> x13, Pallas kernels: 6.74 us -> 7.3 us  [load(): pl.pallas_call(functools.partial(load_kernel, at, size, parts), out_shape...]
    ppermute x11 -> x13, waiting for transfers between devices: 6.72 us -> 6.6 us  [swap(): return lax.ppermute(x, 'layer', [(i, i ^ bits) for i in range(4)])]
    pallas_call x5 -> x6, Pallas kernels: 5.9 us -> 5.93 us  [partial_products(): pl.pallas_call(functools.partial(partial_kernel, tuple(steps), shapes, le...]
  transfers between devices with their start and end apart: 25 -> 29, of which waited for: 14 -> 15; matrix products, arithmetic and copies ran while one was open for 0% -> 0% of each run, Pallas kernels for 16% -> 16%
where the time goes in v10:
time: 106 us
  starting transfers between devices  47.4 us (45%)
  waiting for transfers between devices  37.8 us (36%)
  Pallas kernels  18 us (17%)
  local copies, waits for them, and re-layouts  1.9 us (2%)
    ppermute x16, waiting for transfers between devices, shift(): return lax.ppermute(x, axis, [(i, (i + by) % n) for i in range(n)])  31.2 us
    ppermute x16, starting transfers between devices, shift(): return lax.ppermute(x, axis, [(i, (i + by) % n) for i in range(n)])  29.3 us
    ppermute x13, starting transfers between devices, swap(): return lax.ppermute(x, 'layer', [(i, i ^ bits) for i in range(4)])  18.1 us
    pallas_call x13, Pallas kernels, load(): pl.pallas_call(functools.partial(load_kernel, at, size, parts), out_shape...  7.3 us
    ppermute x13, waiting for transfers between devices, swap(): return lax.ppermute(x, 'layer', [(i, i ^ bits) for i in range(4)])  6.6 us
    pallas_call x6, Pallas kernels, partial_products(): pl.pallas_call(functools.partial(partial_kernel, tuple(steps), shapes, le...  5.93 us
    pallas_call x2, Pallas kernels, mask_right(): pl.pallas_call(mask_right_kernel, out_shape=jax.ShapeDtypeStruct((layers,...  2.27 us
  transfers between devices with their start and end apart: 29, of which 15 were waited for; matrix products, arithmetic and copies ran while one was open for 0% of the time, Pallas kernels for 16%

profile of v10, /device:TPU:0, one launch (start us, length us, event | category | flops | bytes accessed | tf_op | source)
XLA Modules:
  0.0 105.6 jit_solution(12969208196722538982)
XLA Ops:
  2.9 2.6 %collective-permute-start = (bf16[384,256]{1,0:T(8,128)(2,1)S(1)}, bf16[384,256]{1,0:T(8,128)(2,1)S(1)}, u32[]{:S(2)}, u32[]{:S(2)}) collective-permute-start(bf16[384,256]{1,0:T(8,128)(2,1)S(1)} %shard_map.46.refs_0_), channel_id=1, source_target_pairs={{0,1},{1,2},{2,3},{3,0},{4,5},{5,6},{6,7},{7,4},{8,9},{9,10},{10,1... | collective-permute-start | bytes 589832 | tf_op jit(solution)/shard_map/ppermute | solution.py:228
  6.1 2.1 %collective-permute-start.4 = (bf16[384,256]{1,0:T(8,128)(2,1)S(1)}, bf16[384,256]{1,0:T(8,128)(2,1)S(1)}, u32[]{:S(2)}, u32[]{:S(2)}) collective-permute-start(bf16[384,256]{1,0:T(8,128)(2,1)S(1)} %shard_map.47.refs_0_), channel_id=1, source_target_pairs={{0,3},{1,0},{2,1},{3,2},{4,7},{5,4},{6,5},{7,6},{8,11},{9,8},{10,9... | collective-permute-start | bytes 589832 | tf_op jit(solution)/shard_map/ppermute | solution.py:228
  8.2 5.2 %collective-permute-done.arrived.refs_1_ = bf16[384,256]{1,0:T(8,128)(2,1)S(1)} collective-permute-done((bf16[384,256]{1,0:T(8,128)(2,1)S(1)}, bf16[384,256]{1,0:T(8,128)(2,1)S(1)}, u32[]{:S(2)}, u32[]{:S(2)}) %collective-permute-start) | collective-permute-done | bytes 196640 | tf_op jit(solution)/shard_map/ppermute | solution.py:228
  14.0 3.3 %collective-permute-done.4.arrived.refs_2_ = bf16[384,256]{1,0:T(8,128)(2,1)S(1)} collective-permute-done((bf16[384,256]{1,0:T(8,128)(2,1)S(1)}, bf16[384,256]{1,0:T(8,128)(2,1)S(1)}, u32[]{:S(2)}, u32[]{:S(2)}) %collective-permute-start.4) | collective-permute-done | bytes 196640 | tf_op jit(solution)/shard_map/ppermute | solution.py:228
  17.9 2.3 %collective-permute-start.6 = (bf16[576,256]{1,0:T(8,128)(2,1)S(1)}, bf16[576,256]{1,0:T(8,128)(2,1)S(1)}, u32[]{:S(2)}, u32[]{:S(2)}) collective-permute-start(bf16[576,256]{1,0:T(8,128)(2,1)S(1)} %shard_map.49.refs_0_), channel_id=1, source_target_pairs={{0,3},{1,0},{2,1},{3,2},{4,7},{5,4},{6,5},{7,6},{8,11},{9,8},{10,9... | collective-permute-start | bytes 884744 | tf_op jit(solution)/shard_map/ppermute | solution.py:228
  22.5 4.9 %collective-permute-done.1.arrived.refs_3_.refs_1_ = bf16[576,256]{1,0:T(8,128)(2,1)S(1)} collective-permute-done((bf16[576,256]{1,0:T(8,128)(2,1)S(1)}, bf16[576,256]{1,0:T(8,128)(2,1)S(1)}, u32[]{:S(2)}, u32[]{:S(2)}) %collective-permute-start.1) | collective-permute-done | bytes 294944 | tf_op jit(solution)/shard_map/ppermute | solution.py:228
  28.0 2.7 %collective-permute-start.5 = (bf16[576,256]{1,0:T(8,128)(2,1)S(1)}, bf16[576,256]{1,0:T(8,128)(2,1)S(1)}, u32[]{:S(2)}, u32[]{:S(2)}) collective-permute-start(bf16[576,256]{1,0:T(8,128)(2,1)S(1)} %shard_map.52.refs_0_), channel_id=1, source_target_pairs={{0,1},{1,2},{2,3},{3,0},{4,5},{5,6},{6,7},{7,4},{8,9},{9,10},{10,1... | collective-permute-start | bytes 884744 | tf_op jit(solution)/shard_map/ppermute | solution.py:228
  30.8 2.6 %collective-permute-done.6.arrived.refs_4_.refs_2_ = bf16[576,256]{1,0:T(8,128)(2,1)S(1)} collective-permute-done((bf16[576,256]{1,0:T(8,128)(2,1)S(1)}, bf16[576,256]{1,0:T(8,128)(2,1)S(1)}, u32[]{:S(2)}, u32[]{:S(2)}) %collective-permute-start.6) | collective-permute-done | bytes 294944 | tf_op jit(solution)/shard_map/ppermute | solution.py:228
  37.3 3.2 %collective-permute-done.5.arrived.refs_3_.refs_1_ = bf16[576,256]{1,0:T(8,128)(2,1)S(1)} collective-permute-done((bf16[576,256]{1,0:T(8,128)(2,1)S(1)}, bf16[576,256]{1,0:T(8,128)(2,1)S(1)}, u32[]{:S(2)}, u32[]{:S(2)}) %collective-permute-start.5) | collective-permute-done | bytes 294944 | tf_op jit(solution)/shard_map/ppermute | solution.py:228
  41.0 4.3 %collective-permute-start.7 = (bf16[576,256]{1,0:T(8,128)(2,1)S(1)}, bf16[576,256]{1,0:T(8,128)(2,1)S(1)}, u32[]{:S(2)}, u32[]{:S(2)}) collective-permute-start(bf16[576,256]{1,0:T(8,128)(2,1)S(1)} %shard_map.55.refs_0_), channel_id=1, source_target_pairs={{0,1},{1,2},{2,3},{3,0},{4,5},{5,6},{6,7},{7,4},{8,9},{9,10},{10,1... | collective-permute-start | bytes 884744 | tf_op jit(solution)/shard_map/ppermute | solution.py:228
  45.3 3.4 %collective-permute-done.9.arrived.refs_4_.refs_2_ = bf16[576,256]{1,0:T(8,128)(2,1)S(1)} collective-permute-done((bf16[576,256]{1,0:T(8,128)(2,1)S(1)}, bf16[576,256]{1,0:T(8,128)(2,1)S(1)}, u32[]{:S(2)}, u32[]{:S(2)}) %collective-permute-start.9) | collective-permute-done | bytes 294944 | tf_op jit(solution)/shard_map/ppermute | solution.py:228
  51.0 1.8 %collective-permute-start.12 = (s16[800,256]{1,0:T(8,128)(2,1)S(1)}, s16[800,256]{1,0:T(8,128)(2,1)S(1)}, u32[]{:S(2)}, u32[]{:S(2)}) collective-permute-start(s16[800,256]{1,0:T(8,128)(2,1)S(1)} %get-tuple-element.41), channel_id=1, source_target_pairs={{0,16},{8,24},{16,0},{24,8},{1,17},{9,25},{17,1},{25,9},{2,18},{10... | collective-permute-start | bytes 1228808 | tf_op jit(solution)/shard_map/ppermute | solution.py:232
  55.4 4.7 %collective-permute-start.10 = (bf16[320,256]{1,0:T(8,128)(2,1)S(1)}, bf16[320,256]{1,0:T(8,128)(2,1)S(1)}, u32[]{:S(2)}, u32[]{:S(2)}) collective-permute-start(bf16[320,256]{1,0:T(8,128)(2,1)S(1)} %shard_map.59.refs_0_), channel_id=1, source_target_pairs={{0,1},{1,2},{2,3},{3,0},{4,5},{5,6},{6,7},{7,4},{8,9},{9,10},{10,1... | collective-permute-start | bytes 491528 | tf_op jit(solution)/shard_map/ppermute | solution.py:228
  60.0 2.4 %collective-permute-done.13.arrived.refs_4_.refs_2_ = bf16[576,256]{1,0:T(8,128)(2,1)S(1)} collective-permute-done((bf16[576,256]{1,0:T(8,128)(2,1)S(1)}, bf16[576,256]{1,0:T(8,128)(2,1)S(1)}, u32[]{:S(2)}, u32[]{:S(2)}) %collective-permute-start.13) | collective-permute-done | bytes 294944 | tf_op jit(solution)/shard_map/ppermute | solution.py:228
  63.0 2.3 %collective-permute-start.15 = (bf16[320,256]{1,0:T(8,128)(2,1)S(1)}, bf16[320,256]{1,0:T(8,128)(2,1)S(1)}, u32[]{:S(2)}, u32[]{:S(2)}) collective-permute-start(bf16[320,256]{1,0:T(8,128)(2,1)S(1)} %shard_map.60.refs_7_), channel_id=1, source_target_pairs={{0,3},{1,0},{2,1},{3,2},{4,7},{5,4},{6,5},{7,6},{8,11},{9,8},{10,9... | collective-permute-start | bytes 491528 | tf_op jit(solution)/shard_map/ppermute | solution.py:228
  66.4 2.0 %collective-permute-start.18 = (s16[800,256]{1,0:T(8,128)(2,1)S(1)}, s16[800,256]{1,0:T(8,128)(2,1)S(1)}, u32[]{:S(2)}, u32[]{:S(2)}) collective-permute-start(s16[800,256]{1,0:T(8,128)(2,1)S(1)} %get-tuple-element.45), channel_id=1, source_target_pairs={{0,8},{8,0},{16,24},{24,16},{1,9},{9,1},{17,25},{25,17},{2,10},{10... | collective-permute-start | bytes 1228808 | tf_op jit(solution)/shard_map/ppermute | solution.py:232
  72.3 2.0 %collective-permute-start.20 = (s16[800,256]{1,0:T(8,128)(2,1)S(1)}, s16[800,256]{1,0:T(8,128)(2,1)S(1)}, u32[]{:S(2)}, u32[]{:S(2)}) collective-permute-start(s16[800,256]{1,0:T(8,128)(2,1)S(1)} %get-tuple-element.49), channel_id=1, source_target_pairs={{0,16},{8,24},{16,0},{24,8},{1,17},{9,25},{17,1},{25,9},{2,18},{10... | collective-permute-start | bytes 1228808 | tf_op jit(solution)/shard_map/ppermute | solution.py:232
  74.3 2.3 %collective-permute-start.17 = (s16[400,256]{1,0:T(8,128)(2,1)S(1)}, s16[400,256]{1,0:T(8,128)(2,1)S(1)}, u32[]{:S(2)}, u32[]{:S(2)}) collective-permute-start(s16[400,256]{1,0:T(8,128)(2,1)S(1)} %shard_map.62.refs_2_), channel_id=1, source_target_pairs={{0,8},{8,0},{16,24},{24,16},{1,9},{9,1},{17,25},{25,17},{2,10},{10... | collective-permute-start | bytes 614408 | tf_op jit(solution)/shard_map/ppermute | solution.py:232
  76.5 4.1 %collective-permute-start.16 = (bf16[448,256]{1,0:T(8,128)(2,1)S(1)}, bf16[448,256]{1,0:T(8,128)(2,1)S(1)}, u32[]{:S(2)}, u32[]{:S(2)}) collective-permute-start(bf16[448,256]{1,0:T(8,128)(2,1)S(1)} %shard_map.65.refs_7_), channel_id=1, source_target_pairs={{0,3},{1,0},{2,1},{3,2},{4,7},{5,4},{6,5},{7,6},{8,11},{9,8},{10,9... | collective-permute-start | bytes 688136 | tf_op jit(solution)/shard_map/ppermute | solution.py:228
  81.5 2.3 %collective-permute-start.19 = (bf16[384,256]{1,0:T(8,128)(2,1)S(1)}, bf16[384,256]{1,0:T(8,128)(2,1)S(1)}, u32[]{:S(2)}, u32[]{:S(2)}) collective-permute-start(bf16[384,256]{1,0:T(8,128)(2,1)S(1)} %shard_map.69.refs_7_), channel_id=1, source_target_pairs={{0,1},{1,2},{2,3},{3,0},{4,5},{5,6},{6,7},{7,4},{8,9},{9,10},{10,1... | collective-permute-start | bytes 589832 | tf_op jit(solution)/shard_map/ppermute | solution.py:228
  83.8 1.9 %collective-permute-done.16.refs_4_.refs_2_ = bf16[448,256]{1,0:T(8,128)(2,1)S(1)} collective-permute-done((bf16[448,256]{1,0:T(8,128)(2,1)S(1)}, bf16[448,256]{1,0:T(8,128)(2,1)S(1)}, u32[]{:S(2)}, u32[]{:S(2)}) %collective-permute-start.16) | collective-permute-done | bytes 229408 | tf_op jit(solution)/shard_map/ppermute | solution.py:228
  87.4 2.0 %collective-permute-start.26 = (s16[400,256]{1,0:T(8,128)(2,1)S(1)}, s16[400,256]{1,0:T(8,128)(2,1)S(1)}, u32[]{:S(2)}, u32[]{:S(2)}) collective-permute-start(s16[400,256]{1,0:T(8,128)(2,1)S(1)} %shard_map.71.refs_6_), channel_id=1, source_target_pairs={{0,8},{8,0},{16,24},{24,16},{1,9},{9,1},{17,25},{25,17},{2,10},{10... | collective-permute-start | bytes 614408 | tf_op jit(solution)/shard_map/ppermute | solution.py:232
  97.0 3.9 %collective-permute-done.25.refs_1_ = s16[144,256]{1,0:T(8,128)(2,1)S(1)} collective-permute-done((s16[144,256]{1,0:T(8,128)(2,1)S(1)}, s16[144,256]{1,0:T(8,128)(2,1)S(1)}, u32[]{:S(2)}, u32[]{:S(2)}) %collective-permute-start.25) | collective-permute-done | bytes 73760 | tf_op jit(solution)/shard_map/ppermute | solution.py:232
  101.0 2.1 %collective-permute-done.23.refs_2_ = s16[400,256]{1,0:T(8,128)(2,1)S(1)} collective-permute-done((s16[400,256]{1,0:T(8,128)(2,1)S(1)}, s16[400,256]{1,0:T(8,128)(2,1)S(1)}, u32[]{:S(2)}, u32[]{:S(2)}) %collective-permute-start.23) | collective-permute-done | bytes 204832 | tf_op jit(solution)/shard_map/ppermute | solution.py:232
  (77 shorter events, 34.7 us)
Async XLA Ops:
  0.0 21.4 %collective-permute-start.3 = (bf16[512,4,256]{2,1,0:T(4,128)(2,1)}, bf16[512,4,256]{2,1,0:T(4,128)(2,1)S(1)}, u32[]{:S(2)}, u32[]{:S(2)}) collective-permute-start(bf16[512,4,256]{2,1,0:T(4,128)(2,1)} %values_ref.1), channel_id=1, source_target_pairs={{0,4},{4,0},{1,5},{5,1},{2,6},{6,2},{3,7},{7,3},{8,12},{12,8},{9,1... | collective-permute-start | bytes 3145736 | tf_op jit(solution)/shard_map/ppermute | solution.py:228
  2.9 10.5 %collective-permute-start = (bf16[384,256]{1,0:T(8,128)(2,1)S(1)}, bf16[384,256]{1,0:T(8,128)(2,1)S(1)}, u32[]{:S(2)}, u32[]{:S(2)}) collective-permute-start(bf16[384,256]{1,0:T(8,128)(2,1)S(1)} %shard_map.46.refs_0_), channel_id=1, source_target_pairs={{0,1},{1,2},{2,3},{3,0},{4,5},{5,6},{6,7},{7,4},{8,9},{9,10},{10,1... | collective-permute-start | bytes 589832 | tf_op jit(solution)/shard_map/ppermute | solution.py:228
  6.1 11.2 %collective-permute-start.4 = (bf16[384,256]{1,0:T(8,128)(2,1)S(1)}, bf16[384,256]{1,0:T(8,128)(2,1)S(1)}, u32[]{:S(2)}, u32[]{:S(2)}) collective-permute-start(bf16[384,256]{1,0:T(8,128)(2,1)S(1)} %shard_map.47.refs_0_), channel_id=1, source_target_pairs={{0,3},{1,0},{2,1},{3,2},{4,7},{5,4},{6,5},{7,6},{8,11},{9,8},{10,9... | collective-permute-start | bytes 589832 | tf_op jit(solution)/shard_map/ppermute | solution.py:228
  14.0 13.5 %collective-permute-start.1 = (bf16[576,256]{1,0:T(8,128)(2,1)S(1)}, bf16[576,256]{1,0:T(8,128)(2,1)S(1)}, u32[]{:S(2)}, u32[]{:S(2)}) collective-permute-start(bf16[576,256]{1,0:T(8,128)(2,1)S(1)} %shard_map.48.refs_0_), channel_id=1, source_target_pairs={{0,1},{1,2},{2,3},{3,0},{4,5},{5,6},{6,7},{7,4},{8,9},{9,10},{10,1... | collective-permute-start | bytes 884744 | tf_op jit(solution)/shard_map/ppermute | solution.py:228
  17.9 15.5 %collective-permute-start.6 = (bf16[576,256]{1,0:T(8,128)(2,1)S(1)}, bf16[576,256]{1,0:T(8,128)(2,1)S(1)}, u32[]{:S(2)}, u32[]{:S(2)}) collective-permute-start(bf16[576,256]{1,0:T(8,128)(2,1)S(1)} %shard_map.49.refs_0_), channel_id=1, source_target_pairs={{0,3},{1,0},{2,1},{3,2},{4,7},{5,4},{6,5},{7,6},{8,11},{9,8},{10,9... | collective-permute-start | bytes 884744 | tf_op jit(solution)/shard_map/ppermute | solution.py:228
  28.0 12.4 %collective-permute-start.5 = (bf16[576,256]{1,0:T(8,128)(2,1)S(1)}, bf16[576,256]{1,0:T(8,128)(2,1)S(1)}, u32[]{:S(2)}, u32[]{:S(2)}) collective-permute-start(bf16[576,256]{1,0:T(8,128)(2,1)S(1)} %shard_map.52.refs_0_), channel_id=1, source_target_pairs={{0,1},{1,2},{2,3},{3,0},{4,5},{5,6},{6,7},{7,4},{8,9},{9,10},{10,1... | collective-permute-start | bytes 884744 | tf_op jit(solution)/shard_map/ppermute | solution.py:228
  34.0 14.8 %collective-permute-start.9 = (bf16[576,256]{1,0:T(8,128)(2,1)S(1)}, bf16[576,256]{1,0:T(8,128)(2,1)S(1)}, u32[]{:S(2)}, u32[]{:S(2)}) collective-permute-start(bf16[576,256]{1,0:T(8,128)(2,1)S(1)} %shard_map.53.refs_7_), channel_id=1, source_target_pairs={{0,3},{1,0},{2,1},{3,2},{4,7},{5,4},{6,5},{7,6},{8,11},{9,8},{10,9... | collective-permute-start | bytes 884744 | tf_op jit(solution)/shard_map/ppermute | solution.py:228
  35.7 17.1 %collective-permute-start.8 = (s16[800,256]{1,0:T(8,128)(2,1)S(1)}, s16[800,256]{1,0:T(8,128)(2,1)S(1)}, u32[]{:S(2)}, u32[]{:S(2)}) collective-permute-start(s16[800,256]{1,0:T(8,128)(2,1)S(1)} %get-tuple-element.38), channel_id=1, source_target_pairs={{0,8},{8,0},{16,24},{24,16},{1,9},{9,1},{17,25},{25,17},{2,10},{10... | collective-permute-start | bytes 1228808 | tf_op jit(solution)/shard_map/ppermute | solution.py:232
  41.0 13.8 %collective-permute-start.7 = (bf16[576,256]{1,0:T(8,128)(2,1)S(1)}, bf16[576,256]{1,0:T(8,128)(2,1)S(1)}, u32[]{:S(2)}, u32[]{:S(2)}) collective-permute-start(bf16[576,256]{1,0:T(8,128)(2,1)S(1)} %shard_map.55.refs_0_), channel_id=1, source_target_pairs={{0,1},{1,2},{2,3},{3,0},{4,5},{5,6},{6,7},{7,4},{8,9},{9,10},{10,1... | collective-permute-start | bytes 884744 | tf_op jit(solution)/shard_map/ppermute | solution.py:228
  49.3 13.2 %collective-permute-start.13 = (bf16[576,256]{1,0:T(8,128)(2,1)S(1)}, bf16[576,256]{1,0:T(8,128)(2,1)S(1)}, u32[]{:S(2)}, u32[]{:S(2)}) collective-permute-start(bf16[576,256]{1,0:T(8,128)(2,1)S(1)} %shard_map.56.refs_7_), channel_id=1, source_target_pairs={{0,3},{1,0},{2,1},{3,2},{4,7},{5,4},{6,5},{7,6},{8,11},{9,8},{10,9... | collective-permute-start | bytes 884744 | tf_op jit(solution)/shard_map/ppermute | solution.py:228
  51.0 17.4 %collective-permute-start.12 = (s16[800,256]{1,0:T(8,128)(2,1)S(1)}, s16[800,256]{1,0:T(8,128)(2,1)S(1)}, u32[]{:S(2)}, u32[]{:S(2)}) collective-permute-start(s16[800,256]{1,0:T(8,128)(2,1)S(1)} %get-tuple-element.41), channel_id=1, source_target_pairs={{0,16},{8,24},{16,0},{24,8},{1,17},{9,25},{17,1},{25,9},{2,18},{10... | collective-permute-start | bytes 1228808 | tf_op jit(solution)/shard_map/ppermute | solution.py:232
  53.0 15.6 %collective-permute-start.11 = (s16[400,256]{1,0:T(8,128)(2,1)S(1)}, s16[400,256]{1,0:T(8,128)(2,1)S(1)}, u32[]{:S(2)}, u32[]{:S(2)}) collective-permute-start(s16[400,256]{1,0:T(8,128)(2,1)S(1)} %shard_map.58.refs_0_), channel_id=1, source_target_pairs={{0,16},{8,24},{16,0},{24,8},{1,17},{9,25},{17,1},{25,9},{2,18},{10... | collective-permute-start | bytes 614408 | tf_op jit(solution)/shard_map/ppermute | solution.py:232
  55.4 13.4 %collective-permute-start.10 = (bf16[320,256]{1,0:T(8,128)(2,1)S(1)}, bf16[320,256]{1,0:T(8,128)(2,1)S(1)}, u32[]{:S(2)}, u32[]{:S(2)}) collective-permute-start(bf16[320,256]{1,0:T(8,128)(2,1)S(1)} %shard_map.59.refs_0_), channel_id=1, source_target_pairs={{0,1},{1,2},{2,3},{3,0},{4,5},{5,6},{6,7},{7,4},{8,9},{9,10},{10,1... | collective-permute-start | bytes 491528 | tf_op jit(solution)/shard_map/ppermute | solution.py:228
  63.0 7.6 %collective-permute-start.15 = (bf16[320,256]{1,0:T(8,128)(2,1)S(1)}, bf16[320,256]{1,0:T(8,128)(2,1)S(1)}, u32[]{:S(2)}, u32[]{:S(2)}) collective-permute-start(bf16[320,256]{1,0:T(8,128)(2,1)S(1)} %shard_map.60.refs_7_), channel_id=1, source_target_pairs={{0,3},{1,0},{2,1},{3,2},{4,7},{5,4},{6,5},{7,6},{8,11},{9,8},{10,9... | collective-permute-start | bytes 491528 | tf_op jit(solution)/shard_map/ppermute | solution.py:228
  66.4 14.2 %collective-permute-start.18 = (s16[800,256]{1,0:T(8,128)(2,1)S(1)}, s16[800,256]{1,0:T(8,128)(2,1)S(1)}, u32[]{:S(2)}, u32[]{:S(2)}) collective-permute-start(s16[800,256]{1,0:T(8,128)(2,1)S(1)} %get-tuple-element.45), channel_id=1, source_target_pairs={{0,8},{8,0},{16,24},{24,16},{1,9},{9,1},{17,25},{25,17},{2,10},{10... | collective-permute-start | bytes 1228808 | tf_op jit(solution)/shard_map/ppermute | solution.py:232
  69.3 11.6 %collective-permute-start.14 = (bf16[448,256]{1,0:T(8,128)(2,1)S(1)}, bf16[448,256]{1,0:T(8,128)(2,1)S(1)}, u32[]{:S(2)}, u32[]{:S(2)}) collective-permute-start(bf16[448,256]{1,0:T(8,128)(2,1)S(1)} %shard_map.64.refs_0_), channel_id=1, source_target_pairs={{0,1},{1,2},{2,3},{3,0},{4,5},{5,6},{6,7},{7,4},{8,9},{9,10},{10,1... | collective-permute-start | bytes 688136 | tf_op jit(solution)/shard_map/ppermute | solution.py:228
  72.3 15.0 %collective-permute-start.20 = (s16[800,256]{1,0:T(8,128)(2,1)S(1)}, s16[800,256]{1,0:T(8,128)(2,1)S(1)}, u32[]{:S(2)}, u32[]{:S(2)}) collective-permute-start(s16[800,256]{1,0:T(8,128)(2,1)S(1)} %get-tuple-element.49), channel_id=1, source_target_pairs={{0,16},{8,24},{16,0},{24,8},{1,17},{9,25},{17,1},{25,9},{2,18},{10... | collective-permute-start | bytes 1228808 | tf_op jit(solution)/shard_map/ppermute | solution.py:232
  76.5 9.2 %collective-permute-start.16 = (bf16[448,256]{1,0:T(8,128)(2,1)S(1)}, bf16[448,256]{1,0:T(8,128)(2,1)S(1)}, u32[]{:S(2)}, u32[]{:S(2)}) collective-permute-start(bf16[448,256]{1,0:T(8,128)(2,1)S(1)} %shard_map.65.refs_7_), channel_id=1, source_target_pairs={{0,3},{1,0},{2,1},{3,2},{4,7},{5,4},{6,5},{7,6},{8,11},{9,8},{10,9... | collective-permute-start | bytes 688136 | tf_op jit(solution)/shard_map/ppermute | solution.py:228
  81.5 8.3 %collective-permute-start.19 = (bf16[384,256]{1,0:T(8,128)(2,1)S(1)}, bf16[384,256]{1,0:T(8,128)(2,1)S(1)}, u32[]{:S(2)}, u32[]{:S(2)}) collective-permute-start(bf16[384,256]{1,0:T(8,128)(2,1)S(1)} %shard_map.69.refs_7_), channel_id=1, source_target_pairs={{0,1},{1,2},{2,3},{3,0},{4,5},{5,6},{6,7},{7,4},{8,9},{9,10},{10,1... | collective-permute-start | bytes 589832 | tf_op jit(solution)/shard_map/ppermute | solution.py:228
  86.9 7.7 %collective-permute-start.27 = (s16[400,256]{1,0:T(8,128)(2,1)S(1)}, s16[400,256]{1,0:T(8,128)(2,1)S(1)}, u32[]{:S(2)}, u32[]{:S(2)}) collective-permute-start(s16[400,256]{1,0:T(8,128)(2,1)S(1)} %shard_map.67.refs_3_), channel_id=1, source_target_pairs={{0,16},{8,24},{16,0},{24,8},{1,17},{9,25},{17,1},{25,9},{2,18},{10... | collective-permute-start | bytes 614408 | tf_op jit(solution)/shard_map/ppermute | solution.py:232
  87.4 9.4 %collective-permute-start.26 = (s16[400,256]{1,0:T(8,128)(2,1)S(1)}, s16[400,256]{1,0:T(8,128)(2,1)S(1)}, u32[]{:S(2)}, u32[]{:S(2)}) collective-permute-start(s16[400,256]{1,0:T(8,128)(2,1)S(1)} %shard_map.71.refs_6_), channel_id=1, source_target_pairs={{0,8},{8,0},{16,24},{24,16},{1,9},{9,1},{17,25},{25,17},{2,10},{10... | collective-permute-start | bytes 614408 | tf_op jit(solution)/shard_map/ppermute | solution.py:232
  90.9 10.0 %collective-permute-start.21 = (s16[400,256]{1,0:T(8,128)(2,1)S(1)}, s16[400,256]{1,0:T(8,128)(2,1)S(1)}, u32[]{:S(2)}, u32[]{:S(2)}) collective-permute-start(s16[400,256]{1,0:T(8,128)(2,1)S(1)} %get-tuple-element.52), channel_id=1, source_target_pairs={{0,8},{8,0},{16,24},{24,16},{1,9},{9,1},{17,25},{25,17},{2,10},{10... | collective-permute-start | bytes 614408 | tf_op jit(solution)/shard_map/ppermute | solution.py:232
  92.1 8.8 %collective-permute-start.22 = (s16[400,256]{1,0:T(8,128)(2,1)S(1)}, s16[400,256]{1,0:T(8,128)(2,1)S(1)}, u32[]{:S(2)}, u32[]{:S(2)}) collective-permute-start(s16[400,256]{1,0:T(8,128)(2,1)S(1)} %get-tuple-element.53), channel_id=1, source_target_pairs={{0,16},{8,24},{16,0},{24,8},{1,17},{9,25},{17,1},{25,9},{2,18},{10... | collective-permute-start | bytes 614408 | tf_op jit(solution)/shard_map/ppermute | solution.py:232
  93.6 9.5 %collective-permute-start.23 = (s16[400,256]{1,0:T(8,128)(2,1)S(1)}, s16[400,256]{1,0:T(8,128)(2,1)S(1)}, u32[]{:S(2)}, u32[]{:S(2)}) collective-permute-start(s16[400,256]{1,0:T(8,128)(2,1)S(1)} %get-tuple-element.54), channel_id=1, source_target_pairs={{0,24},{8,16},{16,8},{24,0},{1,25},{9,17},{17,9},{25,1},{2,26},{10... | collective-permute-start | bytes 614408 | tf_op jit(solution)/shard_map/ppermute | solution.py:232
  (10 other events, 43.0 us)

commit v11 on v9

--- a/solution.py
+++ b/solution.py
@@ -200,26 +200,35 @@
     )(kept, *received, *before, *after)
 
 
-def normalise_kernel(n_chunks, rows_total, column_ref, *refs):
-    chunks, out_ref = refs[:n_chunks], refs[n_chunks]
-    colmean = column_ref[...] / rows_total
-    at = 0
-    for chunk in chunks:
-        rows = chunk.shape[0]
-        out_ref[at : at + rows, :] = (chunk[...] / (colmean + 1e-06)).astype(jnp.bfloat16)
-        at += rows
-
-
-def normalise(column, chunks, rows_total):
+def normalise_kernel(n_sums, rows_total, *refs):
+    sums, chunks = refs[:n_sums], refs[n_sums:-3]
+    out_ref, block, sems = refs[-3:]
+    colmean = sum(ref[...] for ref in sums) / rows_total
+    at, copies = 0, []
+    for i, chunk in enumerate(chunks):
+        rows = pl.ds(at, chunk.shape[0])
+        block[rows, :] = (chunk[...] / (colmean + 1e-06)).astype(jnp.bfloat16)
+        copies.append(pltpu.make_async_copy(block.at[rows], out_ref.at[rows], sems.at[i]))
+        copies[-1].start()
+        at += chunk.shape[0]
+    for copy in copies:
+        copy.wait()
+
+
+def normalise(sums, chunks, rows_total):
     rows, columns = sum(chunk.shape[0] for chunk in chunks), chunks[0].shape[1]
     return pl.pallas_call(
-        functools.partial(normalise_kernel, len(chunks), rows_total),
+        functools.partial(normalise_kernel, len(sums), rows_total),
         out_shape=jax.ShapeDtypeStruct((rows, columns), jnp.bfloat16),
-        in_specs=[VMEM] * (1 + len(chunks)),
-        out_specs=VMEM,
+        in_specs=[VMEM] * (len(sums) + len(chunks)),
+        out_specs=pl.BlockSpec(memory_space=pl.ANY),
+        scratch_shapes=[
+            pltpu.VMEM((rows, columns), jnp.bfloat16),
+            pltpu.SemaphoreType.DMA((len(chunks),)),
+        ],
         compiler_params=PARAMS,
         cost_estimate=cost(4 * rows * columns, 6 * rows * columns),
-    )(column, *chunks)
+    )(*sums, *chunks)
 
 
 def shift(x, axis, by):
@@ -258,7 +267,8 @@
                     first, rows = first + d * (rows // 2), rows // 2
                 parts.append((first, rows))
             arrived = found[riders[0]][d][-1][0] if riders else left
-            block = load(left, pattern, at, size, arrived, tuple(parts), last)
+            if slot or d == 0:
+                block = load(left, pattern, at, size, arrived, tuple(parts), last)
             last[:] = [block]
             got = shift(block, "col", 1 - 2 * d)
             first = 0
@@ -278,7 +288,7 @@
         if i + 1 < len(sizes):
             ks, sent_ks = (0, second(i)), ((3 - second(i), 3),)
         else:
-            ks, sent_ks = (0,), ((1,), (2,), (3,))
+            ks, sent_ks = (0,), ((3,), (1,), (2,))
         mine, sent = partial_products(steps, sources(i), pieces, last, ks, sent_ks)
         kept.append(mine)
         received.append([swap(x, k[0]) for x, k in zip(sent, sent_ks)])
@@ -322,8 +332,8 @@
     for i in range(len(squares), len(sizes)):
         square(i)
 
-    column = lax.psum(columns[-1], "row")
-    out = normalise(column, squares, rows_local * n_rows)
+    sums = columns[-1:] + [shift(columns[-1], "row", i) for i in range(1, n_rows)]
+    out = normalise(sums, squares, rows_local * n_rows)
     return out.reshape(rows_local, 1, columns_local)
 
 

time: 104 us -> 103 us (level)
  blocking collectives: 2.47 us -> 0 us
  waiting for transfers between devices: 54 us -> 55.2 us
    psum x1 -> x0, blocking collectives: 2.47 us -> none  [per_device(): column = lax.psum(columns[-1], 'row')]
    ppermute x14 -> x15, waiting for transfers between devices: 47.2 us -> 48.3 us  [shift(): return lax.ppermute(x, axis, [(i, (i + by) % n) for i in range(n)])]
    ppermute x14 -> x15, starting transfers between devices: 12.7 us -> 13.4 us  [shift(): return lax.ppermute(x, axis, [(i, (i + by) % n) for i in range(n)])]
    pallas_call x12 -> x11, Pallas kernels: 6.74 us -> 6.18 us  [load(): pl.pallas_call(functools.partial(load_kernel, at, size, parts), out_shape...]
  transfers between devices with their start and end apart: 25 -> 26, of which waited for: 14 -> 16; matrix products, arithmetic and copies ran while one was open for 0% -> 0% of each run, Pallas kernels for 16% -> 15%
where the time goes in v11:
time: 103 us; the launch traced here: 102 us
  waiting for transfers between devices  55.2 us (54%)
  starting transfers between devices  27.7 us (27%)
  Pallas kernels  16.8 us (16%)
  local copies, waits for them, and re-layouts  1.9 us (2%)
    ppermute x15, waiting for transfers between devices, shift(): return lax.ppermute(x, axis, [(i, (i + by) % n) for i in range(n)])  48.3 us
    ppermute x11, starting transfers between devices, swap(): return lax.ppermute(x, 'layer', [(i, i ^ bits) for i in range(4)])  14.3 us
    ppermute x15, starting transfers between devices, shift(): return lax.ppermute(x, axis, [(i, (i + by) % n) for i in range(n)])  13.4 us
    ppermute x11, waiting for transfers between devices, swap(): return lax.ppermute(x, 'layer', [(i, i ^ bits) for i in range(4)])  6.93 us
    pallas_call x11, Pallas kernels, load(): pl.pallas_call(functools.partial(load_kernel, at, size, parts), out_shape...  6.18 us
    pallas_call x5, Pallas kernels, partial_products(): pl.pallas_call(functools.partial(partial_kernel, tuple(steps), shapes, le...  5.91 us
    pallas_call x2, Pallas kernels, mask_right(): pl.pallas_call(mask_right_kernel, out_shape=jax.ShapeDtypeStruct((layers,...  2.27 us
  transfers between devices with their start and end apart: 26, of which 16 were waited for; matrix products, arithmetic and copies ran while one was open for 0% of the time, Pallas kernels for 15%

profile of v11, /device:TPU:0, one launch (start us, length us, event | category | flops | bytes accessed | tf_op | source)
XLA Modules:
  0.0 101.9 jit_solution(9621853703139846876)
XLA Ops:
  2.9 2.6 %collective-permute-start = (bf16[384,256]{1,0:T(8,128)(2,1)S(1)}, bf16[384,256]{1,0:T(8,128)(2,1)S(1)}, u32[]{:S(2)}, u32[]{:S(2)}) collective-permute-start(bf16[384,256]{1,0:T(8,128)(2,1)S(1)} %shard_map.46.refs_0_), channel_id=1, source_target_pairs={{0,1},{1,2},{2,3},{3,0},{4,5},{5,6},{6,7},{7,4},{8,9},{9,10},{10,1... | collective-permute-start | bytes 589832 | tf_op jit(solution)/shard_map/ppermute | solution.py:236
  5.5 2.1 %collective-permute-start.4 = (bf16[384,256]{1,0:T(8,128)(2,1)S(1)}, bf16[384,256]{1,0:T(8,128)(2,1)S(1)}, u32[]{:S(2)}, u32[]{:S(2)}) collective-permute-start(bf16[384,256]{1,0:T(8,128)(2,1)S(1)} %shard_map.46.refs_0_), channel_id=1, source_target_pairs={{0,3},{1,0},{2,1},{3,2},{4,7},{5,4},{6,5},{7,6},{8,11},{9,8},{10,9... | collective-permute-start | bytes 589832 | tf_op jit(solution)/shard_map/ppermute | solution.py:236
  7.6 5.7 %collective-permute-done.arrived.refs_1_ = bf16[384,256]{1,0:T(8,128)(2,1)S(1)} collective-permute-done((bf16[384,256]{1,0:T(8,128)(2,1)S(1)}, bf16[384,256]{1,0:T(8,128)(2,1)S(1)}, u32[]{:S(2)}, u32[]{:S(2)}) %collective-permute-start) | collective-permute-done | bytes 196640 | tf_op jit(solution)/shard_map/ppermute | solution.py:236
  14.0 2.8 %collective-permute-done.4.arrived.refs_2_ = bf16[384,256]{1,0:T(8,128)(2,1)S(1)} collective-permute-done((bf16[384,256]{1,0:T(8,128)(2,1)S(1)}, bf16[384,256]{1,0:T(8,128)(2,1)S(1)}, u32[]{:S(2)}, u32[]{:S(2)}) %collective-permute-start.4) | collective-permute-done | bytes 196640 | tf_op jit(solution)/shard_map/ppermute | solution.py:236
  17.4 2.8 %collective-permute-start.6 = (bf16[704,256]{1,0:T(8,128)(2,1)S(1)}, bf16[704,256]{1,0:T(8,128)(2,1)S(1)}, u32[]{:S(2)}, u32[]{:S(2)}) collective-permute-start(bf16[704,256]{1,0:T(8,128)(2,1)S(1)} %shard_map.48.refs_0_), channel_id=1, source_target_pairs={{0,3},{1,0},{2,1},{3,2},{4,7},{5,4},{6,5},{7,6},{8,11},{9,8},{10,9... | collective-permute-start | bytes 1081352 | tf_op jit(solution)/shard_map/ppermute | solution.py:236
  22.5 6.4 %collective-permute-done.1.arrived.refs_3_.refs_1_ = bf16[704,256]{1,0:T(8,128)(2,1)S(1)} collective-permute-done((bf16[704,256]{1,0:T(8,128)(2,1)S(1)}, bf16[704,256]{1,0:T(8,128)(2,1)S(1)}, u32[]{:S(2)}, u32[]{:S(2)}) %collective-permute-start.1) | collective-permute-done | bytes 360480 | tf_op jit(solution)/shard_map/ppermute | solution.py:236
  29.6 7.0 %collective-permute-done.6.arrived.refs_4_.refs_2_ = bf16[704,256]{1,0:T(8,128)(2,1)S(1)} collective-permute-done((bf16[704,256]{1,0:T(8,128)(2,1)S(1)}, bf16[704,256]{1,0:T(8,128)(2,1)S(1)}, u32[]{:S(2)}, u32[]{:S(2)}) %collective-permute-start.6) | collective-permute-done | bytes 360480 | tf_op jit(solution)/shard_map/ppermute | solution.py:236
  38.3 1.6 %collective-permute-start.8 = (s16[800,256]{1,0:T(8,128)(2,1)S(1)}, s16[800,256]{1,0:T(8,128)(2,1)S(1)}, u32[]{:S(2)}, u32[]{:S(2)}) collective-permute-start(s16[800,256]{1,0:T(8,128)(2,1)S(1)} %get-tuple-element.33), channel_id=1, source_target_pairs={{0,8},{8,0},{16,24},{24,16},{1,9},{9,1},{17,25},{25,17},{2,10},{10... | collective-permute-start | bytes 1228808 | tf_op jit(solution)/shard_map/ppermute | solution.py:240
  39.9 5.5 %collective-permute-done.5.arrived.refs_3_.refs_1_ = bf16[768,256]{1,0:T(8,128)(2,1)S(1)} collective-permute-done((bf16[768,256]{1,0:T(8,128)(2,1)S(1)}, bf16[768,256]{1,0:T(8,128)(2,1)S(1)}, u32[]{:S(2)}, u32[]{:S(2)}) %collective-permute-start.5) | collective-permute-done | bytes 393248 | tf_op jit(solution)/shard_map/ppermute | solution.py:236
  46.0 10.3 %collective-permute-done.9.arrived.refs_4_.refs_2_ = bf16[768,256]{1,0:T(8,128)(2,1)S(1)} collective-permute-done((bf16[768,256]{1,0:T(8,128)(2,1)S(1)}, bf16[768,256]{1,0:T(8,128)(2,1)S(1)}, u32[]{:S(2)}, u32[]{:S(2)}) %collective-permute-start.9) | collective-permute-done | bytes 393248 | tf_op jit(solution)/shard_map/ppermute | solution.py:236
  58.4 1.6 %collective-permute-start.14 = (s16[1056,256]{1,0:T(8,128)(2,1)S(1)}, s16[1056,256]{1,0:T(8,128)(2,1)S(1)}, u32[]{:S(2)}, u32[]{:S(2)}) collective-permute-start(s16[1056,256]{1,0:T(8,128)(2,1)S(1)} %get-tuple-element.36), channel_id=1, source_target_pairs={{0,16},{8,24},{16,0},{24,8},{1,17},{9,25},{17,1},{25,9},{2,18},{10... | collective-permute-start | bytes 1622024 | tf_op jit(solution)/shard_map/ppermute | solution.py:240
  60.8 2.0 %collective-permute-start.10 = (bf16[448,256]{1,0:T(8,128)(2,1)S(1)}, bf16[448,256]{1,0:T(8,128)(2,1)S(1)}, u32[]{:S(2)}, u32[]{:S(2)}) collective-permute-start(bf16[448,256]{1,0:T(8,128)(2,1)S(1)} %shard_map.58.refs_0_), channel_id=1, source_target_pairs={{0,1},{1,2},{2,3},{3,0},{4,5},{5,6},{6,7},{7,4},{8,9},{9,10},{10,1... | collective-permute-start | bytes 688136 | tf_op jit(solution)/shard_map/ppermute | solution.py:236
  62.8 7.1 %collective-permute-done.11.arrived.refs_4_.refs_2_ = bf16[640,256]{1,0:T(8,128)(2,1)S(1)} collective-permute-done((bf16[640,256]{1,0:T(8,128)(2,1)S(1)}, bf16[640,256]{1,0:T(8,128)(2,1)S(1)}, u32[]{:S(2)}, u32[]{:S(2)}) %collective-permute-start.11) | collective-permute-done | bytes 327712 | tf_op jit(solution)/shard_map/ppermute | solution.py:236
  70.6 1.9 %collective-permute-start.13 = (s16[400,256]{1,0:T(8,128)(2,1)S(1)}, s16[400,256]{1,0:T(8,128)(2,1)S(1)}, u32[]{:S(2)}, u32[]{:S(2)}) collective-permute-start(s16[400,256]{1,0:T(8,128)(2,1)S(1)} %shard_map.57.refs_0_), channel_id=1, source_target_pairs={{0,16},{8,24},{16,0},{24,8},{1,17},{9,25},{17,1},{25,9},{2,18},{10... | collective-permute-start | bytes 614408 | tf_op jit(solution)/shard_map/ppermute | solution.py:240
  73.9 1.6 %collective-permute-start.17 = (s16[1056,256]{1,0:T(8,128)(2,1)S(1)}, s16[1056,256]{1,0:T(8,128)(2,1)S(1)}, u32[]{:S(2)}, u32[]{:S(2)}) collective-permute-start(s16[1056,256]{1,0:T(8,128)(2,1)S(1)} %get-tuple-element.40), channel_id=1, source_target_pairs={{0,8},{8,0},{16,24},{24,16},{1,9},{9,1},{17,25},{25,17},{2,10},{10... | collective-permute-start | bytes 1622024 | tf_op jit(solution)/shard_map/ppermute | solution.py:240
  78.8 1.9 %collective-permute-start.21 = (s16[800,256]{1,0:T(8,128)(2,1)S(1)}, s16[800,256]{1,0:T(8,128)(2,1)S(1)}, u32[]{:S(2)}, u32[]{:S(2)}) collective-permute-start(s16[800,256]{1,0:T(8,128)(2,1)S(1)} %get-tuple-element.46), channel_id=1, source_target_pairs={{0,16},{8,24},{16,0},{24,8},{1,17},{9,25},{17,1},{25,9},{2,18},{10... | collective-permute-start | bytes 1228808 | tf_op jit(solution)/shard_map/ppermute | solution.py:240
  80.7 1.5 %collective-permute-start.24 = (s16[528,256]{1,0:T(8,128)(2,1)S(1)}, s16[528,256]{1,0:T(8,128)(2,1)S(1)}, u32[]{:S(2)}, u32[]{:S(2)}) collective-permute-start(s16[528,256]{1,0:T(8,128)(2,1)S(1)} %shard_map.61.refs_2_), channel_id=1, source_target_pairs={{0,8},{8,0},{16,24},{24,16},{1,9},{9,1},{17,25},{25,17},{2,10},{10... | collective-permute-start | bytes 811016 | tf_op jit(solution)/shard_map/ppermute | solution.py:240
  83.4 1.7 %collective-permute-start.15 = (bf16[128,256]{1,0:T(8,128)(2,1)S(1)}, bf16[128,256]{1,0:T(8,128)(2,1)S(1)}, u32[]{:S(2)}, u32[]{:S(2)}) collective-permute-start(bf16[128,256]{1,0:T(8,128)(2,1)S(1)} %shard_map.63.refs_0_), channel_id=1, source_target_pairs={{0,1},{1,2},{2,3},{3,0},{4,5},{5,6},{6,7},{7,4},{8,9},{9,10},{10,1... | collective-permute-start | bytes 196616 | tf_op jit(solution)/shard_map/ppermute | solution.py:236
  85.1 1.7 %collective-permute-done.17.received_ref.refs_0_ = s16[1056,256]{1,0:T(8,128)(2,1)S(1)} collective-permute-done((s16[1056,256]{1,0:T(8,128)(2,1)S(1)}, s16[1056,256]{1,0:T(8,128)(2,1)S(1)}, u32[]{:S(2)}, u32[]{:S(2)}) %collective-permute-start.17) | collective-permute-done | bytes 540704 | tf_op jit(solution)/shard_map/ppermute | solution.py:240
  87.3 2.2 %collective-permute-done.15.refs_3_ = bf16[128,256]{1,0:T(8,128)(2,1)S(1)} collective-permute-done((bf16[128,256]{1,0:T(8,128)(2,1)S(1)}, bf16[128,256]{1,0:T(8,128)(2,1)S(1)}, u32[]{:S(2)}, u32[]{:S(2)}) %collective-permute-start.15) | collective-permute-done | bytes 65568 | tf_op jit(solution)/shard_map/ppermute | solution.py:236
  91.1 1.5 %collective-permute-start.18 = (s16[272,256]{1,0:T(8,128)(2,1)S(1)}, s16[272,256]{1,0:T(8,128)(2,1)S(1)}, u32[]{:S(2)}, u32[]{:S(2)}) collective-permute-start(s16[272,256]{1,0:T(8,128)(2,1)S(1)} %get-tuple-element.43), channel_id=1, source_target_pairs={{0,24},{8,16},{16,8},{24,0},{1,25},{9,17},{17,9},{25,1},{2,26},{10... | collective-permute-start | bytes 417800 | tf_op jit(solution)/shard_map/ppermute | solution.py:240
  92.6 1.9 %collective-permute-start.19 = (s16[272,256]{1,0:T(8,128)(2,1)S(1)}, s16[272,256]{1,0:T(8,128)(2,1)S(1)}, u32[]{:S(2)}, u32[]{:S(2)}) collective-permute-start(s16[272,256]{1,0:T(8,128)(2,1)S(1)} %get-tuple-element.44), channel_id=1, source_target_pairs={{0,8},{8,0},{16,24},{24,16},{1,9},{9,1},{17,25},{25,17},{2,10},{10... | collective-permute-start | bytes 417800 | tf_op jit(solution)/shard_map/ppermute | solution.py:240
  95.0 1.6 %collective-permute-done.22.refs_1_ = s16[400,256]{1,0:T(8,128)(2,1)S(1)} collective-permute-done((s16[400,256]{1,0:T(8,128)(2,1)S(1)}, s16[400,256]{1,0:T(8,128)(2,1)S(1)}, u32[]{:S(2)}, u32[]{:S(2)}) %collective-permute-start.22) | collective-permute-done | bytes 204832 | tf_op jit(solution)/shard_map/ppermute | solution.py:240
  97.8 1.7 %collective-permute-done.19.refs_1_ = s16[272,256]{1,0:T(8,128)(2,1)S(1)} collective-permute-done((s16[272,256]{1,0:T(8,128)(2,1)S(1)}, s16[272,256]{1,0:T(8,128)(2,1)S(1)}, u32[]{:S(2)}, u32[]{:S(2)}) %collective-permute-start.19) | collective-permute-done | bytes 139296 | tf_op jit(solution)/shard_map/ppermute | solution.py:240
  (66 shorter events, 25.0 us)
Async XLA Ops:
  0.0 21.4 %collective-permute-start.3 = (bf16[512,4,256]{2,1,0:T(4,128)(2,1)}, bf16[512,4,256]{2,1,0:T(4,128)(2,1)S(1)}, u32[]{:S(2)}, u32[]{:S(2)}) collective-permute-start(bf16[512,4,256]{2,1,0:T(4,128)(2,1)} %values_ref.1), channel_id=1, source_target_pairs={{0,4},{4,0},{1,5},{5,1},{2,6},{6,2},{3,7},{7,3},{8,12},{12,8},{9,1... | collective-permute-start | bytes 3145736 | tf_op jit(solution)/shard_map/ppermute | solution.py:236
  2.9 10.5 %collective-permute-start = (bf16[384,256]{1,0:T(8,128)(2,1)S(1)}, bf16[384,256]{1,0:T(8,128)(2,1)S(1)}, u32[]{:S(2)}, u32[]{:S(2)}) collective-permute-start(bf16[384,256]{1,0:T(8,128)(2,1)S(1)} %shard_map.46.refs_0_), channel_id=1, source_target_pairs={{0,1},{1,2},{2,3},{3,0},{4,5},{5,6},{6,7},{7,4},{8,9},{9,10},{10,1... | collective-permute-start | bytes 589832 | tf_op jit(solution)/shard_map/ppermute | solution.py:236
  5.5 11.2 %collective-permute-start.4 = (bf16[384,256]{1,0:T(8,128)(2,1)S(1)}, bf16[384,256]{1,0:T(8,128)(2,1)S(1)}, u32[]{:S(2)}, u32[]{:S(2)}) collective-permute-start(bf16[384,256]{1,0:T(8,128)(2,1)S(1)} %shard_map.46.refs_0_), channel_id=1, source_target_pairs={{0,3},{1,0},{2,1},{3,2},{4,7},{5,4},{6,5},{7,6},{8,11},{9,8},{10,9... | collective-permute-start | bytes 589832 | tf_op jit(solution)/shard_map/ppermute | solution.py:236
  14.0 15.0 %collective-permute-start.1 = (bf16[704,256]{1,0:T(8,128)(2,1)S(1)}, bf16[704,256]{1,0:T(8,128)(2,1)S(1)}, u32[]{:S(2)}, u32[]{:S(2)}) collective-permute-start(bf16[704,256]{1,0:T(8,128)(2,1)S(1)} %shard_map.47.refs_0_), channel_id=1, source_target_pairs={{0,1},{1,2},{2,3},{3,0},{4,5},{5,6},{6,7},{7,4},{8,9},{9,10},{10,1... | collective-permute-start | bytes 1081352 | tf_op jit(solution)/shard_map/ppermute | solution.py:236
  17.4 19.2 %collective-permute-start.6 = (bf16[704,256]{1,0:T(8,128)(2,1)S(1)}, bf16[704,256]{1,0:T(8,128)(2,1)S(1)}, u32[]{:S(2)}, u32[]{:S(2)}) collective-permute-start(bf16[704,256]{1,0:T(8,128)(2,1)S(1)} %shard_map.48.refs_0_), channel_id=1, source_target_pairs={{0,3},{1,0},{2,1},{3,2},{4,7},{5,4},{6,5},{7,6},{8,11},{9,8},{10,9... | collective-permute-start | bytes 1081352 | tf_op jit(solution)/shard_map/ppermute | solution.py:236
  29.5 15.8 %collective-permute-start.5 = (bf16[768,256]{1,0:T(8,128)(2,1)S(1)}, bf16[768,256]{1,0:T(8,128)(2,1)S(1)}, u32[]{:S(2)}, u32[]{:S(2)}) collective-permute-start(bf16[768,256]{1,0:T(8,128)(2,1)S(1)} %shard_map.51.refs_0_), channel_id=1, source_target_pairs={{0,1},{1,2},{2,3},{3,0},{4,5},{5,6},{6,7},{7,4},{8,9},{9,10},{10,1... | collective-permute-start | bytes 1179656 | tf_op jit(solution)/shard_map/ppermute | solution.py:236
  37.1 19.2 %collective-permute-start.9 = (bf16[768,256]{1,0:T(8,128)(2,1)S(1)}, bf16[768,256]{1,0:T(8,128)(2,1)S(1)}, u32[]{:S(2)}, u32[]{:S(2)}) collective-permute-start(bf16[768,256]{1,0:T(8,128)(2,1)S(1)} %shard_map.52.refs_7_), channel_id=1, source_target_pairs={{0,3},{1,0},{2,1},{3,2},{4,7},{5,4},{6,5},{7,6},{8,11},{9,8},{10,9... | collective-permute-start | bytes 1179656 | tf_op jit(solution)/shard_map/ppermute | solution.py:236
  38.3 21.8 %collective-permute-start.8 = (s16[800,256]{1,0:T(8,128)(2,1)S(1)}, s16[800,256]{1,0:T(8,128)(2,1)S(1)}, u32[]{:S(2)}, u32[]{:S(2)}) collective-permute-start(s16[800,256]{1,0:T(8,128)(2,1)S(1)} %get-tuple-element.33), channel_id=1, source_target_pairs={{0,8},{8,0},{16,24},{24,16},{1,9},{9,1},{17,25},{25,17},{2,10},{10... | collective-permute-start | bytes 1228808 | tf_op jit(solution)/shard_map/ppermute | solution.py:240
  45.9 14.3 %collective-permute-start.7 = (bf16[640,256]{1,0:T(8,128)(2,1)S(1)}, bf16[640,256]{1,0:T(8,128)(2,1)S(1)}, u32[]{:S(2)}, u32[]{:S(2)}) collective-permute-start(bf16[640,256]{1,0:T(8,128)(2,1)S(1)} %shard_map.54.refs_0_), channel_id=1, source_target_pairs={{0,1},{1,2},{2,3},{3,0},{4,5},{5,6},{6,7},{7,4},{8,9},{9,10},{10,1... | collective-permute-start | bytes 983048 | tf_op jit(solution)/shard_map/ppermute | solution.py:236
  56.9 13.1 %collective-permute-start.11 = (bf16[640,256]{1,0:T(8,128)(2,1)S(1)}, bf16[640,256]{1,0:T(8,128)(2,1)S(1)}, u32[]{:S(2)}, u32[]{:S(2)}) collective-permute-start(bf16[640,256]{1,0:T(8,128)(2,1)S(1)} %shard_map.55.refs_7_), channel_id=1, source_target_pairs={{0,3},{1,0},{2,1},{3,2},{4,7},{5,4},{6,5},{7,6},{8,11},{9,8},{10,9... | collective-permute-start | bytes 983048 | tf_op jit(solution)/shard_map/ppermute | solution.py:236
  58.4 17.1 %collective-permute-start.14 = (s16[1056,256]{1,0:T(8,128)(2,1)S(1)}, s16[1056,256]{1,0:T(8,128)(2,1)S(1)}, u32[]{:S(2)}, u32[]{:S(2)}) collective-permute-start(s16[1056,256]{1,0:T(8,128)(2,1)S(1)} %get-tuple-element.36), channel_id=1, source_target_pairs={{0,16},{8,24},{16,0},{24,8},{1,17},{9,25},{17,1},{25,9},{2,18},{10... | collective-permute-start | bytes 1622024 | tf_op jit(solution)/shard_map/ppermute | solution.py:240
  60.8 15.8 %collective-permute-start.10 = (bf16[448,256]{1,0:T(8,128)(2,1)S(1)}, bf16[448,256]{1,0:T(8,128)(2,1)S(1)}, u32[]{:S(2)}, u32[]{:S(2)}) collective-permute-start(bf16[448,256]{1,0:T(8,128)(2,1)S(1)} %shard_map.58.refs_0_), channel_id=1, source_target_pairs={{0,1},{1,2},{2,3},{3,0},{4,5},{5,6},{6,7},{7,4},{8,9},{9,10},{10,1... | collective-permute-start | bytes 688136 | tf_op jit(solution)/shard_map/ppermute | solution.py:236
  70.5 6.6 %collective-permute-start.12 = (bf16[448,256]{1,0:T(8,128)(2,1)S(1)}, bf16[448,256]{1,0:T(8,128)(2,1)S(1)}, u32[]{:S(2)}, u32[]{:S(2)}) collective-permute-start(bf16[448,256]{1,0:T(8,128)(2,1)S(1)} %shard_map.59.refs_7_), channel_id=1, source_target_pairs={{0,3},{1,0},{2,1},{3,2},{4,7},{5,4},{6,5},{7,6},{8,11},{9,8},{10,9... | collective-permute-start | bytes 688136 | tf_op jit(solution)/shard_map/ppermute | solution.py:236
  70.6 5.8 %collective-permute-start.13 = (s16[400,256]{1,0:T(8,128)(2,1)S(1)}, s16[400,256]{1,0:T(8,128)(2,1)S(1)}, u32[]{:S(2)}, u32[]{:S(2)}) collective-permute-start(s16[400,256]{1,0:T(8,128)(2,1)S(1)} %shard_map.57.refs_0_), channel_id=1, source_target_pairs={{0,16},{8,24},{16,0},{24,8},{1,17},{9,25},{17,1},{25,9},{2,18},{10... | collective-permute-start | bytes 614408 | tf_op jit(solution)/shard_map/ppermute | solution.py:240
  73.9 12.9 %collective-permute-start.17 = (s16[1056,256]{1,0:T(8,128)(2,1)S(1)}, s16[1056,256]{1,0:T(8,128)(2,1)S(1)}, u32[]{:S(2)}, u32[]{:S(2)}) collective-permute-start(s16[1056,256]{1,0:T(8,128)(2,1)S(1)} %get-tuple-element.40), channel_id=1, source_target_pairs={{0,8},{8,0},{16,24},{24,16},{1,9},{9,1},{17,25},{25,17},{2,10},{10... | collective-permute-start | bytes 1622024 | tf_op jit(solution)/shard_map/ppermute | solution.py:240
  78.8 11.5 %collective-permute-start.21 = (s16[800,256]{1,0:T(8,128)(2,1)S(1)}, s16[800,256]{1,0:T(8,128)(2,1)S(1)}, u32[]{:S(2)}, u32[]{:S(2)}) collective-permute-start(s16[800,256]{1,0:T(8,128)(2,1)S(1)} %get-tuple-element.46), channel_id=1, source_target_pairs={{0,16},{8,24},{16,0},{24,8},{1,17},{9,25},{17,1},{25,9},{2,18},{10... | collective-permute-start | bytes 1228808 | tf_op jit(solution)/shard_map/ppermute | solution.py:240
  80.7 13.8 %collective-permute-start.24 = (s16[528,256]{1,0:T(8,128)(2,1)S(1)}, s16[528,256]{1,0:T(8,128)(2,1)S(1)}, u32[]{:S(2)}, u32[]{:S(2)}) collective-permute-start(s16[528,256]{1,0:T(8,128)(2,1)S(1)} %shard_map.61.refs_2_), channel_id=1, source_target_pairs={{0,8},{8,0},{16,24},{24,16},{1,9},{9,1},{17,25},{25,17},{2,10},{10... | collective-permute-start | bytes 811016 | tf_op jit(solution)/shard_map/ppermute | solution.py:240
  82.2 5.2 %collective-permute-start.16 = (bf16[128,256]{1,0:T(8,128)(2,1)S(1)}, bf16[128,256]{1,0:T(8,128)(2,1)S(1)}, u32[]{:S(2)}, u32[]{:S(2)}) collective-permute-start(bf16[128,256]{1,0:T(8,128)(2,1)S(1)} %shard_map.64.refs_7_), channel_id=1, source_target_pairs={{0,3},{1,0},{2,1},{3,2},{4,7},{5,4},{6,5},{7,6},{8,11},{9,8},{10,9... | collective-permute-start | bytes 196616 | tf_op jit(solution)/shard_map/ppermute | solution.py:236
  83.4 6.1 %collective-permute-start.15 = (bf16[128,256]{1,0:T(8,128)(2,1)S(1)}, bf16[128,256]{1,0:T(8,128)(2,1)S(1)}, u32[]{:S(2)}, u32[]{:S(2)}) collective-permute-start(bf16[128,256]{1,0:T(8,128)(2,1)S(1)} %shard_map.63.refs_0_), channel_id=1, source_target_pairs={{0,1},{1,2},{2,3},{3,0},{4,5},{5,6},{6,7},{7,4},{8,9},{9,10},{10,1... | collective-permute-start | bytes 196616 | tf_op jit(solution)/shard_map/ppermute | solution.py:236
  87.0 7.8 %collective-permute-start.23 = (s16[528,256]{1,0:T(8,128)(2,1)S(1)}, s16[528,256]{1,0:T(8,128)(2,1)S(1)}, u32[]{:S(2)}, u32[]{:S(2)}) collective-permute-start(s16[528,256]{1,0:T(8,128)(2,1)S(1)} %shard_map.66.refs_7_), channel_id=1, source_target_pairs={{0,16},{8,24},{16,0},{24,8},{1,17},{9,25},{17,1},{25,9},{2,18},{10... | collective-permute-start | bytes 811016 | tf_op jit(solution)/shard_map/ppermute | solution.py:240
  90.5 6.1 %collective-permute-start.22 = (s16[400,256]{1,0:T(8,128)(2,1)S(1)}, s16[400,256]{1,0:T(8,128)(2,1)S(1)}, u32[]{:S(2)}, u32[]{:S(2)}) collective-permute-start(s16[400,256]{1,0:T(8,128)(2,1)S(1)} %shard_map.68.refs_3_), channel_id=1, source_target_pairs={{0,8},{8,0},{16,24},{24,16},{1,9},{9,1},{17,25},{25,17},{2,10},{10... | collective-permute-start | bytes 614408 | tf_op jit(solution)/shard_map/ppermute | solution.py:240
  91.1 6.8 %collective-permute-start.18 = (s16[272,256]{1,0:T(8,128)(2,1)S(1)}, s16[272,256]{1,0:T(8,128)(2,1)S(1)}, u32[]{:S(2)}, u32[]{:S(2)}) collective-permute-start(s16[272,256]{1,0:T(8,128)(2,1)S(1)} %get-tuple-element.43), channel_id=1, source_target_pairs={{0,24},{8,16},{16,8},{24,0},{1,25},{9,17},{17,9},{25,1},{2,26},{10... | collective-permute-start | bytes 417800 | tf_op jit(solution)/shard_map/ppermute | solution.py:240
  92.6 6.9 %collective-permute-start.19 = (s16[272,256]{1,0:T(8,128)(2,1)S(1)}, s16[272,256]{1,0:T(8,128)(2,1)S(1)}, u32[]{:S(2)}, u32[]{:S(2)}) collective-permute-start(s16[272,256]{1,0:T(8,128)(2,1)S(1)} %get-tuple-element.44), channel_id=1, source_target_pairs={{0,8},{8,0},{16,24},{24,16},{1,9},{9,1},{17,25},{25,17},{2,10},{10... | collective-permute-start | bytes 417800 | tf_op jit(solution)/shard_map/ppermute | solution.py:240
  94.5 5.1 %collective-permute-start.20 = (s16[272,256]{1,0:T(8,128)(2,1)S(1)}, s16[272,256]{1,0:T(8,128)(2,1)S(1)}, u32[]{:S(2)}, u32[]{:S(2)}) collective-permute-start(s16[272,256]{1,0:T(8,128)(2,1)S(1)} %get-tuple-element.45), channel_id=1, source_target_pairs={{0,16},{8,24},{16,0},{24,8},{1,17},{9,25},{17,1},{25,9},{2,18},{10... | collective-permute-start | bytes 417800 | tf_op jit(solution)/shard_map/ppermute | solution.py:240
  (7 other events, 24.3 us)

commit v12 on v11

--- a/solution.py
+++ b/solution.py
@@ -9,7 +9,7 @@
 from jax.sharding import PartitionSpec as P
 
 TILE = 256
-SIXTEENTHS = (3, 4, 4, 3, 2)
+PARTS = (7, 8, 8, 6, 3)
 SCALE_ROWS = 16
 CODE = 64.0
 TOP = 32767.0
@@ -204,10 +204,11 @@
     sums, chunks = refs[:n_sums], refs[n_sums:-3]
     out_ref, block, sems = refs[-3:]
     colmean = sum(ref[...] for ref in sums) / rows_total
+    scale = 1.0 / (colmean + 1e-06)
     at, copies = 0, []
     for i, chunk in enumerate(chunks):
         rows = pl.ds(at, chunk.shape[0])
-        block[rows, :] = (chunk[...] / (colmean + 1e-06)).astype(jnp.bfloat16)
+        block[rows, :] = (chunk[...] * scale).astype(jnp.bfloat16)
         copies.append(pltpu.make_async_copy(block.at[rows], out_ref.at[rows], sems.at[i]))
         copies[-1].start()
         at += chunk.shape[0]
@@ -243,7 +244,7 @@
 def per_device(left_values, left_pattern, right_values, right_pattern):
     n_rows, n_cols = lax.axis_size("row"), lax.axis_size("col")
     rows_local, _, columns_local = left_values.shape
-    sizes = [rows_local * part // sum(SIXTEENTHS) for part in SIXTEENTHS]
+    sizes = [rows_local * part // sum(PARTS) for part in PARTS]
 
     left = left_values.reshape(rows_local, columns_local)
     pattern = left_pattern.reshape(-1)

time: 103 us -> 107 us (1.039); the launches traced: 102 us -> 107 us
  waiting for transfers between devices: 55.2 us -> 60.2 us
    ppermute x15, waiting for transfers between devices: 48.3 us -> 52.2 us  [shift(): return lax.ppermute(x, axis, [(i, (i + by) % n) for i in range(n)])]
    ppermute x11, starting transfers between devices: 14.3 us -> 15.4 us  [swap(): return lax.ppermute(x, 'layer', [(i, i ^ bits) for i in range(4)])]
    ppermute x11, waiting for transfers between devices: 6.93 us -> 8.02 us  [swap(): return lax.ppermute(x, 'layer', [(i, i ^ bits) for i in range(4)])]
  transfers between devices with their start and end apart: 26 -> 26, of which waited for: 16 -> 15; matrix products, arithmetic and copies ran while one was open for 0% -> 0% of each run, Pallas kernels for 15% -> 15%
where the time goes in v12:
time: 107 us
  waiting for transfers between devices  60.2 us (56%)
  starting transfers between devices  27.9 us (26%)
  Pallas kernels  16.9 us (16%)
  local copies, waits for them, and re-layouts  1.9 us (2%)
    ppermute x15, waiting for transfers between devices, shift(): return lax.ppermute(x, axis, [(i, (i + by) % n) for i in range(n)])  52.2 us
    ppermute x11, starting transfers between devices, swap(): return lax.ppermute(x, 'layer', [(i, i ^ bits) for i in range(4)])  15.4 us
    ppermute x15, starting transfers between devices, shift(): return lax.ppermute(x, axis, [(i, (i + by) % n) for i in range(n)])  12.5 us
    ppermute x11, waiting for transfers between devices, swap(): return lax.ppermute(x, 'layer', [(i, i ^ bits) for i in range(4)])  8.02 us
    pallas_call x11, Pallas kernels, load(): pl.pallas_call(functools.partial(load_kernel, at, size, parts), out_shape...  6.18 us
    pallas_call x5, Pallas kernels, partial_products(): pl.pallas_call(functools.partial(partial_kernel, tuple(steps), shapes, le...  5.99 us
    pallas_call x2, Pallas kernels, mask_right(): pl.pallas_call(mask_right_kernel, out_shape=jax.ShapeDtypeStruct((layers,...  2.27 us
  transfers between devices with their start and end apart: 26, of which 15 were waited for; matrix products, arithmetic and copies ran while one was open for 0% of the time, Pallas kernels for 15%

profile of v12, /device:TPU:0, one launch (start us, length us, event | category | flops | bytes accessed | tf_op | source)
XLA Modules:
  0.0 107.2 jit_solution(14550521319206355775)
XLA Ops:
  2.9 2.6 %collective-permute-start = (bf16[448,256]{1,0:T(8,128)(2,1)S(1)}, bf16[448,256]{1,0:T(8,128)(2,1)S(1)}, u32[]{:S(2)}, u32[]{:S(2)}) collective-permute-start(bf16[448,256]{1,0:T(8,128)(2,1)S(1)} %shard_map.46.refs_0_), channel_id=1, source_target_pairs={{0,1},{1,2},{2,3},{3,0},{4,5},{5,6},{6,7},{7,4},{8,9},{9,10},{10,1... | collective-permute-start | bytes 688136 | tf_op jit(solution)/shard_map/ppermute | solution.py:237
  5.5 2.1 %collective-permute-start.4 = (bf16[448,256]{1,0:T(8,128)(2,1)S(1)}, bf16[448,256]{1,0:T(8,128)(2,1)S(1)}, u32[]{:S(2)}, u32[]{:S(2)}) collective-permute-start(bf16[448,256]{1,0:T(8,128)(2,1)S(1)} %shard_map.46.refs_0_), channel_id=1, source_target_pairs={{0,3},{1,0},{2,1},{3,2},{4,7},{5,4},{6,5},{7,6},{8,11},{9,8},{10,9... | collective-permute-start | bytes 688136 | tf_op jit(solution)/shard_map/ppermute | solution.py:237
  7.6 6.4 %collective-permute-done.arrived.refs_1_ = bf16[448,256]{1,0:T(8,128)(2,1)S(1)} collective-permute-done((bf16[448,256]{1,0:T(8,128)(2,1)S(1)}, bf16[448,256]{1,0:T(8,128)(2,1)S(1)}, u32[]{:S(2)}, u32[]{:S(2)}) %collective-permute-start) | collective-permute-done | bytes 229408 | tf_op jit(solution)/shard_map/ppermute | solution.py:237
  14.7 3.5 %collective-permute-done.4.arrived.refs_2_ = bf16[448,256]{1,0:T(8,128)(2,1)S(1)} collective-permute-done((bf16[448,256]{1,0:T(8,128)(2,1)S(1)}, bf16[448,256]{1,0:T(8,128)(2,1)S(1)}, u32[]{:S(2)}, u32[]{:S(2)}) %collective-permute-start.4) | collective-permute-done | bytes 229408 | tf_op jit(solution)/shard_map/ppermute | solution.py:237
  18.8 2.8 %collective-permute-start.6 = (bf16[736,256]{1,0:T(8,128)(2,1)S(1)}, bf16[736,256]{1,0:T(8,128)(2,1)S(1)}, u32[]{:S(2)}, u32[]{:S(2)}) collective-permute-start(bf16[736,256]{1,0:T(8,128)(2,1)S(1)} %shard_map.48.refs_0_), channel_id=1, source_target_pairs={{0,3},{1,0},{2,1},{3,2},{4,7},{5,4},{6,5},{7,6},{8,11},{9,8},{10,9... | collective-permute-start | bytes 1130504 | tf_op jit(solution)/shard_map/ppermute | solution.py:237
  23.9 6.7 %collective-permute-done.1.arrived.refs_3_.refs_1_ = bf16[736,256]{1,0:T(8,128)(2,1)S(1)} collective-permute-done((bf16[736,256]{1,0:T(8,128)(2,1)S(1)}, bf16[736,256]{1,0:T(8,128)(2,1)S(1)}, u32[]{:S(2)}, u32[]{:S(2)}) %collective-permute-start.1) | collective-permute-done | bytes 376864 | tf_op jit(solution)/shard_map/ppermute | solution.py:237
  31.3 7.4 %collective-permute-done.6.arrived.refs_4_.refs_2_ = bf16[736,256]{1,0:T(8,128)(2,1)S(1)} collective-permute-done((bf16[736,256]{1,0:T(8,128)(2,1)S(1)}, bf16[736,256]{1,0:T(8,128)(2,1)S(1)}, u32[]{:S(2)}, u32[]{:S(2)}) %collective-permute-start.6) | collective-permute-done | bytes 376864 | tf_op jit(solution)/shard_map/ppermute | solution.py:237
  40.6 1.5 %collective-permute-start.8 = (s16[928,256]{1,0:T(8,128)(2,1)S(1)}, s16[928,256]{1,0:T(8,128)(2,1)S(1)}, u32[]{:S(2)}, u32[]{:S(2)}) collective-permute-start(s16[928,256]{1,0:T(8,128)(2,1)S(1)} %get-tuple-element.33), channel_id=1, source_target_pairs={{0,8},{8,0},{16,24},{24,16},{1,9},{9,1},{17,25},{25,17},{2,10},{10... | collective-permute-start | bytes 1425416 | tf_op jit(solution)/shard_map/ppermute | solution.py:241
  42.1 5.0 %collective-permute-done.5.arrived.refs_3_.refs_1_ = bf16[768,256]{1,0:T(8,128)(2,1)S(1)} collective-permute-done((bf16[768,256]{1,0:T(8,128)(2,1)S(1)}, bf16[768,256]{1,0:T(8,128)(2,1)S(1)}, u32[]{:S(2)}, u32[]{:S(2)}) %collective-permute-start.5) | collective-permute-done | bytes 393248 | tf_op jit(solution)/shard_map/ppermute | solution.py:237
  47.8 11.2 %collective-permute-done.9.arrived.refs_4_.refs_2_ = bf16[768,256]{1,0:T(8,128)(2,1)S(1)} collective-permute-done((bf16[768,256]{1,0:T(8,128)(2,1)S(1)}, bf16[768,256]{1,0:T(8,128)(2,1)S(1)}, u32[]{:S(2)}, u32[]{:S(2)}) %collective-permute-start.9) | collective-permute-done | bytes 393248 | tf_op jit(solution)/shard_map/ppermute | solution.py:237
  59.6 1.5 %shard_map.56 = (f32[512,256]{1,0:T(8,128)S(1)}, f32[512,256]{1,0:T(8,128)S(1)}, s16[1056,256]{1,0:T(8,128)(2,1)S(1)}) custom-call(bf16[736,256]{1,0:T(8,128)(2,1)S(1)} %shard_map.47.refs_0_, bf16[736,256]{1,0:T(8,128)(2,1)S(1)} %collective-permute-done.1.arrived.refs_3_.refs_1_, bf16[736,256]{1,0:T(8,128)(2,1)S(1)} %collective-permute-done.6.arrived.refs_4_.refs_2_, ...), custom_call_target="tpu_custom_call" | custom-call | flops 1073741824 | bytes 3932160 | tf_op jit(solution)/shard_map/pallas_call | solution.py:140
  61.1 1.6 %collective-permute-start.14 = (s16[1056,256]{1,0:T(8,128)(2,1)S(1)}, s16[1056,256]{1,0:T(8,128)(2,1)S(1)}, u32[]{:S(2)}, u32[]{:S(2)}) collective-permute-start(s16[1056,256]{1,0:T(8,128)(2,1)S(1)} %get-tuple-element.36), channel_id=1, source_target_pairs={{0,16},{8,24},{16,0},{24,8},{1,17},{9,25},{17,1},{25,9},{2,18},{10... | collective-permute-start | bytes 1622024 | tf_op jit(solution)/shard_map/ppermute | solution.py:241
  64.0 2.0 %collective-permute-start.10 = (bf16[384,256]{1,0:T(8,128)(2,1)S(1)}, bf16[384,256]{1,0:T(8,128)(2,1)S(1)}, u32[]{:S(2)}, u32[]{:S(2)}) collective-permute-start(bf16[384,256]{1,0:T(8,128)(2,1)S(1)} %shard_map.58.refs_0_), channel_id=1, source_target_pairs={{0,1},{1,2},{2,3},{3,0},{4,5},{5,6},{6,7},{7,4},{8,9},{9,10},{10,1... | collective-permute-start | bytes 589832 | tf_op jit(solution)/shard_map/ppermute | solution.py:237
  66.0 7.4 %collective-permute-done.11.arrived.refs_4_.refs_2_ = bf16[640,256]{1,0:T(8,128)(2,1)S(1)} collective-permute-done((bf16[640,256]{1,0:T(8,128)(2,1)S(1)}, bf16[640,256]{1,0:T(8,128)(2,1)S(1)}, u32[]{:S(2)}, u32[]{:S(2)}) %collective-permute-start.11) | collective-permute-done | bytes 327712 | tf_op jit(solution)/shard_map/ppermute | solution.py:237
  75.5 1.6 %collective-permute-start.17 = (s16[1056,256]{1,0:T(8,128)(2,1)S(1)}, s16[1056,256]{1,0:T(8,128)(2,1)S(1)}, u32[]{:S(2)}, u32[]{:S(2)}) collective-permute-start(s16[1056,256]{1,0:T(8,128)(2,1)S(1)} %get-tuple-element.40), channel_id=1, source_target_pairs={{0,8},{8,0},{16,24},{24,16},{1,9},{9,1},{17,25},{25,17},{2,10},{10... | collective-permute-start | bytes 1622024 | tf_op jit(solution)/shard_map/ppermute | solution.py:241
  77.2 2.3 %collective-permute-done.13.refs_1_ = s16[464,256]{1,0:T(8,128)(2,1)S(1)} collective-permute-done((s16[464,256]{1,0:T(8,128)(2,1)S(1)}, s16[464,256]{1,0:T(8,128)(2,1)S(1)}, u32[]{:S(2)}, u32[]{:S(2)}) %collective-permute-start.13) | collective-permute-done | bytes 237600 | tf_op jit(solution)/shard_map/ppermute | solution.py:241
  81.9 1.6 %collective-permute-start.21 = (s16[800,256]{1,0:T(8,128)(2,1)S(1)}, s16[800,256]{1,0:T(8,128)(2,1)S(1)}, u32[]{:S(2)}, u32[]{:S(2)}) collective-permute-start(s16[800,256]{1,0:T(8,128)(2,1)S(1)} %get-tuple-element.46), channel_id=1, source_target_pairs={{0,16},{8,24},{16,0},{24,8},{1,17},{9,25},{17,1},{25,9},{2,18},{10... | collective-permute-start | bytes 1228808 | tf_op jit(solution)/shard_map/ppermute | solution.py:241
  83.5 1.5 %collective-permute-start.24 = (s16[528,256]{1,0:T(8,128)(2,1)S(1)}, s16[528,256]{1,0:T(8,128)(2,1)S(1)}, u32[]{:S(2)}, u32[]{:S(2)}) collective-permute-start(s16[528,256]{1,0:T(8,128)(2,1)S(1)} %shard_map.61.refs_2_), channel_id=1, source_target_pairs={{0,8},{8,0},{16,24},{24,16},{1,9},{9,1},{17,25},{25,17},{2,10},{10... | collective-permute-start | bytes 811016 | tf_op jit(solution)/shard_map/ppermute | solution.py:241
  89.0 3.0 %collective-permute-done.15.refs_3_ = bf16[96,256]{1,0:T(8,128)(2,1)S(1)} collective-permute-done((bf16[96,256]{1,0:T(8,128)(2,1)S(1)}, bf16[96,256]{1,0:T(8,128)(2,1)S(1)}, u32[]{:S(2)}, u32[]{:S(2)}) %collective-permute-start.15) | collective-permute-done | bytes 49184 | tf_op jit(solution)/shard_map/ppermute | solution.py:237
  92.8 1.6 %collective-permute-done.21.received_ref.refs_0_ = s16[800,256]{1,0:T(8,128)(2,1)S(1)} collective-permute-done((s16[800,256]{1,0:T(8,128)(2,1)S(1)}, s16[800,256]{1,0:T(8,128)(2,1)S(1)}, u32[]{:S(2)}, u32[]{:S(2)}) %collective-permute-start.21) | collective-permute-done | bytes 409632 | tf_op jit(solution)/shard_map/ppermute | solution.py:241
  94.5 1.7 %collective-permute-start.22 = (s16[400,256]{1,0:T(8,128)(2,1)S(1)}, s16[400,256]{1,0:T(8,128)(2,1)S(1)}, u32[]{:S(2)}, u32[]{:S(2)}) collective-permute-start(s16[400,256]{1,0:T(8,128)(2,1)S(1)} %shard_map.68.refs_3_), channel_id=1, source_target_pairs={{0,8},{8,0},{16,24},{24,16},{1,9},{9,1},{17,25},{25,17},{2,10},{10... | collective-permute-start | bytes 614408 | tf_op jit(solution)/shard_map/ppermute | solution.py:241
  96.2 2.5 %collective-permute-start.18 = (s16[208,256]{1,0:T(8,128)(2,1)S(1)}, s16[208,256]{1,0:T(8,128)(2,1)S(1)}, u32[]{:S(2)}, u32[]{:S(2)}) collective-permute-start(s16[208,256]{1,0:T(8,128)(2,1)S(1)} %get-tuple-element.43), channel_id=1, source_target_pairs={{0,24},{8,16},{16,8},{24,0},{1,25},{9,17},{17,9},{25,1},{2,26},{10... | collective-permute-start | bytes 319496 | tf_op jit(solution)/shard_map/ppermute | solution.py:241
  98.7 1.5 %collective-permute-start.19 = (s16[208,256]{1,0:T(8,128)(2,1)S(1)}, s16[208,256]{1,0:T(8,128)(2,1)S(1)}, u32[]{:S(2)}, u32[]{:S(2)}) collective-permute-start(s16[208,256]{1,0:T(8,128)(2,1)S(1)} %get-tuple-element.44), channel_id=1, source_target_pairs={{0,8},{8,0},{16,24},{24,16},{1,9},{9,1},{17,25},{25,17},{2,10},{10... | collective-permute-start | bytes 319496 | tf_op jit(solution)/shard_map/ppermute | solution.py:241
  100.7 2.8 %collective-permute-done.18.refs_0_ = s16[208,256]{1,0:T(8,128)(2,1)S(1)} collective-permute-done((s16[208,256]{1,0:T(8,128)(2,1)S(1)}, s16[208,256]{1,0:T(8,128)(2,1)S(1)}, u32[]{:S(2)}, u32[]{:S(2)}) %collective-permute-start.18) | collective-permute-done | bytes 106528 | tf_op jit(solution)/shard_map/ppermute | solution.py:241
  (66 shorter events, 25.1 us)
Async XLA Ops:
  0.0 22.8 %collective-permute-start.3 = (bf16[512,4,256]{2,1,0:T(4,128)(2,1)}, bf16[512,4,256]{2,1,0:T(4,128)(2,1)S(1)}, u32[]{:S(2)}, u32[]{:S(2)}) collective-permute-start(bf16[512,4,256]{2,1,0:T(4,128)(2,1)} %values_ref.1), channel_id=1, source_target_pairs={{0,4},{4,0},{1,5},{5,1},{2,6},{6,2},{3,7},{7,3},{8,12},{12,8},{9,1... | collective-permute-start | bytes 3145736 | tf_op jit(solution)/shard_map/ppermute | solution.py:237
  2.9 11.2 %collective-permute-start = (bf16[448,256]{1,0:T(8,128)(2,1)S(1)}, bf16[448,256]{1,0:T(8,128)(2,1)S(1)}, u32[]{:S(2)}, u32[]{:S(2)}) collective-permute-start(bf16[448,256]{1,0:T(8,128)(2,1)S(1)} %shard_map.46.refs_0_), channel_id=1, source_target_pairs={{0,1},{1,2},{2,3},{3,0},{4,5},{5,6},{6,7},{7,4},{8,9},{9,10},{10,1... | collective-permute-start | bytes 688136 | tf_op jit(solution)/shard_map/ppermute | solution.py:237
  5.5 12.7 %collective-permute-start.4 = (bf16[448,256]{1,0:T(8,128)(2,1)S(1)}, bf16[448,256]{1,0:T(8,128)(2,1)S(1)}, u32[]{:S(2)}, u32[]{:S(2)}) collective-permute-start(bf16[448,256]{1,0:T(8,128)(2,1)S(1)} %shard_map.46.refs_0_), channel_id=1, source_target_pairs={{0,3},{1,0},{2,1},{3,2},{4,7},{5,4},{6,5},{7,6},{8,11},{9,8},{10,9... | collective-permute-start | bytes 688136 | tf_op jit(solution)/shard_map/ppermute | solution.py:237
  14.7 16.0 %collective-permute-start.1 = (bf16[736,256]{1,0:T(8,128)(2,1)S(1)}, bf16[736,256]{1,0:T(8,128)(2,1)S(1)}, u32[]{:S(2)}, u32[]{:S(2)}) collective-permute-start(bf16[736,256]{1,0:T(8,128)(2,1)S(1)} %shard_map.47.refs_0_), channel_id=1, source_target_pairs={{0,1},{1,2},{2,3},{3,0},{4,5},{5,6},{6,7},{7,4},{8,9},{9,10},{10,1... | collective-permute-start | bytes 1130504 | tf_op jit(solution)/shard_map/ppermute | solution.py:237
  18.8 19.9 %collective-permute-start.6 = (bf16[736,256]{1,0:T(8,128)(2,1)S(1)}, bf16[736,256]{1,0:T(8,128)(2,1)S(1)}, u32[]{:S(2)}, u32[]{:S(2)}) collective-permute-start(bf16[736,256]{1,0:T(8,128)(2,1)S(1)} %shard_map.48.refs_0_), channel_id=1, source_target_pairs={{0,3},{1,0},{2,1},{3,2},{4,7},{5,4},{6,5},{7,6},{8,11},{9,8},{10,9... | collective-permute-start | bytes 1130504 | tf_op jit(solution)/shard_map/ppermute | solution.py:237
  31.2 15.9 %collective-permute-start.5 = (bf16[768,256]{1,0:T(8,128)(2,1)S(1)}, bf16[768,256]{1,0:T(8,128)(2,1)S(1)}, u32[]{:S(2)}, u32[]{:S(2)}) collective-permute-start(bf16[768,256]{1,0:T(8,128)(2,1)S(1)} %shard_map.51.refs_0_), channel_id=1, source_target_pairs={{0,1},{1,2},{2,3},{3,0},{4,5},{5,6},{6,7},{7,4},{8,9},{9,10},{10,1... | collective-permute-start | bytes 1179656 | tf_op jit(solution)/shard_map/ppermute | solution.py:237
  39.3 19.7 %collective-permute-start.9 = (bf16[768,256]{1,0:T(8,128)(2,1)S(1)}, bf16[768,256]{1,0:T(8,128)(2,1)S(1)}, u32[]{:S(2)}, u32[]{:S(2)}) collective-permute-start(bf16[768,256]{1,0:T(8,128)(2,1)S(1)} %shard_map.52.refs_7_), channel_id=1, source_target_pairs={{0,3},{1,0},{2,1},{3,2},{4,7},{5,4},{6,5},{7,6},{8,11},{9,8},{10,9... | collective-permute-start | bytes 1179656 | tf_op jit(solution)/shard_map/ppermute | solution.py:237
  40.6 22.1 %collective-permute-start.8 = (s16[928,256]{1,0:T(8,128)(2,1)S(1)}, s16[928,256]{1,0:T(8,128)(2,1)S(1)}, u32[]{:S(2)}, u32[]{:S(2)}) collective-permute-start(s16[928,256]{1,0:T(8,128)(2,1)S(1)} %get-tuple-element.33), channel_id=1, source_target_pairs={{0,8},{8,0},{16,24},{24,16},{1,9},{9,1},{17,25},{25,17},{2,10},{10... | collective-permute-start | bytes 1425416 | tf_op jit(solution)/shard_map/ppermute | solution.py:241
  47.7 15.7 %collective-permute-start.7 = (bf16[640,256]{1,0:T(8,128)(2,1)S(1)}, bf16[640,256]{1,0:T(8,128)(2,1)S(1)}, u32[]{:S(2)}, u32[]{:S(2)}) collective-permute-start(bf16[640,256]{1,0:T(8,128)(2,1)S(1)} %shard_map.54.refs_0_), channel_id=1, source_target_pairs={{0,1},{1,2},{2,3},{3,0},{4,5},{5,6},{6,7},{7,4},{8,9},{9,10},{10,1... | collective-permute-start | bytes 983048 | tf_op jit(solution)/shard_map/ppermute | solution.py:237
  59.6 13.8 %collective-permute-start.11 = (bf16[640,256]{1,0:T(8,128)(2,1)S(1)}, bf16[640,256]{1,0:T(8,128)(2,1)S(1)}, u32[]{:S(2)}, u32[]{:S(2)}) collective-permute-start(bf16[640,256]{1,0:T(8,128)(2,1)S(1)} %shard_map.55.refs_7_), channel_id=1, source_target_pairs={{0,3},{1,0},{2,1},{3,2},{4,7},{5,4},{6,5},{7,6},{8,11},{9,8},{10,9... | collective-permute-start | bytes 983048 | tf_op jit(solution)/shard_map/ppermute | solution.py:237
  61.1 15.9 %collective-permute-start.14 = (s16[1056,256]{1,0:T(8,128)(2,1)S(1)}, s16[1056,256]{1,0:T(8,128)(2,1)S(1)}, u32[]{:S(2)}, u32[]{:S(2)}) collective-permute-start(s16[1056,256]{1,0:T(8,128)(2,1)S(1)} %get-tuple-element.36), channel_id=1, source_target_pairs={{0,16},{8,24},{16,0},{24,8},{1,17},{9,25},{17,1},{25,9},{2,18},{10... | collective-permute-start | bytes 1622024 | tf_op jit(solution)/shard_map/ppermute | solution.py:241
  62.8 16.7 %collective-permute-start.13 = (s16[464,256]{1,0:T(8,128)(2,1)S(1)}, s16[464,256]{1,0:T(8,128)(2,1)S(1)}, u32[]{:S(2)}, u32[]{:S(2)}) collective-permute-start(s16[464,256]{1,0:T(8,128)(2,1)S(1)} %shard_map.57.refs_0_), channel_id=1, source_target_pairs={{0,16},{8,24},{16,0},{24,8},{1,17},{9,25},{17,1},{25,9},{2,18},{10... | collective-permute-start | bytes 712712 | tf_op jit(solution)/shard_map/ppermute | solution.py:241
  64.0 15.7 %collective-permute-start.10 = (bf16[384,256]{1,0:T(8,128)(2,1)S(1)}, bf16[384,256]{1,0:T(8,128)(2,1)S(1)}, u32[]{:S(2)}, u32[]{:S(2)}) collective-permute-start(bf16[384,256]{1,0:T(8,128)(2,1)S(1)} %shard_map.58.refs_0_), channel_id=1, source_target_pairs={{0,1},{1,2},{2,3},{3,0},{4,5},{5,6},{6,7},{7,4},{8,9},{9,10},{10,1... | collective-permute-start | bytes 589832 | tf_op jit(solution)/shard_map/ppermute | solution.py:237
  73.9 6.3 %collective-permute-start.12 = (bf16[384,256]{1,0:T(8,128)(2,1)S(1)}, bf16[384,256]{1,0:T(8,128)(2,1)S(1)}, u32[]{:S(2)}, u32[]{:S(2)}) collective-permute-start(bf16[384,256]{1,0:T(8,128)(2,1)S(1)} %shard_map.59.refs_7_), channel_id=1, source_target_pairs={{0,3},{1,0},{2,1},{3,2},{4,7},{5,4},{6,5},{7,6},{8,11},{9,8},{10,9... | collective-permute-start | bytes 589832 | tf_op jit(solution)/shard_map/ppermute | solution.py:237
  75.5 11.5 %collective-permute-start.17 = (s16[1056,256]{1,0:T(8,128)(2,1)S(1)}, s16[1056,256]{1,0:T(8,128)(2,1)S(1)}, u32[]{:S(2)}, u32[]{:S(2)}) collective-permute-start(s16[1056,256]{1,0:T(8,128)(2,1)S(1)} %get-tuple-element.40), channel_id=1, source_target_pairs={{0,8},{8,0},{16,24},{24,16},{1,9},{9,1},{17,25},{25,17},{2,10},{10... | collective-permute-start | bytes 1622024 | tf_op jit(solution)/shard_map/ppermute | solution.py:241
  81.9 12.5 %collective-permute-start.21 = (s16[800,256]{1,0:T(8,128)(2,1)S(1)}, s16[800,256]{1,0:T(8,128)(2,1)S(1)}, u32[]{:S(2)}, u32[]{:S(2)}) collective-permute-start(s16[800,256]{1,0:T(8,128)(2,1)S(1)} %get-tuple-element.46), channel_id=1, source_target_pairs={{0,16},{8,24},{16,0},{24,8},{1,17},{9,25},{17,1},{25,9},{2,18},{10... | collective-permute-start | bytes 1228808 | tf_op jit(solution)/shard_map/ppermute | solution.py:241
  83.5 16.7 %collective-permute-start.24 = (s16[528,256]{1,0:T(8,128)(2,1)S(1)}, s16[528,256]{1,0:T(8,128)(2,1)S(1)}, u32[]{:S(2)}, u32[]{:S(2)}) collective-permute-start(s16[528,256]{1,0:T(8,128)(2,1)S(1)} %shard_map.61.refs_2_), channel_id=1, source_target_pairs={{0,8},{8,0},{16,24},{24,16},{1,9},{9,1},{17,25},{25,17},{2,10},{10... | collective-permute-start | bytes 811016 | tf_op jit(solution)/shard_map/ppermute | solution.py:241
  85.0 4.1 %collective-permute-start.16 = (bf16[96,256]{1,0:T(8,128)(2,1)S(1)}, bf16[96,256]{1,0:T(8,128)(2,1)S(1)}, u32[]{:S(2)}, u32[]{:S(2)}) collective-permute-start(bf16[96,256]{1,0:T(8,128)(2,1)S(1)} %shard_map.64.refs_7_), channel_id=1, source_target_pairs={{0,3},{1,0},{2,1},{3,2},{4,7},{5,4},{6,5},{7,6},{8,11},{9,8},{10,9... | collective-permute-start | bytes 147464 | tf_op jit(solution)/shard_map/ppermute | solution.py:237
  86.2 5.9 %collective-permute-start.15 = (bf16[96,256]{1,0:T(8,128)(2,1)S(1)}, bf16[96,256]{1,0:T(8,128)(2,1)S(1)}, u32[]{:S(2)}, u32[]{:S(2)}) collective-permute-start(bf16[96,256]{1,0:T(8,128)(2,1)S(1)} %shard_map.63.refs_0_), channel_id=1, source_target_pairs={{0,1},{1,2},{2,3},{3,0},{4,5},{5,6},{6,7},{7,4},{8,9},{9,10},{10,1... | collective-permute-start | bytes 147464 | tf_op jit(solution)/shard_map/ppermute | solution.py:237
  87.2 13.2 %collective-permute-start.23 = (s16[528,256]{1,0:T(8,128)(2,1)S(1)}, s16[528,256]{1,0:T(8,128)(2,1)S(1)}, u32[]{:S(2)}, u32[]{:S(2)}) collective-permute-start(s16[528,256]{1,0:T(8,128)(2,1)S(1)} %shard_map.66.refs_7_), channel_id=1, source_target_pairs={{0,16},{8,24},{16,0},{24,8},{1,17},{9,25},{17,1},{25,9},{2,18},{10... | collective-permute-start | bytes 811016 | tf_op jit(solution)/shard_map/ppermute | solution.py:241
  94.5 6.0 %collective-permute-start.22 = (s16[400,256]{1,0:T(8,128)(2,1)S(1)}, s16[400,256]{1,0:T(8,128)(2,1)S(1)}, u32[]{:S(2)}, u32[]{:S(2)}) collective-permute-start(s16[400,256]{1,0:T(8,128)(2,1)S(1)} %shard_map.68.refs_3_), channel_id=1, source_target_pairs={{0,8},{8,0},{16,24},{24,16},{1,9},{9,1},{17,25},{25,17},{2,10},{10... | collective-permute-start | bytes 614408 | tf_op jit(solution)/shard_map/ppermute | solution.py:241
  96.2 7.3 %collective-permute-start.18 = (s16[208,256]{1,0:T(8,128)(2,1)S(1)}, s16[208,256]{1,0:T(8,128)(2,1)S(1)}, u32[]{:S(2)}, u32[]{:S(2)}) collective-permute-start(s16[208,256]{1,0:T(8,128)(2,1)S(1)} %get-tuple-element.43), channel_id=1, source_target_pairs={{0,24},{8,16},{16,8},{24,0},{1,25},{9,17},{17,9},{25,1},{2,26},{10... | collective-permute-start | bytes 319496 | tf_op jit(solution)/shard_map/ppermute | solution.py:241
  98.7 5.3 %collective-permute-start.19 = (s16[208,256]{1,0:T(8,128)(2,1)S(1)}, s16[208,256]{1,0:T(8,128)(2,1)S(1)}, u32[]{:S(2)}, u32[]{:S(2)}) collective-permute-start(s16[208,256]{1,0:T(8,128)(2,1)S(1)} %get-tuple-element.44), channel_id=1, source_target_pairs={{0,8},{8,0},{16,24},{24,16},{1,9},{9,1},{17,25},{25,17},{2,10},{10... | collective-permute-start | bytes 319496 | tf_op jit(solution)/shard_map/ppermute | solution.py:241
  100.2 4.7 %collective-permute-start.20 = (s16[208,256]{1,0:T(8,128)(2,1)S(1)}, s16[208,256]{1,0:T(8,128)(2,1)S(1)}, u32[]{:S(2)}, u32[]{:S(2)}) collective-permute-start(s16[208,256]{1,0:T(8,128)(2,1)S(1)} %get-tuple-element.45), channel_id=1, source_target_pairs={{0,16},{8,24},{16,0},{24,8},{1,17},{9,25},{17,1},{25,9},{2,18},{10... | collective-permute-start | bytes 319496 | tf_op jit(solution)/shard_map/ppermute | solution.py:241
  (7 other events, 26.0 us)

commit v13 on v11

--- a/solution.py
+++ b/solution.py
@@ -256,14 +256,21 @@
     found = [([], []) for _ in sizes]
     kept, received, last = [], [], []
 
+    def is_last(c):
+        return c + 1 == len(sizes)
+
     def open_slot(slot):
         at, size = (starts[slot], sizes[slot]) if slot < len(sizes) else (0, 0)
         for d in (0, 1):
-            riders = [c for c in range(min(slot, len(sizes))) if len(found[c][d]) < reach]
+            riders = [
+                c for c in range(min(slot, len(sizes))) if len(found[c][d]) < reach - d * is_last(c)
+            ]
+            if not size and not riders:
+                continue
             parts = []
             for c in riders:
                 _, first, rows = found[c][d][-1]
-                if len(found[c][d]) == reach - 1:
+                if len(found[c][d]) == reach - 1 and not is_last(c):
                     first, rows = first + d * (rows // 2), rows // 2
                 parts.append((first, rows))
             arrived = found[riders[0]][d][-1][0] if riders else left
@@ -281,8 +288,9 @@
                     own.append((block, first, size))
 
     def sources(i):
-        (*below, last_below), (*above, last_above) = found[i]
-        return [[part] for part in [own[i]] + below + above] + [[last_below, last_above]]
+        below, above = (found[i][d][: reach - 1] for d in (0, 1))
+        farthest = [part for d in (0, 1) for part in found[i][d][reach - 1 :]]
+        return [[part] for part in [own[i]] + below + above] + [farthest]
 
     def sum_chunk(i):
         if i + 1 < len(sizes):

time: 103 us -> 103 us (level); the launches traced: 102 us -> 103 us
  starting transfers between devices: 27.7 us -> 30.1 us
    ppermute x11, starting transfers between devices: 14.3 us -> 16.7 us  [swap(): return lax.ppermute(x, 'layer', [(i, i ^ bits) for i in range(4)])]
    ppermute x15 -> x14, waiting for transfers between devices: 48.3 us -> 47.5 us  [shift(): return lax.ppermute(x, axis, [(i, (i + by) % n) for i in range(n)])]
    pallas_call x11 -> x10, Pallas kernels: 6.18 us -> 5.64 us  [load(): pl.pallas_call(functools.partial(load_kernel, at, size, parts), out_shape...]
    ppermute x15 -> x14, starting transfers between devices: 13.4 us -> 13.5 us  [shift(): return lax.ppermute(x, axis, [(i, (i + by) % n) for i in range(n)])]
  transfers between devices with their start and end apart: 26 -> 25, of which waited for: 16 -> 15; matrix products, arithmetic and copies ran while one was open for 0% -> 0% of each run, Pallas kernels for 15% -> 15%
where the time goes in v13:
time: 103 us
  waiting for transfers between devices  54.5 us (53%)
  starting transfers between devices  30.1 us (29%)
  Pallas kernels  16.3 us (16%)
  local copies, waits for them, and re-layouts  1.9 us (2%)
    ppermute x14, waiting for transfers between devices, shift(): return lax.ppermute(x, axis, [(i, (i + by) % n) for i in range(n)])  47.5 us
    ppermute x11, starting transfers between devices, swap(): return lax.ppermute(x, 'layer', [(i, i ^ bits) for i in range(4)])  16.7 us
    ppermute x14, starting transfers between devices, shift(): return lax.ppermute(x, axis, [(i, (i + by) % n) for i in range(n)])  13.5 us
    ppermute x11, waiting for transfers between devices, swap(): return lax.ppermute(x, 'layer', [(i, i ^ bits) for i in range(4)])  7.02 us
    pallas_call x5, Pallas kernels, partial_products(): pl.pallas_call(functools.partial(partial_kernel, tuple(steps), shapes, le...  5.92 us
    pallas_call x10, Pallas kernels, load(): pl.pallas_call(functools.partial(load_kernel, at, size, parts), out_shape...  5.64 us
    pallas_call x2, Pallas kernels, mask_right(): pl.pallas_call(mask_right_kernel, out_shape=jax.ShapeDtypeStruct((layers,...  2.27 us
  transfers between devices with their start and end apart: 25, of which 15 were waited for; matrix products, arithmetic and copies ran while one was open for 0% of the time, Pallas kernels for 15%

profile of v13, /device:TPU:0, one launch (start us, length us, event | category | flops | bytes accessed | tf_op | source)
XLA Modules:
  0.0 103.2 jit_solution(2005571913513995976)
XLA Ops:
  2.9 2.6 %collective-permute-start = (bf16[384,256]{1,0:T(8,128)(2,1)S(1)}, bf16[384,256]{1,0:T(8,128)(2,1)S(1)}, u32[]{:S(2)}, u32[]{:S(2)}) collective-permute-start(bf16[384,256]{1,0:T(8,128)(2,1)S(1)} %shard_map.46.refs_0_), channel_id=1, source_target_pairs={{0,1},{1,2},{2,3},{3,0},{4,5},{5,6},{6,7},{7,4},{8,9},{9,10},{10,1... | collective-permute-start | bytes 589832 | tf_op jit(solution)/shard_map/ppermute | solution.py:236
  5.5 2.1 %collective-permute-start.4 = (bf16[384,256]{1,0:T(8,128)(2,1)S(1)}, bf16[384,256]{1,0:T(8,128)(2,1)S(1)}, u32[]{:S(2)}, u32[]{:S(2)}) collective-permute-start(bf16[384,256]{1,0:T(8,128)(2,1)S(1)} %shard_map.46.refs_0_), channel_id=1, source_target_pairs={{0,3},{1,0},{2,1},{3,2},{4,7},{5,4},{6,5},{7,6},{8,11},{9,8},{10,9... | collective-permute-start | bytes 589832 | tf_op jit(solution)/shard_map/ppermute | solution.py:236
  7.6 5.7 %collective-permute-done.arrived.refs_1_ = bf16[384,256]{1,0:T(8,128)(2,1)S(1)} collective-permute-done((bf16[384,256]{1,0:T(8,128)(2,1)S(1)}, bf16[384,256]{1,0:T(8,128)(2,1)S(1)}, u32[]{:S(2)}, u32[]{:S(2)}) %collective-permute-start) | collective-permute-done | bytes 196640 | tf_op jit(solution)/shard_map/ppermute | solution.py:236
  14.0 2.8 %collective-permute-done.4.arrived.refs_2_ = bf16[384,256]{1,0:T(8,128)(2,1)S(1)} collective-permute-done((bf16[384,256]{1,0:T(8,128)(2,1)S(1)}, bf16[384,256]{1,0:T(8,128)(2,1)S(1)}, u32[]{:S(2)}, u32[]{:S(2)}) %collective-permute-start.4) | collective-permute-done | bytes 196640 | tf_op jit(solution)/shard_map/ppermute | solution.py:236
  17.4 2.8 %collective-permute-start.6 = (bf16[704,256]{1,0:T(8,128)(2,1)S(1)}, bf16[704,256]{1,0:T(8,128)(2,1)S(1)}, u32[]{:S(2)}, u32[]{:S(2)}) collective-permute-start(bf16[704,256]{1,0:T(8,128)(2,1)S(1)} %shard_map.48.refs_0_), channel_id=1, source_target_pairs={{0,3},{1,0},{2,1},{3,2},{4,7},{5,4},{6,5},{7,6},{8,11},{9,8},{10,9... | collective-permute-start | bytes 1081352 | tf_op jit(solution)/shard_map/ppermute | solution.py:236
  22.5 6.4 %collective-permute-done.1.arrived.refs_3_.refs_1_ = bf16[704,256]{1,0:T(8,128)(2,1)S(1)} collective-permute-done((bf16[704,256]{1,0:T(8,128)(2,1)S(1)}, bf16[704,256]{1,0:T(8,128)(2,1)S(1)}, u32[]{:S(2)}, u32[]{:S(2)}) %collective-permute-start.1) | collective-permute-done | bytes 360480 | tf_op jit(solution)/shard_map/ppermute | solution.py:236
  29.6 7.0 %collective-permute-done.6.arrived.refs_4_.refs_2_ = bf16[704,256]{1,0:T(8,128)(2,1)S(1)} collective-permute-done((bf16[704,256]{1,0:T(8,128)(2,1)S(1)}, bf16[704,256]{1,0:T(8,128)(2,1)S(1)}, u32[]{:S(2)}, u32[]{:S(2)}) %collective-permute-start.6) | collective-permute-done | bytes 360480 | tf_op jit(solution)/shard_map/ppermute | solution.py:236
  38.3 1.6 %collective-permute-start.8 = (s16[800,256]{1,0:T(8,128)(2,1)S(1)}, s16[800,256]{1,0:T(8,128)(2,1)S(1)}, u32[]{:S(2)}, u32[]{:S(2)}) collective-permute-start(s16[800,256]{1,0:T(8,128)(2,1)S(1)} %get-tuple-element.33), channel_id=1, source_target_pairs={{0,8},{8,0},{16,24},{24,16},{1,9},{9,1},{17,25},{25,17},{2,10},{10... | collective-permute-start | bytes 1228808 | tf_op jit(solution)/shard_map/ppermute | solution.py:240
  39.9 5.5 %collective-permute-done.5.arrived.refs_3_.refs_1_ = bf16[768,256]{1,0:T(8,128)(2,1)S(1)} collective-permute-done((bf16[768,256]{1,0:T(8,128)(2,1)S(1)}, bf16[768,256]{1,0:T(8,128)(2,1)S(1)}, u32[]{:S(2)}, u32[]{:S(2)}) %collective-permute-start.5) | collective-permute-done | bytes 393248 | tf_op jit(solution)/shard_map/ppermute | solution.py:236
  46.0 10.3 %collective-permute-done.9.arrived.refs_4_.refs_2_ = bf16[768,256]{1,0:T(8,128)(2,1)S(1)} collective-permute-done((bf16[768,256]{1,0:T(8,128)(2,1)S(1)}, bf16[768,256]{1,0:T(8,128)(2,1)S(1)}, u32[]{:S(2)}, u32[]{:S(2)}) %collective-permute-start.9) | collective-permute-done | bytes 393248 | tf_op jit(solution)/shard_map/ppermute | solution.py:236
  58.4 1.6 %collective-permute-start.14 = (s16[1056,256]{1,0:T(8,128)(2,1)S(1)}, s16[1056,256]{1,0:T(8,128)(2,1)S(1)}, u32[]{:S(2)}, u32[]{:S(2)}) collective-permute-start(s16[1056,256]{1,0:T(8,128)(2,1)S(1)} %get-tuple-element.36), channel_id=1, source_target_pairs={{0,16},{8,24},{16,0},{24,8},{1,17},{9,25},{17,1},{25,9},{2,18},{10... | collective-permute-start | bytes 1622024 | tf_op jit(solution)/shard_map/ppermute | solution.py:240
  60.8 2.0 %collective-permute-start.10 = (bf16[448,256]{1,0:T(8,128)(2,1)S(1)}, bf16[448,256]{1,0:T(8,128)(2,1)S(1)}, u32[]{:S(2)}, u32[]{:S(2)}) collective-permute-start(bf16[448,256]{1,0:T(8,128)(2,1)S(1)} %shard_map.58.refs_0_), channel_id=1, source_target_pairs={{0,1},{1,2},{2,3},{3,0},{4,5},{5,6},{6,7},{7,4},{8,9},{9,10},{10,1... | collective-permute-start | bytes 688136 | tf_op jit(solution)/shard_map/ppermute | solution.py:236
  62.8 7.1 %collective-permute-done.11.arrived.refs_4_.refs_2_ = bf16[640,256]{1,0:T(8,128)(2,1)S(1)} collective-permute-done((bf16[640,256]{1,0:T(8,128)(2,1)S(1)}, bf16[640,256]{1,0:T(8,128)(2,1)S(1)}, u32[]{:S(2)}, u32[]{:S(2)}) %collective-permute-start.11) | collective-permute-done | bytes 327712 | tf_op jit(solution)/shard_map/ppermute | solution.py:236
  70.6 1.9 %collective-permute-start.13 = (s16[400,256]{1,0:T(8,128)(2,1)S(1)}, s16[400,256]{1,0:T(8,128)(2,1)S(1)}, u32[]{:S(2)}, u32[]{:S(2)}) collective-permute-start(s16[400,256]{1,0:T(8,128)(2,1)S(1)} %shard_map.57.refs_0_), channel_id=1, source_target_pairs={{0,16},{8,24},{16,0},{24,8},{1,17},{9,25},{17,1},{25,9},{2,18},{10... | collective-permute-start | bytes 614408 | tf_op jit(solution)/shard_map/ppermute | solution.py:240
  73.9 1.6 %collective-permute-start.16 = (s16[1056,256]{1,0:T(8,128)(2,1)S(1)}, s16[1056,256]{1,0:T(8,128)(2,1)S(1)}, u32[]{:S(2)}, u32[]{:S(2)}) collective-permute-start(s16[1056,256]{1,0:T(8,128)(2,1)S(1)} %get-tuple-element.40), channel_id=1, source_target_pairs={{0,8},{8,0},{16,24},{24,16},{1,9},{9,1},{17,25},{25,17},{2,10},{10... | collective-permute-start | bytes 1622024 | tf_op jit(solution)/shard_map/ppermute | solution.py:240
  78.4 2.3 %collective-permute-start.20 = (s16[800,256]{1,0:T(8,128)(2,1)S(1)}, s16[800,256]{1,0:T(8,128)(2,1)S(1)}, u32[]{:S(2)}, u32[]{:S(2)}) collective-permute-start(s16[800,256]{1,0:T(8,128)(2,1)S(1)} %get-tuple-element.46), channel_id=1, source_target_pairs={{0,16},{8,24},{16,0},{24,8},{1,17},{9,25},{17,1},{25,9},{2,18},{10... | collective-permute-start | bytes 1228808 | tf_op jit(solution)/shard_map/ppermute | solution.py:240
  80.7 1.5 %collective-permute-start.23 = (s16[528,256]{1,0:T(8,128)(2,1)S(1)}, s16[528,256]{1,0:T(8,128)(2,1)S(1)}, u32[]{:S(2)}, u32[]{:S(2)}) collective-permute-start(s16[528,256]{1,0:T(8,128)(2,1)S(1)} %shard_map.61.refs_2_), channel_id=1, source_target_pairs={{0,8},{8,0},{16,24},{24,16},{1,9},{9,1},{17,25},{25,17},{2,10},{10... | collective-permute-start | bytes 811016 | tf_op jit(solution)/shard_map/ppermute | solution.py:240
  82.2 3.0 %collective-permute-start.15 = (bf16[256,256]{1,0:T(8,128)(2,1)S(1)}, bf16[256,256]{1,0:T(8,128)(2,1)S(1)}, u32[]{:S(2)}, u32[]{:S(2)}) collective-permute-start(bf16[256,256]{1,0:T(8,128)(2,1)S(1)} %shard_map.63.refs_7_), channel_id=1, source_target_pairs={{0,1},{1,2},{2,3},{3,0},{4,5},{5,6},{6,7},{7,4},{8,9},{9,10},{10,1... | collective-permute-start | bytes 393224 | tf_op jit(solution)/shard_map/ppermute | solution.py:236
  85.2 1.6 %collective-permute-done.16.received_ref.refs_0_ = s16[1056,256]{1,0:T(8,128)(2,1)S(1)} collective-permute-done((s16[1056,256]{1,0:T(8,128)(2,1)S(1)}, s16[1056,256]{1,0:T(8,128)(2,1)S(1)}, u32[]{:S(2)}, u32[]{:S(2)}) %collective-permute-start.16) | collective-permute-done | bytes 540704 | tf_op jit(solution)/shard_map/ppermute | solution.py:240
  87.4 1.5 %collective-permute-done.15.refs_3_ = bf16[256,256]{1,0:T(8,128)(2,1)S(1)} collective-permute-done((bf16[256,256]{1,0:T(8,128)(2,1)S(1)}, bf16[256,256]{1,0:T(8,128)(2,1)S(1)}, u32[]{:S(2)}, u32[]{:S(2)}) %collective-permute-start.15) | collective-permute-done | bytes 131104 | tf_op jit(solution)/shard_map/ppermute | solution.py:236
  89.9 2.1 %collective-permute-start.21 = (s16[400,256]{1,0:T(8,128)(2,1)S(1)}, s16[400,256]{1,0:T(8,128)(2,1)S(1)}, u32[]{:S(2)}, u32[]{:S(2)}) collective-permute-start(s16[400,256]{1,0:T(8,128)(2,1)S(1)} %shard_map.67.refs_3_), channel_id=1, source_target_pairs={{0,8},{8,0},{16,24},{24,16},{1,9},{9,1},{17,25},{25,17},{2,10},{10... | collective-permute-start | bytes 614408 | tf_op jit(solution)/shard_map/ppermute | solution.py:240
  92.0 1.8 %collective-permute-start.17 = (s16[272,256]{1,0:T(8,128)(2,1)S(1)}, s16[272,256]{1,0:T(8,128)(2,1)S(1)}, u32[]{:S(2)}, u32[]{:S(2)}) collective-permute-start(s16[272,256]{1,0:T(8,128)(2,1)S(1)} %get-tuple-element.43), channel_id=1, source_target_pairs={{0,24},{8,16},{16,8},{24,0},{1,25},{9,17},{17,9},{25,1},{2,26},{10... | collective-permute-start | bytes 417800 | tf_op jit(solution)/shard_map/ppermute | solution.py:240
  93.8 1.9 %collective-permute-start.18 = (s16[272,256]{1,0:T(8,128)(2,1)S(1)}, s16[272,256]{1,0:T(8,128)(2,1)S(1)}, u32[]{:S(2)}, u32[]{:S(2)}) collective-permute-start(s16[272,256]{1,0:T(8,128)(2,1)S(1)} %get-tuple-element.44), channel_id=1, source_target_pairs={{0,8},{8,0},{16,24},{24,16},{1,9},{9,1},{17,25},{25,17},{2,10},{10... | collective-permute-start | bytes 417800 | tf_op jit(solution)/shard_map/ppermute | solution.py:240
  96.4 2.5 %collective-permute-done.17.refs_0_ = s16[272,256]{1,0:T(8,128)(2,1)S(1)} collective-permute-done((s16[272,256]{1,0:T(8,128)(2,1)S(1)}, s16[272,256]{1,0:T(8,128)(2,1)S(1)}, u32[]{:S(2)}, u32[]{:S(2)}) %collective-permute-start.17) | collective-permute-done | bytes 139296 | tf_op jit(solution)/shard_map/ppermute | solution.py:240
  (63 shorter events, 23.5 us)
Async XLA Ops:
  0.0 21.4 %collective-permute-start.3 = (bf16[512,4,256]{2,1,0:T(4,128)(2,1)}, bf16[512,4,256]{2,1,0:T(4,128)(2,1)S(1)}, u32[]{:S(2)}, u32[]{:S(2)}) collective-permute-start(bf16[512,4,256]{2,1,0:T(4,128)(2,1)} %values_ref.1), channel_id=1, source_target_pairs={{0,4},{4,0},{1,5},{5,1},{2,6},{6,2},{3,7},{7,3},{8,12},{12,8},{9,1... | collective-permute-start | bytes 3145736 | tf_op jit(solution)/shard_map/ppermute | solution.py:236
  2.9 10.5 %collective-permute-start = (bf16[384,256]{1,0:T(8,128)(2,1)S(1)}, bf16[384,256]{1,0:T(8,128)(2,1)S(1)}, u32[]{:S(2)}, u32[]{:S(2)}) collective-permute-start(bf16[384,256]{1,0:T(8,128)(2,1)S(1)} %shard_map.46.refs_0_), channel_id=1, source_target_pairs={{0,1},{1,2},{2,3},{3,0},{4,5},{5,6},{6,7},{7,4},{8,9},{9,10},{10,1... | collective-permute-start | bytes 589832 | tf_op jit(solution)/shard_map/ppermute | solution.py:236
  5.5 11.2 %collective-permute-start.4 = (bf16[384,256]{1,0:T(8,128)(2,1)S(1)}, bf16[384,256]{1,0:T(8,128)(2,1)S(1)}, u32[]{:S(2)}, u32[]{:S(2)}) collective-permute-start(bf16[384,256]{1,0:T(8,128)(2,1)S(1)} %shard_map.46.refs_0_), channel_id=1, source_target_pairs={{0,3},{1,0},{2,1},{3,2},{4,7},{5,4},{6,5},{7,6},{8,11},{9,8},{10,9... | collective-permute-start | bytes 589832 | tf_op jit(solution)/shard_map/ppermute | solution.py:236
  14.0 15.0 %collective-permute-start.1 = (bf16[704,256]{1,0:T(8,128)(2,1)S(1)}, bf16[704,256]{1,0:T(8,128)(2,1)S(1)}, u32[]{:S(2)}, u32[]{:S(2)}) collective-permute-start(bf16[704,256]{1,0:T(8,128)(2,1)S(1)} %shard_map.47.refs_0_), channel_id=1, source_target_pairs={{0,1},{1,2},{2,3},{3,0},{4,5},{5,6},{6,7},{7,4},{8,9},{9,10},{10,1... | collective-permute-start | bytes 1081352 | tf_op jit(solution)/shard_map/ppermute | solution.py:236
  17.4 19.2 %collective-permute-start.6 = (bf16[704,256]{1,0:T(8,128)(2,1)S(1)}, bf16[704,256]{1,0:T(8,128)(2,1)S(1)}, u32[]{:S(2)}, u32[]{:S(2)}) collective-permute-start(bf16[704,256]{1,0:T(8,128)(2,1)S(1)} %shard_map.48.refs_0_), channel_id=1, source_target_pairs={{0,3},{1,0},{2,1},{3,2},{4,7},{5,4},{6,5},{7,6},{8,11},{9,8},{10,9... | collective-permute-start | bytes 1081352 | tf_op jit(solution)/shard_map/ppermute | solution.py:236
  29.5 15.8 %collective-permute-start.5 = (bf16[768,256]{1,0:T(8,128)(2,1)S(1)}, bf16[768,256]{1,0:T(8,128)(2,1)S(1)}, u32[]{:S(2)}, u32[]{:S(2)}) collective-permute-start(bf16[768,256]{1,0:T(8,128)(2,1)S(1)} %shard_map.51.refs_0_), channel_id=1, source_target_pairs={{0,1},{1,2},{2,3},{3,0},{4,5},{5,6},{6,7},{7,4},{8,9},{9,10},{10,1... | collective-permute-start | bytes 1179656 | tf_op jit(solution)/shard_map/ppermute | solution.py:236
  37.1 19.2 %collective-permute-start.9 = (bf16[768,256]{1,0:T(8,128)(2,1)S(1)}, bf16[768,256]{1,0:T(8,128)(2,1)S(1)}, u32[]{:S(2)}, u32[]{:S(2)}) collective-permute-start(bf16[768,256]{1,0:T(8,128)(2,1)S(1)} %shard_map.52.refs_7_), channel_id=1, source_target_pairs={{0,3},{1,0},{2,1},{3,2},{4,7},{5,4},{6,5},{7,6},{8,11},{9,8},{10,9... | collective-permute-start | bytes 1179656 | tf_op jit(solution)/shard_map/ppermute | solution.py:236
  38.3 21.8 %collective-permute-start.8 = (s16[800,256]{1,0:T(8,128)(2,1)S(1)}, s16[800,256]{1,0:T(8,128)(2,1)S(1)}, u32[]{:S(2)}, u32[]{:S(2)}) collective-permute-start(s16[800,256]{1,0:T(8,128)(2,1)S(1)} %get-tuple-element.33), channel_id=1, source_target_pairs={{0,8},{8,0},{16,24},{24,16},{1,9},{9,1},{17,25},{25,17},{2,10},{10... | collective-permute-start | bytes 1228808 | tf_op jit(solution)/shard_map/ppermute | solution.py:240
  45.9 14.3 %collective-permute-start.7 = (bf16[640,256]{1,0:T(8,128)(2,1)S(1)}, bf16[640,256]{1,0:T(8,128)(2,1)S(1)}, u32[]{:S(2)}, u32[]{:S(2)}) collective-permute-start(bf16[640,256]{1,0:T(8,128)(2,1)S(1)} %shard_map.54.refs_0_), channel_id=1, source_target_pairs={{0,1},{1,2},{2,3},{3,0},{4,5},{5,6},{6,7},{7,4},{8,9},{9,10},{10,1... | collective-permute-start | bytes 983048 | tf_op jit(solution)/shard_map/ppermute | solution.py:236
  56.9 13.1 %collective-permute-start.11 = (bf16[640,256]{1,0:T(8,128)(2,1)S(1)}, bf16[640,256]{1,0:T(8,128)(2,1)S(1)}, u32[]{:S(2)}, u32[]{:S(2)}) collective-permute-start(bf16[640,256]{1,0:T(8,128)(2,1)S(1)} %shard_map.55.refs_7_), channel_id=1, source_target_pairs={{0,3},{1,0},{2,1},{3,2},{4,7},{5,4},{6,5},{7,6},{8,11},{9,8},{10,9... | collective-permute-start | bytes 983048 | tf_op jit(solution)/shard_map/ppermute | solution.py:236
  58.4 17.1 %collective-permute-start.14 = (s16[1056,256]{1,0:T(8,128)(2,1)S(1)}, s16[1056,256]{1,0:T(8,128)(2,1)S(1)}, u32[]{:S(2)}, u32[]{:S(2)}) collective-permute-start(s16[1056,256]{1,0:T(8,128)(2,1)S(1)} %get-tuple-element.36), channel_id=1, source_target_pairs={{0,16},{8,24},{16,0},{24,8},{1,17},{9,25},{17,1},{25,9},{2,18},{10... | collective-permute-start | bytes 1622024 | tf_op jit(solution)/shard_map/ppermute | solution.py:240
  60.8 15.9 %collective-permute-start.10 = (bf16[448,256]{1,0:T(8,128)(2,1)S(1)}, bf16[448,256]{1,0:T(8,128)(2,1)S(1)}, u32[]{:S(2)}, u32[]{:S(2)}) collective-permute-start(bf16[448,256]{1,0:T(8,128)(2,1)S(1)} %shard_map.58.refs_0_), channel_id=1, source_target_pairs={{0,1},{1,2},{2,3},{3,0},{4,5},{5,6},{6,7},{7,4},{8,9},{9,10},{10,1... | collective-permute-start | bytes 688136 | tf_op jit(solution)/shard_map/ppermute | solution.py:236
  70.5 6.7 %collective-permute-start.12 = (bf16[448,256]{1,0:T(8,128)(2,1)S(1)}, bf16[448,256]{1,0:T(8,128)(2,1)S(1)}, u32[]{:S(2)}, u32[]{:S(2)}) collective-permute-start(bf16[448,256]{1,0:T(8,128)(2,1)S(1)} %shard_map.59.refs_7_), channel_id=1, source_target_pairs={{0,3},{1,0},{2,1},{3,2},{4,7},{5,4},{6,5},{7,6},{8,11},{9,8},{10,9... | collective-permute-start | bytes 688136 | tf_op jit(solution)/shard_map/ppermute | solution.py:236
  70.6 5.9 %collective-permute-start.13 = (s16[400,256]{1,0:T(8,128)(2,1)S(1)}, s16[400,256]{1,0:T(8,128)(2,1)S(1)}, u32[]{:S(2)}, u32[]{:S(2)}) collective-permute-start(s16[400,256]{1,0:T(8,128)(2,1)S(1)} %shard_map.57.refs_0_), channel_id=1, source_target_pairs={{0,16},{8,24},{16,0},{24,8},{1,17},{9,25},{17,1},{25,9},{2,18},{10... | collective-permute-start | bytes 614408 | tf_op jit(solution)/shard_map/ppermute | solution.py:240
  73.9 12.9 %collective-permute-start.16 = (s16[1056,256]{1,0:T(8,128)(2,1)S(1)}, s16[1056,256]{1,0:T(8,128)(2,1)S(1)}, u32[]{:S(2)}, u32[]{:S(2)}) collective-permute-start(s16[1056,256]{1,0:T(8,128)(2,1)S(1)} %get-tuple-element.40), channel_id=1, source_target_pairs={{0,8},{8,0},{16,24},{24,16},{1,9},{9,1},{17,25},{25,17},{2,10},{10... | collective-permute-start | bytes 1622024 | tf_op jit(solution)/shard_map/ppermute | solution.py:240
  78.4 11.4 %collective-permute-start.20 = (s16[800,256]{1,0:T(8,128)(2,1)S(1)}, s16[800,256]{1,0:T(8,128)(2,1)S(1)}, u32[]{:S(2)}, u32[]{:S(2)}) collective-permute-start(s16[800,256]{1,0:T(8,128)(2,1)S(1)} %get-tuple-element.46), channel_id=1, source_target_pairs={{0,16},{8,24},{16,0},{24,8},{1,17},{9,25},{17,1},{25,9},{2,18},{10... | collective-permute-start | bytes 1228808 | tf_op jit(solution)/shard_map/ppermute | solution.py:240
  80.7 15.1 %collective-permute-start.23 = (s16[528,256]{1,0:T(8,128)(2,1)S(1)}, s16[528,256]{1,0:T(8,128)(2,1)S(1)}, u32[]{:S(2)}, u32[]{:S(2)}) collective-permute-start(s16[528,256]{1,0:T(8,128)(2,1)S(1)} %shard_map.61.refs_2_), channel_id=1, source_target_pairs={{0,8},{8,0},{16,24},{24,16},{1,9},{9,1},{17,25},{25,17},{2,10},{10... | collective-permute-start | bytes 811016 | tf_op jit(solution)/shard_map/ppermute | solution.py:240
  82.2 6.8 %collective-permute-start.15 = (bf16[256,256]{1,0:T(8,128)(2,1)S(1)}, bf16[256,256]{1,0:T(8,128)(2,1)S(1)}, u32[]{:S(2)}, u32[]{:S(2)}) collective-permute-start(bf16[256,256]{1,0:T(8,128)(2,1)S(1)} %shard_map.63.refs_7_), channel_id=1, source_target_pairs={{0,1},{1,2},{2,3},{3,0},{4,5},{5,6},{6,7},{7,4},{8,9},{9,10},{10,1... | collective-permute-start | bytes 393224 | tf_op jit(solution)/shard_map/ppermute | solution.py:236
  87.0 9.0 %collective-permute-start.22 = (s16[528,256]{1,0:T(8,128)(2,1)S(1)}, s16[528,256]{1,0:T(8,128)(2,1)S(1)}, u32[]{:S(2)}, u32[]{:S(2)}) collective-permute-start(s16[528,256]{1,0:T(8,128)(2,1)S(1)} %shard_map.65.refs_6_), channel_id=1, source_target_pairs={{0,16},{8,24},{16,0},{24,8},{1,17},{9,25},{17,1},{25,9},{2,18},{10... | collective-permute-start | bytes 811016 | tf_op jit(solution)/shard_map/ppermute | solution.py:240
  89.9 6.4 %collective-permute-start.21 = (s16[400,256]{1,0:T(8,128)(2,1)S(1)}, s16[400,256]{1,0:T(8,128)(2,1)S(1)}, u32[]{:S(2)}, u32[]{:S(2)}) collective-permute-start(s16[400,256]{1,0:T(8,128)(2,1)S(1)} %shard_map.67.refs_3_), channel_id=1, source_target_pairs={{0,8},{8,0},{16,24},{24,16},{1,9},{9,1},{17,25},{25,17},{2,10},{10... | collective-permute-start | bytes 614408 | tf_op jit(solution)/shard_map/ppermute | solution.py:240
  92.0 7.0 %collective-permute-start.17 = (s16[272,256]{1,0:T(8,128)(2,1)S(1)}, s16[272,256]{1,0:T(8,128)(2,1)S(1)}, u32[]{:S(2)}, u32[]{:S(2)}) collective-permute-start(s16[272,256]{1,0:T(8,128)(2,1)S(1)} %get-tuple-element.43), channel_id=1, source_target_pairs={{0,24},{8,16},{16,8},{24,0},{1,25},{9,17},{17,9},{25,1},{2,26},{10... | collective-permute-start | bytes 417800 | tf_op jit(solution)/shard_map/ppermute | solution.py:240
  93.8 6.5 %collective-permute-start.18 = (s16[272,256]{1,0:T(8,128)(2,1)S(1)}, s16[272,256]{1,0:T(8,128)(2,1)S(1)}, u32[]{:S(2)}, u32[]{:S(2)}) collective-permute-start(s16[272,256]{1,0:T(8,128)(2,1)S(1)} %get-tuple-element.44), channel_id=1, source_target_pairs={{0,8},{8,0},{16,24},{24,16},{1,9},{9,1},{17,25},{25,17},{2,10},{10... | collective-permute-start | bytes 417800 | tf_op jit(solution)/shard_map/ppermute | solution.py:240
  95.7 5.1 %collective-permute-start.19 = (s16[272,256]{1,0:T(8,128)(2,1)S(1)}, s16[272,256]{1,0:T(8,128)(2,1)S(1)}, u32[]{:S(2)}, u32[]{:S(2)}) collective-permute-start(s16[272,256]{1,0:T(8,128)(2,1)S(1)} %get-tuple-element.45), channel_id=1, source_target_pairs={{0,16},{8,24},{16,0},{24,8},{1,17},{9,25},{17,1},{25,9},{2,18},{10... | collective-permute-start | bytes 417800 | tf_op jit(solution)/shard_map/ppermute | solution.py:240
  100.9 1.2 %collective-permute-start.24 = (f32[1,256]{1,0:T(1,128)S(1)}, f32[1,256]{1,0:T(1,128)S(1)}, u32[]{:S(2)}, u32[]{:S(2)}) collective-permute-start(f32[1,256]{1,0:T(1,128)S(1)} %get-tuple-element.51.refs_0_), channel_id=1, source_target_pairs={{0,4},{4,0},{1,5},{5,1},{2,6},{6,2},{3,7},{7,3},{8,12},{12,8},{9,1... | collective-permute-start | bytes 3080 | tf_op jit(solution)/shard_map/ppermute | solution.py:236
  (6 other events, 23.1 us)

commit v14 on v11

--- a/solution.py
+++ b/solution.py
@@ -98,7 +98,8 @@
     _, piece_rows, columns = pieces[0].shape
 
     def right(step, k):
-        inner = lax.rem(col + (step + n_cols), n_cols) * TILE
+        up = jnp.where(lax.rem(row, 2) == 0, step, -step)
+        inner = lax.rem(col + up + n_cols, n_cols) * TILE
         piece = lax.rem(row - lax.div(inner, piece_rows) + n_pieces, n_pieces)
         start = pl.multiple_of(lax.rem(inner, piece_rows), TILE)
         tile = pieces[0][layer ^ k, pl.ds(start, TILE), :]
@@ -236,6 +237,16 @@
     return lax.ppermute(x, axis, [(i, (i + by) % n) for i in range(n)])
 
 
+def turn(x, by):
+    n_rows, n_cols = lax.axis_size("row"), lax.axis_size("col")
+    pairs = [
+        (r * n_cols + c, r * n_cols + (c + by * (1 - 2 * (r % 2))) % n_cols)
+        for r in range(n_rows)
+        for c in range(n_cols)
+    ]
+    return lax.ppermute(x, ("row", "col"), pairs)
+
+
 def swap(x, bits):
     return lax.ppermute(x, "layer", [(i, i ^ bits) for i in range(4)])
 
@@ -270,7 +281,7 @@
             if slot or d == 0:
                 block = load(left, pattern, at, size, arrived, tuple(parts), last)
             last[:] = [block]
-            got = shift(block, "col", 1 - 2 * d)
+            got = turn(block, 1 - 2 * d)
             first = 0
             for c, (_, rows) in zip(riders, parts):
                 found[c][d].append((got, first, rows))

time: 103 us -> 105 us (1.019)
  starting transfers between devices: 27.7 us -> 40.1 us
  waiting for transfers between devices: 55.2 us -> 45.6 us
    ppermute x15 -> x3, waiting for transfers between devices: 48.3 us -> 1.13 us  [shift(): return lax.ppermute(x, axis, [(i, (i + by) % n) for i in range(n)])]
    ppermute x0 -> x12, waiting for transfers between devices: none -> 36.9 us  [turn(): return lax.ppermute(x, ('row', 'col'), pairs)]
    ppermute x0 -> x12, starting transfers between devices: none -> 24.5 us  [turn(): return lax.ppermute(x, ('row', 'col'), pairs)]
    ppermute x15 -> x3, starting transfers between devices: 13.4 us -> 0.53 us  [shift(): return lax.ppermute(x, axis, [(i, (i + by) % n) for i in range(n)])]
where the time goes in v14:
time: 105 us
  waiting for transfers between devices  45.6 us (43%)
  starting transfers between devices  40.1 us (38%)
  Pallas kernels  16.8 us (16%)
  local copies, waits for them, and re-layouts  1.9 us (2%)
    ppermute x12, waiting for transfers between devices, turn(): return lax.ppermute(x, ('row', 'col'), pairs)  36.9 us
    ppermute x12, starting transfers between devices, turn(): return lax.ppermute(x, ('row', 'col'), pairs)  24.5 us
    ppermute x11, starting transfers between devices, swap(): return lax.ppermute(x, 'layer', [(i, i ^ bits) for i in range(4)])  15.1 us
    ppermute x11, waiting for transfers between devices, swap(): return lax.ppermute(x, 'layer', [(i, i ^ bits) for i in range(4)])  7.57 us
    pallas_call x11, Pallas kernels, load(): pl.pallas_call(functools.partial(load_kernel, at, size, parts), out_shape...  6.18 us
    pallas_call x5, Pallas kernels, partial_products(): pl.pallas_call(functools.partial(partial_kernel, tuple(steps), shapes, le...  5.86 us
    pallas_call x2, Pallas kernels, mask_right(): pl.pallas_call(mask_right_kernel, out_shape=jax.ShapeDtypeStruct((layers,...  2.27 us
  transfers between devices with their start and end apart: 26, of which 16 were waited for; matrix products, arithmetic and copies ran while one was open for 0% of the time, Pallas kernels for 15%

profile of v14, /device:TPU:0, one launch (start us, length us, event | category | flops | bytes accessed | tf_op | source)
XLA Modules:
  0.0 104.6 jit_solution(11503282085561057958)
XLA Ops:
  2.9 2.6 %collective-permute-start = (bf16[384,256]{1,0:T(8,128)(2,1)S(1)}, bf16[384,256]{1,0:T(8,128)(2,1)S(1)}, u32[]{:S(2)}, u32[]{:S(2)}) collective-permute-start(bf16[384,256]{1,0:T(8,128)(2,1)S(1)} %shard_map.46.refs_0_), channel_id=1, source_target_pairs={{0,1},{1,2},{2,3},{3,0},{4,7},{5,4},{6,5},{7,6},{8,9},{9,10},{10,1... | collective-permute-start | bytes 589832 | tf_op jit(solution)/shard_map/ppermute | solution.py:247
  5.5 2.1 %collective-permute-start.4 = (bf16[384,256]{1,0:T(8,128)(2,1)S(1)}, bf16[384,256]{1,0:T(8,128)(2,1)S(1)}, u32[]{:S(2)}, u32[]{:S(2)}) collective-permute-start(bf16[384,256]{1,0:T(8,128)(2,1)S(1)} %shard_map.46.refs_0_), channel_id=1, source_target_pairs={{0,3},{1,0},{2,1},{3,2},{4,5},{5,6},{6,7},{7,4},{8,11},{9,8},{10,9... | collective-permute-start | bytes 589832 | tf_op jit(solution)/shard_map/ppermute | solution.py:247
  7.6 5.8 %collective-permute-done.arrived.refs_1_ = bf16[384,256]{1,0:T(8,128)(2,1)S(1)} collective-permute-done((bf16[384,256]{1,0:T(8,128)(2,1)S(1)}, bf16[384,256]{1,0:T(8,128)(2,1)S(1)}, u32[]{:S(2)}, u32[]{:S(2)}) %collective-permute-start) | collective-permute-done | bytes 196640 | tf_op jit(solution)/shard_map/ppermute | solution.py:247
  14.0 3.0 %collective-permute-start.1 = (bf16[704,256]{1,0:T(8,128)(2,1)S(1)}, bf16[704,256]{1,0:T(8,128)(2,1)S(1)}, u32[]{:S(2)}, u32[]{:S(2)}) collective-permute-start(bf16[704,256]{1,0:T(8,128)(2,1)S(1)} %shard_map.47.refs_0_), channel_id=1, source_target_pairs={{0,1},{1,2},{2,3},{3,0},{4,7},{5,4},{6,5},{7,6},{8,9},{9,10},{10,1... | collective-permute-start | bytes 1081352 | tf_op jit(solution)/shard_map/ppermute | solution.py:247
  17.6 3.0 %collective-permute-start.6 = (bf16[704,256]{1,0:T(8,128)(2,1)S(1)}, bf16[704,256]{1,0:T(8,128)(2,1)S(1)}, u32[]{:S(2)}, u32[]{:S(2)}) collective-permute-start(bf16[704,256]{1,0:T(8,128)(2,1)S(1)} %shard_map.48.refs_0_), channel_id=1, source_target_pairs={{0,3},{1,0},{2,1},{3,2},{4,5},{5,6},{6,7},{7,4},{8,11},{9,8},{10,9... | collective-permute-start | bytes 1081352 | tf_op jit(solution)/shard_map/ppermute | solution.py:247
  22.9 6.5 %collective-permute-done.1.arrived.refs_3_.refs_1_ = bf16[704,256]{1,0:T(8,128)(2,1)S(1)} collective-permute-done((bf16[704,256]{1,0:T(8,128)(2,1)S(1)}, bf16[704,256]{1,0:T(8,128)(2,1)S(1)}, u32[]{:S(2)}, u32[]{:S(2)}) %collective-permute-start.1) | collective-permute-done | bytes 360480 | tf_op jit(solution)/shard_map/ppermute | solution.py:247
  30.0 4.8 %collective-permute-start.5 = (bf16[768,256]{1,0:T(8,128)(2,1)S(1)}, bf16[768,256]{1,0:T(8,128)(2,1)S(1)}, u32[]{:S(2)}, u32[]{:S(2)}) collective-permute-start(bf16[768,256]{1,0:T(8,128)(2,1)S(1)} %shard_map.51.refs_0_), channel_id=1, source_target_pairs={{0,1},{1,2},{2,3},{3,0},{4,7},{5,4},{6,5},{7,6},{8,9},{9,10},{10,1... | collective-permute-start | bytes 1179656 | tf_op jit(solution)/shard_map/ppermute | solution.py:247
  36.7 1.7 %collective-permute-start.9 = (bf16[768,256]{1,0:T(8,128)(2,1)S(1)}, bf16[768,256]{1,0:T(8,128)(2,1)S(1)}, u32[]{:S(2)}, u32[]{:S(2)}) collective-permute-start(bf16[768,256]{1,0:T(8,128)(2,1)S(1)} %shard_map.52.refs_7_), channel_id=1, source_target_pairs={{0,3},{1,0},{2,1},{3,2},{4,5},{5,6},{6,7},{7,4},{8,11},{9,8},{10,9... | collective-permute-start | bytes 1179656 | tf_op jit(solution)/shard_map/ppermute | solution.py:247
  39.5 1.6 %collective-permute-start.8 = (s16[800,256]{1,0:T(8,128)(2,1)S(1)}, s16[800,256]{1,0:T(8,128)(2,1)S(1)}, u32[]{:S(2)}, u32[]{:S(2)}) collective-permute-start(s16[800,256]{1,0:T(8,128)(2,1)S(1)} %get-tuple-element.33), channel_id=1, source_target_pairs={{0,8},{8,0},{16,24},{24,16},{1,9},{9,1},{17,25},{25,17},{2,10},{10... | collective-permute-start | bytes 1228808 | tf_op jit(solution)/shard_map/ppermute | solution.py:251
  41.0 6.8 %collective-permute-done.5.arrived.refs_3_.refs_1_ = bf16[768,256]{1,0:T(8,128)(2,1)S(1)} collective-permute-done((bf16[768,256]{1,0:T(8,128)(2,1)S(1)}, bf16[768,256]{1,0:T(8,128)(2,1)S(1)}, u32[]{:S(2)}, u32[]{:S(2)}) %collective-permute-start.5) | collective-permute-done | bytes 393248 | tf_op jit(solution)/shard_map/ppermute | solution.py:247
  49.1 7.0 %collective-permute-done.9.arrived.refs_4_.refs_2_ = bf16[768,256]{1,0:T(8,128)(2,1)S(1)} collective-permute-done((bf16[768,256]{1,0:T(8,128)(2,1)S(1)}, bf16[768,256]{1,0:T(8,128)(2,1)S(1)}, u32[]{:S(2)}, u32[]{:S(2)}) %collective-permute-start.9) | collective-permute-done | bytes 393248 | tf_op jit(solution)/shard_map/ppermute | solution.py:247
  59.3 1.6 %collective-permute-start.14 = (s16[1056,256]{1,0:T(8,128)(2,1)S(1)}, s16[1056,256]{1,0:T(8,128)(2,1)S(1)}, u32[]{:S(2)}, u32[]{:S(2)}) collective-permute-start(s16[1056,256]{1,0:T(8,128)(2,1)S(1)} %get-tuple-element.36), channel_id=1, source_target_pairs={{0,16},{8,24},{16,0},{24,8},{1,17},{9,25},{17,1},{25,9},{2,18},{10... | collective-permute-start | bytes 1622024 | tf_op jit(solution)/shard_map/ppermute | solution.py:251
  61.0 1.9 %collective-permute-done.7.arrived.refs_3_.refs_1_ = bf16[640,256]{1,0:T(8,128)(2,1)S(1)} collective-permute-done((bf16[640,256]{1,0:T(8,128)(2,1)S(1)}, bf16[640,256]{1,0:T(8,128)(2,1)S(1)}, u32[]{:S(2)}, u32[]{:S(2)}) %collective-permute-start.7) | collective-permute-done | bytes 327712 | tf_op jit(solution)/shard_map/ppermute | solution.py:247
  63.5 4.3 %collective-permute-done.11.arrived.refs_4_.refs_2_ = bf16[640,256]{1,0:T(8,128)(2,1)S(1)} collective-permute-done((bf16[640,256]{1,0:T(8,128)(2,1)S(1)}, bf16[640,256]{1,0:T(8,128)(2,1)S(1)}, u32[]{:S(2)}, u32[]{:S(2)}) %collective-permute-start.11) | collective-permute-done | bytes 327712 | tf_op jit(solution)/shard_map/ppermute | solution.py:247
  68.4 3.4 %collective-permute-start.12 = (bf16[448,256]{1,0:T(8,128)(2,1)S(1)}, bf16[448,256]{1,0:T(8,128)(2,1)S(1)}, u32[]{:S(2)}, u32[]{:S(2)}) collective-permute-start(bf16[448,256]{1,0:T(8,128)(2,1)S(1)} %shard_map.59.refs_7_), channel_id=1, source_target_pairs={{0,3},{1,0},{2,1},{3,2},{4,5},{5,6},{6,7},{7,4},{8,11},{9,8},{10,9... | collective-permute-start | bytes 688136 | tf_op jit(solution)/shard_map/ppermute | solution.py:247
  74.7 1.6 %collective-permute-start.17 = (s16[1056,256]{1,0:T(8,128)(2,1)S(1)}, s16[1056,256]{1,0:T(8,128)(2,1)S(1)}, u32[]{:S(2)}, u32[]{:S(2)}) collective-permute-start(s16[1056,256]{1,0:T(8,128)(2,1)S(1)} %get-tuple-element.40), channel_id=1, source_target_pairs={{0,8},{8,0},{16,24},{24,16},{1,9},{9,1},{17,25},{25,17},{2,10},{10... | collective-permute-start | bytes 1622024 | tf_op jit(solution)/shard_map/ppermute | solution.py:251
  76.5 2.6 %collective-permute-done.13.refs_1_ = s16[400,256]{1,0:T(8,128)(2,1)S(1)} collective-permute-done((s16[400,256]{1,0:T(8,128)(2,1)S(1)}, s16[400,256]{1,0:T(8,128)(2,1)S(1)}, u32[]{:S(2)}, u32[]{:S(2)}) %collective-permute-start.13) | collective-permute-done | bytes 204832 | tf_op jit(solution)/shard_map/ppermute | solution.py:251
  81.5 1.6 %collective-permute-start.21 = (s16[800,256]{1,0:T(8,128)(2,1)S(1)}, s16[800,256]{1,0:T(8,128)(2,1)S(1)}, u32[]{:S(2)}, u32[]{:S(2)}) collective-permute-start(s16[800,256]{1,0:T(8,128)(2,1)S(1)} %get-tuple-element.46), channel_id=1, source_target_pairs={{0,16},{8,24},{16,0},{24,8},{1,17},{9,25},{17,1},{25,9},{2,18},{10... | collective-permute-start | bytes 1228808 | tf_op jit(solution)/shard_map/ppermute | solution.py:251
  84.5 2.0 %collective-permute-start.15 = (bf16[128,256]{1,0:T(8,128)(2,1)S(1)}, bf16[128,256]{1,0:T(8,128)(2,1)S(1)}, u32[]{:S(2)}, u32[]{:S(2)}) collective-permute-start(bf16[128,256]{1,0:T(8,128)(2,1)S(1)} %shard_map.63.refs_0_), channel_id=1, source_target_pairs={{0,1},{1,2},{2,3},{3,0},{4,7},{5,4},{6,5},{7,6},{8,9},{9,10},{10,1... | collective-permute-start | bytes 196616 | tf_op jit(solution)/shard_map/ppermute | solution.py:247
  88.8 1.8 %collective-permute-done.15.refs_3_ = bf16[128,256]{1,0:T(8,128)(2,1)S(1)} collective-permute-done((bf16[128,256]{1,0:T(8,128)(2,1)S(1)}, bf16[128,256]{1,0:T(8,128)(2,1)S(1)}, u32[]{:S(2)}, u32[]{:S(2)}) %collective-permute-start.15) | collective-permute-done | bytes 65568 | tf_op jit(solution)/shard_map/ppermute | solution.py:247
  92.3 1.7 %collective-permute-start.22 = (s16[400,256]{1,0:T(8,128)(2,1)S(1)}, s16[400,256]{1,0:T(8,128)(2,1)S(1)}, u32[]{:S(2)}, u32[]{:S(2)}) collective-permute-start(s16[400,256]{1,0:T(8,128)(2,1)S(1)} %shard_map.68.refs_3_), channel_id=1, source_target_pairs={{0,8},{8,0},{16,24},{24,16},{1,9},{9,1},{17,25},{25,17},{2,10},{10... | collective-permute-start | bytes 614408 | tf_op jit(solution)/shard_map/ppermute | solution.py:251
  94.0 1.6 %collective-permute-start.18 = (s16[272,256]{1,0:T(8,128)(2,1)S(1)}, s16[272,256]{1,0:T(8,128)(2,1)S(1)}, u32[]{:S(2)}, u32[]{:S(2)}) collective-permute-start(s16[272,256]{1,0:T(8,128)(2,1)S(1)} %get-tuple-element.43), channel_id=1, source_target_pairs={{0,24},{8,16},{16,8},{24,0},{1,25},{9,17},{17,9},{25,1},{2,26},{10... | collective-permute-start | bytes 417800 | tf_op jit(solution)/shard_map/ppermute | solution.py:251
  95.5 1.6 %collective-permute-start.19 = (s16[272,256]{1,0:T(8,128)(2,1)S(1)}, s16[272,256]{1,0:T(8,128)(2,1)S(1)}, u32[]{:S(2)}, u32[]{:S(2)}) collective-permute-start(s16[272,256]{1,0:T(8,128)(2,1)S(1)} %get-tuple-element.44), channel_id=1, source_target_pairs={{0,8},{8,0},{16,24},{24,16},{1,9},{9,1},{17,25},{25,17},{2,10},{10... | collective-permute-start | bytes 417800 | tf_op jit(solution)/shard_map/ppermute | solution.py:251
  98.2 2.5 %collective-permute-done.18.refs_0_ = s16[272,256]{1,0:T(8,128)(2,1)S(1)} collective-permute-done((s16[272,256]{1,0:T(8,128)(2,1)S(1)}, s16[272,256]{1,0:T(8,128)(2,1)S(1)}, u32[]{:S(2)}, u32[]{:S(2)}) %collective-permute-start.18) | collective-permute-done | bytes 139296 | tf_op jit(solution)/shard_map/ppermute | solution.py:251
  (66 shorter events, 31.4 us)
Async XLA Ops:
  0.0 21.7 %collective-permute-start.3 = (bf16[512,4,256]{2,1,0:T(4,128)(2,1)}, bf16[512,4,256]{2,1,0:T(4,128)(2,1)S(1)}, u32[]{:S(2)}, u32[]{:S(2)}) collective-permute-start(bf16[512,4,256]{2,1,0:T(4,128)(2,1)} %values_ref.1), channel_id=1, source_target_pairs={{0,4},{4,0},{1,5},{5,1},{2,6},{6,2},{3,7},{7,3},{8,12},{12,8},{9,1... | collective-permute-start | bytes 3145736 | tf_op jit(solution)/shard_map/ppermute | solution.py:237
  2.9 10.5 %collective-permute-start = (bf16[384,256]{1,0:T(8,128)(2,1)S(1)}, bf16[384,256]{1,0:T(8,128)(2,1)S(1)}, u32[]{:S(2)}, u32[]{:S(2)}) collective-permute-start(bf16[384,256]{1,0:T(8,128)(2,1)S(1)} %shard_map.46.refs_0_), channel_id=1, source_target_pairs={{0,1},{1,2},{2,3},{3,0},{4,7},{5,4},{6,5},{7,6},{8,9},{9,10},{10,1... | collective-permute-start | bytes 589832 | tf_op jit(solution)/shard_map/ppermute | solution.py:247
  5.5 11.4 %collective-permute-start.4 = (bf16[384,256]{1,0:T(8,128)(2,1)S(1)}, bf16[384,256]{1,0:T(8,128)(2,1)S(1)}, u32[]{:S(2)}, u32[]{:S(2)}) collective-permute-start(bf16[384,256]{1,0:T(8,128)(2,1)S(1)} %shard_map.46.refs_0_), channel_id=1, source_target_pairs={{0,3},{1,0},{2,1},{3,2},{4,5},{5,6},{6,7},{7,4},{8,11},{9,8},{10,9... | collective-permute-start | bytes 589832 | tf_op jit(solution)/shard_map/ppermute | solution.py:247
  14.0 15.4 %collective-permute-start.1 = (bf16[704,256]{1,0:T(8,128)(2,1)S(1)}, bf16[704,256]{1,0:T(8,128)(2,1)S(1)}, u32[]{:S(2)}, u32[]{:S(2)}) collective-permute-start(bf16[704,256]{1,0:T(8,128)(2,1)S(1)} %shard_map.47.refs_0_), channel_id=1, source_target_pairs={{0,1},{1,2},{2,3},{3,0},{4,7},{5,4},{6,5},{7,6},{8,9},{9,10},{10,1... | collective-permute-start | bytes 1081352 | tf_op jit(solution)/shard_map/ppermute | solution.py:247
  17.6 18.6 %collective-permute-start.6 = (bf16[704,256]{1,0:T(8,128)(2,1)S(1)}, bf16[704,256]{1,0:T(8,128)(2,1)S(1)}, u32[]{:S(2)}, u32[]{:S(2)}) collective-permute-start(bf16[704,256]{1,0:T(8,128)(2,1)S(1)} %shard_map.48.refs_0_), channel_id=1, source_target_pairs={{0,3},{1,0},{2,1},{3,2},{4,5},{5,6},{6,7},{7,4},{8,11},{9,8},{10,9... | collective-permute-start | bytes 1081352 | tf_op jit(solution)/shard_map/ppermute | solution.py:247
  30.0 17.8 %collective-permute-start.5 = (bf16[768,256]{1,0:T(8,128)(2,1)S(1)}, bf16[768,256]{1,0:T(8,128)(2,1)S(1)}, u32[]{:S(2)}, u32[]{:S(2)}) collective-permute-start(bf16[768,256]{1,0:T(8,128)(2,1)S(1)} %shard_map.51.refs_0_), channel_id=1, source_target_pairs={{0,1},{1,2},{2,3},{3,0},{4,7},{5,4},{6,5},{7,6},{8,9},{9,10},{10,1... | collective-permute-start | bytes 1179656 | tf_op jit(solution)/shard_map/ppermute | solution.py:247
  36.7 19.4 %collective-permute-start.9 = (bf16[768,256]{1,0:T(8,128)(2,1)S(1)}, bf16[768,256]{1,0:T(8,128)(2,1)S(1)}, u32[]{:S(2)}, u32[]{:S(2)}) collective-permute-start(bf16[768,256]{1,0:T(8,128)(2,1)S(1)} %shard_map.52.refs_7_), channel_id=1, source_target_pairs={{0,3},{1,0},{2,1},{3,2},{4,5},{5,6},{6,7},{7,4},{8,11},{9,8},{10,9... | collective-permute-start | bytes 1179656 | tf_op jit(solution)/shard_map/ppermute | solution.py:247
  39.5 21.4 %collective-permute-start.8 = (s16[800,256]{1,0:T(8,128)(2,1)S(1)}, s16[800,256]{1,0:T(8,128)(2,1)S(1)}, u32[]{:S(2)}, u32[]{:S(2)}) collective-permute-start(s16[800,256]{1,0:T(8,128)(2,1)S(1)} %get-tuple-element.33), channel_id=1, source_target_pairs={{0,8},{8,0},{16,24},{24,16},{1,9},{9,1},{17,25},{25,17},{2,10},{10... | collective-permute-start | bytes 1228808 | tf_op jit(solution)/shard_map/ppermute | solution.py:251
  48.4 14.5 %collective-permute-start.7 = (bf16[640,256]{1,0:T(8,128)(2,1)S(1)}, bf16[640,256]{1,0:T(8,128)(2,1)S(1)}, u32[]{:S(2)}, u32[]{:S(2)}) collective-permute-start(bf16[640,256]{1,0:T(8,128)(2,1)S(1)} %shard_map.54.refs_0_), channel_id=1, source_target_pairs={{0,1},{1,2},{2,3},{3,0},{4,7},{5,4},{6,5},{7,6},{8,9},{9,10},{10,1... | collective-permute-start | bytes 983048 | tf_op jit(solution)/shard_map/ppermute | solution.py:247
  56.7 11.1 %collective-permute-start.11 = (bf16[640,256]{1,0:T(8,128)(2,1)S(1)}, bf16[640,256]{1,0:T(8,128)(2,1)S(1)}, u32[]{:S(2)}, u32[]{:S(2)}) collective-permute-start(bf16[640,256]{1,0:T(8,128)(2,1)S(1)} %shard_map.55.refs_7_), channel_id=1, source_target_pairs={{0,3},{1,0},{2,1},{3,2},{4,5},{5,6},{6,7},{7,4},{8,11},{9,8},{10,9... | collective-permute-start | bytes 983048 | tf_op jit(solution)/shard_map/ppermute | solution.py:247
  59.3 17.0 %collective-permute-start.14 = (s16[1056,256]{1,0:T(8,128)(2,1)S(1)}, s16[1056,256]{1,0:T(8,128)(2,1)S(1)}, u32[]{:S(2)}, u32[]{:S(2)}) collective-permute-start(s16[1056,256]{1,0:T(8,128)(2,1)S(1)} %get-tuple-element.36), channel_id=1, source_target_pairs={{0,16},{8,24},{16,0},{24,8},{1,17},{9,25},{17,1},{25,9},{2,18},{10... | collective-permute-start | bytes 1622024 | tf_op jit(solution)/shard_map/ppermute | solution.py:251
  63.4 15.8 %collective-permute-start.10 = (bf16[448,256]{1,0:T(8,128)(2,1)S(1)}, bf16[448,256]{1,0:T(8,128)(2,1)S(1)}, u32[]{:S(2)}, u32[]{:S(2)}) collective-permute-start(bf16[448,256]{1,0:T(8,128)(2,1)S(1)} %shard_map.58.refs_0_), channel_id=1, source_target_pairs={{0,1},{1,2},{2,3},{3,0},{4,7},{5,4},{6,5},{7,6},{8,9},{9,10},{10,1... | collective-permute-start | bytes 688136 | tf_op jit(solution)/shard_map/ppermute | solution.py:247
  68.4 11.4 %collective-permute-start.12 = (bf16[448,256]{1,0:T(8,128)(2,1)S(1)}, bf16[448,256]{1,0:T(8,128)(2,1)S(1)}, u32[]{:S(2)}, u32[]{:S(2)}) collective-permute-start(bf16[448,256]{1,0:T(8,128)(2,1)S(1)} %shard_map.59.refs_7_), channel_id=1, source_target_pairs={{0,3},{1,0},{2,1},{3,2},{4,5},{5,6},{6,7},{7,4},{8,11},{9,8},{10,9... | collective-permute-start | bytes 688136 | tf_op jit(solution)/shard_map/ppermute | solution.py:247
  71.8 7.3 %collective-permute-start.13 = (s16[400,256]{1,0:T(8,128)(2,1)S(1)}, s16[400,256]{1,0:T(8,128)(2,1)S(1)}, u32[]{:S(2)}, u32[]{:S(2)}) collective-permute-start(s16[400,256]{1,0:T(8,128)(2,1)S(1)} %shard_map.57.refs_0_), channel_id=1, source_target_pairs={{0,16},{8,24},{16,0},{24,8},{1,17},{9,25},{17,1},{25,9},{2,18},{10... | collective-permute-start | bytes 614408 | tf_op jit(solution)/shard_map/ppermute | solution.py:251
  74.7 11.8 %collective-permute-start.17 = (s16[1056,256]{1,0:T(8,128)(2,1)S(1)}, s16[1056,256]{1,0:T(8,128)(2,1)S(1)}, u32[]{:S(2)}, u32[]{:S(2)}) collective-permute-start(s16[1056,256]{1,0:T(8,128)(2,1)S(1)} %get-tuple-element.40), channel_id=1, source_target_pairs={{0,8},{8,0},{16,24},{24,16},{1,9},{9,1},{17,25},{25,17},{2,10},{10... | collective-permute-start | bytes 1622024 | tf_op jit(solution)/shard_map/ppermute | solution.py:251
  81.5 10.7 %collective-permute-start.21 = (s16[800,256]{1,0:T(8,128)(2,1)S(1)}, s16[800,256]{1,0:T(8,128)(2,1)S(1)}, u32[]{:S(2)}, u32[]{:S(2)}) collective-permute-start(s16[800,256]{1,0:T(8,128)(2,1)S(1)} %get-tuple-element.46), channel_id=1, source_target_pairs={{0,16},{8,24},{16,0},{24,8},{1,17},{9,25},{17,1},{25,9},{2,18},{10... | collective-permute-start | bytes 1228808 | tf_op jit(solution)/shard_map/ppermute | solution.py:251
  83.0 14.1 %collective-permute-start.24 = (s16[528,256]{1,0:T(8,128)(2,1)S(1)}, s16[528,256]{1,0:T(8,128)(2,1)S(1)}, u32[]{:S(2)}, u32[]{:S(2)}) collective-permute-start(s16[528,256]{1,0:T(8,128)(2,1)S(1)} %shard_map.61.refs_2_), channel_id=1, source_target_pairs={{0,8},{8,0},{16,24},{24,16},{1,9},{9,1},{17,25},{25,17},{2,10},{10... | collective-permute-start | bytes 811016 | tf_op jit(solution)/shard_map/ppermute | solution.py:251
  84.5 4.3 %collective-permute-start.16 = (bf16[128,256]{1,0:T(8,128)(2,1)S(1)}, bf16[128,256]{1,0:T(8,128)(2,1)S(1)}, u32[]{:S(2)}, u32[]{:S(2)}) collective-permute-start(bf16[128,256]{1,0:T(8,128)(2,1)S(1)} %shard_map.64.refs_7_), channel_id=1, source_target_pairs={{0,3},{1,0},{2,1},{3,2},{4,5},{5,6},{6,7},{7,4},{8,11},{9,8},{10,9... | collective-permute-start | bytes 196616 | tf_op jit(solution)/shard_map/ppermute | solution.py:247
  84.5 6.1 %collective-permute-start.15 = (bf16[128,256]{1,0:T(8,128)(2,1)S(1)}, bf16[128,256]{1,0:T(8,128)(2,1)S(1)}, u32[]{:S(2)}, u32[]{:S(2)}) collective-permute-start(bf16[128,256]{1,0:T(8,128)(2,1)S(1)} %shard_map.63.refs_0_), channel_id=1, source_target_pairs={{0,1},{1,2},{2,3},{3,0},{4,7},{5,4},{6,5},{7,6},{8,9},{9,10},{10,1... | collective-permute-start | bytes 196616 | tf_op jit(solution)/shard_map/ppermute | solution.py:247
  86.7 10.9 %collective-permute-start.23 = (s16[528,256]{1,0:T(8,128)(2,1)S(1)}, s16[528,256]{1,0:T(8,128)(2,1)S(1)}, u32[]{:S(2)}, u32[]{:S(2)}) collective-permute-start(s16[528,256]{1,0:T(8,128)(2,1)S(1)} %shard_map.66.refs_7_), channel_id=1, source_target_pairs={{0,16},{8,24},{16,0},{24,8},{1,17},{9,25},{17,1},{25,9},{2,18},{10... | collective-permute-start | bytes 811016 | tf_op jit(solution)/shard_map/ppermute | solution.py:251
  92.3 5.8 %collective-permute-start.22 = (s16[400,256]{1,0:T(8,128)(2,1)S(1)}, s16[400,256]{1,0:T(8,128)(2,1)S(1)}, u32[]{:S(2)}, u32[]{:S(2)}) collective-permute-start(s16[400,256]{1,0:T(8,128)(2,1)S(1)} %shard_map.68.refs_3_), channel_id=1, source_target_pairs={{0,8},{8,0},{16,24},{24,16},{1,9},{9,1},{17,25},{25,17},{2,10},{10... | collective-permute-start | bytes 614408 | tf_op jit(solution)/shard_map/ppermute | solution.py:251
  94.0 6.8 %collective-permute-start.18 = (s16[272,256]{1,0:T(8,128)(2,1)S(1)}, s16[272,256]{1,0:T(8,128)(2,1)S(1)}, u32[]{:S(2)}, u32[]{:S(2)}) collective-permute-start(s16[272,256]{1,0:T(8,128)(2,1)S(1)} %get-tuple-element.43), channel_id=1, source_target_pairs={{0,24},{8,16},{16,8},{24,0},{1,25},{9,17},{17,9},{25,1},{2,26},{10... | collective-permute-start | bytes 417800 | tf_op jit(solution)/shard_map/ppermute | solution.py:251
  95.5 6.1 %collective-permute-start.19 = (s16[272,256]{1,0:T(8,128)(2,1)S(1)}, s16[272,256]{1,0:T(8,128)(2,1)S(1)}, u32[]{:S(2)}, u32[]{:S(2)}) collective-permute-start(s16[272,256]{1,0:T(8,128)(2,1)S(1)} %get-tuple-element.44), channel_id=1, source_target_pairs={{0,8},{8,0},{16,24},{24,16},{1,9},{9,1},{17,25},{25,17},{2,10},{10... | collective-permute-start | bytes 417800 | tf_op jit(solution)/shard_map/ppermute | solution.py:251
  97.1 5.1 %collective-permute-start.20 = (s16[272,256]{1,0:T(8,128)(2,1)S(1)}, s16[272,256]{1,0:T(8,128)(2,1)S(1)}, u32[]{:S(2)}, u32[]{:S(2)}) collective-permute-start(s16[272,256]{1,0:T(8,128)(2,1)S(1)} %get-tuple-element.45), channel_id=1, source_target_pairs={{0,16},{8,24},{16,0},{24,8},{1,17},{9,25},{17,1},{25,9},{2,18},{10... | collective-permute-start | bytes 417800 | tf_op jit(solution)/shard_map/ppermute | solution.py:251
  (7 other events, 25.0 us)

commit v15 on v11

--- a/solution.py
+++ b/solution.py
@@ -284,8 +284,11 @@
         (*below, last_below), (*above, last_above) = found[i]
         return [[part] for part in [own[i]] + below + above] + [[last_below, last_above]]
 
+    def direct(i):
+        return i in (0, len(sizes) - 1)
+
     def sum_chunk(i):
-        if i + 1 < len(sizes):
+        if not direct(i):
             ks, sent_ks = (0, second(i)), ((3 - second(i), 3),)
         else:
             ks, sent_ks = (0,), ((3,), (1,), (2,))
@@ -324,11 +327,11 @@
                 for tiles, values in raw:
                     pieces.append(mask_right(tiles, values, last))
                     last[:] = pieces[-1:]
+        if i == 1:
+            square(0)
         sum_chunk(i)
-        if i > 0:
+        if i > 0 and not direct(i - 1):
             send_on(i - 1)
-        if 1 < i < len(sizes) - 2:
-            square(i - 2)
     for i in range(len(squares), len(sizes)):
         square(i)
 

time: 103 us -> 102 us (level)
  waiting for transfers between devices: 55.2 us -> 53.7 us
  starting transfers between devices: 27.7 us -> 28.9 us
    ppermute x11 -> x12, starting transfers between devices: 14.3 us -> 16.4 us  [swap(): return lax.ppermute(x, 'layer', [(i, i ^ bits) for i in range(4)])]
    ppermute x11 -> x12, waiting for transfers between devices: 6.93 us -> 5.01 us  [swap(): return lax.ppermute(x, 'layer', [(i, i ^ bits) for i in range(4)])]
  transfers between devices with their start and end apart: 26 -> 27, of which waited for: 16 -> 15; matrix products, arithmetic and copies ran while one was open for 0% -> 0% of each run, Pallas kernels for 15% -> 15%
where the time goes in v15:
time: 102 us
  waiting for transfers between devices  53.7 us (53%)
  starting transfers between devices  28.9 us (28%)
  Pallas kernels  16.8 us (16%)
  local copies, waits for them, and re-layouts  1.9 us (2%)
    ppermute x15, waiting for transfers between devices, shift(): return lax.ppermute(x, axis, [(i, (i + by) % n) for i in range(n)])  48.7 us
    ppermute x12, starting transfers between devices, swap(): return lax.ppermute(x, 'layer', [(i, i ^ bits) for i in range(4)])  16.4 us
    ppermute x15, starting transfers between devices, shift(): return lax.ppermute(x, axis, [(i, (i + by) % n) for i in range(n)])  12.5 us
    pallas_call x11, Pallas kernels, load(): pl.pallas_call(functools.partial(load_kernel, at, size, parts), out_shape...  6.18 us
    pallas_call x5, Pallas kernels, partial_products(): pl.pallas_call(functools.partial(partial_kernel, tuple(steps), shapes, le...  6.02 us
    ppermute x12, waiting for transfers between devices, swap(): return lax.ppermute(x, 'layer', [(i, i ^ bits) for i in range(4)])  5.01 us
    pallas_call x2, Pallas kernels, mask_right(): pl.pallas_call(mask_right_kernel, out_shape=jax.ShapeDtypeStruct((layers,...  2.27 us
  transfers between devices with their start and end apart: 27, of which 15 were waited for; matrix products, arithmetic and copies ran while one was open for 0% of the time, Pallas kernels for 15%

profile of v15, /device:TPU:0, one launch (start us, length us, event | category | flops | bytes accessed | tf_op | source)
XLA Modules:
  0.0 101.7 jit_solution(2834580607135442082)
XLA Ops:
  2.9 2.6 %collective-permute-start = (bf16[384,256]{1,0:T(8,128)(2,1)S(1)}, bf16[384,256]{1,0:T(8,128)(2,1)S(1)}, u32[]{:S(2)}, u32[]{:S(2)}) collective-permute-start(bf16[384,256]{1,0:T(8,128)(2,1)S(1)} %shard_map.46.refs_0_), channel_id=1, source_target_pairs={{0,1},{1,2},{2,3},{3,0},{4,5},{5,6},{6,7},{7,4},{8,9},{9,10},{10,1... | collective-permute-start | bytes 589832 | tf_op jit(solution)/shard_map/ppermute | solution.py:236
  5.5 2.1 %collective-permute-start.4 = (bf16[384,256]{1,0:T(8,128)(2,1)S(1)}, bf16[384,256]{1,0:T(8,128)(2,1)S(1)}, u32[]{:S(2)}, u32[]{:S(2)}) collective-permute-start(bf16[384,256]{1,0:T(8,128)(2,1)S(1)} %shard_map.46.refs_0_), channel_id=1, source_target_pairs={{0,3},{1,0},{2,1},{3,2},{4,7},{5,4},{6,5},{7,6},{8,11},{9,8},{10,9... | collective-permute-start | bytes 589832 | tf_op jit(solution)/shard_map/ppermute | solution.py:236
  7.6 5.7 %collective-permute-done.arrived.refs_1_ = bf16[384,256]{1,0:T(8,128)(2,1)S(1)} collective-permute-done((bf16[384,256]{1,0:T(8,128)(2,1)S(1)}, bf16[384,256]{1,0:T(8,128)(2,1)S(1)}, u32[]{:S(2)}, u32[]{:S(2)}) %collective-permute-start) | collective-permute-done | bytes 196640 | tf_op jit(solution)/shard_map/ppermute | solution.py:236
  14.0 2.8 %collective-permute-done.4.arrived.refs_2_ = bf16[384,256]{1,0:T(8,128)(2,1)S(1)} collective-permute-done((bf16[384,256]{1,0:T(8,128)(2,1)S(1)}, bf16[384,256]{1,0:T(8,128)(2,1)S(1)}, u32[]{:S(2)}, u32[]{:S(2)}) %collective-permute-start.4) | collective-permute-done | bytes 196640 | tf_op jit(solution)/shard_map/ppermute | solution.py:236
  17.4 2.8 %collective-permute-start.6 = (bf16[704,256]{1,0:T(8,128)(2,1)S(1)}, bf16[704,256]{1,0:T(8,128)(2,1)S(1)}, u32[]{:S(2)}, u32[]{:S(2)}) collective-permute-start(bf16[704,256]{1,0:T(8,128)(2,1)S(1)} %shard_map.48.refs_0_), channel_id=1, source_target_pairs={{0,3},{1,0},{2,1},{3,2},{4,7},{5,4},{6,5},{7,6},{8,11},{9,8},{10,9... | collective-permute-start | bytes 1081352 | tf_op jit(solution)/shard_map/ppermute | solution.py:236
  22.5 6.4 %collective-permute-done.1.arrived.refs_3_.refs_1_ = bf16[704,256]{1,0:T(8,128)(2,1)S(1)} collective-permute-done((bf16[704,256]{1,0:T(8,128)(2,1)S(1)}, bf16[704,256]{1,0:T(8,128)(2,1)S(1)}, u32[]{:S(2)}, u32[]{:S(2)}) %collective-permute-start.1) | collective-permute-done | bytes 360480 | tf_op jit(solution)/shard_map/ppermute | solution.py:236
  29.6 7.0 %collective-permute-done.6.arrived.refs_4_.refs_2_ = bf16[704,256]{1,0:T(8,128)(2,1)S(1)} collective-permute-done((bf16[704,256]{1,0:T(8,128)(2,1)S(1)}, bf16[704,256]{1,0:T(8,128)(2,1)S(1)}, u32[]{:S(2)}, u32[]{:S(2)}) %collective-permute-start.6) | collective-permute-done | bytes 360480 | tf_op jit(solution)/shard_map/ppermute | solution.py:236
  38.4 1.6 %collective-permute-start.10 = (s16[400,256]{1,0:T(8,128)(2,1)S(1)}, s16[400,256]{1,0:T(8,128)(2,1)S(1)}, u32[]{:S(2)}, u32[]{:S(2)}) collective-permute-start(s16[400,256]{1,0:T(8,128)(2,1)S(1)} %get-tuple-element.34), channel_id=1, source_target_pairs={{0,8},{8,0},{16,24},{24,16},{1,9},{9,1},{17,25},{25,17},{2,10},{10... | collective-permute-start | bytes 614408 | tf_op jit(solution)/shard_map/ppermute | solution.py:240
  39.9 1.5 %collective-permute-start.11 = (s16[400,256]{1,0:T(8,128)(2,1)S(1)}, s16[400,256]{1,0:T(8,128)(2,1)S(1)}, u32[]{:S(2)}, u32[]{:S(2)}) collective-permute-start(s16[400,256]{1,0:T(8,128)(2,1)S(1)} %get-tuple-element.35), channel_id=1, source_target_pairs={{0,16},{8,24},{16,0},{24,8},{1,17},{9,25},{17,1},{25,9},{2,18},{10... | collective-permute-start | bytes 614408 | tf_op jit(solution)/shard_map/ppermute | solution.py:240
  41.9 3.4 %collective-permute-done.5.arrived.refs_3_.refs_1_ = bf16[768,256]{1,0:T(8,128)(2,1)S(1)} collective-permute-done((bf16[768,256]{1,0:T(8,128)(2,1)S(1)}, bf16[768,256]{1,0:T(8,128)(2,1)S(1)}, u32[]{:S(2)}, u32[]{:S(2)}) %collective-permute-start.5) | collective-permute-done | bytes 393248 | tf_op jit(solution)/shard_map/ppermute | solution.py:236
  46.0 10.3 %collective-permute-done.8.arrived.refs_4_.refs_2_ = bf16[768,256]{1,0:T(8,128)(2,1)S(1)} collective-permute-done((bf16[768,256]{1,0:T(8,128)(2,1)S(1)}, bf16[768,256]{1,0:T(8,128)(2,1)S(1)}, u32[]{:S(2)}, u32[]{:S(2)}) %collective-permute-start.8) | collective-permute-done | bytes 393248 | tf_op jit(solution)/shard_map/ppermute | solution.py:236
  58.7 1.6 %collective-permute-start.15 = (s16[1056,256]{1,0:T(8,128)(2,1)S(1)}, s16[1056,256]{1,0:T(8,128)(2,1)S(1)}, u32[]{:S(2)}, u32[]{:S(2)}) collective-permute-start(s16[1056,256]{1,0:T(8,128)(2,1)S(1)} %get-tuple-element.39), channel_id=1, source_target_pairs={{0,16},{8,24},{16,0},{24,8},{1,17},{9,25},{17,1},{25,9},{2,18},{10... | collective-permute-start | bytes 1622024 | tf_op jit(solution)/shard_map/ppermute | solution.py:240
  60.9 2.0 %collective-permute-start.12 = (bf16[448,256]{1,0:T(8,128)(2,1)S(1)}, bf16[448,256]{1,0:T(8,128)(2,1)S(1)}, u32[]{:S(2)}, u32[]{:S(2)}) collective-permute-start(bf16[448,256]{1,0:T(8,128)(2,1)S(1)} %shard_map.58.refs_0_), channel_id=1, source_target_pairs={{0,1},{1,2},{2,3},{3,0},{4,5},{5,6},{6,7},{7,4},{8,9},{9,10},{10,1... | collective-permute-start | bytes 688136 | tf_op jit(solution)/shard_map/ppermute | solution.py:236
  62.9 7.0 %collective-permute-done.13.arrived.refs_4_.refs_2_ = bf16[640,256]{1,0:T(8,128)(2,1)S(1)} collective-permute-done((bf16[640,256]{1,0:T(8,128)(2,1)S(1)}, bf16[640,256]{1,0:T(8,128)(2,1)S(1)}, u32[]{:S(2)}, u32[]{:S(2)}) %collective-permute-start.13) | collective-permute-done | bytes 327712 | tf_op jit(solution)/shard_map/ppermute | solution.py:236
  70.6 1.5 %shard_map.60 = (f32[512,256]{1,0:T(8,128)S(1)}, f32[512,256]{1,0:T(8,128)S(1)}, s16[1056,256]{1,0:T(8,128)(2,1)S(1)}) custom-call(bf16[768,256]{1,0:T(8,128)(2,1)S(1)} %shard_map.51.refs_0_, bf16[768,256]{1,0:T(8,128)(2,1)S(1)} %collective-permute-done.5.arrived.refs_3_.refs_1_, bf16[768,256]{1,0:T(8,128)(2,1)S(1)} %collective-permute-done.8.arrived.refs_4_.refs_2_, ...), custom_call_target="tpu_custom_call" | custom-call | flops 1073741824 | bytes 3932160 | tf_op jit(solution)/shard_map/pallas_call | solution.py:140
  72.1 1.9 %collective-permute-start.18 = (s16[1056,256]{1,0:T(8,128)(2,1)S(1)}, s16[1056,256]{1,0:T(8,128)(2,1)S(1)}, u32[]{:S(2)}, u32[]{:S(2)}) collective-permute-start(s16[1056,256]{1,0:T(8,128)(2,1)S(1)} %get-tuple-element.42), channel_id=1, source_target_pairs={{0,8},{8,0},{16,24},{24,16},{1,9},{9,1},{17,25},{25,17},{2,10},{10... | collective-permute-start | bytes 1622024 | tf_op jit(solution)/shard_map/ppermute | solution.py:240
  74.7 1.9 %collective-permute-done.14.arrived.refs_4_.refs_2_ = bf16[448,256]{1,0:T(8,128)(2,1)S(1)} collective-permute-done((bf16[448,256]{1,0:T(8,128)(2,1)S(1)}, bf16[448,256]{1,0:T(8,128)(2,1)S(1)}, u32[]{:S(2)}, u32[]{:S(2)}) %collective-permute-start.14) | collective-permute-done | bytes 229408 | tf_op jit(solution)/shard_map/ppermute | solution.py:236
  78.2 1.9 %collective-permute-start.22 = (s16[800,256]{1,0:T(8,128)(2,1)S(1)}, s16[800,256]{1,0:T(8,128)(2,1)S(1)}, u32[]{:S(2)}, u32[]{:S(2)}) collective-permute-start(s16[800,256]{1,0:T(8,128)(2,1)S(1)} %get-tuple-element.48), channel_id=1, source_target_pairs={{0,16},{8,24},{16,0},{24,8},{1,17},{9,25},{17,1},{25,9},{2,18},{10... | collective-permute-start | bytes 1228808 | tf_op jit(solution)/shard_map/ppermute | solution.py:240
  80.1 1.5 %collective-permute-start.25 = (s16[528,256]{1,0:T(8,128)(2,1)S(1)}, s16[528,256]{1,0:T(8,128)(2,1)S(1)}, u32[]{:S(2)}, u32[]{:S(2)}) collective-permute-start(s16[528,256]{1,0:T(8,128)(2,1)S(1)} %shard_map.61.refs_0_), channel_id=1, source_target_pairs={{0,8},{8,0},{16,24},{24,16},{1,9},{9,1},{17,25},{25,17},{2,10},{10... | collective-permute-start | bytes 811016 | tf_op jit(solution)/shard_map/ppermute | solution.py:240
  81.6 1.8 %collective-permute-start.17 = (bf16[128,256]{1,0:T(8,128)(2,1)S(1)}, bf16[128,256]{1,0:T(8,128)(2,1)S(1)}, u32[]{:S(2)}, u32[]{:S(2)}) collective-permute-start(bf16[128,256]{1,0:T(8,128)(2,1)S(1)} %shard_map.63.refs_7_), channel_id=1, source_target_pairs={{0,3},{1,0},{2,1},{3,2},{4,7},{5,4},{6,5},{7,6},{8,11},{9,8},{10,9... | collective-permute-start | bytes 196616 | tf_op jit(solution)/shard_map/ppermute | solution.py:236
  84.6 1.9 %collective-permute-start.24 = (s16[528,256]{1,0:T(8,128)(2,1)S(1)}, s16[528,256]{1,0:T(8,128)(2,1)S(1)}, u32[]{:S(2)}, u32[]{:S(2)}) collective-permute-start(s16[528,256]{1,0:T(8,128)(2,1)S(1)} %shard_map.65.refs_7_), channel_id=1, source_target_pairs={{0,16},{8,24},{16,0},{24,8},{1,17},{9,25},{17,1},{25,9},{2,18},{10... | collective-permute-start | bytes 811016 | tf_op jit(solution)/shard_map/ppermute | solution.py:240
  86.5 3.0 %collective-permute-done.16.refs_3_ = bf16[128,256]{1,0:T(8,128)(2,1)S(1)} collective-permute-done((bf16[128,256]{1,0:T(8,128)(2,1)S(1)}, bf16[128,256]{1,0:T(8,128)(2,1)S(1)}, u32[]{:S(2)}, u32[]{:S(2)}) %collective-permute-start.16) | collective-permute-done | bytes 65568 | tf_op jit(solution)/shard_map/ppermute | solution.py:236
  92.5 1.8 %collective-permute-start.20 = (s16[272,256]{1,0:T(8,128)(2,1)S(1)}, s16[272,256]{1,0:T(8,128)(2,1)S(1)}, u32[]{:S(2)}, u32[]{:S(2)}) collective-permute-start(s16[272,256]{1,0:T(8,128)(2,1)S(1)} %get-tuple-element.46), channel_id=1, source_target_pairs={{0,8},{8,0},{16,24},{24,16},{1,9},{9,1},{17,25},{25,17},{2,10},{10... | collective-permute-start | bytes 417800 | tf_op jit(solution)/shard_map/ppermute | solution.py:240
  97.7 1.5 %collective-permute-done.20.refs_1_ = s16[272,256]{1,0:T(8,128)(2,1)S(1)} collective-permute-done((s16[272,256]{1,0:T(8,128)(2,1)S(1)}, s16[272,256]{1,0:T(8,128)(2,1)S(1)}, u32[]{:S(2)}, u32[]{:S(2)}) %collective-permute-start.20) | collective-permute-done | bytes 139296 | tf_op jit(solution)/shard_map/ppermute | solution.py:240
  (67 shorter events, 25.8 us)
Async XLA Ops:
  0.0 21.4 %collective-permute-start.3 = (bf16[512,4,256]{2,1,0:T(4,128)(2,1)}, bf16[512,4,256]{2,1,0:T(4,128)(2,1)S(1)}, u32[]{:S(2)}, u32[]{:S(2)}) collective-permute-start(bf16[512,4,256]{2,1,0:T(4,128)(2,1)} %values_ref.1), channel_id=1, source_target_pairs={{0,4},{4,0},{1,5},{5,1},{2,6},{6,2},{3,7},{7,3},{8,12},{12,8},{9,1... | collective-permute-start | bytes 3145736 | tf_op jit(solution)/shard_map/ppermute | solution.py:236
  2.9 10.5 %collective-permute-start = (bf16[384,256]{1,0:T(8,128)(2,1)S(1)}, bf16[384,256]{1,0:T(8,128)(2,1)S(1)}, u32[]{:S(2)}, u32[]{:S(2)}) collective-permute-start(bf16[384,256]{1,0:T(8,128)(2,1)S(1)} %shard_map.46.refs_0_), channel_id=1, source_target_pairs={{0,1},{1,2},{2,3},{3,0},{4,5},{5,6},{6,7},{7,4},{8,9},{9,10},{10,1... | collective-permute-start | bytes 589832 | tf_op jit(solution)/shard_map/ppermute | solution.py:236
  5.5 11.2 %collective-permute-start.4 = (bf16[384,256]{1,0:T(8,128)(2,1)S(1)}, bf16[384,256]{1,0:T(8,128)(2,1)S(1)}, u32[]{:S(2)}, u32[]{:S(2)}) collective-permute-start(bf16[384,256]{1,0:T(8,128)(2,1)S(1)} %shard_map.46.refs_0_), channel_id=1, source_target_pairs={{0,3},{1,0},{2,1},{3,2},{4,7},{5,4},{6,5},{7,6},{8,11},{9,8},{10,9... | collective-permute-start | bytes 589832 | tf_op jit(solution)/shard_map/ppermute | solution.py:236
  14.0 15.0 %collective-permute-start.1 = (bf16[704,256]{1,0:T(8,128)(2,1)S(1)}, bf16[704,256]{1,0:T(8,128)(2,1)S(1)}, u32[]{:S(2)}, u32[]{:S(2)}) collective-permute-start(bf16[704,256]{1,0:T(8,128)(2,1)S(1)} %shard_map.47.refs_0_), channel_id=1, source_target_pairs={{0,1},{1,2},{2,3},{3,0},{4,5},{5,6},{6,7},{7,4},{8,9},{9,10},{10,1... | collective-permute-start | bytes 1081352 | tf_op jit(solution)/shard_map/ppermute | solution.py:236
  17.4 19.2 %collective-permute-start.6 = (bf16[704,256]{1,0:T(8,128)(2,1)S(1)}, bf16[704,256]{1,0:T(8,128)(2,1)S(1)}, u32[]{:S(2)}, u32[]{:S(2)}) collective-permute-start(bf16[704,256]{1,0:T(8,128)(2,1)S(1)} %shard_map.48.refs_0_), channel_id=1, source_target_pairs={{0,3},{1,0},{2,1},{3,2},{4,7},{5,4},{6,5},{7,6},{8,11},{9,8},{10,9... | collective-permute-start | bytes 1081352 | tf_op jit(solution)/shard_map/ppermute | solution.py:236
  29.5 15.8 %collective-permute-start.5 = (bf16[768,256]{1,0:T(8,128)(2,1)S(1)}, bf16[768,256]{1,0:T(8,128)(2,1)S(1)}, u32[]{:S(2)}, u32[]{:S(2)}) collective-permute-start(bf16[768,256]{1,0:T(8,128)(2,1)S(1)} %shard_map.51.refs_0_), channel_id=1, source_target_pairs={{0,1},{1,2},{2,3},{3,0},{4,5},{5,6},{6,7},{7,4},{8,9},{9,10},{10,1... | collective-permute-start | bytes 1179656 | tf_op jit(solution)/shard_map/ppermute | solution.py:236
  37.1 19.2 %collective-permute-start.8 = (bf16[768,256]{1,0:T(8,128)(2,1)S(1)}, bf16[768,256]{1,0:T(8,128)(2,1)S(1)}, u32[]{:S(2)}, u32[]{:S(2)}) collective-permute-start(bf16[768,256]{1,0:T(8,128)(2,1)S(1)} %shard_map.52.refs_7_), channel_id=1, source_target_pairs={{0,3},{1,0},{2,1},{3,2},{4,7},{5,4},{6,5},{7,6},{8,11},{9,8},{10,9... | collective-permute-start | bytes 1179656 | tf_op jit(solution)/shard_map/ppermute | solution.py:236
  38.4 18.6 %collective-permute-start.10 = (s16[400,256]{1,0:T(8,128)(2,1)S(1)}, s16[400,256]{1,0:T(8,128)(2,1)S(1)}, u32[]{:S(2)}, u32[]{:S(2)}) collective-permute-start(s16[400,256]{1,0:T(8,128)(2,1)S(1)} %get-tuple-element.34), channel_id=1, source_target_pairs={{0,8},{8,0},{16,24},{24,16},{1,9},{9,1},{17,25},{25,17},{2,10},{10... | collective-permute-start | bytes 614408 | tf_op jit(solution)/shard_map/ppermute | solution.py:240
  39.9 17.0 %collective-permute-start.11 = (s16[400,256]{1,0:T(8,128)(2,1)S(1)}, s16[400,256]{1,0:T(8,128)(2,1)S(1)}, u32[]{:S(2)}, u32[]{:S(2)}) collective-permute-start(s16[400,256]{1,0:T(8,128)(2,1)S(1)} %get-tuple-element.35), channel_id=1, source_target_pairs={{0,16},{8,24},{16,0},{24,8},{1,17},{9,25},{17,1},{25,9},{2,18},{10... | collective-permute-start | bytes 614408 | tf_op jit(solution)/shard_map/ppermute | solution.py:240
  41.5 15.5 %collective-permute-start.9 = (s16[400,256]{1,0:T(8,128)(2,1)S(1)}, s16[400,256]{1,0:T(8,128)(2,1)S(1)}, u32[]{:S(2)}, u32[]{:S(2)}) collective-permute-start(s16[400,256]{1,0:T(8,128)(2,1)S(1)} %get-tuple-element.33), channel_id=1, source_target_pairs={{0,24},{8,16},{16,8},{24,0},{1,25},{9,17},{17,9},{25,1},{2,26},{10... | collective-permute-start | bytes 614408 | tf_op jit(solution)/shard_map/ppermute | solution.py:240
  45.9 14.4 %collective-permute-start.7 = (bf16[640,256]{1,0:T(8,128)(2,1)S(1)}, bf16[640,256]{1,0:T(8,128)(2,1)S(1)}, u32[]{:S(2)}, u32[]{:S(2)}) collective-permute-start(bf16[640,256]{1,0:T(8,128)(2,1)S(1)} %shard_map.54.refs_0_), channel_id=1, source_target_pairs={{0,1},{1,2},{2,3},{3,0},{4,5},{5,6},{6,7},{7,4},{8,9},{9,10},{10,1... | collective-permute-start | bytes 983048 | tf_op jit(solution)/shard_map/ppermute | solution.py:236
  56.9 13.1 %collective-permute-start.13 = (bf16[640,256]{1,0:T(8,128)(2,1)S(1)}, bf16[640,256]{1,0:T(8,128)(2,1)S(1)}, u32[]{:S(2)}, u32[]{:S(2)}) collective-permute-start(bf16[640,256]{1,0:T(8,128)(2,1)S(1)} %shard_map.55.refs_3_), channel_id=1, source_target_pairs={{0,3},{1,0},{2,1},{3,2},{4,7},{5,4},{6,5},{7,6},{8,11},{9,8},{10,9... | collective-permute-start | bytes 983048 | tf_op jit(solution)/shard_map/ppermute | solution.py:236
  58.7 15.3 %collective-permute-start.15 = (s16[1056,256]{1,0:T(8,128)(2,1)S(1)}, s16[1056,256]{1,0:T(8,128)(2,1)S(1)}, u32[]{:S(2)}, u32[]{:S(2)}) collective-permute-start(s16[1056,256]{1,0:T(8,128)(2,1)S(1)} %get-tuple-element.39), channel_id=1, source_target_pairs={{0,16},{8,24},{16,0},{24,8},{1,17},{9,25},{17,1},{25,9},{2,18},{10... | collective-permute-start | bytes 1622024 | tf_op jit(solution)/shard_map/ppermute | solution.py:240
  60.9 13.2 %collective-permute-start.12 = (bf16[448,256]{1,0:T(8,128)(2,1)S(1)}, bf16[448,256]{1,0:T(8,128)(2,1)S(1)}, u32[]{:S(2)}, u32[]{:S(2)}) collective-permute-start(bf16[448,256]{1,0:T(8,128)(2,1)S(1)} %shard_map.58.refs_0_), channel_id=1, source_target_pairs={{0,1},{1,2},{2,3},{3,0},{4,5},{5,6},{6,7},{7,4},{8,9},{9,10},{10,1... | collective-permute-start | bytes 688136 | tf_op jit(solution)/shard_map/ppermute | solution.py:236
  70.5 6.1 %collective-permute-start.14 = (bf16[448,256]{1,0:T(8,128)(2,1)S(1)}, bf16[448,256]{1,0:T(8,128)(2,1)S(1)}, u32[]{:S(2)}, u32[]{:S(2)}) collective-permute-start(bf16[448,256]{1,0:T(8,128)(2,1)S(1)} %shard_map.59.refs_7_), channel_id=1, source_target_pairs={{0,3},{1,0},{2,1},{3,2},{4,7},{5,4},{6,5},{7,6},{8,11},{9,8},{10,9... | collective-permute-start | bytes 688136 | tf_op jit(solution)/shard_map/ppermute | solution.py:236
  72.1 12.3 %collective-permute-start.18 = (s16[1056,256]{1,0:T(8,128)(2,1)S(1)}, s16[1056,256]{1,0:T(8,128)(2,1)S(1)}, u32[]{:S(2)}, u32[]{:S(2)}) collective-permute-start(s16[1056,256]{1,0:T(8,128)(2,1)S(1)} %get-tuple-element.42), channel_id=1, source_target_pairs={{0,8},{8,0},{16,24},{24,16},{1,9},{9,1},{17,25},{25,17},{2,10},{10... | collective-permute-start | bytes 1622024 | tf_op jit(solution)/shard_map/ppermute | solution.py:240
  78.2 12.1 %collective-permute-start.22 = (s16[800,256]{1,0:T(8,128)(2,1)S(1)}, s16[800,256]{1,0:T(8,128)(2,1)S(1)}, u32[]{:S(2)}, u32[]{:S(2)}) collective-permute-start(s16[800,256]{1,0:T(8,128)(2,1)S(1)} %get-tuple-element.48), channel_id=1, source_target_pairs={{0,16},{8,24},{16,0},{24,8},{1,17},{9,25},{17,1},{25,9},{2,18},{10... | collective-permute-start | bytes 1228808 | tf_op jit(solution)/shard_map/ppermute | solution.py:240
  80.1 14.2 %collective-permute-start.25 = (s16[528,256]{1,0:T(8,128)(2,1)S(1)}, s16[528,256]{1,0:T(8,128)(2,1)S(1)}, u32[]{:S(2)}, u32[]{:S(2)}) collective-permute-start(s16[528,256]{1,0:T(8,128)(2,1)S(1)} %shard_map.61.refs_0_), channel_id=1, source_target_pairs={{0,8},{8,0},{16,24},{24,16},{1,9},{9,1},{17,25},{25,17},{2,10},{10... | collective-permute-start | bytes 811016 | tf_op jit(solution)/shard_map/ppermute | solution.py:240
  83.4 6.1 %collective-permute-start.16 = (bf16[128,256]{1,0:T(8,128)(2,1)S(1)}, bf16[128,256]{1,0:T(8,128)(2,1)S(1)}, u32[]{:S(2)}, u32[]{:S(2)}) collective-permute-start(bf16[128,256]{1,0:T(8,128)(2,1)S(1)} %shard_map.62.refs_0_), channel_id=1, source_target_pairs={{0,1},{1,2},{2,3},{3,0},{4,5},{5,6},{6,7},{7,4},{8,9},{9,10},{10,1... | collective-permute-start | bytes 196616 | tf_op jit(solution)/shard_map/ppermute | solution.py:236
  84.6 10.2 %collective-permute-start.24 = (s16[528,256]{1,0:T(8,128)(2,1)S(1)}, s16[528,256]{1,0:T(8,128)(2,1)S(1)}, u32[]{:S(2)}, u32[]{:S(2)}) collective-permute-start(s16[528,256]{1,0:T(8,128)(2,1)S(1)} %shard_map.65.refs_7_), channel_id=1, source_target_pairs={{0,16},{8,24},{16,0},{24,8},{1,17},{9,25},{17,1},{25,9},{2,18},{10... | collective-permute-start | bytes 811016 | tf_op jit(solution)/shard_map/ppermute | solution.py:240
  90.5 5.8 %collective-permute-start.23 = (s16[400,256]{1,0:T(8,128)(2,1)S(1)}, s16[400,256]{1,0:T(8,128)(2,1)S(1)}, u32[]{:S(2)}, u32[]{:S(2)}) collective-permute-start(s16[400,256]{1,0:T(8,128)(2,1)S(1)} %shard_map.67.refs_3_), channel_id=1, source_target_pairs={{0,8},{8,0},{16,24},{24,16},{1,9},{9,1},{17,25},{25,17},{2,10},{10... | collective-permute-start | bytes 614408 | tf_op jit(solution)/shard_map/ppermute | solution.py:240
  91.0 6.7 %collective-permute-start.19 = (s16[272,256]{1,0:T(8,128)(2,1)S(1)}, s16[272,256]{1,0:T(8,128)(2,1)S(1)}, u32[]{:S(2)}, u32[]{:S(2)}) collective-permute-start(s16[272,256]{1,0:T(8,128)(2,1)S(1)} %get-tuple-element.45), channel_id=1, source_target_pairs={{0,24},{8,16},{16,8},{24,0},{1,25},{9,17},{17,9},{25,1},{2,26},{10... | collective-permute-start | bytes 417800 | tf_op jit(solution)/shard_map/ppermute | solution.py:240
  92.5 6.8 %collective-permute-start.20 = (s16[272,256]{1,0:T(8,128)(2,1)S(1)}, s16[272,256]{1,0:T(8,128)(2,1)S(1)}, u32[]{:S(2)}, u32[]{:S(2)}) collective-permute-start(s16[272,256]{1,0:T(8,128)(2,1)S(1)} %get-tuple-element.46), channel_id=1, source_target_pairs={{0,8},{8,0},{16,24},{24,16},{1,9},{9,1},{17,25},{25,17},{2,10},{10... | collective-permute-start | bytes 417800 | tf_op jit(solution)/shard_map/ppermute | solution.py:240
  94.3 5.1 %collective-permute-start.21 = (s16[272,256]{1,0:T(8,128)(2,1)S(1)}, s16[272,256]{1,0:T(8,128)(2,1)S(1)}, u32[]{:S(2)}, u32[]{:S(2)}) collective-permute-start(s16[272,256]{1,0:T(8,128)(2,1)S(1)} %get-tuple-element.47), channel_id=1, source_target_pairs={{0,16},{8,24},{16,0},{24,8},{1,17},{9,25},{17,1},{25,9},{2,18},{10... | collective-permute-start | bytes 417800 | tf_op jit(solution)/shard_map/ppermute | solution.py:240
  (8 other events, 29.1 us)

commit v16 on v15

--- a/solution.py
+++ b/solution.py
@@ -285,7 +285,7 @@
         return [[part] for part in [own[i]] + below + above] + [[last_below, last_above]]
 
     def direct(i):
-        return i in (0, len(sizes) - 1)
+        return i in (0, 1, len(sizes) - 1)
 
     def sum_chunk(i):
         if not direct(i):
@@ -327,8 +327,8 @@
                 for tiles, values in raw:
                     pieces.append(mask_right(tiles, values, last))
                     last[:] = pieces[-1:]
-        if i == 1:
-            square(0)
+        if i in (1, 2):
+            square(i - 1)
         sum_chunk(i)
         if i > 0 and not direct(i - 1):
             send_on(i - 1)

time: 102 us -> 102 us (level)
    ppermute x15, waiting for transfers between devices: 48.7 us -> 40.1 us  [shift(): return lax.ppermute(x, axis, [(i, (i + by) % n) for i in range(n)])]
    ppermute x12 -> x13, waiting for transfers between devices: 5.01 us -> 13 us  [swap(): return lax.ppermute(x, 'layer', [(i, i ^ bits) for i in range(4)])]
    ppermute x12 -> x13, starting transfers between devices: 16.4 us -> 17.2 us  [swap(): return lax.ppermute(x, 'layer', [(i, i ^ bits) for i in range(4)])]
  transfers between devices with their start and end apart: 27 -> 28, of which waited for: 15 -> 14; matrix products, arithmetic and copies ran while one was open for 0% -> 0% of each run, Pallas kernels for 15% -> 15%
where the time goes in v16:
time: 102 us
  waiting for transfers between devices  53.1 us (52%)
  starting transfers between devices  29.7 us (29%)
  Pallas kernels  16.8 us (16%)
  local copies, waits for them, and re-layouts  1.9 us (2%)
    ppermute x15, waiting for transfers between devices, shift(): return lax.ppermute(x, axis, [(i, (i + by) % n) for i in range(n)])  40.1 us
    ppermute x13, starting transfers between devices, swap(): return lax.ppermute(x, 'layer', [(i, i ^ bits) for i in range(4)])  17.2 us
    ppermute x13, waiting for transfers between devices, swap(): return lax.ppermute(x, 'layer', [(i, i ^ bits) for i in range(4)])  13 us
    ppermute x15, starting transfers between devices, shift(): return lax.ppermute(x, axis, [(i, (i + by) % n) for i in range(n)])  12.5 us
    pallas_call x11, Pallas kernels, load(): pl.pallas_call(functools.partial(load_kernel, at, size, parts), out_shape...  6.18 us
    pallas_call x5, Pallas kernels, partial_products(): pl.pallas_call(functools.partial(partial_kernel, tuple(steps), shapes, le...  6.09 us
    pallas_call x2, Pallas kernels, mask_right(): pl.pallas_call(mask_right_kernel, out_shape=jax.ShapeDtypeStruct((layers,...  2.27 us
  transfers between devices with their start and end apart: 28, of which 14 were waited for; matrix products, arithmetic and copies ran while one was open for 0% of the time, Pallas kernels for 15%

profile of v16, /device:TPU:0, one launch (start us, length us, event | category | flops | bytes accessed | tf_op | source)
XLA Modules:
  0.0 101.8 jit_solution(3828932941496288097)
XLA Ops:
  2.9 2.6 %collective-permute-start = (bf16[384,256]{1,0:T(8,128)(2,1)S(1)}, bf16[384,256]{1,0:T(8,128)(2,1)S(1)}, u32[]{:S(2)}, u32[]{:S(2)}) collective-permute-start(bf16[384,256]{1,0:T(8,128)(2,1)S(1)} %shard_map.46.refs_0_), channel_id=1, source_target_pairs={{0,1},{1,2},{2,3},{3,0},{4,5},{5,6},{6,7},{7,4},{8,9},{9,10},{10,1... | collective-permute-start | bytes 589832 | tf_op jit(solution)/shard_map/ppermute | solution.py:236
  5.5 2.1 %collective-permute-start.4 = (bf16[384,256]{1,0:T(8,128)(2,1)S(1)}, bf16[384,256]{1,0:T(8,128)(2,1)S(1)}, u32[]{:S(2)}, u32[]{:S(2)}) collective-permute-start(bf16[384,256]{1,0:T(8,128)(2,1)S(1)} %shard_map.46.refs_0_), channel_id=1, source_target_pairs={{0,3},{1,0},{2,1},{3,2},{4,7},{5,4},{6,5},{7,6},{8,11},{9,8},{10,9... | collective-permute-start | bytes 589832 | tf_op jit(solution)/shard_map/ppermute | solution.py:236
  7.6 5.7 %collective-permute-done.arrived.refs_1_ = bf16[384,256]{1,0:T(8,128)(2,1)S(1)} collective-permute-done((bf16[384,256]{1,0:T(8,128)(2,1)S(1)}, bf16[384,256]{1,0:T(8,128)(2,1)S(1)}, u32[]{:S(2)}, u32[]{:S(2)}) %collective-permute-start) | collective-permute-done | bytes 196640 | tf_op jit(solution)/shard_map/ppermute | solution.py:236
  14.0 2.8 %collective-permute-done.4.arrived.refs_2_ = bf16[384,256]{1,0:T(8,128)(2,1)S(1)} collective-permute-done((bf16[384,256]{1,0:T(8,128)(2,1)S(1)}, bf16[384,256]{1,0:T(8,128)(2,1)S(1)}, u32[]{:S(2)}, u32[]{:S(2)}) %collective-permute-start.4) | collective-permute-done | bytes 196640 | tf_op jit(solution)/shard_map/ppermute | solution.py:236
  17.4 2.8 %collective-permute-start.6 = (bf16[704,256]{1,0:T(8,128)(2,1)S(1)}, bf16[704,256]{1,0:T(8,128)(2,1)S(1)}, u32[]{:S(2)}, u32[]{:S(2)}) collective-permute-start(bf16[704,256]{1,0:T(8,128)(2,1)S(1)} %shard_map.48.refs_0_), channel_id=1, source_target_pairs={{0,3},{1,0},{2,1},{3,2},{4,7},{5,4},{6,5},{7,6},{8,11},{9,8},{10,9... | collective-permute-start | bytes 1081352 | tf_op jit(solution)/shard_map/ppermute | solution.py:236
  22.5 6.4 %collective-permute-done.1.arrived.refs_3_.refs_1_ = bf16[704,256]{1,0:T(8,128)(2,1)S(1)} collective-permute-done((bf16[704,256]{1,0:T(8,128)(2,1)S(1)}, bf16[704,256]{1,0:T(8,128)(2,1)S(1)}, u32[]{:S(2)}, u32[]{:S(2)}) %collective-permute-start.1) | collective-permute-done | bytes 360480 | tf_op jit(solution)/shard_map/ppermute | solution.py:236
  29.6 7.0 %collective-permute-done.6.arrived.refs_4_.refs_2_ = bf16[704,256]{1,0:T(8,128)(2,1)S(1)} collective-permute-done((bf16[704,256]{1,0:T(8,128)(2,1)S(1)}, bf16[704,256]{1,0:T(8,128)(2,1)S(1)}, u32[]{:S(2)}, u32[]{:S(2)}) %collective-permute-start.6) | collective-permute-done | bytes 360480 | tf_op jit(solution)/shard_map/ppermute | solution.py:236
  38.4 1.6 %collective-permute-start.10 = (s16[400,256]{1,0:T(8,128)(2,1)S(1)}, s16[400,256]{1,0:T(8,128)(2,1)S(1)}, u32[]{:S(2)}, u32[]{:S(2)}) collective-permute-start(s16[400,256]{1,0:T(8,128)(2,1)S(1)} %get-tuple-element.35), channel_id=1, source_target_pairs={{0,8},{8,0},{16,24},{24,16},{1,9},{9,1},{17,25},{25,17},{2,10},{10... | collective-permute-start | bytes 614408 | tf_op jit(solution)/shard_map/ppermute | solution.py:240
  39.9 1.5 %collective-permute-start.11 = (s16[400,256]{1,0:T(8,128)(2,1)S(1)}, s16[400,256]{1,0:T(8,128)(2,1)S(1)}, u32[]{:S(2)}, u32[]{:S(2)}) collective-permute-start(s16[400,256]{1,0:T(8,128)(2,1)S(1)} %get-tuple-element.36), channel_id=1, source_target_pairs={{0,16},{8,24},{16,0},{24,8},{1,17},{9,25},{17,1},{25,9},{2,18},{10... | collective-permute-start | bytes 614408 | tf_op jit(solution)/shard_map/ppermute | solution.py:240
  41.9 3.4 %collective-permute-done.5.arrived.refs_3_.refs_1_ = bf16[768,256]{1,0:T(8,128)(2,1)S(1)} collective-permute-done((bf16[768,256]{1,0:T(8,128)(2,1)S(1)}, bf16[768,256]{1,0:T(8,128)(2,1)S(1)}, u32[]{:S(2)}, u32[]{:S(2)}) %collective-permute-start.5) | collective-permute-done | bytes 393248 | tf_op jit(solution)/shard_map/ppermute | solution.py:236
  46.0 10.3 %collective-permute-done.8.arrived.refs_4_.refs_2_ = bf16[768,256]{1,0:T(8,128)(2,1)S(1)} collective-permute-done((bf16[768,256]{1,0:T(8,128)(2,1)S(1)}, bf16[768,256]{1,0:T(8,128)(2,1)S(1)}, u32[]{:S(2)}, u32[]{:S(2)}) %collective-permute-start.8) | collective-permute-done | bytes 393248 | tf_op jit(solution)/shard_map/ppermute | solution.py:236
  57.2 1.6 %shard_map.57 = (f32[512,256]{1,0:T(8,128)S(1)}, s16[528,256]{1,0:T(8,128)(2,1)S(1)}, s16[528,256]{1,0:T(8,128)(2,1)S(1)}, s16[528,256]{1,0:T(8,128)(2,1)S(1)}) custom-call(bf16[704,256]{1,0:T(8,128)(2,1)S(1)} %shard_map.47.refs_0_, bf16[704,256]{1,0:T(8,128)(2,1)S(1)} %collective-permute-done.1.arrived.refs_3_.refs_1_, ...), custom_call_target="tpu_custom_call" | custom-call | flops 1073741824 | bytes 3932160 | tf_op jit(solution)/shard_map/pallas_call | solution.py:140
  58.8 2.6 %collective-permute-start.15 = (s16[528,256]{1,0:T(8,128)(2,1)S(1)}, s16[528,256]{1,0:T(8,128)(2,1)S(1)}, u32[]{:S(2)}, u32[]{:S(2)}) collective-permute-start(s16[528,256]{1,0:T(8,128)(2,1)S(1)} %get-tuple-element.39), channel_id=1, source_target_pairs={{0,24},{8,16},{16,8},{24,0},{1,25},{9,17},{17,9},{25,1},{2,26},{10... | collective-permute-start | bytes 811016 | tf_op jit(solution)/shard_map/ppermute | solution.py:240
  62.9 2.1 %collective-permute-start.12 = (bf16[448,256]{1,0:T(8,128)(2,1)S(1)}, bf16[448,256]{1,0:T(8,128)(2,1)S(1)}, u32[]{:S(2)}, u32[]{:S(2)}) collective-permute-start(bf16[448,256]{1,0:T(8,128)(2,1)S(1)} %shard_map.58.refs_0_), channel_id=1, source_target_pairs={{0,1},{1,2},{2,3},{3,0},{4,5},{5,6},{6,7},{7,4},{8,9},{9,10},{10,1... | collective-permute-start | bytes 688136 | tf_op jit(solution)/shard_map/ppermute | solution.py:236
  64.9 3.3 %collective-permute-done.13.arrived.refs_4_.refs_2_ = bf16[640,256]{1,0:T(8,128)(2,1)S(1)} collective-permute-done((bf16[640,256]{1,0:T(8,128)(2,1)S(1)}, bf16[640,256]{1,0:T(8,128)(2,1)S(1)}, u32[]{:S(2)}, u32[]{:S(2)}) %collective-permute-start.13) | collective-permute-done | bytes 327712 | tf_op jit(solution)/shard_map/ppermute | solution.py:236
  68.9 2.5 %collective-permute-done.16.refs_1_ = s16[528,256]{1,0:T(8,128)(2,1)S(1)} collective-permute-done((s16[528,256]{1,0:T(8,128)(2,1)S(1)}, s16[528,256]{1,0:T(8,128)(2,1)S(1)}, u32[]{:S(2)}, u32[]{:S(2)}) %collective-permute-start.16) | collective-permute-done | bytes 270368 | tf_op jit(solution)/shard_map/ppermute | solution.py:240
  71.7 1.5 %shard_map.61 = (f32[512,256]{1,0:T(8,128)S(1)}, f32[512,256]{1,0:T(8,128)S(1)}, s16[1056,256]{1,0:T(8,128)(2,1)S(1)}) custom-call(bf16[768,256]{1,0:T(8,128)(2,1)S(1)} %shard_map.51.refs_0_, bf16[768,256]{1,0:T(8,128)(2,1)S(1)} %collective-permute-done.5.arrived.refs_3_.refs_1_, bf16[768,256]{1,0:T(8,128)(2,1)S(1)} %collective-permute-done.8.arrived.refs_4_.refs_2_, ...), custom_call_target="tpu_custom_call" | custom-call | flops 1073741824 | bytes 3932160 | tf_op jit(solution)/shard_map/pallas_call | solution.py:140
  73.1 1.5 %collective-permute-start.20 = (s16[1056,256]{1,0:T(8,128)(2,1)S(1)}, s16[1056,256]{1,0:T(8,128)(2,1)S(1)}, u32[]{:S(2)}, u32[]{:S(2)}) collective-permute-start(s16[1056,256]{1,0:T(8,128)(2,1)S(1)} %get-tuple-element.45), channel_id=1, source_target_pairs={{0,8},{8,0},{16,24},{24,16},{1,9},{9,1},{17,25},{25,17},{2,10},{10... | collective-permute-start | bytes 1622024 | tf_op jit(solution)/shard_map/ppermute | solution.py:240
  76.9 1.5 %collective-permute-start.24 = (s16[800,256]{1,0:T(8,128)(2,1)S(1)}, s16[800,256]{1,0:T(8,128)(2,1)S(1)}, u32[]{:S(2)}, u32[]{:S(2)}) collective-permute-start(s16[800,256]{1,0:T(8,128)(2,1)S(1)} %get-tuple-element.51), channel_id=1, source_target_pairs={{0,16},{8,24},{16,0},{24,8},{1,17},{9,25},{17,1},{25,9},{2,18},{10... | collective-permute-start | bytes 1228808 | tf_op jit(solution)/shard_map/ppermute | solution.py:240
  80.4 5.2 %collective-permute-done.20.received_ref.refs_0_ = s16[1056,256]{1,0:T(8,128)(2,1)S(1)} collective-permute-done((s16[1056,256]{1,0:T(8,128)(2,1)S(1)}, s16[1056,256]{1,0:T(8,128)(2,1)S(1)}, u32[]{:S(2)}, u32[]{:S(2)}) %collective-permute-start.20) | collective-permute-done | bytes 540704 | tf_op jit(solution)/shard_map/ppermute | solution.py:240
  85.8 2.0 %collective-permute-start.26 = (s16[528,256]{1,0:T(8,128)(2,1)S(1)}, s16[528,256]{1,0:T(8,128)(2,1)S(1)}, u32[]{:S(2)}, u32[]{:S(2)}) collective-permute-start(s16[528,256]{1,0:T(8,128)(2,1)S(1)} %shard_map.65.refs_7_), channel_id=1, source_target_pairs={{0,16},{8,24},{16,0},{24,8},{1,17},{9,25},{17,1},{25,9},{2,18},{10... | collective-permute-start | bytes 811016 | tf_op jit(solution)/shard_map/ppermute | solution.py:240
  88.8 1.5 %collective-permute-start.25 = (s16[400,256]{1,0:T(8,128)(2,1)S(1)}, s16[400,256]{1,0:T(8,128)(2,1)S(1)}, u32[]{:S(2)}, u32[]{:S(2)}) collective-permute-start(s16[400,256]{1,0:T(8,128)(2,1)S(1)} %shard_map.67.refs_3_), channel_id=1, source_target_pairs={{0,8},{8,0},{16,24},{24,16},{1,9},{9,1},{17,25},{25,17},{2,10},{10... | collective-permute-start | bytes 614408 | tf_op jit(solution)/shard_map/ppermute | solution.py:240
  91.8 2.0 %collective-permute-start.23 = (s16[272,256]{1,0:T(8,128)(2,1)S(1)}, s16[272,256]{1,0:T(8,128)(2,1)S(1)}, u32[]{:S(2)}, u32[]{:S(2)}) collective-permute-start(s16[272,256]{1,0:T(8,128)(2,1)S(1)} %get-tuple-element.50), channel_id=1, source_target_pairs={{0,16},{8,24},{16,0},{24,8},{1,17},{9,25},{17,1},{25,9},{2,18},{10... | collective-permute-start | bytes 417800 | tf_op jit(solution)/shard_map/ppermute | solution.py:240
  97.8 1.6 %collective-permute-done.22.refs_1_ = s16[272,256]{1,0:T(8,128)(2,1)S(1)} collective-permute-done((s16[272,256]{1,0:T(8,128)(2,1)S(1)}, s16[272,256]{1,0:T(8,128)(2,1)S(1)}, u32[]{:S(2)}, u32[]{:S(2)}) %collective-permute-start.22) | collective-permute-done | bytes 139296 | tf_op jit(solution)/shard_map/ppermute | solution.py:240
  (68 shorter events, 26.4 us)
Async XLA Ops:
  0.0 21.4 %collective-permute-start.3 = (bf16[512,4,256]{2,1,0:T(4,128)(2,1)}, bf16[512,4,256]{2,1,0:T(4,128)(2,1)S(1)}, u32[]{:S(2)}, u32[]{:S(2)}) collective-permute-start(bf16[512,4,256]{2,1,0:T(4,128)(2,1)} %values_ref.1), channel_id=1, source_target_pairs={{0,4},{4,0},{1,5},{5,1},{2,6},{6,2},{3,7},{7,3},{8,12},{12,8},{9,1... | collective-permute-start | bytes 3145736 | tf_op jit(solution)/shard_map/ppermute | solution.py:236
  2.9 10.5 %collective-permute-start = (bf16[384,256]{1,0:T(8,128)(2,1)S(1)}, bf16[384,256]{1,0:T(8,128)(2,1)S(1)}, u32[]{:S(2)}, u32[]{:S(2)}) collective-permute-start(bf16[384,256]{1,0:T(8,128)(2,1)S(1)} %shard_map.46.refs_0_), channel_id=1, source_target_pairs={{0,1},{1,2},{2,3},{3,0},{4,5},{5,6},{6,7},{7,4},{8,9},{9,10},{10,1... | collective-permute-start | bytes 589832 | tf_op jit(solution)/shard_map/ppermute | solution.py:236
  5.5 11.2 %collective-permute-start.4 = (bf16[384,256]{1,0:T(8,128)(2,1)S(1)}, bf16[384,256]{1,0:T(8,128)(2,1)S(1)}, u32[]{:S(2)}, u32[]{:S(2)}) collective-permute-start(bf16[384,256]{1,0:T(8,128)(2,1)S(1)} %shard_map.46.refs_0_), channel_id=1, source_target_pairs={{0,3},{1,0},{2,1},{3,2},{4,7},{5,4},{6,5},{7,6},{8,11},{9,8},{10,9... | collective-permute-start | bytes 589832 | tf_op jit(solution)/shard_map/ppermute | solution.py:236
  14.0 15.0 %collective-permute-start.1 = (bf16[704,256]{1,0:T(8,128)(2,1)S(1)}, bf16[704,256]{1,0:T(8,128)(2,1)S(1)}, u32[]{:S(2)}, u32[]{:S(2)}) collective-permute-start(bf16[704,256]{1,0:T(8,128)(2,1)S(1)} %shard_map.47.refs_0_), channel_id=1, source_target_pairs={{0,1},{1,2},{2,3},{3,0},{4,5},{5,6},{6,7},{7,4},{8,9},{9,10},{10,1... | collective-permute-start | bytes 1081352 | tf_op jit(solution)/shard_map/ppermute | solution.py:236
  17.4 19.2 %collective-permute-start.6 = (bf16[704,256]{1,0:T(8,128)(2,1)S(1)}, bf16[704,256]{1,0:T(8,128)(2,1)S(1)}, u32[]{:S(2)}, u32[]{:S(2)}) collective-permute-start(bf16[704,256]{1,0:T(8,128)(2,1)S(1)} %shard_map.48.refs_0_), channel_id=1, source_target_pairs={{0,3},{1,0},{2,1},{3,2},{4,7},{5,4},{6,5},{7,6},{8,11},{9,8},{10,9... | collective-permute-start | bytes 1081352 | tf_op jit(solution)/shard_map/ppermute | solution.py:236
  29.5 15.8 %collective-permute-start.5 = (bf16[768,256]{1,0:T(8,128)(2,1)S(1)}, bf16[768,256]{1,0:T(8,128)(2,1)S(1)}, u32[]{:S(2)}, u32[]{:S(2)}) collective-permute-start(bf16[768,256]{1,0:T(8,128)(2,1)S(1)} %shard_map.51.refs_0_), channel_id=1, source_target_pairs={{0,1},{1,2},{2,3},{3,0},{4,5},{5,6},{6,7},{7,4},{8,9},{9,10},{10,1... | collective-permute-start | bytes 1179656 | tf_op jit(solution)/shard_map/ppermute | solution.py:236
  37.1 19.2 %collective-permute-start.8 = (bf16[768,256]{1,0:T(8,128)(2,1)S(1)}, bf16[768,256]{1,0:T(8,128)(2,1)S(1)}, u32[]{:S(2)}, u32[]{:S(2)}) collective-permute-start(bf16[768,256]{1,0:T(8,128)(2,1)S(1)} %shard_map.52.refs_7_), channel_id=1, source_target_pairs={{0,3},{1,0},{2,1},{3,2},{4,7},{5,4},{6,5},{7,6},{8,11},{9,8},{10,9... | collective-permute-start | bytes 1179656 | tf_op jit(solution)/shard_map/ppermute | solution.py:236
  38.4 18.6 %collective-permute-start.10 = (s16[400,256]{1,0:T(8,128)(2,1)S(1)}, s16[400,256]{1,0:T(8,128)(2,1)S(1)}, u32[]{:S(2)}, u32[]{:S(2)}) collective-permute-start(s16[400,256]{1,0:T(8,128)(2,1)S(1)} %get-tuple-element.35), channel_id=1, source_target_pairs={{0,8},{8,0},{16,24},{24,16},{1,9},{9,1},{17,25},{25,17},{2,10},{10... | collective-permute-start | bytes 614408 | tf_op jit(solution)/shard_map/ppermute | solution.py:240
  39.9 17.0 %collective-permute-start.11 = (s16[400,256]{1,0:T(8,128)(2,1)S(1)}, s16[400,256]{1,0:T(8,128)(2,1)S(1)}, u32[]{:S(2)}, u32[]{:S(2)}) collective-permute-start(s16[400,256]{1,0:T(8,128)(2,1)S(1)} %get-tuple-element.36), channel_id=1, source_target_pairs={{0,16},{8,24},{16,0},{24,8},{1,17},{9,25},{17,1},{25,9},{2,18},{10... | collective-permute-start | bytes 614408 | tf_op jit(solution)/shard_map/ppermute | solution.py:240
  41.4 15.5 %collective-permute-start.9 = (s16[400,256]{1,0:T(8,128)(2,1)S(1)}, s16[400,256]{1,0:T(8,128)(2,1)S(1)}, u32[]{:S(2)}, u32[]{:S(2)}) collective-permute-start(s16[400,256]{1,0:T(8,128)(2,1)S(1)} %get-tuple-element.34), channel_id=1, source_target_pairs={{0,24},{8,16},{16,8},{24,0},{1,25},{9,17},{17,9},{25,1},{2,26},{10... | collective-permute-start | bytes 614408 | tf_op jit(solution)/shard_map/ppermute | solution.py:240
  45.9 16.4 %collective-permute-start.7 = (bf16[640,256]{1,0:T(8,128)(2,1)S(1)}, bf16[640,256]{1,0:T(8,128)(2,1)S(1)}, u32[]{:S(2)}, u32[]{:S(2)}) collective-permute-start(bf16[640,256]{1,0:T(8,128)(2,1)S(1)} %shard_map.54.refs_0_), channel_id=1, source_target_pairs={{0,1},{1,2},{2,3},{3,0},{4,5},{5,6},{6,7},{7,4},{8,9},{9,10},{10,1... | collective-permute-start | bytes 983048 | tf_op jit(solution)/shard_map/ppermute | solution.py:236
  56.9 11.4 %collective-permute-start.13 = (bf16[640,256]{1,0:T(8,128)(2,1)S(1)}, bf16[640,256]{1,0:T(8,128)(2,1)S(1)}, u32[]{:S(2)}, u32[]{:S(2)}) collective-permute-start(bf16[640,256]{1,0:T(8,128)(2,1)S(1)} %shard_map.55.refs_3_), channel_id=1, source_target_pairs={{0,3},{1,0},{2,1},{3,2},{4,7},{5,4},{6,5},{7,6},{8,11},{9,8},{10,9... | collective-permute-start | bytes 983048 | tf_op jit(solution)/shard_map/ppermute | solution.py:236
  58.8 10.1 %collective-permute-start.15 = (s16[528,256]{1,0:T(8,128)(2,1)S(1)}, s16[528,256]{1,0:T(8,128)(2,1)S(1)}, u32[]{:S(2)}, u32[]{:S(2)}) collective-permute-start(s16[528,256]{1,0:T(8,128)(2,1)S(1)} %get-tuple-element.39), channel_id=1, source_target_pairs={{0,24},{8,16},{16,8},{24,0},{1,25},{9,17},{17,9},{25,1},{2,26},{10... | collective-permute-start | bytes 811016 | tf_op jit(solution)/shard_map/ppermute | solution.py:240
  61.3 10.1 %collective-permute-start.16 = (s16[528,256]{1,0:T(8,128)(2,1)S(1)}, s16[528,256]{1,0:T(8,128)(2,1)S(1)}, u32[]{:S(2)}, u32[]{:S(2)}) collective-permute-start(s16[528,256]{1,0:T(8,128)(2,1)S(1)} %get-tuple-element.40), channel_id=1, source_target_pairs={{0,8},{8,0},{16,24},{24,16},{1,9},{9,1},{17,25},{25,17},{2,10},{10... | collective-permute-start | bytes 811016 | tf_op jit(solution)/shard_map/ppermute | solution.py:240
  61.9 9.5 %collective-permute-start.17 = (s16[528,256]{1,0:T(8,128)(2,1)S(1)}, s16[528,256]{1,0:T(8,128)(2,1)S(1)}, u32[]{:S(2)}, u32[]{:S(2)}) collective-permute-start(s16[528,256]{1,0:T(8,128)(2,1)S(1)} %get-tuple-element.41), channel_id=1, source_target_pairs={{0,16},{8,24},{16,0},{24,8},{1,17},{9,25},{17,1},{25,9},{2,18},{10... | collective-permute-start | bytes 811016 | tf_op jit(solution)/shard_map/ppermute | solution.py:240
  62.9 11.8 %collective-permute-start.12 = (bf16[448,256]{1,0:T(8,128)(2,1)S(1)}, bf16[448,256]{1,0:T(8,128)(2,1)S(1)}, u32[]{:S(2)}, u32[]{:S(2)}) collective-permute-start(bf16[448,256]{1,0:T(8,128)(2,1)S(1)} %shard_map.58.refs_0_), channel_id=1, source_target_pairs={{0,1},{1,2},{2,3},{3,0},{4,5},{5,6},{6,7},{7,4},{8,9},{9,10},{10,1... | collective-permute-start | bytes 688136 | tf_op jit(solution)/shard_map/ppermute | solution.py:236
  73.1 12.5 %collective-permute-start.20 = (s16[1056,256]{1,0:T(8,128)(2,1)S(1)}, s16[1056,256]{1,0:T(8,128)(2,1)S(1)}, u32[]{:S(2)}, u32[]{:S(2)}) collective-permute-start(s16[1056,256]{1,0:T(8,128)(2,1)S(1)} %get-tuple-element.45), channel_id=1, source_target_pairs={{0,8},{8,0},{16,24},{24,16},{1,9},{9,1},{17,25},{25,17},{2,10},{10... | collective-permute-start | bytes 1622024 | tf_op jit(solution)/shard_map/ppermute | solution.py:240
  76.9 11.7 %collective-permute-start.24 = (s16[800,256]{1,0:T(8,128)(2,1)S(1)}, s16[800,256]{1,0:T(8,128)(2,1)S(1)}, u32[]{:S(2)}, u32[]{:S(2)}) collective-permute-start(s16[800,256]{1,0:T(8,128)(2,1)S(1)} %get-tuple-element.51), channel_id=1, source_target_pairs={{0,16},{8,24},{16,0},{24,8},{1,17},{9,25},{17,1},{25,9},{2,18},{10... | collective-permute-start | bytes 1228808 | tf_op jit(solution)/shard_map/ppermute | solution.py:240
  78.4 9.4 %collective-permute-start.19 = (bf16[128,256]{1,0:T(8,128)(2,1)S(1)}, bf16[128,256]{1,0:T(8,128)(2,1)S(1)}, u32[]{:S(2)}, u32[]{:S(2)}) collective-permute-start(bf16[128,256]{1,0:T(8,128)(2,1)S(1)} %shard_map.63.refs_7_), channel_id=1, source_target_pairs={{0,3},{1,0},{2,1},{3,2},{4,7},{5,4},{6,5},{7,6},{8,11},{9,8},{10,9... | collective-permute-start | bytes 196616 | tf_op jit(solution)/shard_map/ppermute | solution.py:236
  79.8 8.0 %collective-permute-start.18 = (bf16[128,256]{1,0:T(8,128)(2,1)S(1)}, bf16[128,256]{1,0:T(8,128)(2,1)S(1)}, u32[]{:S(2)}, u32[]{:S(2)}) collective-permute-start(bf16[128,256]{1,0:T(8,128)(2,1)S(1)} %shard_map.62.refs_0_), channel_id=1, source_target_pairs={{0,1},{1,2},{2,3},{3,0},{4,5},{5,6},{6,7},{7,4},{8,9},{9,10},{10,1... | collective-permute-start | bytes 196616 | tf_op jit(solution)/shard_map/ppermute | solution.py:236
  85.8 9.1 %collective-permute-start.26 = (s16[528,256]{1,0:T(8,128)(2,1)S(1)}, s16[528,256]{1,0:T(8,128)(2,1)S(1)}, u32[]{:S(2)}, u32[]{:S(2)}) collective-permute-start(s16[528,256]{1,0:T(8,128)(2,1)S(1)} %shard_map.65.refs_7_), channel_id=1, source_target_pairs={{0,16},{8,24},{16,0},{24,8},{1,17},{9,25},{17,1},{25,9},{2,18},{10... | collective-permute-start | bytes 811016 | tf_op jit(solution)/shard_map/ppermute | solution.py:240
  88.8 7.6 %collective-permute-start.25 = (s16[400,256]{1,0:T(8,128)(2,1)S(1)}, s16[400,256]{1,0:T(8,128)(2,1)S(1)}, u32[]{:S(2)}, u32[]{:S(2)}) collective-permute-start(s16[400,256]{1,0:T(8,128)(2,1)S(1)} %shard_map.67.refs_3_), channel_id=1, source_target_pairs={{0,8},{8,0},{16,24},{24,16},{1,9},{9,1},{17,25},{25,17},{2,10},{10... | collective-permute-start | bytes 614408 | tf_op jit(solution)/shard_map/ppermute | solution.py:240
  90.4 9.1 %collective-permute-start.22 = (s16[272,256]{1,0:T(8,128)(2,1)S(1)}, s16[272,256]{1,0:T(8,128)(2,1)S(1)}, u32[]{:S(2)}, u32[]{:S(2)}) collective-permute-start(s16[272,256]{1,0:T(8,128)(2,1)S(1)} %get-tuple-element.49), channel_id=1, source_target_pairs={{0,8},{8,0},{16,24},{24,16},{1,9},{9,1},{17,25},{25,17},{2,10},{10... | collective-permute-start | bytes 417800 | tf_op jit(solution)/shard_map/ppermute | solution.py:240
  91.8 7.6 %collective-permute-start.23 = (s16[272,256]{1,0:T(8,128)(2,1)S(1)}, s16[272,256]{1,0:T(8,128)(2,1)S(1)}, u32[]{:S(2)}, u32[]{:S(2)}) collective-permute-start(s16[272,256]{1,0:T(8,128)(2,1)S(1)} %get-tuple-element.50), channel_id=1, source_target_pairs={{0,16},{8,24},{16,0},{24,8},{1,17},{9,25},{17,1},{25,9},{2,18},{10... | collective-permute-start | bytes 417800 | tf_op jit(solution)/shard_map/ppermute | solution.py:240
  (9 other events, 38.2 us)

commit v17 on v16

--- a/solution.py
+++ b/solution.py
@@ -330,8 +330,10 @@
         if i in (1, 2):
             square(i - 1)
         sum_chunk(i)
-        if i > 0 and not direct(i - 1):
-            send_on(i - 1)
+        if i + 1 == len(sizes):
+            for j in range(len(sizes)):
+                if not direct(j):
+                    send_on(j)
     for i in range(len(squares), len(sizes)):
         square(i)
 

time: 102 us -> 102 us (level)
  starting transfers between devices: 29.7 us -> 28.6 us
    ppermute x15, waiting for transfers between devices: 40.1 us -> 45.6 us  [shift(): return lax.ppermute(x, axis, [(i, (i + by) % n) for i in range(n)])]
    ppermute x13, waiting for transfers between devices: 13 us -> 8.24 us  [swap(): return lax.ppermute(x, 'layer', [(i, i ^ bits) for i in range(4)])]
    ppermute x13, starting transfers between devices: 17.2 us -> 16.1 us  [swap(): return lax.ppermute(x, 'layer', [(i, i ^ bits) for i in range(4)])]
where the time goes in v17:
time: 102 us; the launch traced here: 101 us
  waiting for transfers between devices  53.8 us (53%)
  starting transfers between devices  28.6 us (28%)
  Pallas kernels  16.8 us (16%)
  local copies, waits for them, and re-layouts  1.9 us (2%)
    ppermute x15, waiting for transfers between devices, shift(): return lax.ppermute(x, axis, [(i, (i + by) % n) for i in range(n)])  45.6 us
    ppermute x13, starting transfers between devices, swap(): return lax.ppermute(x, 'layer', [(i, i ^ bits) for i in range(4)])  16.1 us
    ppermute x15, starting transfers between devices, shift(): return lax.ppermute(x, axis, [(i, (i + by) % n) for i in range(n)])  12.5 us
    ppermute x13, waiting for transfers between devices, swap(): return lax.ppermute(x, 'layer', [(i, i ^ bits) for i in range(4)])  8.24 us
    pallas_call x11, Pallas kernels, load(): pl.pallas_call(functools.partial(load_kernel, at, size, parts), out_shape...  6.18 us
    pallas_call x5, Pallas kernels, partial_products(): pl.pallas_call(functools.partial(partial_kernel, tuple(steps), shapes, le...  6.1 us
    pallas_call x2, Pallas kernels, mask_right(): pl.pallas_call(mask_right_kernel, out_shape=jax.ShapeDtypeStruct((layers,...  2.27 us
  transfers between devices with their start and end apart: 28, of which 14 were waited for; matrix products, arithmetic and copies ran while one was open for 0% of the time, Pallas kernels for 15%

profile of v17, /device:TPU:0, one launch (start us, length us, event | category | flops | bytes accessed | tf_op | source)
XLA Modules:
  0.0 101.4 jit_solution(18164386900430142890)
XLA Ops:
  2.9 2.6 %collective-permute-start = (bf16[384,256]{1,0:T(8,128)(2,1)S(1)}, bf16[384,256]{1,0:T(8,128)(2,1)S(1)}, u32[]{:S(2)}, u32[]{:S(2)}) collective-permute-start(bf16[384,256]{1,0:T(8,128)(2,1)S(1)} %shard_map.46.refs_0_), channel_id=1, source_target_pairs={{0,1},{1,2},{2,3},{3,0},{4,5},{5,6},{6,7},{7,4},{8,9},{9,10},{10,1... | collective-permute-start | bytes 589832 | tf_op jit(solution)/shard_map/ppermute | solution.py:236
  5.5 2.1 %collective-permute-start.4 = (bf16[384,256]{1,0:T(8,128)(2,1)S(1)}, bf16[384,256]{1,0:T(8,128)(2,1)S(1)}, u32[]{:S(2)}, u32[]{:S(2)}) collective-permute-start(bf16[384,256]{1,0:T(8,128)(2,1)S(1)} %shard_map.46.refs_0_), channel_id=1, source_target_pairs={{0,3},{1,0},{2,1},{3,2},{4,7},{5,4},{6,5},{7,6},{8,11},{9,8},{10,9... | collective-permute-start | bytes 589832 | tf_op jit(solution)/shard_map/ppermute | solution.py:236
  7.6 5.7 %collective-permute-done.arrived.refs_1_ = bf16[384,256]{1,0:T(8,128)(2,1)S(1)} collective-permute-done((bf16[384,256]{1,0:T(8,128)(2,1)S(1)}, bf16[384,256]{1,0:T(8,128)(2,1)S(1)}, u32[]{:S(2)}, u32[]{:S(2)}) %collective-permute-start) | collective-permute-done | bytes 196640 | tf_op jit(solution)/shard_map/ppermute | solution.py:236
  14.0 2.8 %collective-permute-done.4.arrived.refs_2_ = bf16[384,256]{1,0:T(8,128)(2,1)S(1)} collective-permute-done((bf16[384,256]{1,0:T(8,128)(2,1)S(1)}, bf16[384,256]{1,0:T(8,128)(2,1)S(1)}, u32[]{:S(2)}, u32[]{:S(2)}) %collective-permute-start.4) | collective-permute-done | bytes 196640 | tf_op jit(solution)/shard_map/ppermute | solution.py:236
  17.4 2.8 %collective-permute-start.6 = (bf16[704,256]{1,0:T(8,128)(2,1)S(1)}, bf16[704,256]{1,0:T(8,128)(2,1)S(1)}, u32[]{:S(2)}, u32[]{:S(2)}) collective-permute-start(bf16[704,256]{1,0:T(8,128)(2,1)S(1)} %shard_map.48.refs_0_), channel_id=1, source_target_pairs={{0,3},{1,0},{2,1},{3,2},{4,7},{5,4},{6,5},{7,6},{8,11},{9,8},{10,9... | collective-permute-start | bytes 1081352 | tf_op jit(solution)/shard_map/ppermute | solution.py:236
  22.5 6.4 %collective-permute-done.1.arrived.refs_3_.refs_1_ = bf16[704,256]{1,0:T(8,128)(2,1)S(1)} collective-permute-done((bf16[704,256]{1,0:T(8,128)(2,1)S(1)}, bf16[704,256]{1,0:T(8,128)(2,1)S(1)}, u32[]{:S(2)}, u32[]{:S(2)}) %collective-permute-start.1) | collective-permute-done | bytes 360480 | tf_op jit(solution)/shard_map/ppermute | solution.py:236
  29.6 7.0 %collective-permute-done.6.arrived.refs_4_.refs_2_ = bf16[704,256]{1,0:T(8,128)(2,1)S(1)} collective-permute-done((bf16[704,256]{1,0:T(8,128)(2,1)S(1)}, bf16[704,256]{1,0:T(8,128)(2,1)S(1)}, u32[]{:S(2)}, u32[]{:S(2)}) %collective-permute-start.6) | collective-permute-done | bytes 360480 | tf_op jit(solution)/shard_map/ppermute | solution.py:236
  38.4 1.6 %collective-permute-start.10 = (s16[400,256]{1,0:T(8,128)(2,1)S(1)}, s16[400,256]{1,0:T(8,128)(2,1)S(1)}, u32[]{:S(2)}, u32[]{:S(2)}) collective-permute-start(s16[400,256]{1,0:T(8,128)(2,1)S(1)} %get-tuple-element.35), channel_id=1, source_target_pairs={{0,8},{8,0},{16,24},{24,16},{1,9},{9,1},{17,25},{25,17},{2,10},{10... | collective-permute-start | bytes 614408 | tf_op jit(solution)/shard_map/ppermute | solution.py:240
  39.9 1.5 %collective-permute-start.11 = (s16[400,256]{1,0:T(8,128)(2,1)S(1)}, s16[400,256]{1,0:T(8,128)(2,1)S(1)}, u32[]{:S(2)}, u32[]{:S(2)}) collective-permute-start(s16[400,256]{1,0:T(8,128)(2,1)S(1)} %get-tuple-element.36), channel_id=1, source_target_pairs={{0,16},{8,24},{16,0},{24,8},{1,17},{9,25},{17,1},{25,9},{2,18},{10... | collective-permute-start | bytes 614408 | tf_op jit(solution)/shard_map/ppermute | solution.py:240
  41.9 3.4 %collective-permute-done.5.arrived.refs_3_.refs_1_ = bf16[768,256]{1,0:T(8,128)(2,1)S(1)} collective-permute-done((bf16[768,256]{1,0:T(8,128)(2,1)S(1)}, bf16[768,256]{1,0:T(8,128)(2,1)S(1)}, u32[]{:S(2)}, u32[]{:S(2)}) %collective-permute-start.5) | collective-permute-done | bytes 393248 | tf_op jit(solution)/shard_map/ppermute | solution.py:236
  46.0 10.3 %collective-permute-done.8.arrived.refs_4_.refs_2_ = bf16[768,256]{1,0:T(8,128)(2,1)S(1)} collective-permute-done((bf16[768,256]{1,0:T(8,128)(2,1)S(1)}, bf16[768,256]{1,0:T(8,128)(2,1)S(1)}, u32[]{:S(2)}, u32[]{:S(2)}) %collective-permute-start.8) | collective-permute-done | bytes 393248 | tf_op jit(solution)/shard_map/ppermute | solution.py:236
  57.2 1.6 %shard_map.57 = (f32[512,256]{1,0:T(8,128)S(1)}, s16[528,256]{1,0:T(8,128)(2,1)S(1)}, s16[528,256]{1,0:T(8,128)(2,1)S(1)}, s16[528,256]{1,0:T(8,128)(2,1)S(1)}) custom-call(bf16[704,256]{1,0:T(8,128)(2,1)S(1)} %shard_map.47.refs_0_, bf16[704,256]{1,0:T(8,128)(2,1)S(1)} %collective-permute-done.1.arrived.refs_3_.refs_1_, ...), custom_call_target="tpu_custom_call" | custom-call | flops 1073741824 | bytes 3932160 | tf_op jit(solution)/shard_map/pallas_call | solution.py:140
  58.8 2.6 %collective-permute-start.15 = (s16[528,256]{1,0:T(8,128)(2,1)S(1)}, s16[528,256]{1,0:T(8,128)(2,1)S(1)}, u32[]{:S(2)}, u32[]{:S(2)}) collective-permute-start(s16[528,256]{1,0:T(8,128)(2,1)S(1)} %get-tuple-element.39), channel_id=1, source_target_pairs={{0,24},{8,16},{16,8},{24,0},{1,25},{9,17},{17,9},{25,1},{2,26},{10... | collective-permute-start | bytes 811016 | tf_op jit(solution)/shard_map/ppermute | solution.py:240
  62.9 2.0 %collective-permute-start.12 = (bf16[448,256]{1,0:T(8,128)(2,1)S(1)}, bf16[448,256]{1,0:T(8,128)(2,1)S(1)}, u32[]{:S(2)}, u32[]{:S(2)}) collective-permute-start(bf16[448,256]{1,0:T(8,128)(2,1)S(1)} %shard_map.58.refs_0_), channel_id=1, source_target_pairs={{0,1},{1,2},{2,3},{3,0},{4,5},{5,6},{6,7},{7,4},{8,9},{9,10},{10,1... | collective-permute-start | bytes 688136 | tf_op jit(solution)/shard_map/ppermute | solution.py:236
  64.9 3.3 %collective-permute-done.13.arrived.refs_4_.refs_2_ = bf16[640,256]{1,0:T(8,128)(2,1)S(1)} collective-permute-done((bf16[640,256]{1,0:T(8,128)(2,1)S(1)}, bf16[640,256]{1,0:T(8,128)(2,1)S(1)}, u32[]{:S(2)}, u32[]{:S(2)}) %collective-permute-start.13) | collective-permute-done | bytes 327712 | tf_op jit(solution)/shard_map/ppermute | solution.py:236
  68.9 2.5 %collective-permute-done.16.refs_1_ = s16[528,256]{1,0:T(8,128)(2,1)S(1)} collective-permute-done((s16[528,256]{1,0:T(8,128)(2,1)S(1)}, s16[528,256]{1,0:T(8,128)(2,1)S(1)}, u32[]{:S(2)}, u32[]{:S(2)}) %collective-permute-start.16) | collective-permute-done | bytes 270368 | tf_op jit(solution)/shard_map/ppermute | solution.py:240
  71.6 1.5 %shard_map.61 = (f32[512,256]{1,0:T(8,128)S(1)}, f32[512,256]{1,0:T(8,128)S(1)}, s16[1056,256]{1,0:T(8,128)(2,1)S(1)}) custom-call(bf16[768,256]{1,0:T(8,128)(2,1)S(1)} %shard_map.51.refs_0_, bf16[768,256]{1,0:T(8,128)(2,1)S(1)} %collective-permute-done.5.arrived.refs_3_.refs_1_, bf16[768,256]{1,0:T(8,128)(2,1)S(1)} %collective-permute-done.8.arrived.refs_4_.refs_2_, ...), custom_call_target="tpu_custom_call" | custom-call | flops 1073741824 | bytes 3932160 | tf_op jit(solution)/shard_map/pallas_call | solution.py:140
  73.1 1.6 %collective-permute-start.24 = (s16[1056,256]{1,0:T(8,128)(2,1)S(1)}, s16[1056,256]{1,0:T(8,128)(2,1)S(1)}, u32[]{:S(2)}, u32[]{:S(2)}) collective-permute-start(s16[1056,256]{1,0:T(8,128)(2,1)S(1)} %get-tuple-element.52), channel_id=1, source_target_pairs={{0,8},{8,0},{16,24},{24,16},{1,9},{9,1},{17,25},{25,17},{2,10},{10... | collective-permute-start | bytes 1622024 | tf_op jit(solution)/shard_map/ppermute | solution.py:240
  76.9 1.5 %collective-permute-start.23 = (s16[800,256]{1,0:T(8,128)(2,1)S(1)}, s16[800,256]{1,0:T(8,128)(2,1)S(1)}, u32[]{:S(2)}, u32[]{:S(2)}) collective-permute-start(s16[800,256]{1,0:T(8,128)(2,1)S(1)} %get-tuple-element.49), channel_id=1, source_target_pairs={{0,16},{8,24},{16,0},{24,8},{1,17},{9,25},{17,1},{25,9},{2,18},{10... | collective-permute-start | bytes 1228808 | tf_op jit(solution)/shard_map/ppermute | solution.py:240
  80.4 2.2 %collective-permute-done.19.refs_4_ = bf16[128,256]{1,0:T(8,128)(2,1)S(1)} collective-permute-done((bf16[128,256]{1,0:T(8,128)(2,1)S(1)}, bf16[128,256]{1,0:T(8,128)(2,1)S(1)}, u32[]{:S(2)}, u32[]{:S(2)}) %collective-permute-start.19) | collective-permute-done | bytes 65568 | tf_op jit(solution)/shard_map/ppermute | solution.py:236
  82.6 3.2 %collective-permute-done.18.refs_3_ = bf16[128,256]{1,0:T(8,128)(2,1)S(1)} collective-permute-done((bf16[128,256]{1,0:T(8,128)(2,1)S(1)}, bf16[128,256]{1,0:T(8,128)(2,1)S(1)}, u32[]{:S(2)}, u32[]{:S(2)}) %collective-permute-start.18) | collective-permute-done | bytes 65568 | tf_op jit(solution)/shard_map/ppermute | solution.py:236
  87.9 1.5 %collective-permute-start.25 = (s16[400,256]{1,0:T(8,128)(2,1)S(1)}, s16[400,256]{1,0:T(8,128)(2,1)S(1)}, u32[]{:S(2)}, u32[]{:S(2)}) collective-permute-start(s16[400,256]{1,0:T(8,128)(2,1)S(1)} %shard_map.67.refs_3_), channel_id=1, source_target_pairs={{0,8},{8,0},{16,24},{24,16},{1,9},{9,1},{17,25},{25,17},{2,10},{10... | collective-permute-start | bytes 614408 | tf_op jit(solution)/shard_map/ppermute | solution.py:240
  90.6 1.5 %collective-permute-start.21 = (s16[272,256]{1,0:T(8,128)(2,1)S(1)}, s16[272,256]{1,0:T(8,128)(2,1)S(1)}, u32[]{:S(2)}, u32[]{:S(2)}) collective-permute-start(s16[272,256]{1,0:T(8,128)(2,1)S(1)} %get-tuple-element.47), channel_id=1, source_target_pairs={{0,8},{8,0},{16,24},{24,16},{1,9},{9,1},{17,25},{25,17},{2,10},{10... | collective-permute-start | bytes 417800 | tf_op jit(solution)/shard_map/ppermute | solution.py:240
  92.9 4.6 %collective-permute-done.26.refs_1_ = s16[528,256]{1,0:T(8,128)(2,1)S(1)} collective-permute-done((s16[528,256]{1,0:T(8,128)(2,1)S(1)}, s16[528,256]{1,0:T(8,128)(2,1)S(1)}, u32[]{:S(2)}, u32[]{:S(2)}) %collective-permute-start.26) | collective-permute-done | bytes 270368 | tf_op jit(solution)/shard_map/ppermute | solution.py:240
  (68 shorter events, 25.2 us)
Async XLA Ops:
  0.0 21.4 %collective-permute-start.3 = (bf16[512,4,256]{2,1,0:T(4,128)(2,1)}, bf16[512,4,256]{2,1,0:T(4,128)(2,1)S(1)}, u32[]{:S(2)}, u32[]{:S(2)}) collective-permute-start(bf16[512,4,256]{2,1,0:T(4,128)(2,1)} %values_ref.1), channel_id=1, source_target_pairs={{0,4},{4,0},{1,5},{5,1},{2,6},{6,2},{3,7},{7,3},{8,12},{12,8},{9,1... | collective-permute-start | bytes 3145736 | tf_op jit(solution)/shard_map/ppermute | solution.py:236
  2.9 10.5 %collective-permute-start = (bf16[384,256]{1,0:T(8,128)(2,1)S(1)}, bf16[384,256]{1,0:T(8,128)(2,1)S(1)}, u32[]{:S(2)}, u32[]{:S(2)}) collective-permute-start(bf16[384,256]{1,0:T(8,128)(2,1)S(1)} %shard_map.46.refs_0_), channel_id=1, source_target_pairs={{0,1},{1,2},{2,3},{3,0},{4,5},{5,6},{6,7},{7,4},{8,9},{9,10},{10,1... | collective-permute-start | bytes 589832 | tf_op jit(solution)/shard_map/ppermute | solution.py:236
  5.5 11.2 %collective-permute-start.4 = (bf16[384,256]{1,0:T(8,128)(2,1)S(1)}, bf16[384,256]{1,0:T(8,128)(2,1)S(1)}, u32[]{:S(2)}, u32[]{:S(2)}) collective-permute-start(bf16[384,256]{1,0:T(8,128)(2,1)S(1)} %shard_map.46.refs_0_), channel_id=1, source_target_pairs={{0,3},{1,0},{2,1},{3,2},{4,7},{5,4},{6,5},{7,6},{8,11},{9,8},{10,9... | collective-permute-start | bytes 589832 | tf_op jit(solution)/shard_map/ppermute | solution.py:236
  14.0 15.0 %collective-permute-start.1 = (bf16[704,256]{1,0:T(8,128)(2,1)S(1)}, bf16[704,256]{1,0:T(8,128)(2,1)S(1)}, u32[]{:S(2)}, u32[]{:S(2)}) collective-permute-start(bf16[704,256]{1,0:T(8,128)(2,1)S(1)} %shard_map.47.refs_0_), channel_id=1, source_target_pairs={{0,1},{1,2},{2,3},{3,0},{4,5},{5,6},{6,7},{7,4},{8,9},{9,10},{10,1... | collective-permute-start | bytes 1081352 | tf_op jit(solution)/shard_map/ppermute | solution.py:236
  17.4 19.2 %collective-permute-start.6 = (bf16[704,256]{1,0:T(8,128)(2,1)S(1)}, bf16[704,256]{1,0:T(8,128)(2,1)S(1)}, u32[]{:S(2)}, u32[]{:S(2)}) collective-permute-start(bf16[704,256]{1,0:T(8,128)(2,1)S(1)} %shard_map.48.refs_0_), channel_id=1, source_target_pairs={{0,3},{1,0},{2,1},{3,2},{4,7},{5,4},{6,5},{7,6},{8,11},{9,8},{10,9... | collective-permute-start | bytes 1081352 | tf_op jit(solution)/shard_map/ppermute | solution.py:236
  29.5 15.8 %collective-permute-start.5 = (bf16[768,256]{1,0:T(8,128)(2,1)S(1)}, bf16[768,256]{1,0:T(8,128)(2,1)S(1)}, u32[]{:S(2)}, u32[]{:S(2)}) collective-permute-start(bf16[768,256]{1,0:T(8,128)(2,1)S(1)} %shard_map.51.refs_0_), channel_id=1, source_target_pairs={{0,1},{1,2},{2,3},{3,0},{4,5},{5,6},{6,7},{7,4},{8,9},{9,10},{10,1... | collective-permute-start | bytes 1179656 | tf_op jit(solution)/shard_map/ppermute | solution.py:236
  37.1 19.2 %collective-permute-start.8 = (bf16[768,256]{1,0:T(8,128)(2,1)S(1)}, bf16[768,256]{1,0:T(8,128)(2,1)S(1)}, u32[]{:S(2)}, u32[]{:S(2)}) collective-permute-start(bf16[768,256]{1,0:T(8,128)(2,1)S(1)} %shard_map.52.refs_7_), channel_id=1, source_target_pairs={{0,3},{1,0},{2,1},{3,2},{4,7},{5,4},{6,5},{7,6},{8,11},{9,8},{10,9... | collective-permute-start | bytes 1179656 | tf_op jit(solution)/shard_map/ppermute | solution.py:236
  38.4 18.6 %collective-permute-start.10 = (s16[400,256]{1,0:T(8,128)(2,1)S(1)}, s16[400,256]{1,0:T(8,128)(2,1)S(1)}, u32[]{:S(2)}, u32[]{:S(2)}) collective-permute-start(s16[400,256]{1,0:T(8,128)(2,1)S(1)} %get-tuple-element.35), channel_id=1, source_target_pairs={{0,8},{8,0},{16,24},{24,16},{1,9},{9,1},{17,25},{25,17},{2,10},{10... | collective-permute-start | bytes 614408 | tf_op jit(solution)/shard_map/ppermute | solution.py:240
  39.9 17.0 %collective-permute-start.11 = (s16[400,256]{1,0:T(8,128)(2,1)S(1)}, s16[400,256]{1,0:T(8,128)(2,1)S(1)}, u32[]{:S(2)}, u32[]{:S(2)}) collective-permute-start(s16[400,256]{1,0:T(8,128)(2,1)S(1)} %get-tuple-element.36), channel_id=1, source_target_pairs={{0,16},{8,24},{16,0},{24,8},{1,17},{9,25},{17,1},{25,9},{2,18},{10... | collective-permute-start | bytes 614408 | tf_op jit(solution)/shard_map/ppermute | solution.py:240
  41.4 15.5 %collective-permute-start.9 = (s16[400,256]{1,0:T(8,128)(2,1)S(1)}, s16[400,256]{1,0:T(8,128)(2,1)S(1)}, u32[]{:S(2)}, u32[]{:S(2)}) collective-permute-start(s16[400,256]{1,0:T(8,128)(2,1)S(1)} %get-tuple-element.34), channel_id=1, source_target_pairs={{0,24},{8,16},{16,8},{24,0},{1,25},{9,17},{17,9},{25,1},{2,26},{10... | collective-permute-start | bytes 614408 | tf_op jit(solution)/shard_map/ppermute | solution.py:240
  45.9 16.4 %collective-permute-start.7 = (bf16[640,256]{1,0:T(8,128)(2,1)S(1)}, bf16[640,256]{1,0:T(8,128)(2,1)S(1)}, u32[]{:S(2)}, u32[]{:S(2)}) collective-permute-start(bf16[640,256]{1,0:T(8,128)(2,1)S(1)} %shard_map.54.refs_0_), channel_id=1, source_target_pairs={{0,1},{1,2},{2,3},{3,0},{4,5},{5,6},{6,7},{7,4},{8,9},{9,10},{10,1... | collective-permute-start | bytes 983048 | tf_op jit(solution)/shard_map/ppermute | solution.py:236
  56.9 11.4 %collective-permute-start.13 = (bf16[640,256]{1,0:T(8,128)(2,1)S(1)}, bf16[640,256]{1,0:T(8,128)(2,1)S(1)}, u32[]{:S(2)}, u32[]{:S(2)}) collective-permute-start(bf16[640,256]{1,0:T(8,128)(2,1)S(1)} %shard_map.55.refs_3_), channel_id=1, source_target_pairs={{0,3},{1,0},{2,1},{3,2},{4,7},{5,4},{6,5},{7,6},{8,11},{9,8},{10,9... | collective-permute-start | bytes 983048 | tf_op jit(solution)/shard_map/ppermute | solution.py:236
  58.8 10.1 %collective-permute-start.15 = (s16[528,256]{1,0:T(8,128)(2,1)S(1)}, s16[528,256]{1,0:T(8,128)(2,1)S(1)}, u32[]{:S(2)}, u32[]{:S(2)}) collective-permute-start(s16[528,256]{1,0:T(8,128)(2,1)S(1)} %get-tuple-element.39), channel_id=1, source_target_pairs={{0,24},{8,16},{16,8},{24,0},{1,25},{9,17},{17,9},{25,1},{2,26},{10... | collective-permute-start | bytes 811016 | tf_op jit(solution)/shard_map/ppermute | solution.py:240
  61.3 10.1 %collective-permute-start.16 = (s16[528,256]{1,0:T(8,128)(2,1)S(1)}, s16[528,256]{1,0:T(8,128)(2,1)S(1)}, u32[]{:S(2)}, u32[]{:S(2)}) collective-permute-start(s16[528,256]{1,0:T(8,128)(2,1)S(1)} %get-tuple-element.40), channel_id=1, source_target_pairs={{0,8},{8,0},{16,24},{24,16},{1,9},{9,1},{17,25},{25,17},{2,10},{10... | collective-permute-start | bytes 811016 | tf_op jit(solution)/shard_map/ppermute | solution.py:240
  61.9 9.5 %collective-permute-start.17 = (s16[528,256]{1,0:T(8,128)(2,1)S(1)}, s16[528,256]{1,0:T(8,128)(2,1)S(1)}, u32[]{:S(2)}, u32[]{:S(2)}) collective-permute-start(s16[528,256]{1,0:T(8,128)(2,1)S(1)} %get-tuple-element.41), channel_id=1, source_target_pairs={{0,16},{8,24},{16,0},{24,8},{1,17},{9,25},{17,1},{25,9},{2,18},{10... | collective-permute-start | bytes 811016 | tf_op jit(solution)/shard_map/ppermute | solution.py:240
  62.9 11.8 %collective-permute-start.12 = (bf16[448,256]{1,0:T(8,128)(2,1)S(1)}, bf16[448,256]{1,0:T(8,128)(2,1)S(1)}, u32[]{:S(2)}, u32[]{:S(2)}) collective-permute-start(bf16[448,256]{1,0:T(8,128)(2,1)S(1)} %shard_map.58.refs_0_), channel_id=1, source_target_pairs={{0,1},{1,2},{2,3},{3,0},{4,5},{5,6},{6,7},{7,4},{8,9},{9,10},{10,1... | collective-permute-start | bytes 688136 | tf_op jit(solution)/shard_map/ppermute | solution.py:236
  68.8 6.4 %collective-permute-start.14 = (bf16[448,256]{1,0:T(8,128)(2,1)S(1)}, bf16[448,256]{1,0:T(8,128)(2,1)S(1)}, u32[]{:S(2)}, u32[]{:S(2)}) collective-permute-start(bf16[448,256]{1,0:T(8,128)(2,1)S(1)} %shard_map.59.refs_4_), channel_id=1, source_target_pairs={{0,3},{1,0},{2,1},{3,2},{4,7},{5,4},{6,5},{7,6},{8,11},{9,8},{10,9... | collective-permute-start | bytes 688136 | tf_op jit(solution)/shard_map/ppermute | solution.py:236
  73.1 13.6 %collective-permute-start.24 = (s16[1056,256]{1,0:T(8,128)(2,1)S(1)}, s16[1056,256]{1,0:T(8,128)(2,1)S(1)}, u32[]{:S(2)}, u32[]{:S(2)}) collective-permute-start(s16[1056,256]{1,0:T(8,128)(2,1)S(1)} %get-tuple-element.52), channel_id=1, source_target_pairs={{0,8},{8,0},{16,24},{24,16},{1,9},{9,1},{17,25},{25,17},{2,10},{10... | collective-permute-start | bytes 1622024 | tf_op jit(solution)/shard_map/ppermute | solution.py:240
  76.9 10.9 %collective-permute-start.23 = (s16[800,256]{1,0:T(8,128)(2,1)S(1)}, s16[800,256]{1,0:T(8,128)(2,1)S(1)}, u32[]{:S(2)}, u32[]{:S(2)}) collective-permute-start(s16[800,256]{1,0:T(8,128)(2,1)S(1)} %get-tuple-element.49), channel_id=1, source_target_pairs={{0,16},{8,24},{16,0},{24,8},{1,17},{9,25},{17,1},{25,9},{2,18},{10... | collective-permute-start | bytes 1228808 | tf_op jit(solution)/shard_map/ppermute | solution.py:240
  86.9 10.7 %collective-permute-start.26 = (s16[528,256]{1,0:T(8,128)(2,1)S(1)}, s16[528,256]{1,0:T(8,128)(2,1)S(1)}, u32[]{:S(2)}, u32[]{:S(2)}) collective-permute-start(s16[528,256]{1,0:T(8,128)(2,1)S(1)} %shard_map.66.after_ref), channel_id=1, source_target_pairs={{0,16},{8,24},{16,0},{24,8},{1,17},{9,25},{17,1},{25,9},{2,18},{10... | collective-permute-start | bytes 811016 | tf_op jit(solution)/shard_map/ppermute | solution.py:240
  87.9 9.8 %collective-permute-start.25 = (s16[400,256]{1,0:T(8,128)(2,1)S(1)}, s16[400,256]{1,0:T(8,128)(2,1)S(1)}, u32[]{:S(2)}, u32[]{:S(2)}) collective-permute-start(s16[400,256]{1,0:T(8,128)(2,1)S(1)} %shard_map.67.refs_3_), channel_id=1, source_target_pairs={{0,8},{8,0},{16,24},{24,16},{1,9},{9,1},{17,25},{25,17},{2,10},{10... | collective-permute-start | bytes 614408 | tf_op jit(solution)/shard_map/ppermute | solution.py:240
  89.4 8.5 %collective-permute-start.20 = (s16[272,256]{1,0:T(8,128)(2,1)S(1)}, s16[272,256]{1,0:T(8,128)(2,1)S(1)}, u32[]{:S(2)}, u32[]{:S(2)}) collective-permute-start(s16[272,256]{1,0:T(8,128)(2,1)S(1)} %get-tuple-element.46), channel_id=1, source_target_pairs={{0,24},{8,16},{16,8},{24,0},{1,25},{9,17},{17,9},{25,1},{2,26},{10... | collective-permute-start | bytes 417800 | tf_op jit(solution)/shard_map/ppermute | solution.py:240
  90.6 7.9 %collective-permute-start.21 = (s16[272,256]{1,0:T(8,128)(2,1)S(1)}, s16[272,256]{1,0:T(8,128)(2,1)S(1)}, u32[]{:S(2)}, u32[]{:S(2)}) collective-permute-start(s16[272,256]{1,0:T(8,128)(2,1)S(1)} %get-tuple-element.47), channel_id=1, source_target_pairs={{0,8},{8,0},{16,24},{24,16},{1,9},{9,1},{17,25},{25,17},{2,10},{10... | collective-permute-start | bytes 417800 | tf_op jit(solution)/shard_map/ppermute | solution.py:240
  92.1 6.9 %collective-permute-start.22 = (s16[272,256]{1,0:T(8,128)(2,1)S(1)}, s16[272,256]{1,0:T(8,128)(2,1)S(1)}, u32[]{:S(2)}, u32[]{:S(2)}) collective-permute-start(s16[272,256]{1,0:T(8,128)(2,1)S(1)} %get-tuple-element.48), channel_id=1, source_target_pairs={{0,16},{8,24},{16,0},{24,8},{1,17},{9,25},{17,1},{25,9},{2,18},{10... | collective-permute-start | bytes 417800 | tf_op jit(solution)/shard_map/ppermute | solution.py:240
  (9 other events, 34.6 us)
